TPU v7x, 32 devices: a whole 2x2x4 slice. The times are simulated.
32 devices in a mesh: groups: 2 (over x), seq: 8 (over z, y), head: 2 (over core).
Axes of the slice: x: 2, y: 2, z: 4, core: 2. Of those that a mesh axis runs over, the one named last changes fastest.
Arguments:
- queries: bfloat16 [512, 4096], P(('groups', 'seq'), 'head'), parts along dimension 0, may hold values from -24 to 24
- vision: bfloat16 [4096, 7680], P(('groups', 'seq')), parts along dimension 0, may hold values from -6 to 6
- key_matrix: bfloat16 [7680, 512], P('seq', 'head'), may hold values from -0.0625 to 0.0625
- value_matrix: bfloat16 [7680, 512], P('seq', 'head'), may hold values from -0.0625 to 0.0625
- out_weight: bfloat16 [4096, 8192], P('head', 'seq'), may hold values from -0.09375 to 0.09375
- residual: bfloat16 [512, 8192], P(('groups', 'head'), 'seq'), parts along dimension 0, may hold values from -4 to 4
- query_norm_gain: float32 [128], replicated, may hold values from 1 to 12
- key_norm_gain: float32 [128], replicated, may hold values from 1 to 12
- attn_gate: float32 [1], replicated, may hold values from 0.5 to 2
Outputs:
- mixed: bfloat16 [512, 8192], P(('groups', 'head'), 'seq'), parts along dimension 0
There are 2 independent parts, one for each index of `groups`. A program takes and returns all parts, laid end to end along the dimension named above; an argument that names none is the same for every part. Nothing has to cross between parts.
All inputs are finite; a program needn't handle non-finite values.
Results may differ from a plain program's by a relative error of at most 0.015.
The roundings to bfloat16 on the way count: a program that leaves them out, or rounds other values in their place, can miss the bound.
Values may be sent and summed in bfloat16 or wider, within the bound.
No kernel may reach another device: no remote copies, remote signals or barrier semaphores. Data moves between devices by JAX's collectives and lax.ppermute only.
A program may use at most 64 MiB of HBM per device.

v0:
```python
import jax
import jax.numpy as jnp
from jax import lax
from jax.sharding import PartitionSpec as P

HEAD_SIZE = 128


epsilon = 1e-05


def apply_norm(value_heads, gain):
    return (
        value_heads
        * lax.rsqrt(jnp.mean(value_heads * value_heads, axis=-1, keepdims=True) + epsilon)
        * gain
    )


def body(
    queries,
    vision,
    key_matrix,
    value_matrix,
    out_weight,
    residual,
    query_norm_gain,
    key_norm_gain,
    attn_gate,
):
    vision_rows = vision.shape[0]
    column_count = key_matrix.shape[1]
    expanded_keys = jnp.dot(
        vision,
        lax.all_gather(key_matrix, "seq", axis=0, tiled=True),
        preferred_element_type=jnp.float32,
    )
    expanded_values = jnp.dot(
        vision,
        lax.all_gather(value_matrix, "seq", axis=0, tiled=True),
        preferred_element_type=jnp.float32,
    )
    kv_local = column_count // HEAD_SIZE
    key_heads = apply_norm(
        expanded_keys.reshape(vision_rows, kv_local, HEAD_SIZE), key_norm_gain
    ).astype(jnp.bfloat16)
    value_heads = expanded_values.reshape(vision_rows, kv_local, HEAD_SIZE).astype(jnp.bfloat16)
    text_rows = queries.shape[0]
    heads_local = queries.shape[1] // HEAD_SIZE
    heads_per_group = heads_local // kv_local
    norm_result = apply_norm(
        queries.astype(jnp.float32).reshape(text_rows, kv_local, heads_per_group, HEAD_SIZE),
        query_norm_gain,
    ).astype(jnp.bfloat16)
    scale = HEAD_SIZE ** (-0.5)
    start_max = jnp.full((text_rows, kv_local, heads_per_group), -1e30, jnp.float32)
    start_den = jnp.zeros((text_rows, kv_local, heads_per_group), jnp.float32)
    start_num = jnp.zeros((text_rows, kv_local, heads_per_group, HEAD_SIZE), jnp.float32)
    key_piece = lax.all_gather(key_heads, "seq", axis=0, tiled=True)
    value_piece = lax.all_gather(value_heads, "seq", axis=0, tiled=True)
    piece_rows = key_piece.shape[0]
    rows_per_block = 512
    key_blocks = key_piece.reshape(
        piece_rows // rows_per_block, rows_per_block, kv_local, HEAD_SIZE
    )
    value_blocks = value_piece.reshape(
        piece_rows // rows_per_block, rows_per_block, kv_local, HEAD_SIZE
    )

    def advance(state_now, both):
        maxima, denominator, numerator = state_now
        scores = (
            jnp.einsum("tgqd,rgd->tgqr", norm_result, both[0], preferred_element_type=jnp.float32)
            * scale
        )
        new_max = jnp.maximum(maxima, jnp.max(scores, axis=-1))
        rescale = jnp.exp(maxima - new_max)
        weights = jnp.exp(scores - new_max[..., None])
        denominator = denominator * rescale + jnp.sum(weights, axis=-1)
        numerator = numerator * rescale[..., None] + jnp.einsum(
            "tgqr,rgd->tgqd",
            weights.astype(jnp.bfloat16),
            both[1],
            preferred_element_type=jnp.float32,
        )
        return ((new_max, denominator, numerator), None)

    maxima, denominator, numerator = lax.scan(
        advance, (start_max, start_den, start_num), (key_blocks, value_blocks)
    )[0]
    attended = (
        (numerator / denominator[..., None])
        .astype(jnp.bfloat16)
        .reshape(text_rows, heads_local * HEAD_SIZE)
    )
    partial_out = jnp.dot(
        lax.all_gather(attended, "seq", axis=0, tiled=True),
        out_weight,
        preferred_element_type=jnp.float32,
    )
    projected = lax.psum_scatter(
        partial_out.astype(jnp.bfloat16), "head", scatter_dimension=0, tiled=True
    ).astype(jnp.float32)
    return (residual.astype(jnp.float32) + jnp.tanh(attn_gate[0]) * projected).astype(jnp.bfloat16)


def solution(mesh):
    in_specs = (
        P(("groups", "seq"), "head"),
        P(("groups", "seq"), None),
        P("seq", "head"),
        P("seq", "head"),
        P("head", "seq"),
        P(("groups", "head"), "seq"),
        P(),
        P(),
        P(),
    )
    out_specs = P(("groups", "head"), "seq")
    return jax.shard_map(body, mesh=mesh, in_specs=in_specs, out_specs=out_specs, check_vma=False)
```

profile of v0, /device:TPU:0, one launch (start us, length us, event | category | flops | bytes accessed | tf_op | source)
XLA Modules:
  0.0 307.3 jit_solution(3217196021253669261)
XLA Ops:
  6.5 0.0 all-gather.6.cloned.1.call-start
  6.5 0.7 all-gather.6.cloned.1.call-update
  7.3 0.0 all-gather.10.cloned.1.call-start
  7.3 0.7 all-gather.10.cloned.1.call-update
  8.0 0.0 copy-start.2
  8.0 0.0 all-gather.8.cloned.1.call-start
  8.1 74.3 %all-gather.6.cloned.1.call-done = bf16[7680,256]{1,0:T(8,128)(2,1)} async-done(((bf16[960,256]{1,0:T(8,128)(2,1)}), bf16[7680,256]{1,0:T(8,128)(2,1)}) %all-gather.6.cloned.1.call-update) | async-done | bytes 3932176 | tf_op jit(solution)/shard_map/all_gather | solution.py:35
  82.4 5.0 %multiply_reduce_fusion.1 = (f32[256,2]{0,1:T(2,128)S(1)}, f32[256,256]{0,1:T(8,128)S(1)}) fusion(bf16[256,7680]{1,0:T(8,128)(2,1)} %param.12, bf16[7680,256]{1,0:T(8,128)(2,1)} %all-gather.6.cloned.1.call-done), kind=kOutput, calls=%fused_computation.27 | convolution fusion | flops 1006763520 | bytes 8128512 | tf_op jit(solution)/shard_map/dot_general | solution.py:33
  87.3 0.1 copy.23
  87.5 0.0 copy-done.2
  87.5 0.8 multiply_convert_fusion.1
  88.3 0.0 all-gather.8.cloned.1.call-update
  88.3 0.0 copy-start.1
  88.3 0.0 copy-start.3
  88.3 0.0 all-gather.12.cloned.1.call-start
  88.4 64.7 %all-gather.10.cloned.1.call-done = bf16[7680,256]{1,0:T(8,128)(2,1)} async-done(((bf16[960,256]{1,0:T(8,128)(2,1)}), bf16[7680,256]{1,0:T(8,128)(2,1)}) %all-gather.10.cloned.1.call-update) | async-done | bytes 3932176 | tf_op jit(solution)/shard_map/all_gather | solution.py:40
  153.1 4.9 %convolution_convert_fusion.1 = bf16[256,256]{0,1:T(8,128)(2,1)S(1)} fusion(bf16[256,7680]{1,0:T(8,128)(2,1)} %param.12, bf16[7680,256]{1,0:T(8,128)(2,1)} %all-gather.10.cloned.1.call-done), kind=kOutput, calls=%fused_computation.20 | convolution fusion | flops 1006698496 | bytes 7995392 | tf_op jit(solution)/shard_map/dot_general | solution.py:38
  158.0 0.7 copy.26
  158.7 0.0 all-gather.12.cloned.1.call-update
  158.8 0.0 all-gather.14.cloned.1.call-start
  158.8 0.0 copy-done.1
  158.9 0.2 multiply_reduce_fusion
  159.1 0.1 copy.24
  159.2 0.1 copy.25
  159.3 0.0 copy-done.3
  159.3 0.1 multiply_convert_fusion
  159.5 34.3 %all-gather.8.cloned.1.call-done = bf16[2048,2,128]{2,0,1:T(8,128)(2,1)} async-done(((bf16[256,2,128]{2,0,1:T(8,128)(2,1)}), bf16[2048,2,128]{2,0,1:T(8,128)(2,1)}) %all-gather.8.cloned.1.call-update) | async-done | bytes 1048592 | tf_op jit(solution)/shard_map/all_gather | solution.py:59
  193.8 41.0 %all-gather.12.cloned.1.call-done = bf16[2048,2,128]{2,0,1:T(8,128)(2,1)} async-done(((bf16[256,2,128]{2,0,1:T(8,128)(2,1)}), bf16[2048,2,128]{2,0,1:T(8,128)(2,1)}) %all-gather.12.cloned.1.call-update) | async-done | bytes 1048592 | tf_op jit(solution)/shard_map/all_gather | solution.py:60
  234.8 12.4 %while.15 = (s32[]{:T(128)}, f32[32,2,8]{0,2,1:T(8,128)S(1)}, f32[32,2,8]{0,2,1:T(8,128)S(1)}, f32[32,2,8,128]{3,0,2,1:T(8,128)S(1)}, bf16[4,512,2,128]{3,1,0,2:...) while((s32[]{:T(128)}, f32[32,2,8]{0,2,1:T(8,128)S(1)}, ...), condition=%wide.region_5.6_spmd.clone, body=%wide.region_2.5_spmd.clone.sunk | while | flops 135989760 | bytes 4358265 | solution.py:88
  234.8 1.3 fusion.31
  236.2 0.3 fusion.32
  236.5 1.4 fusion.34
  237.9 1.3 fusion.31
  239.3 0.3 fusion.32
  239.6 1.4 fusion.34
  241.1 1.3 fusion.31
  242.4 0.3 fusion.32
  242.7 1.4 fusion.34
  244.2 1.3 fusion.31
  245.5 0.3 fusion.32
  245.8 1.4 fusion.34
  247.3 0.1 divide_convert_fusion
  247.4 0.1 copy.30
  247.5 0.7 copy.38
  248.2 0.0 all-gather.14.cloned.1.call-update
  248.2 0.0 copy-start
  248.2 0.0 reduce-scatter.2.cloned.1.call-start
  248.3 39.0 %all-gather.14.cloned.1.call-done = bf16[256,2048]{1,0:T(8,128)(2,1)} async-done(((bf16[32,2048]{1,0:T(8,128)(2,1)}), bf16[256,2048]{1,0:T(8,128)(2,1)}) %all-gather.14.cloned.1.call-update) | async-done | bytes 1048592 | tf_op jit(solution)/shard_map/all_gather | solution.py:97
  287.2 4.6 %convolution_convert_fusion = bf16[256,1024]{1,0:T(8,128)(2,1)} fusion(bf16[256,2048]{1,0:T(8,128)(2,1)} %all-gather.14.cloned.1.call-done, bf16[2048,1024]{1,0:T(8,128)(2,1)} %param.15), kind=kOutput, calls=%fused_computation.19 | convolution fusion | flops 1074003968 | bytes 5767168 | tf_op jit(solution)/shard_map/dot_general | solution.py:96
  291.8 0.0 reduce-scatter.2.cloned.1.call-update
  292.5 6.2 %reduce-scatter.2.cloned.1.call-done = bf16[128,1024]{1,0:T(8,128)(2,1)} async-done(((bf16[256,1024]{1,0:T(8,128)(2,1)}), bf16[128,1024]{1,0:T(8,128)(2,1)}) %reduce-scatter.2.cloned.1.call-update) | async-done | bytes 262160 | tf_op jit(solution)/shard_map/reduce_scatter | solution.py:101
  298.7 0.0 copy-done
  298.7 1.7 add_convert_fusion
  (20 shorter events, 0.2 us)
Async XLA Ops:
  6.5 75.8 %all-gather.6.cloned.1.call-start = ((), (), s32[]{:S(2)}) async-start(), calls=%async_computation.1 | async-start | bytes 4423680 | tf_op jit(solution)/shard_map/all_gather | solution.py:35
  7.3 145.8 %all-gather.10.cloned.1.call-start = ((), (), s32[]{:S(2)}) async-start(), calls=%async_computation.3 | async-start | bytes 4423680 | tf_op jit(solution)/shard_map/all_gather | solution.py:40
  8.0 79.5 %copy-start.2 = (f32[128]{0:T(128)S(1)}, f32[128]{0:T(128)}, u32[]{:S(2)}) copy-start(f32[128]{0:T(128)} %param.18) | copy-start | bytes 1540
  8.0 185.8 %all-gather.8.cloned.1.call-start = ((), (), s32[]{:S(2)}) async-start(), calls=%async_computation.2 | async-start | bytes 1179648 | tf_op jit(solution)/shard_map/all_gather | solution.py:59
  88.3 70.5 %copy-start.1 = (bf16[32,2048]{1,0:T(8,128)(2,1)S(1)}, bf16[32,2048]{1,0:T(8,128)(2,1)}, u32[]{:S(2)}) copy-start(bf16[32,2048]{1,0:T(8,128)(2,1)} %param.11) | copy-start | bytes 393220
  88.3 71.0 %copy-start.3 = (f32[128]{0:T(128)S(1)}, f32[128]{0:T(128)}, u32[]{:S(2)}) copy-start(f32[128]{0:T(128)} %param.17) | copy-start | bytes 1540
  88.3 146.5 %all-gather.12.cloned.1.call-start = ((), (), s32[]{:S(2)}) async-start(), calls=%async_computation.4 | async-start | bytes 1179648 | tf_op jit(solution)/shard_map/all_gather | solution.py:60
  158.8 128.5 %all-gather.14.cloned.1.call-start = ((), (), s32[]{:S(2)}) async-start(), calls=%async_computation.5 | async-start | bytes 1179648 | tf_op jit(solution)/shard_map/all_gather | solution.py:97
  248.2 50.5 %copy-start = (bf16[128,1024]{1,0:T(8,128)(2,1)S(1)}, bf16[128,1024]{1,0:T(8,128)(2,1)}, u32[]{:S(2)}) copy-start(bf16[128,1024]{1,0:T(8,128)(2,1)} %param.16) | copy-start | bytes 786436
  248.2 50.5 %reduce-scatter.2.cloned.1.call-start = ((), (), s32[]{:S(2)}) async-start(), calls=%async_computation.6 | async-start | bytes 786432 | tf_op jit(solution)/shard_map/reduce_scatter | solution.py:101
Sparse Core Ops, SparseCore 0:
  9.5 72.7 all-gather.5
  84.6 68.4 all-gather.9
  155.2 38.5 all-gather.7
  195.9 38.9 all-gather.11
  248.3 38.8 all-gather.13
  292.0 6.7 reduce-scatter.1
where the time goes:
time: 308 us; the launch traced here: 307 us
  waiting for transfers between devices  261 us (85%)
  matrix products  25.4 us (8%)
  between operations  14.3 us (5%)
  other arithmetic  4.31 us (1%)
    all_gather x1, waiting for transfers between devices, body(): lax.all_gather(key_matrix, 'seq', axis=0, tiled=True)  74.3 us
    all_gather x1, waiting for transfers between devices, body(): lax.all_gather(value_matrix, 'seq', axis=0, tiled=True)  64.7 us
    all_gather x1, waiting for transfers between devices, body(): value_piece = lax.all_gather(value_heads, 'seq', axis=0, tiled=True)  41 us
    all_gather x1, waiting for transfers between devices, body(): lax.all_gather(attended, 'seq', axis=0, tiled=True)  39 us
    all_gather x1, waiting for transfers between devices, body(): key_piece = lax.all_gather(key_heads, 'seq', axis=0, tiled=True)  34.3 us
    reduce_scatter x1, waiting for transfers between devices, body(): lax.psum_scatter(partial_out.astype(jnp.bfloat16), 'head', scatter_dimens...  6.19 us
  transfers between devices with their start and end apart: 6, of which 6 were waited for; matrix products, arithmetic and copies ran while one was open for 4% of the time, Pallas kernels for 0%

commit v1 on v0

v1 whole, which is shorter than its diff:
```python
import functools

import jax
import jax.numpy as jnp
from jax import lax
from jax.sharding import PartitionSpec as P

HEAD_SIZE = 128
epsilon = 1e-05
AXES = ("groups", "seq", "head")


def body(
    sizes,
    queries,
    vision,
    key_matrix,
    value_matrix,
    out_weight,
    residual,
    query_norm_gain,
    key_norm_gain,
    attn_gate,
):
    groups, seq, cores = sizes
    pairs = seq // 2
    group = lax.axis_index("groups")
    place = lax.axis_index("seq")
    core = lax.axis_index("head")
    side = place % 2
    f32, bf16 = jnp.float32, jnp.bfloat16

    def plane_shift(array, by_group, by_side):
        perm = []
        for g in range(groups):
            for s in range(seq):
                for c in range(cores):
                    to_g = (g + by_group) % groups
                    to_s = s // 2 * 2 + (s + by_side) % 2
                    perm.append(
                        ((g * seq + s) * cores + c, (to_g * seq + to_s) * cores + c)
                    )
        return lax.ppermute(array, AXES, perm)

    def core_swap(array):
        return lax.ppermute(array, "head", [(c, (c + 1) % cores) for c in range(cores)])

    lines = [[2 * z + y for z in range(pairs)] for y in range(2)]

    def gather_pairs(array):
        return lax.all_gather(array, "seq", axis=0, tiled=True, axis_index_groups=lines)

    offsets = [(g, y) for g in range(groups) for y in range(2)]

    slab = key_matrix.shape[0]
    part = slab // groups

    def prepare(matrix):
        mine = lax.dynamic_slice_in_dim(matrix, group * part, part, axis=0)
        half = mine.shape[1] // 2
        return jnp.where(side == 0, mine, jnp.roll(mine, half, axis=1))

    key_weight = gather_pairs(prepare(key_matrix))
    value_weight = gather_pairs(prepare(value_matrix))

    rows_q = queries.shape[0]
    half_q = queries.shape[1] // 2
    q_own = lax.dynamic_slice_in_dim(queries, side * half_q, half_q, axis=1)
    q_send = lax.dynamic_slice_in_dim(queries, (1 - side) * half_q, half_q, axis=1)
    q_recv = plane_shift(q_send, 0, 1)
    q_pair = jnp.where(
        side == 0,
        jnp.concatenate([q_own, q_recv], axis=0),
        jnp.concatenate([q_recv, q_own], axis=0),
    ).astype(f32)
    heads = half_q // HEAD_SIZE
    q_heads = q_pair.reshape(2 * rows_q, heads, HEAD_SIZE).transpose(1, 0, 2)
    normed = (
        q_heads
        * lax.rsqrt(jnp.mean(q_heads * q_heads, axis=-1, keepdims=True) + epsilon)
        * query_norm_gain
    ).astype(bf16)
    normed = normed.reshape(heads * 2 * rows_q, HEAD_SIZE)

    rows = vision.shape[0]
    half = rows // cores
    classes = (
        vision.reshape(rows, pairs, 2, groups, part)
        .transpose(3, 2, 0, 1, 4)
        .reshape(groups, 2, cores, half, pairs * part)
    )

    def take(by_group, by_side, which_core):
        return lax.dynamic_slice(
            classes,
            ((group + by_group) % groups, (side + by_side) % 2, which_core, 0, 0),
            (1, 1, 1, half, pairs * part),
        ).reshape(half, pairs * part)

    received = [plane_shift(take(g, y, core), g, y) for g, y in offsets[1:]]
    firsts = jnp.concatenate([take(0, 0, core)] + received, axis=0)
    seconds = jnp.concatenate(
        [take(0, 0, 1 - core), core_swap(jnp.concatenate(received, axis=0))], axis=0
    )

    def project(weight, dtype):
        first = jnp.dot(firsts, weight, preferred_element_type=f32)
        second = jnp.dot(seconds, weight, preferred_element_type=f32)
        both = jnp.stack(
            [
                first.reshape(groups, 2, half, 2, HEAD_SIZE),
                second.reshape(groups, 2, half, 2, HEAD_SIZE),
            ],
            axis=2,
        )
        total = None
        for g, y in offsets:
            piece = jnp.concatenate(
                [both[(-g) % groups, y, :, :, y, :], both[(-g) % groups, 1 - y, :, :, y, :]],
                axis=0,
            ).reshape(2 * rows, HEAD_SIZE)
            if (g, y) != (0, 0):
                piece = plane_shift(piece.astype(dtype), g, y).astype(f32)
            total = piece if total is None else total + piece
        return total

    keys = project(key_weight, f32)
    keys = (
        keys * lax.rsqrt(jnp.mean(keys * keys, axis=-1, keepdims=True) + epsilon) * key_norm_gain
    ).astype(bf16)
    keys = gather_pairs(keys)
    values = gather_pairs(project(value_weight, bf16).astype(bf16))

    scores = jnp.dot(normed, keys.T, preferred_element_type=f32) * HEAD_SIZE ** (-0.5)
    weights = jnp.exp(scores - jnp.max(scores, axis=-1, keepdims=True))
    denominator = jnp.sum(weights, axis=-1, keepdims=True)
    numerator = jnp.dot(weights.astype(bf16), values, preferred_element_type=f32)
    attended = (numerator / denominator).astype(bf16)
    attended = (
        attended.reshape(heads, 2 * rows_q, HEAD_SIZE)
        .transpose(1, 0, 2)
        .reshape(2 * rows_q, heads * HEAD_SIZE)
    )
    attended = gather_pairs(attended)
    other = plane_shift(attended, 0, 1)
    depth = heads * HEAD_SIZE
    weight_own = lax.dynamic_slice_in_dim(out_weight, side * depth, depth, axis=0)
    weight_other = lax.dynamic_slice_in_dim(out_weight, (1 - side) * depth, depth, axis=0)
    projected = jnp.dot(attended, weight_own, preferred_element_type=f32) + jnp.dot(
        other, weight_other, preferred_element_type=f32
    )
    out_rows = residual.shape[0]
    send = lax.dynamic_slice_in_dim(projected, (1 - core) * out_rows, out_rows, axis=0)
    mine = lax.dynamic_slice_in_dim(projected, core * out_rows, out_rows, axis=0)
    mine = mine + core_swap(send.astype(bf16)).astype(f32)
    return (residual.astype(f32) + jnp.tanh(attn_gate[0]) * mine).astype(bf16)


def solution(mesh):
    in_specs = (
        P(("groups", "seq"), "head"),
        P(("groups", "seq"), None),
        P("seq", "head"),
        P("seq", "head"),
        P("head", "seq"),
        P(("groups", "head"), "seq"),
        P(),
        P(),
        P(),
    )
    out_specs = P(("groups", "head"), "seq")
    sizes = tuple(mesh.shape[axis] for axis in AXES)
    return jax.shard_map(
        functools.partial(body, sizes),
        mesh=mesh,
        in_specs=in_specs,
        out_specs=out_specs,
        check_vma=False,
    )
```

time: 308 us -> 190 us (0.62)
  waiting for transfers between devices: 261 us -> 16.1 us
  blocking collectives: 0 us -> 87.4 us
  local copies, waits for them, and re-layouts: 1.9 us -> 46.8 us
  starting transfers between devices: 0.2 us -> 14.3 us
  between operations: 14.3 us -> 1.05 us
  matrix products: 25.4 us -> 17.3 us
    all_gather x5 -> x0, waiting for transfers between devices: 253 us -> none  [the longest x1 74.3 us: body(): lax.all_gather(key_matrix, 'seq', axis=0, tiled=True)]
    all_gather x0 -> x5, blocking collectives: none -> 87.4 us  [gather_pairs(): lax.all_gather(array, 'seq', axis=0, tiled=True, axis_index_groups=lines)]
    dynamic_slice x0 -> x7, local copies, waits for them, and re-layouts: none -> 21.3 us  [the longest x6 19.8 us: take(): lax.dynamic_slice(classes, ((group + by_group) % groups, (side + by_side)...]
    ppermute x0 -> x13, waiting for transfers between devices: none -> 16.1 us  [the longest x11 15.3 us: plane_shift(): return lax.ppermute(array, AXES, perm)]
    ppermute x0 -> x13, starting transfers between devices: none -> 14.3 us  [the longest x11 14.3 us: plane_shift(): return lax.ppermute(array, AXES, perm)]
    reshape x1 -> x2, local copies, waits for them, and re-layouts: 0.13 us -> 8.42 us  [the longest x1 8.33 us: body(): classes = vision.reshape(rows, pairs, 2, groups, part).transpose(3, 2, 0,...]
    dot_general x11 -> x8, matrix products: 25.4 us -> 17.3 us  [the longest x2 5.81 us: project(): second = jnp.dot(seconds, weight, preferred_element_type=f32)]
    unnamed x11 -> x18, local copies, waits for them, and re-layouts: 0.8 us -> 7.27 us
  transfers between devices with their start and end apart: 6 -> 13, of which waited for: 6 -> 4; matrix products, arithmetic and copies ran while one was open for 4% -> 12% of each run, Pallas kernels for 0% -> 0%
where the time goes in v1:
time: 190 us; the launch traced here: 189 us
  blocking collectives  87.4 us (46%)
  local copies, waits for them, and re-layouts  46.8 us (25%)
  matrix products  17.3 us (9%)
  waiting for transfers between devices  16.1 us (8%)
  starting transfers between devices  14.3 us (8%)
  other arithmetic  6.14 us (3%)
    all_gather x5, blocking collectives, gather_pairs(): lax.all_gather(array, 'seq', axis=0, tiled=True, axis_index_groups=lines)  87.4 us
    dynamic_slice x6, local copies, waits for them, and re-layouts, take(): lax.dynamic_slice(classes, ((group + by_group) % groups, (side + by_side)...  19.8 us
    ppermute x11, waiting for transfers between devices, plane_shift(): return lax.ppermute(array, AXES, perm)  15.3 us
    ppermute x11, starting transfers between devices, plane_shift(): return lax.ppermute(array, AXES, perm)  14.3 us
    reshape x1, local copies, waits for them, and re-layouts, body(): classes = vision.reshape(rows, pairs, 2, groups, part).transpose(3, 2, 0,...  8.33 us
    unnamed x18, local copies, waits for them, and re-layouts  7.27 us
    dot_general x2, matrix products, project(): second = jnp.dot(seconds, weight, preferred_element_type=f32)  5.81 us
    dot_general x2, matrix products, project(): first = jnp.dot(firsts, weight, preferred_element_type=f32)  5.24 us
  transfers between devices with their start and end apart: 13, of which 4 were waited for; matrix products, arithmetic and copies ran while one was open for 12% of the time, Pallas kernels for 0%

profile of v1, /device:TPU:0, one launch (start us, length us, event | category | flops | bytes accessed | tf_op | source)
XLA Modules:
  0.0 189.2 jit_solution(8906189046797346903)
XLA Ops:
  0.0 6.3 %copy.61 = bf16[256,7680]{0,1:T(8,128)(2,1)} copy(bf16[256,7680]{1,0:T(8,128)(2,1)} %param.10) | data formatting | bytes 7864320 | tf_op args[1]
  6.3 4.2 %copy.62 = bf16[2,2,256,4,480]{2,4,3,1,0:T(8,128)(2,1)} copy(bf16[2,2,256,4,480]{2,4,0,1,3:T(8,128)(2,1)} %bitcast.96) | data formatting | bytes 7864320 | tf_op jit(solution)/shard_map/transpose | solution.py:89
  10.5 8.3 %reshape.79 = bf16[2,2,2,128,1920]{3,2,4,1,0:T(2,128)(2,1)} reshape(bf16[2,2,256,4,480]{2,4,3,1,0:T(8,128)(2,1)} %copy.62) | data formatting | bytes 7864320 | tf_op jit(solution)/shard_map/reshape | solution.py:90
  18.8 8.4 %constant_dynamic-slice_fusion.2 = (bf16[1,1,1,128,1920]{3,2,4,1,0:T(2,128)(2,1)S(1)}, bf16[1,1,1,128,1920]{3,2,4,1,0:T(2,128)(2,1)S(1)}, bf16[1,1,1,128,1920]{3...) fusion(bf16[2,2,2,128,1920]{3,2,4,1,0:T(2,128)(2,1)} %reshape.79, ...), kind=kLoop, calls=%fused_computation.67 | loop fusion | bytes 4915224 | tf_op jit(solution)/shard_map/dynamic_slice | solution.py:94
  27.2 3.1 %copy.64 = bf16[1,1,1,128,1920]{4,3,2,1,0:T(8,128)(2,1)} copy(bf16[1,1,1,128,1920]{3,2,4,1,0:T(2,128)(2,1)} %get-tuple-element.10) | data formatting | bytes 983040 | tf_op jit(solution)/shard_map/dynamic_slice | solution.py:94
  30.4 3.0 %collective-permute-start.1 = (bf16[128,1920]{1,0:T(8,128)(2,1)}, bf16[128,1920]{1,0:T(8,128)(2,1)}, u32[]{:S(2)}, u32[]{:S(2)}) collective-permute-start(bf16[128,1920]{1,0:T(8,128)(2,1)} %bitcast.112), channel_id=1, source_target_pairs={{0,2},{1,3},{2,0},{3,1},{4,6},{5,7},{6,4},{7,5},{8,10},{9,11},{10,... | collective-permute-start | bytes 1474568 | tf_op jit(solution)/shard_map/ppermute | solution.py:43
  33.3 3.0 %copy.65 = bf16[1,1,1,128,1920]{4,3,2,1,0:T(8,128)(2,1)} copy(bf16[1,1,1,128,1920]{3,2,4,1,0:T(2,128)(2,1)} %get-tuple-element.9) | data formatting | bytes 983040 | tf_op jit(solution)/shard_map/dynamic_slice | solution.py:94
  36.4 1.3 collective-permute-start.2
  37.7 1.8 copy.66
  39.5 0.1 collective-permute-start.3
  39.6 1.5 constant_dynamic-slice_fusion.7
  41.1 2.0 %collective-permute-start = (bf16[32,1024]{1,0:T(8,128)(2,1)}, bf16[32,1024]{1,0:T(8,128)(2,1)}, u32[]{:S(2)}, u32[]{:S(2)}) collective-permute-start(bf16[32,1024]{1,0:T(8,128)(2,1)} %get-tuple-element.32), channel_id=1, source_target_pairs={{0,2},{1,3},{2,0},{3,1},{4,6},{5,7},{6,4},{7,5},{8,10},{9,11},{10,... | collective-permute-start | bytes 196616 | tf_op jit(solution)/shard_map/ppermute | solution.py:43
  43.2 0.1 maximum_select_fusion
  43.3 22.1 %all_gather.15 = bf16[1920,256]{1,0:T(8,128)(2,1)S(1)} all-gather(bf16[480,256]{1,0:T(8,128)(2,1)S(1)} %maximum_select_fusion), channel_id=1, replica_groups={{0,4,8,12},{2,6,10,14},{1,5,9,13},{3,7,11,15},{16,20,24,28},{18,22,26,3..., dimensions={0}, use_global_device_ids=true | all-gather | bytes 1228800 | tf_op jit(solution)/shard_map/all_gather | solution.py:51
  65.3 1.2 fusion.41
  66.6 1.0 maximum_select_fusion.1
  67.6 0.0 copy-start.4
  67.6 19.4 %all_gather.17 = bf16[1920,256]{1,0:T(8,128)(2,1)} all-gather(bf16[480,256]{1,0:T(8,128)(2,1)S(1)} %maximum_select_fusion.1), channel_id=1, replica_groups={{0,4,8,12},{2,6,10,14},{1,5,9,13},{3,7,11,15},{16,20,24,28},{18,22,26,3..., dimensions={0}, use_global_device_ids=true | all-gather | bytes 1228800 | tf_op jit(solution)/shard_map/all_gather | solution.py:51
  87.0 1.7 copy.67
  88.7 1.7 copy.63
  90.5 0.9 copy.80
  91.3 0.1 fusion.28
  91.5 0.1 copy.58
  91.6 0.0 collective-permute-done.3
  91.6 2.6 %pad_maximum_fusion.2 = bf16[384,1920]{1,0:T(8,128)(2,1)} fusion(bf16[128,1920]{1,0:T(8,128)(2,1)} %collective-permute-done.3, bf16[128,1920]{1,0:T(8,128)(2,1)} %collective-permute-done.2, bf16[128,1920]{1,0:T(8,128)(2,1)} %collective-permute-done.1), kind=kLoop, calls=%fused_computation.13 | loop fusion | flops 4423680 | bytes 2949120 | tf_op jit(solution)/shard_map/concatenate | solution.py:103
  94.1 0.1 copy.59
  94.2 0.1 fusion.30
  94.4 3.1 %fusion.22 = f32[512,256]{1,0:T(8,128)} fusion(bf16[1920,256]{1,0:T(8,128)(2,1)S(1)} %all_gather.15, bf16[128,1920]{1,0:T(8,128)(2,1)} %collective-permute-done.3, bf16[128,1920]{1,0:T(8,128)(2,1)} %collective-permute-done.2, bf16[128,1920]{1,0:T(8,128)(2,1)} %collective-permute-done.1, bf16[128,1920]{1,0:T(8,128)(2,1)} %bitcast.117), kind=kOutput, calls=%fused_computation.24 | convolution fusion | flops 511180800 | bytes 3473408 | tf_op jit(solution)/shard_map/dot_general | solution.py:107
  97.5 1.3 stack_reshape.12
  98.8 2.2 %fusion.21 = f32[512,256]{1,0:T(8,128)S(1)} fusion(bf16[1920,256]{1,0:T(8,128)(2,1)S(1)} %copy-done.1, bf16[128,1920]{1,0:T(8,128)(2,1)} %collective-permute-done.3, bf16[128,1920]{1,0:T(8,128)(2,1)} %collective-permute-done.2, bf16[128,1920]{1,0:T(8,128)(2,1)} %collective-permute-done.1, bf16[128,1920]{1,0:T(8,128)(2,1)} %bitcast.118), kind=kOutput, calls=%fused_computation.23 | convolution fusion | flops 511180800 | bytes 3473408 | tf_op jit(solution)/shard_map/dot_general | solution.py:107
  101.0 0.3 stack_reshape.14
  101.4 3.3 %fusion.13 = f32[512,256]{1,0:T(8,128)} fusion(bf16[1920,256]{1,0:T(8,128)(2,1)} %all_gather.17, bf16[384,1920]{1,0:T(8,128)(2,1)} %collective-permute-done.4, bf16[128,1920]{1,0:T(8,128)(2,1)} %bitcast.115), kind=kOutput, calls=%fused_computation.15 | convolution fusion | flops 507248640 | bytes 3473408 | tf_op jit(solution)/shard_map/dot_general | solution.py:108
  104.7 1.3 stack_reshape.15
  106.0 0.1 convert.21
  106.1 2.5 %fusion.14 = f32[512,256]{1,0:T(8,128)S(1)} fusion(bf16[1920,256]{1,0:T(8,128)(2,1)} %copy-done, bf16[384,1920]{1,0:T(8,128)(2,1)} %collective-permute-done.4, bf16[128,1920]{1,0:T(8,128)(2,1)} %bitcast.116), kind=kOutput, calls=%fused_computation.16 | convolution fusion | flops 507248640 | bytes 3473408 | tf_op jit(solution)/shard_map/dot_general | solution.py:108
  108.7 0.3 stack_reshape.13
  108.9 0.1 constant_dynamic-update-slice_fusion
  109.0 0.9 fusion.39
  109.9 0.0 copy-start.5
  109.9 0.5 collective-permute-start.5
  110.5 1.5 collective-permute-start.6
  112.0 1.5 collective-permute-start.8
  113.6 0.8 collective-permute-start.9
  114.4 1.4 collective-permute-start.10
  115.8 5.7 %collective-permute-done.8 = bf16[512,128]{1,0:T(8,128)(2,1)S(1)} collective-permute-done((bf16[512,128]{1,0:T(8,128)(2,1)S(1)}, bf16[512,128]{1,0:T(8,128)(2,1)S(1)}, u32[]{:S(2)}, u32[]{:S(2)}) %collective-permute-start.8) | collective-permute-done | bytes 131104 | tf_op jit(solution)/shard_map/ppermute | solution.py:43
  121.5 1.3 collective-permute-start.7
  122.8 3.5 %collective-permute-done.10 = bf16[512,128]{1,0:T(8,128)(2,1)S(1)} collective-permute-done((bf16[512,128]{1,0:T(8,128)(2,1)S(1)}, bf16[512,128]{1,0:T(8,128)(2,1)S(1)}, u32[]{:S(2)}, u32[]{:S(2)}) %collective-permute-start.10) | collective-permute-done | bytes 131104 | tf_op jit(solution)/shard_map/ppermute | solution.py:43
  126.3 0.1 fusion.25
  126.4 16.0 %all_gather.18 = bf16[2048,128]{1,0:T(8,128)(2,1)S(1)} all-gather(bf16[512,128]{1,0:T(8,128)(2,1)S(1)} %fusion.25), channel_id=1, replica_groups={{0,4,8,12},{2,6,10,14},{1,5,9,13},{3,7,11,15},{16,20,24,28},{18,22,26,3..., dimensions={0}, use_global_device_ids=true | all-gather | bytes 655360 | tf_op jit(solution)/shard_map/all_gather | solution.py:51
  142.3 0.2 multiply_reduce_fusion.1
  142.5 0.1 multiply_convert_fusion
  142.7 15.0 %all_gather.16 = bf16[2048,128]{1,0:T(8,128)(2,1)S(1)} all-gather(bf16[512,128]{1,0:T(8,128)(2,1)S(1)} %multiply_convert_fusion), channel_id=1, replica_groups={{0,4,8,12},{2,6,10,14},{1,5,9,13},{3,7,11,15},{16,20,24,28},{18,22,26,3..., dimensions={0}, use_global_device_ids=true | all-gather | bytes 655360 | tf_op jit(solution)/shard_map/all_gather | solution.py:51
  157.6 0.8 multiply_reduce_fusion
  158.4 0.8 fusion
  159.2 0.8 fusion.18
  160.1 0.1 copy.74
  160.2 15.0 %all_gather.19 = bf16[256,1024]{1,0:T(8,128)(2,1)S(1)} all-gather(bf16[64,1024]{1,0:T(8,128)(2,1)S(1)} %bitcast.102), channel_id=1, replica_groups={{0,4,8,12},{2,6,10,14},{1,5,9,13},{3,7,11,15},{16,20,24,28},{18,22,26,3..., dimensions={0}, use_global_device_ids=true | all-gather | bytes 655360 | tf_op jit(solution)/shard_map/all_gather | solution.py:51
  175.2 0.8 collective-permute-start.11
  176.0 2.3 %fusion.6 = f32[256,1024]{1,0:T(8,128)S(1)} fusion(bf16[256,1024]{1,0:T(8,128)(2,1)S(1)} %all_gather.19, bf16[2048,1024]{1,0:T(8,128)(2,1)} %param.13, s32[]{:T(128)S(6)} %select_n.103), kind=kOutput, calls=%fused_computation.7 | convolution fusion | flops 536870912 | bytes 3670020 | tf_op jit(solution)/shard_map/dot_general | solution.py:149
  178.3 6.1 %collective-permute-done.11 = bf16[256,1024]{1,0:T(8,128)(2,1)S(1)} collective-permute-done((bf16[256,1024]{1,0:T(8,128)(2,1)S(1)}, bf16[256,1024]{1,0:T(8,128)(2,1)S(1)}, u32[]{:S(2)}, u32[]{:S(2)}) %collective-permute-start.11) | collective-permute-done | bytes 524320 | tf_op jit(solution)/shard_map/ppermute | solution.py:43
  184.4 2.3 %fusion.10 = f32[256,1024]{1,0:T(8,128)S(1)} fusion(f32[256,1024]{1,0:T(8,128)S(1)} %fusion.6, bf16[256,1024]{1,0:T(8,128)(2,1)S(1)} %collective-permute-done.11, bf16[2048,1024]{1,0:T(8,128)(2,1)} %param.13, s32[]{:T(128)S(6)} %select_n.104), kind=kOutput, calls=%fused_computation.14 | convolution fusion | flops 537133056 | bytes 4718596 | tf_op jit(solution)/shard_map/dot_general | solution.py:149
  186.8 0.1 collective-permute-start.12
  187.6 0.8 collective-permute-done.12
  188.4 0.8 add_convert_fusion
  (39 shorter events, 0.5 us)
Async XLA Ops:
  27.2 15.9 %copy-start.2 = (bf16[960,256]{1,0:T(8,128)(2,1)S(1)}, bf16[960,256]{1,0:T(8,128)(2,1)}, u32[]{:S(2)}) copy-start(bf16[960,256]{1,0:T(8,128)(2,1)} %param.11) | copy-start | bytes 1474564
  30.4 61.2 %collective-permute-start.1 = (bf16[128,1920]{1,0:T(8,128)(2,1)}, bf16[128,1920]{1,0:T(8,128)(2,1)}, u32[]{:S(2)}, u32[]{:S(2)}) collective-permute-start(bf16[128,1920]{1,0:T(8,128)(2,1)} %bitcast.112), channel_id=1, source_target_pairs={{0,2},{1,3},{2,0},{3,1},{4,6},{5,7},{6,4},{7,5},{8,10},{9,11},{10,... | collective-permute-start | bytes 1474568 | tf_op jit(solution)/shard_map/ppermute | solution.py:43
  36.4 55.2 %collective-permute-start.2 = (bf16[128,1920]{1,0:T(8,128)(2,1)}, bf16[128,1920]{1,0:T(8,128)(2,1)}, u32[]{:S(2)}, u32[]{:S(2)}) collective-permute-start(bf16[128,1920]{1,0:T(8,128)(2,1)} %bitcast.113), channel_id=1, source_target_pairs={{0,16},{1,17},{2,18},{3,19},{4,20},{5,21},{6,22},{7,23},{8,24},{9,... | collective-permute-start | bytes 1474568 | tf_op jit(solution)/shard_map/ppermute | solution.py:43
  39.5 52.1 %collective-permute-start.3 = (bf16[128,1920]{1,0:T(8,128)(2,1)}, bf16[128,1920]{1,0:T(8,128)(2,1)}, u32[]{:S(2)}, u32[]{:S(2)}) collective-permute-start(bf16[128,1920]{1,0:T(8,128)(2,1)} %bitcast.114), channel_id=1, source_target_pairs={{0,18},{1,19},{2,16},{3,17},{4,22},{5,23},{6,20},{7,21},{8,26},{9,... | collective-permute-start | bytes 1474568 | tf_op jit(solution)/shard_map/ppermute | solution.py:43
  41.1 49.3 %collective-permute-start = (bf16[32,1024]{1,0:T(8,128)(2,1)}, bf16[32,1024]{1,0:T(8,128)(2,1)}, u32[]{:S(2)}, u32[]{:S(2)}) collective-permute-start(bf16[32,1024]{1,0:T(8,128)(2,1)} %get-tuple-element.32), channel_id=1, source_target_pairs={{0,2},{1,3},{2,0},{3,1},{4,6},{5,7},{6,4},{7,5},{8,10},{9,11},{10,... | collective-permute-start | bytes 196616 | tf_op jit(solution)/shard_map/ppermute | solution.py:43
  65.3 29.1 %copy-start = (bf16[1920,256]{1,0:T(8,128)(2,1)}, bf16[1920,256]{1,0:T(8,128)(2,1)S(1)}, u32[]{:S(2)}) copy-start(bf16[1920,256]{1,0:T(8,128)(2,1)S(1)} %all_gather.15) | copy-start | bytes 2949124
  67.6 26.6 %copy-start.4 = (f32[128]{0:T(128)S(1)}, f32[128]{0:T(128)}, u32[]{:S(2)}) copy-start(f32[128]{0:T(128)} %param.15) | copy-start | bytes 1540
  94.1 7.2 %collective-permute-start.4 = (bf16[384,1920]{1,0:T(8,128)(2,1)}, bf16[384,1920]{1,0:T(8,128)(2,1)}, u32[]{:S(2)}, u32[]{:S(2)}) collective-permute-start(bf16[384,1920]{1,0:T(8,128)(2,1)} %pad_maximum_fusion.2), channel_id=1, source_target_pairs={{0,1},{1,0},{2,3},{3,2},{4,5},{5,4},{6,7},{7,6},{8,9},{9,8},{10,11... | collective-permute-start | bytes 4423688 | tf_op jit(solution)/shard_map/ppermute | solution.py:46
  94.4 4.4 %copy-start.1 = (bf16[1920,256]{1,0:T(8,128)(2,1)S(1)}, bf16[1920,256]{1,0:T(8,128)(2,1)}, u32[]{:S(2)}) copy-start(bf16[1920,256]{1,0:T(8,128)(2,1)} %all_gather.17) | copy-start | bytes 2949124
  109.9 32.6 %copy-start.5 = (f32[128]{0:T(128)S(1)}, f32[128]{0:T(128)}, u32[]{:S(2)}) copy-start(f32[128]{0:T(128)} %param.16) | copy-start | bytes 1540
  109.9 32.4 %collective-permute-start.5 = (f32[512,128]{1,0:T(8,128)S(1)}, f32[512,128]{1,0:T(8,128)S(1)}, u32[]{:S(2)}, u32[]{:S(2)}) collective-permute-start(f32[512,128]{1,0:T(8,128)S(1)} %bitcast.119), channel_id=1, source_target_pairs={{0,2},{1,3},{2,0},{3,1},{4,6},{5,7},{6,4},{7,5},{8,10},{9,11},{10,... | collective-permute-start | bytes 786440 | tf_op jit(solution)/shard_map/ppermute | solution.py:43
  110.5 31.8 %collective-permute-start.6 = (f32[512,128]{1,0:T(8,128)S(1)}, f32[512,128]{1,0:T(8,128)S(1)}, u32[]{:S(2)}, u32[]{:S(2)}) collective-permute-start(f32[512,128]{1,0:T(8,128)S(1)} %bitcast.120), channel_id=1, source_target_pairs={{0,16},{1,17},{2,18},{3,19},{4,20},{5,21},{6,22},{7,23},{8,24},{9,... | collective-permute-start | bytes 786440 | tf_op jit(solution)/shard_map/ppermute | solution.py:43
  112.0 9.5 %collective-permute-start.8 = (bf16[512,128]{1,0:T(8,128)(2,1)S(1)}, bf16[512,128]{1,0:T(8,128)(2,1)S(1)}, u32[]{:S(2)}, u32[]{:S(2)}) collective-permute-start(bf16[512,128]{1,0:T(8,128)(2,1)S(1)} %bitcast.123), channel_id=1, source_target_pairs={{0,2},{1,3},{2,0},{3,1},{4,6},{5,7},{6,4},{7,5},{8,10},{9,11},{10,... | collective-permute-start | bytes 393224 | tf_op jit(solution)/shard_map/ppermute | solution.py:43
  113.6 9.3 %collective-permute-start.9 = (bf16[512,128]{1,0:T(8,128)(2,1)S(1)}, bf16[512,128]{1,0:T(8,128)(2,1)S(1)}, u32[]{:S(2)}, u32[]{:S(2)}) collective-permute-start(bf16[512,128]{1,0:T(8,128)(2,1)S(1)} %bitcast.122), channel_id=1, source_target_pairs={{0,16},{1,17},{2,18},{3,19},{4,20},{5,21},{6,22},{7,23},{8,24},{9,... | collective-permute-start | bytes 393224 | tf_op jit(solution)/shard_map/ppermute | solution.py:43
  114.4 11.9 %collective-permute-start.10 = (bf16[512,128]{1,0:T(8,128)(2,1)S(1)}, bf16[512,128]{1,0:T(8,128)(2,1)S(1)}, u32[]{:S(2)}, u32[]{:S(2)}) collective-permute-start(bf16[512,128]{1,0:T(8,128)(2,1)S(1)} %bitcast.124), channel_id=1, source_target_pairs={{0,18},{1,19},{2,16},{3,17},{4,22},{5,23},{6,20},{7,21},{8,26},{9,... | collective-permute-start | bytes 393224 | tf_op jit(solution)/shard_map/ppermute | solution.py:43
  121.5 20.8 %collective-permute-start.7 = (f32[512,128]{1,0:T(8,128)S(1)}, f32[512,128]{1,0:T(8,128)S(1)}, u32[]{:S(2)}, u32[]{:S(2)}) collective-permute-start(f32[512,128]{1,0:T(8,128)S(1)} %bitcast.121), channel_id=1, source_target_pairs={{0,18},{1,19},{2,16},{3,17},{4,22},{5,23},{6,20},{7,21},{8,26},{9,... | collective-permute-start | bytes 786440 | tf_op jit(solution)/shard_map/ppermute | solution.py:43
  175.2 9.2 %collective-permute-start.11 = (bf16[256,1024]{1,0:T(8,128)(2,1)S(1)}, bf16[256,1024]{1,0:T(8,128)(2,1)S(1)}, u32[]{:S(2)}, u32[]{:S(2)}) collective-permute-start(bf16[256,1024]{1,0:T(8,128)(2,1)S(1)} %all_gather.19), channel_id=1, source_target_pairs={{0,2},{1,3},{2,0},{3,1},{4,6},{5,7},{6,4},{7,5},{8,10},{9,11},{10,... | collective-permute-start | bytes 1572872 | tf_op jit(solution)/shard_map/ppermute | solution.py:43
  176.0 12.4 %copy-start.3 = (bf16[128,1024]{1,0:T(8,128)(2,1)S(1)}, bf16[128,1024]{1,0:T(8,128)(2,1)}, u32[]{:S(2)}) copy-start(bf16[128,1024]{1,0:T(8,128)(2,1)} %param.14) | copy-start | bytes 786436
  186.8 1.6 collective-permute-start.12

commit v2 on v1

v2 whole, which is shorter than its diff:
```python
import functools

import jax
import jax.numpy as jnp
from jax import lax
from jax.experimental import pallas as pl
from jax.experimental.pallas import tpu as pltpu
from jax.sharding import PartitionSpec as P

HEAD_SIZE = 128
epsilon = 1e-05
AXES = ("groups", "seq", "head")
VMEM_BYTES = 48 * 1024 * 1024
f32, bf16 = jnp.float32, jnp.bfloat16


def pack_kernel(groups, pairs, part, index_ref, near_ref, far_ref, *outs):
    sends, own_far = outs[:-1], outs[-1]
    for g in range(groups):
        for y in range(2):
            starts = [((2 * z + y) * groups + g) * part for z in range(pairs)]

            def columns(ref):
                return jnp.concatenate([ref[:, s : s + part] for s in starts], axis=1)

            for k, send in enumerate(sends):

                @pl.when(index_ref[k] == g * 2 + y)
                def _():
                    send[...] = columns(near_ref)

            @pl.when(index_ref[0] == g * 2 + y)
            def _():
                own_far[...] = columns(far_ref)


def pack(vision, index, core, groups, pairs, part):
    rows, width = vision.shape
    half = rows // 2
    block = 32
    steps = half // block
    count = groups * 2
    depth = pairs * part
    scalars = jnp.concatenate([index, jnp.stack([core])]).astype(jnp.int32)
    return pl.pallas_call(
        functools.partial(pack_kernel, groups, pairs, part),
        grid_spec=pltpu.PrefetchScalarGridSpec(
            num_scalar_prefetch=1,
            grid=(steps,),
            in_specs=[
                pl.BlockSpec((block, width), lambda i, s: (s[count] * steps + i, 0)),
                pl.BlockSpec((block, width), lambda i, s: ((1 - s[count]) * steps + i, 0)),
            ],
            out_specs=[pl.BlockSpec((block, depth), lambda i, s: (i, 0))] * (count + 1),
        ),
        out_shape=[jax.ShapeDtypeStruct((half, depth), vision.dtype)] * (count + 1),
        compiler_params=pltpu.CompilerParams(vmem_limit_bytes=VMEM_BYTES),
        name="pack",
    )(scalars, vision, vision)


def project_kernel(groups, *refs):
    count = groups * 2
    near, own_far, far, weight = refs[:count], refs[count], refs[count + 1], refs[count + 2]
    outs = refs[count + 3 :]
    half = own_far.shape[0]
    firsts = jnp.concatenate([ref[...] for ref in near], axis=0)
    seconds = jnp.concatenate([own_far[...], far[...]], axis=0)
    w = weight[...]
    for part, lhs in enumerate((firsts, seconds)):
        result = jnp.dot(lhs, w, preferred_element_type=f32)
        for source in range(count):
            by_group, by_side = source // 2, source % 2
            for side in range(2):
                out = outs[(-by_group) % groups * 2 + side]
                start = (0 if by_side == side else 2 * half) + part * half
                out[start : start + half, :] = result[
                    source * half : (source + 1) * half, side * HEAD_SIZE : (side + 1) * HEAD_SIZE
                ].astype(out.dtype)


def project(near, own_far, far, weight, dtype):
    count = len(near)
    half = own_far.shape[0]
    shapes = [
        jax.ShapeDtypeStruct((4 * half, HEAD_SIZE), f32 if k == 0 else dtype) for k in range(count)
    ]
    return pl.pallas_call(
        functools.partial(project_kernel, count // 2),
        out_shape=shapes,
        compiler_params=pltpu.CompilerParams(vmem_limit_bytes=VMEM_BYTES),
        name="project",
    )(*near, own_far, far, weight)


def attend_kernel(q_ref, k_ref, v_ref, out_ref):
    text = out_ref.shape[0]
    heads = q_ref.shape[0] // text
    keys, values = k_ref[...], v_ref[...]
    for h in range(heads):
        scores = (
            lax.dot_general(
                q_ref[h * text : (h + 1) * text, :],
                keys,
                (((1,), (1,)), ((), ())),
                preferred_element_type=f32,
            )
            * HEAD_SIZE ** (-0.5)
        )
        weights = jnp.exp(scores - jnp.max(scores, axis=-1, keepdims=True))
        denominator = jnp.sum(weights, axis=-1, keepdims=True)
        numerator = jnp.dot(weights.astype(bf16), values, preferred_element_type=f32)
        out_ref[:, h * HEAD_SIZE : (h + 1) * HEAD_SIZE] = (numerator / denominator).astype(bf16)


def attend(normed, keys, values, text):
    heads = normed.shape[0] // text
    return pl.pallas_call(
        attend_kernel,
        out_shape=jax.ShapeDtypeStruct((text, heads * HEAD_SIZE), bf16),
        compiler_params=pltpu.CompilerParams(vmem_limit_bytes=VMEM_BYTES),
        name="attend",
    )(normed, keys, values)


def norm(array, gain):
    mean = jnp.mean(array * array, axis=-1, keepdims=True)
    return (array * lax.rsqrt(mean + epsilon) * gain).astype(bf16)


def body(
    sizes,
    queries,
    vision,
    key_matrix,
    value_matrix,
    out_weight,
    residual,
    query_norm_gain,
    key_norm_gain,
    attn_gate,
):
    groups, seq, cores = sizes
    pairs = seq // 2
    group = lax.axis_index("groups")
    side = lax.axis_index("seq") % 2
    core = lax.axis_index("head")

    def plane_shift(array, by_group, by_side):
        perm = []
        for g in range(groups):
            for s in range(seq):
                for c in range(cores):
                    to_g = (g + by_group) % groups
                    to_s = s // 2 * 2 + (s + by_side) % 2
                    perm.append(
                        ((g * seq + s) * cores + c, (to_g * seq + to_s) * cores + c)
                    )
        return lax.ppermute(array, AXES, perm)

    def core_swap(array):
        return lax.ppermute(array, "head", [(c, (c + 1) % cores) for c in range(cores)])

    lines = [[2 * z + y for z in range(pairs)] for y in range(2)]

    def gather_pairs(array):
        return lax.all_gather(array, "seq", axis=0, tiled=True, axis_index_groups=lines)

    offsets = [(g, y) for g in range(groups) for y in range(2)]

    part = key_matrix.shape[0] // groups

    def prepare(matrix):
        mine = lax.dynamic_slice_in_dim(matrix, group * part, part, axis=0)
        half = mine.shape[1] // 2
        return jnp.where(side == 0, mine, jnp.roll(mine, half, axis=1))

    index = jnp.stack([(group + g) % groups * 2 + (side + y) % 2 for g, y in offsets])
    packed = pack(vision, index, core, groups, pairs, part)
    received = [plane_shift(packed[k], g, y) for k, (g, y) in enumerate(offsets) if k]
    near = [packed[0]] + received
    own_far = packed[-1]

    key_send, _ = lax.optimization_barrier((prepare(key_matrix), packed[1]))
    key_weight = gather_pairs(key_send)
    joined, _ = lax.optimization_barrier((jnp.concatenate(received, axis=0), key_weight))
    far = core_swap(joined)

    rows_q = queries.shape[0]
    half_q = queries.shape[1] // 2
    heads = half_q // HEAD_SIZE
    q_own = lax.dynamic_slice_in_dim(queries, side * half_q, half_q, axis=1)
    q_send = lax.dynamic_slice_in_dim(queries, (1 - side) * half_q, half_q, axis=1)
    q_recv = plane_shift(q_send, 0, 1)
    q_pair = jnp.where(
        side == 0,
        jnp.concatenate([q_own, q_recv], axis=0),
        jnp.concatenate([q_recv, q_own], axis=0),
    )
    q_heads = jnp.concatenate(
        [q_pair[:, h * HEAD_SIZE : (h + 1) * HEAD_SIZE] for h in range(heads)], axis=0
    )
    normed = norm(q_heads.astype(f32), query_norm_gain)

    def scatter(pieces):
        total = pieces[0]
        for k, (g, y) in enumerate(offsets):
            if k:
                total = total + plane_shift(pieces[k], g, y).astype(f32)
        return total

    key_pieces = project(near, own_far, far, key_weight, f32)
    value_send, key_pieces = lax.optimization_barrier((prepare(value_matrix), key_pieces))
    key_total = scatter(key_pieces)
    value_weight = gather_pairs(value_send)
    value_pieces = project(near, own_far, far, value_weight, bf16)
    keys, value_pieces = lax.optimization_barrier((norm(key_total, key_norm_gain), value_pieces))
    value_total = scatter(value_pieces)
    keys = gather_pairs(keys)
    value_rows, keys = lax.optimization_barrier((value_total.astype(bf16), keys))
    values = gather_pairs(value_rows)

    attended = gather_pairs(attend(normed, keys, values, 2 * rows_q))
    other = plane_shift(attended, 0, 1)
    depth = heads * HEAD_SIZE
    weight_own = lax.dynamic_slice_in_dim(out_weight, side * depth, depth, axis=0)
    weight_other = lax.dynamic_slice_in_dim(out_weight, (1 - side) * depth, depth, axis=0)
    projected = jnp.dot(attended, weight_own, preferred_element_type=f32) + jnp.dot(
        other, weight_other, preferred_element_type=f32
    )
    out_rows = residual.shape[0]
    send = lax.dynamic_slice_in_dim(projected, (1 - core) * out_rows, out_rows, axis=0)
    mine = lax.dynamic_slice_in_dim(projected, core * out_rows, out_rows, axis=0)
    mine = mine + core_swap(send.astype(bf16)).astype(f32)
    return (residual.astype(f32) + jnp.tanh(attn_gate[0]) * mine).astype(bf16)


def solution(mesh):
    in_specs = (
        P(("groups", "seq"), "head"),
        P(("groups", "seq"), None),
        P("seq", "head"),
        P("seq", "head"),
        P("head", "seq"),
        P(("groups", "head"), "seq"),
        P(),
        P(),
        P(),
    )
    out_specs = P(("groups", "head"), "seq")
    sizes = tuple(mesh.shape[axis] for axis in AXES)
    return jax.shard_map(
        functools.partial(body, sizes),
        mesh=mesh,
        in_specs=in_specs,
        out_specs=out_specs,
        check_vma=False,
    )
```

time: 190 us -> 136 us (0.72)
  local copies, waits for them, and re-layouts: 46.8 us -> 2.92 us
  matrix products: 17.3 us -> 4.61 us
  Pallas kernels: 0 us -> 12 us
  waiting for transfers between devices: 16.1 us -> 10.1 us
  other arithmetic: 6.14 us -> 3.61 us
    dynamic_slice x7 -> x1, local copies, waits for them, and re-layouts: 21.3 us -> 1.51 us  [body(): q_own = lax.dynamic_slice_in_dim(queries, side * half_q, half_q, axis=1)]
    dot_general x6 -> x0, matrix products: 12.7 us -> none  [the longest x2 5.81 us: project(): second = jnp.dot(seconds, weight, preferred_element_type=f32)]
    pallas_call x0 -> x4, Pallas kernels: none -> 12 us  [the longest x1 5.55 us: pack(): pl.pallas_call(functools.partial(pack_kernel, groups, pairs, part), grid_...]
    ppermute x11, waiting for transfers between devices: 15.3 us -> 6.39 us  [plane_shift(): return lax.ppermute(array, AXES, perm)]
    reshape x2 -> x0, local copies, waits for them, and re-layouts: 8.42 us -> none  [the longest x1 8.33 us: body(): classes = vision.reshape(rows, pairs, 2, groups, part).transpose(3, 2, 0,...]
    unnamed x18 -> x15, local copies, waits for them, and re-layouts: 7.27 us -> 0.11 us
    transpose x1 -> x0, local copies, waits for them, and re-layouts: 4.23 us -> none  [body(): classes = vision.reshape(rows, pairs, 2, groups, part).transpose(3, 2, 0,...]
    another operation x6 -> x0, local copies, waits for them, and re-layouts: 3.25 us -> none  [project(): jnp.stack([first.reshape(groups, 2, half, 2, HEAD_SIZE), second.reshape(g...]
  transfers between devices with their start and end apart: 13 -> 13, of which waited for: 4 -> 3; matrix products, arithmetic and copies ran while one was open for 12% -> 5% of each run, Pallas kernels for 0% -> 1%
where the time goes in v2:
time: 136 us
  blocking collectives  87.6 us (64%)
  starting transfers between devices  14.2 us (10%)
  Pallas kernels  12 us (9%)
  waiting for transfers between devices  10.1 us (7%)
  matrix products  4.61 us (3%)
  other arithmetic  3.61 us (3%)
  local copies, waits for them, and re-layouts  2.92 us (2%)
    all_gather x5, blocking collectives, gather_pairs(): lax.all_gather(array, 'seq', axis=0, tiled=True, axis_index_groups=lines)  87.6 us
    ppermute x11, starting transfers between devices, plane_shift(): return lax.ppermute(array, AXES, perm)  14.1 us
    ppermute x11, waiting for transfers between devices, plane_shift(): return lax.ppermute(array, AXES, perm)  6.39 us
    pallas_call x1, Pallas kernels, pack(): pl.pallas_call(functools.partial(pack_kernel, groups, pairs, part), grid_...  5.55 us
    pallas_call x1, Pallas kernels, attend(): pl.pallas_call(attend_kernel, out_shape=jax.ShapeDtypeStruct((text, heads...  3.98 us
    ppermute x2, waiting for transfers between devices, core_swap(): lax.ppermute(array, 'head', [(c, (c + 1) % cores) for c in range(cores)])  3.68 us
  transfers between devices with their start and end apart: 13, of which 3 were waited for; matrix products, arithmetic and copies ran while one was open for 5% of the time, Pallas kernels for 1%

profile of v2, /device:TPU:0, one launch (start us, length us, event | category | flops | bytes accessed | tf_op | source)
XLA Modules:
  0.0 135.9 jit_solution(6431531661376734180)
XLA Ops:
  0.0 0.1 concatenate.26.index_ref
  0.1 5.6 %pack.1 = (bf16[128,1920]{1,0:T(8,128)(2,1)S(1)}, bf16[128,1920]{1,0:T(8,128)(2,1)}, bf16[128,1920]{1,0:T(8,128)(2,1)S(1)}, bf16[128,1920]{1,0:T(8,128)(2,1)S(1)}, bf16[128,1920]{1,0:T(8,128)(2,1)S(1)}) custom-call(s32[5]{0:T(128)S(1)} %concatenate.26.index_ref, bf16[256,7680]{1,0:T(8,128)(2,1)} %far_ref.1, bf16[256,7680]{1,0:T(8,128)(2,1)} %far_ref.1), custom_call_target="tpu_custom_call" | custom-call | tf_op jit(solution)/shard_map/pack/pallas_call | solution.py:45
  5.6 3.0 %collective-permute-start.1 = (bf16[128,1920]{1,0:T(8,128)(2,1)}, bf16[128,1920]{1,0:T(8,128)(2,1)S(1)}, u32[]{:S(2)}, u32[]{:S(2)}) collective-permute-start(bf16[128,1920]{1,0:T(8,128)(2,1)} %get-tuple-element.33), channel_id=1, source_target_pairs={{0,2},{1,3},{2,0},{3,1},{4,6},{5,7},{6,4},{7,5},{8,10},{9,11},{10,... | collective-permute-start | bytes 1474568 | tf_op jit(solution)/shard_map/ppermute | solution.py:159
  8.6 1.4 %collective-permute-start.2 = (bf16[128,1920]{1,0:T(8,128)(2,1)S(1)}, bf16[128,1920]{1,0:T(8,128)(2,1)S(1)}, u32[]{:S(2)}, u32[]{:S(2)}) collective-permute-start(bf16[128,1920]{1,0:T(8,128)(2,1)S(1)} %get-tuple-element.34), channel_id=1, source_target_pairs={{0,16},{1,17},{2,18},{3,19},{4,20},{5,21},{6,22},{7,23},{8,24},{9,... | collective-permute-start | bytes 1474568 | tf_op jit(solution)/shard_map/ppermute | solution.py:159
  10.0 0.0 collective-permute-start.3
  10.1 1.5 %constant_dynamic-slice_fusion.3 = (bf16[32,1024]{1,0:T(8,128)(2,1)S(1)}, bf16[32,1024]{1,0:T(8,128)(2,1)}) fusion(bf16[32,2048]{1,0:T(8,128)(2,1)} %param.9, s32[]{:T(128)S(6)} %select_n.71, s32[]{:T(128)S(6)} %select_n.72), kind=kLoop, calls=%fused_computation.33 | loop fusion | bytes 262152 | tf_op jit(solution)/shard_map/dynamic_slice | solution.py:192
  11.6 2.0 %collective-permute-start = (bf16[32,1024]{1,0:T(8,128)(2,1)}, bf16[32,1024]{1,0:T(8,128)(2,1)}, u32[]{:S(2)}, u32[]{:S(2)}) collective-permute-start(bf16[32,1024]{1,0:T(8,128)(2,1)} %get-tuple-element.66), channel_id=1, source_target_pairs={{0,2},{1,3},{2,0},{3,1},{4,6},{5,7},{6,4},{7,5},{8,10},{9,11},{10,... | collective-permute-start | bytes 196616 | tf_op jit(solution)/shard_map/ppermute | solution.py:159
  13.6 0.0 copy-start
  13.6 1.2 fusion.12
  14.8 1.0 maximum_select_fusion.1
  15.8 0.0 copy-start.2
  15.8 22.1 %all_gather.15.refs_6_ = bf16[1920,256]{1,0:T(8,128)(2,1)S(1)} all-gather(bf16[480,256]{1,0:T(8,128)(2,1)S(1)} %maximum_select_fusion.1), channel_id=1, replica_groups={{0,4,8,12},{2,6,10,14},{1,5,9,13},{3,7,11,15},{16,20,24,28},{18,22,26,3..., dimensions={0}, use_global_device_ids=true | all-gather | bytes 1228800 | tf_op jit(solution)/shard_map/all_gather | solution.py:167
  37.9 0.0 copy-done
  37.9 0.1 maximum_select_fusion
  38.0 0.0 collective-permute-done
  38.0 0.9 maximum_select_fusion.2
  39.0 0.0 collective-permute-done.1.refs_1_
  39.0 0.0 collective-permute-done.2.refs_2_
  39.0 0.0 collective-permute-done.3.refs_3_
  39.0 0.1 pad_maximum_fusion
  39.1 0.1 collective-permute-start.4
  39.3 0.1 fusion.7
  39.5 0.0 copy-done.2
  39.5 0.1 fusion.9.q_ref
  39.6 2.8 %collective-permute-done.4.refs_5_ = bf16[384,1920]{1,0:T(8,128)(2,1)S(1)} collective-permute-done((bf16[384,1920]{1,0:T(8,128)(2,1)S(1)}, bf16[384,1920]{1,0:T(8,128)(2,1)S(1)}, u32[]{:S(2)}, u32[]{:S(2)}) %collective-permute-start.4) | collective-permute-done | bytes 1474592 | tf_op jit(solution)/shard_map/ppermute | solution.py:162
  42.5 1.2 project.2
  43.7 0.6 collective-permute-start.5
  44.3 1.5 %collective-permute-start.6 = (f32[512,128]{1,0:T(8,128)S(1)}, f32[512,128]{1,0:T(8,128)S(1)}, u32[]{:S(2)}, u32[]{:S(2)}) collective-permute-start(f32[512,128]{1,0:T(8,128)S(1)} %get-tuple-element.45), channel_id=1, source_target_pairs={{0,16},{1,17},{2,18},{3,19},{4,20},{5,21},{6,22},{7,23},{8,24},{9,... | collective-permute-start | bytes 786440 | tf_op jit(solution)/shard_map/ppermute | solution.py:159
  45.8 1.5 %collective-permute-start.7 = (f32[512,128]{1,0:T(8,128)S(1)}, f32[512,128]{1,0:T(8,128)S(1)}, u32[]{:S(2)}, u32[]{:S(2)}) collective-permute-start(f32[512,128]{1,0:T(8,128)S(1)} %get-tuple-element.46), channel_id=1, source_target_pairs={{0,18},{1,19},{2,16},{3,17},{4,22},{5,23},{6,20},{7,21},{8,26},{9,... | collective-permute-start | bytes 786440 | tf_op jit(solution)/shard_map/ppermute | solution.py:159
  47.3 19.8 %all_gather.16.refs_6_ = bf16[1920,256]{1,0:T(8,128)(2,1)S(1)} all-gather(bf16[480,256]{1,0:T(8,128)(2,1)S(1)} %maximum_select_fusion), channel_id=1, replica_groups={{0,4,8,12},{2,6,10,14},{1,5,9,13},{3,7,11,15},{16,20,24,28},{18,22,26,3..., dimensions={0}, use_global_device_ids=true | all-gather | bytes 1228800 | tf_op jit(solution)/shard_map/all_gather | solution.py:167
  67.1 0.0 copy-start.3
  67.1 1.2 project.3
  68.3 0.0 collective-permute-done.5
  68.3 0.0 collective-permute-done.6
  68.3 0.0 collective-permute-done.7
  68.3 0.2 multiply_reduce_fusion
  68.5 0.0 copy-done.3
  68.5 0.1 multiply_convert_fusion
  68.7 1.5 %collective-permute-start.10 = (bf16[512,128]{1,0:T(8,128)(2,1)S(1)}, bf16[512,128]{1,0:T(8,128)(2,1)S(1)}, u32[]{:S(2)}, u32[]{:S(2)}) collective-permute-start(bf16[512,128]{1,0:T(8,128)(2,1)S(1)} %get-tuple-element.55), channel_id=1, source_target_pairs={{0,18},{1,19},{2,16},{3,17},{4,22},{5,23},{6,20},{7,21},{8,26},{9,... | collective-permute-start | bytes 393224 | tf_op jit(solution)/shard_map/ppermute | solution.py:159
  70.1 1.5 %collective-permute-start.8 = (bf16[512,128]{1,0:T(8,128)(2,1)S(1)}, bf16[512,128]{1,0:T(8,128)(2,1)S(1)}, u32[]{:S(2)}, u32[]{:S(2)}) collective-permute-start(bf16[512,128]{1,0:T(8,128)(2,1)S(1)} %get-tuple-element.53), channel_id=1, source_target_pairs={{0,2},{1,3},{2,0},{3,1},{4,6},{5,7},{6,4},{7,5},{8,10},{9,11},{10,... | collective-permute-start | bytes 393224 | tf_op jit(solution)/shard_map/ppermute | solution.py:159
  71.6 0.6 collective-permute-start.9
  72.2 16.0 %all_gather.17.k_ref = bf16[2048,128]{1,0:T(8,128)(2,1)S(1)} all-gather(bf16[512,128]{1,0:T(8,128)(2,1)S(1)} %multiply_convert_fusion), channel_id=1, replica_groups={{0,4,8,12},{2,6,10,14},{1,5,9,13},{3,7,11,15},{16,20,24,28},{18,22,26,3..., dimensions={0}, use_global_device_ids=true | all-gather | bytes 655360 | tf_op jit(solution)/shard_map/all_gather | solution.py:167
  88.2 0.0 collective-permute-done.10
  88.2 0.0 collective-permute-done.8
  88.2 0.0 collective-permute-done.9
  88.2 0.1 add_convert_fusion.1
  88.3 15.0 %all_gather.18.v_ref = bf16[2048,128]{1,0:T(8,128)(2,1)S(1)} all-gather(bf16[512,128]{1,0:T(8,128)(2,1)S(1)} %add_convert_fusion.1), channel_id=1, replica_groups={{0,4,8,12},{2,6,10,14},{1,5,9,13},{3,7,11,15},{16,20,24,28},{18,22,26,3..., dimensions={0}, use_global_device_ids=true | all-gather | bytes 655360 | tf_op jit(solution)/shard_map/all_gather | solution.py:167
  103.3 4.0 %attend.1 = bf16[64,1024]{1,0:T(8,128)(2,1)S(1)} custom-call(bf16[512,128]{1,0:T(8,128)(2,1)S(1)} %fusion.9.q_ref, bf16[2048,128]{1,0:T(8,128)(2,1)S(1)} %all_gather.17.k_ref, bf16[2048,128]{1,0:T(8,128)(2,1)S(1)} %all_gather.18.v_ref), custom_call_target="tpu_custom_call" | custom-call | tf_op jit(solution)/shard_map/attend/pallas_call | solution.py:118
  107.3 14.7 %all_gather.19 = bf16[256,1024]{1,0:T(8,128)(2,1)S(1)} all-gather(bf16[64,1024]{1,0:T(8,128)(2,1)S(1)} %attend.1), channel_id=1, replica_groups={{0,4,8,12},{2,6,10,14},{1,5,9,13},{3,7,11,15},{16,20,24,28},{18,22,26,3..., dimensions={0}, use_global_device_ids=true | all-gather | bytes 655360 | tf_op jit(solution)/shard_map/all_gather | solution.py:167
  122.0 0.5 collective-permute-start.11
  122.5 2.3 %fusion.2 = f32[256,1024]{1,0:T(8,128)S(1)} fusion(bf16[256,1024]{1,0:T(8,128)(2,1)S(1)} %all_gather.19, bf16[2048,1024]{1,0:T(8,128)(2,1)} %param.13, s32[]{:T(128)S(6)} %select_n.71), kind=kOutput, calls=%fused_computation.2 | convolution fusion | flops 536870912 | bytes 3670020 | tf_op jit(solution)/shard_map/dot_general | solution.py:228
  124.8 0.0 copy-start.1
  124.8 6.4 %collective-permute-done.11 = bf16[256,1024]{1,0:T(8,128)(2,1)S(1)} collective-permute-done((bf16[256,1024]{1,0:T(8,128)(2,1)S(1)}, bf16[256,1024]{1,0:T(8,128)(2,1)S(1)}, u32[]{:S(2)}, u32[]{:S(2)}) %collective-permute-start.11) | collective-permute-done | bytes 524320 | tf_op jit(solution)/shard_map/ppermute | solution.py:159
  131.2 2.3 %fusion.4 = f32[256,1024]{1,0:T(8,128)S(1)} fusion(f32[256,1024]{1,0:T(8,128)S(1)} %fusion.2, bf16[256,1024]{1,0:T(8,128)(2,1)S(1)} %collective-permute-done.11, bf16[2048,1024]{1,0:T(8,128)(2,1)} %param.13, s32[]{:T(128)S(6)} %select_n.72), kind=kOutput, calls=%fused_computation.5 | convolution fusion | flops 537133056 | bytes 4718596 | tf_op jit(solution)/shard_map/dot_general | solution.py:228
  133.5 0.1 collective-permute-start.12
  134.3 0.8 collective-permute-done.12
  135.1 0.0 copy-done.1
  135.1 0.8 add_convert_fusion
  (11 shorter events, 0.2 us)
Async XLA Ops:
  5.6 33.3 %collective-permute-start.1 = (bf16[128,1920]{1,0:T(8,128)(2,1)}, bf16[128,1920]{1,0:T(8,128)(2,1)S(1)}, u32[]{:S(2)}, u32[]{:S(2)}) collective-permute-start(bf16[128,1920]{1,0:T(8,128)(2,1)} %get-tuple-element.33), channel_id=1, source_target_pairs={{0,2},{1,3},{2,0},{3,1},{4,6},{5,7},{6,4},{7,5},{8,10},{9,11},{10,... | collective-permute-start | bytes 1474568 | tf_op jit(solution)/shard_map/ppermute | solution.py:159
  8.6 30.4 %collective-permute-start.2 = (bf16[128,1920]{1,0:T(8,128)(2,1)S(1)}, bf16[128,1920]{1,0:T(8,128)(2,1)S(1)}, u32[]{:S(2)}, u32[]{:S(2)}) collective-permute-start(bf16[128,1920]{1,0:T(8,128)(2,1)S(1)} %get-tuple-element.34), channel_id=1, source_target_pairs={{0,16},{1,17},{2,18},{3,19},{4,20},{5,21},{6,22},{7,23},{8,24},{9,... | collective-permute-start | bytes 1474568 | tf_op jit(solution)/shard_map/ppermute | solution.py:159
  10.0 29.0 %collective-permute-start.3 = (bf16[128,1920]{1,0:T(8,128)(2,1)S(1)}, bf16[128,1920]{1,0:T(8,128)(2,1)S(1)}, u32[]{:S(2)}, u32[]{:S(2)}) collective-permute-start(bf16[128,1920]{1,0:T(8,128)(2,1)S(1)} %get-tuple-element.35), channel_id=1, source_target_pairs={{0,18},{1,19},{2,16},{3,17},{4,22},{5,23},{6,20},{7,21},{8,26},{9,... | collective-permute-start | bytes 1474568 | tf_op jit(solution)/shard_map/ppermute | solution.py:159
  11.6 26.4 %collective-permute-start = (bf16[32,1024]{1,0:T(8,128)(2,1)}, bf16[32,1024]{1,0:T(8,128)(2,1)}, u32[]{:S(2)}, u32[]{:S(2)}) collective-permute-start(bf16[32,1024]{1,0:T(8,128)(2,1)} %get-tuple-element.66), channel_id=1, source_target_pairs={{0,2},{1,3},{2,0},{3,1},{4,6},{5,7},{6,4},{7,5},{8,10},{9,11},{10,... | collective-permute-start | bytes 196616 | tf_op jit(solution)/shard_map/ppermute | solution.py:159
  13.6 24.3 %copy-start = (bf16[960,256]{1,0:T(8,128)(2,1)S(1)}, bf16[960,256]{1,0:T(8,128)(2,1)}, u32[]{:S(2)}) copy-start(bf16[960,256]{1,0:T(8,128)(2,1)} %param.12) | copy-start | bytes 1474564
  15.8 23.7 %copy-start.2 = (f32[128]{0:T(128)S(1)}, f32[128]{0:T(128)}, u32[]{:S(2)}) copy-start(f32[128]{0:T(128)} %param.15) | copy-start | bytes 1540
  39.1 3.3 %collective-permute-start.4 = (bf16[384,1920]{1,0:T(8,128)(2,1)S(1)}, bf16[384,1920]{1,0:T(8,128)(2,1)S(1)}, u32[]{:S(2)}, u32[]{:S(2)}) collective-permute-start(bf16[384,1920]{1,0:T(8,128)(2,1)S(1)} %pad_maximum_fusion), channel_id=1, source_target_pairs={{0,1},{1,0},{2,3},{3,2},{4,5},{5,4},{6,7},{7,6},{8,9},{9,8},{10,11... | collective-permute-start | bytes 4423688 | tf_op jit(solution)/shard_map/ppermute | solution.py:162
  43.7 24.6 %collective-permute-start.5 = (f32[512,128]{1,0:T(8,128)S(1)}, f32[512,128]{1,0:T(8,128)S(1)}, u32[]{:S(2)}, u32[]{:S(2)}) collective-permute-start(f32[512,128]{1,0:T(8,128)S(1)} %get-tuple-element.44), channel_id=1, source_target_pairs={{0,2},{1,3},{2,0},{3,1},{4,6},{5,7},{6,4},{7,5},{8,10},{9,11},{10,... | collective-permute-start | bytes 786440 | tf_op jit(solution)/shard_map/ppermute | solution.py:159
  44.3 24.0 %collective-permute-start.6 = (f32[512,128]{1,0:T(8,128)S(1)}, f32[512,128]{1,0:T(8,128)S(1)}, u32[]{:S(2)}, u32[]{:S(2)}) collective-permute-start(f32[512,128]{1,0:T(8,128)S(1)} %get-tuple-element.45), channel_id=1, source_target_pairs={{0,16},{1,17},{2,18},{3,19},{4,20},{5,21},{6,22},{7,23},{8,24},{9,... | collective-permute-start | bytes 786440 | tf_op jit(solution)/shard_map/ppermute | solution.py:159
  45.8 22.6 %collective-permute-start.7 = (f32[512,128]{1,0:T(8,128)S(1)}, f32[512,128]{1,0:T(8,128)S(1)}, u32[]{:S(2)}, u32[]{:S(2)}) collective-permute-start(f32[512,128]{1,0:T(8,128)S(1)} %get-tuple-element.46), channel_id=1, source_target_pairs={{0,18},{1,19},{2,16},{3,17},{4,22},{5,23},{6,20},{7,21},{8,26},{9,... | collective-permute-start | bytes 786440 | tf_op jit(solution)/shard_map/ppermute | solution.py:159
  67.1 1.5 %copy-start.3 = (f32[128]{0:T(128)S(1)}, f32[128]{0:T(128)}, u32[]{:S(2)}) copy-start(f32[128]{0:T(128)} %param.16) | copy-start | bytes 1540
  68.7 19.6 %collective-permute-start.10 = (bf16[512,128]{1,0:T(8,128)(2,1)S(1)}, bf16[512,128]{1,0:T(8,128)(2,1)S(1)}, u32[]{:S(2)}, u32[]{:S(2)}) collective-permute-start(bf16[512,128]{1,0:T(8,128)(2,1)S(1)} %get-tuple-element.55), channel_id=1, source_target_pairs={{0,18},{1,19},{2,16},{3,17},{4,22},{5,23},{6,20},{7,21},{8,26},{9,... | collective-permute-start | bytes 393224 | tf_op jit(solution)/shard_map/ppermute | solution.py:159
  70.1 18.1 %collective-permute-start.8 = (bf16[512,128]{1,0:T(8,128)(2,1)S(1)}, bf16[512,128]{1,0:T(8,128)(2,1)S(1)}, u32[]{:S(2)}, u32[]{:S(2)}) collective-permute-start(bf16[512,128]{1,0:T(8,128)(2,1)S(1)} %get-tuple-element.53), channel_id=1, source_target_pairs={{0,2},{1,3},{2,0},{3,1},{4,6},{5,7},{6,4},{7,5},{8,10},{9,11},{10,... | collective-permute-start | bytes 393224 | tf_op jit(solution)/shard_map/ppermute | solution.py:159
  71.6 16.6 %collective-permute-start.9 = (bf16[512,128]{1,0:T(8,128)(2,1)S(1)}, bf16[512,128]{1,0:T(8,128)(2,1)S(1)}, u32[]{:S(2)}, u32[]{:S(2)}) collective-permute-start(bf16[512,128]{1,0:T(8,128)(2,1)S(1)} %get-tuple-element.54), channel_id=1, source_target_pairs={{0,16},{1,17},{2,18},{3,19},{4,20},{5,21},{6,22},{7,23},{8,24},{9,... | collective-permute-start | bytes 393224 | tf_op jit(solution)/shard_map/ppermute | solution.py:159
  122.0 9.2 %collective-permute-start.11 = (bf16[256,1024]{1,0:T(8,128)(2,1)S(1)}, bf16[256,1024]{1,0:T(8,128)(2,1)S(1)}, u32[]{:S(2)}, u32[]{:S(2)}) collective-permute-start(bf16[256,1024]{1,0:T(8,128)(2,1)S(1)} %all_gather.19), channel_id=1, source_target_pairs={{0,2},{1,3},{2,0},{3,1},{4,6},{5,7},{6,4},{7,5},{8,10},{9,11},{10,... | collective-permute-start | bytes 1572872 | tf_op jit(solution)/shard_map/ppermute | solution.py:159
  124.8 10.3 %copy-start.1 = (bf16[128,1024]{1,0:T(8,128)(2,1)S(1)}, bf16[128,1024]{1,0:T(8,128)(2,1)}, u32[]{:S(2)}) copy-start(bf16[128,1024]{1,0:T(8,128)(2,1)} %param.14) | copy-start | bytes 786436
  133.5 1.6 %collective-permute-start.12 = (bf16[128,1024]{1,0:T(8,128)(2,1)S(1)}, bf16[128,1024]{1,0:T(8,128)(2,1)S(1)}, u32[]{:S(2)}, u32[]{:S(2)}) collective-permute-start(bf16[128,1024]{1,0:T(8,128)(2,1)S(1)} %dynamic-slice_convert_fusion), channel_id=1, source_target_pairs={{0,1},{1,0},{2,3},{3,2},{4,5},{5,4},{6,7},{7,6},{8,9},{9,8},{10,11... | collective-permute-start | bytes 786440 | tf_op jit(solution)/shard_map/ppermute | solution.py:162

commit v3 on v2

v3 whole, which is shorter than its diff:
```python
import functools

import jax
import jax.numpy as jnp
from jax import lax
from jax.experimental import pallas as pl
from jax.experimental.pallas import tpu as pltpu
from jax.sharding import PartitionSpec as P

HEAD_SIZE = 128
epsilon = 1e-05
AXES = ("groups", "seq", "head")
VMEM_BYTES = 48 * 1024 * 1024
f32, bf16 = jnp.float32, jnp.bfloat16


def pack_kernel(groups, pairs, part, count, index_ref, rows_ref, *outs):
    for g in range(groups):
        for y in range(2):
            starts = [((2 * z + y) * groups + g) * part for z in range(pairs)]
            for k, out in enumerate(outs):

                @pl.when(index_ref[k] == g * 2 + y)
                def _():
                    out[...] = jnp.concatenate(
                        [rows_ref[:, s : s + part] for s in starts], axis=1
                    )


def pack(vision, index, core, groups, pairs, part, name):
    rows, width = vision.shape
    half = rows // 2
    block = 32
    steps = half // block
    count = len(index)
    depth = pairs * part
    scalars = jnp.stack([*index, core]).astype(jnp.int32)
    return pl.pallas_call(
        functools.partial(pack_kernel, groups, pairs, part, count),
        grid_spec=pltpu.PrefetchScalarGridSpec(
            num_scalar_prefetch=1,
            grid=(steps,),
            in_specs=[pl.BlockSpec((block, width), lambda i, s: (s[count] * steps + i, 0))],
            out_specs=[pl.BlockSpec((block, depth), lambda i, s: (i, 0))] * count,
        ),
        out_shape=[jax.ShapeDtypeStruct((half, depth), vision.dtype)] * count,
        compiler_params=pltpu.CompilerParams(vmem_limit_bytes=VMEM_BYTES),
        name=name,
    )(scalars, vision)


def project_kernel(groups, pairs, shifts, scalars, *refs):
    count = groups * 2
    near, far, slabs = refs[:count], refs[count : 2 * count], refs[2 * count : -count - 1]
    outs, placed = refs[-count - 1 : -1], refs[-1]
    half = near[0].shape[0]
    side, place = scalars[0], scalars[1]
    for shift, slab in zip(shifts, slabs):
        if isinstance(shift, tuple):
            continue
        placed[lax.rem(place + pairs - shift, pairs)] = slab[...]
    for shift, slab in zip(shifts, slabs):
        if isinstance(shift, tuple):

            @pl.when(place >= pairs // 2)
            def _():
                placed[lax.rem(place + pairs - shift[0], pairs)] = slab[...]

    w = jnp.concatenate([placed[z] for z in range(pairs)], axis=0)
    swapped = jnp.concatenate([w[:, HEAD_SIZE:], w[:, :HEAD_SIZE]], axis=1)
    w = jnp.where(side == 0, w, swapped)
    for part, pieces in enumerate((near, far)):
        lhs = jnp.concatenate([ref[...] for ref in pieces], axis=0)
        result = jnp.dot(lhs, w, preferred_element_type=f32)
        for source in range(count):
            by_group, by_side = source // 2, source % 2
            for to in range(2):
                out = outs[(-by_group) % groups * 2 + to]
                start = (0 if by_side == to else 2 * half) + part * half
                out[start : start + half, :] = result[
                    source * half : (source + 1) * half, to * HEAD_SIZE : (to + 1) * HEAD_SIZE
                ].astype(out.dtype)


def project(near, far, shifts, slabs, side, place, pairs, dtype, name):
    count = len(near)
    half = near[0].shape[0]
    vmem = pl.BlockSpec(memory_space=pltpu.VMEM)
    return pl.pallas_call(
        functools.partial(project_kernel, count // 2, pairs, shifts),
        in_specs=[pl.BlockSpec(memory_space=pltpu.SMEM)] + [vmem] * (2 * count + len(slabs)),
        out_specs=[vmem] * count,
        out_shape=[
            jax.ShapeDtypeStruct((4 * half, HEAD_SIZE), dtype if k else f32) for k in range(count)
        ],
        scratch_shapes=[pltpu.VMEM((pairs,) + slabs[0].shape, bf16)],
        compiler_params=pltpu.CompilerParams(vmem_limit_bytes=VMEM_BYTES),
        name=name,
    )(jnp.stack([side, place]).astype(jnp.int32), *near, *far, *slabs)


def score_kernel(heads, q_ref, *refs):
    keys, weights_ref, denominator_ref = refs[:-2], refs[-2], refs[-1]
    block = keys[0].shape[0]
    text = q_ref.shape[0] // heads
    for h in range(heads):
        rows = slice(h * text, (h + 1) * text)
        scores = [
            lax.dot_general(
                q_ref[rows, :], k[...], (((1,), (1,)), ((), ())), preferred_element_type=f32
            )
            * HEAD_SIZE ** (-0.5)
            for k in keys
        ]
        top = functools.reduce(
            jnp.maximum, [jnp.max(s, axis=-1, keepdims=True) for s in scores]
        )
        total = jnp.zeros_like(top)
        for n, s in enumerate(scores):
            weights = jnp.exp(s - top)
            total = total + jnp.sum(weights, axis=-1, keepdims=True)
            weights_ref[rows, n * block : (n + 1) * block] = weights.astype(bf16)
        denominator_ref[rows, :] = jnp.broadcast_to(total, (text, HEAD_SIZE))


def score(normed, keys, heads):
    rows = normed.shape[0]
    return pl.pallas_call(
        functools.partial(score_kernel, heads),
        out_shape=[
            jax.ShapeDtypeStruct((rows, len(keys) * keys[0].shape[0]), bf16),
            jax.ShapeDtypeStruct((rows, HEAD_SIZE), f32),
        ],
        compiler_params=pltpu.CompilerParams(vmem_limit_bytes=VMEM_BYTES),
        name="score",
    )(normed, *keys)


def mix_kernel(weights_ref, denominator_ref, *refs):
    values, out_ref = refs[:-1], refs[-1]
    text = out_ref.shape[0]
    v = jnp.concatenate([ref[...] for ref in values], axis=0)
    numerator = jnp.dot(weights_ref[...], v, preferred_element_type=f32)
    attended = (numerator / denominator_ref[...]).astype(bf16)
    for h in range(out_ref.shape[1] // HEAD_SIZE):
        out_ref[:, h * HEAD_SIZE : (h + 1) * HEAD_SIZE] = attended[h * text : (h + 1) * text, :]


def mix(weights, denominator, values, heads):
    rows = weights.shape[0]
    return pl.pallas_call(
        mix_kernel,
        out_shape=jax.ShapeDtypeStruct((rows // heads, heads * HEAD_SIZE), bf16),
        compiler_params=pltpu.CompilerParams(vmem_limit_bytes=VMEM_BYTES),
        name="mix",
    )(weights, denominator, *values)


def after(array, *others):
    return lax.optimization_barrier((array, others))[0]


def norm(array, gain):
    mean = jnp.mean(array * array, axis=-1, keepdims=True)
    return (array * lax.rsqrt(mean + epsilon) * gain).astype(bf16)


def body(
    sizes,
    queries,
    vision,
    key_matrix,
    value_matrix,
    out_weight,
    residual,
    query_norm_gain,
    key_norm_gain,
    attn_gate,
):
    groups, seq, cores = sizes
    pairs = seq // 2
    group = lax.axis_index("groups")
    side = lax.axis_index("seq") % 2
    place = lax.axis_index("seq") // 2
    core = lax.axis_index("head")

    def permute(array, target):
        perm = []
        for g in range(groups):
            for z in range(pairs):
                for y in range(2):
                    for c in range(cores):
                        to = target(g, z, y, c)
                        if to is not None:
                            tg, tz, ty, tc = to
                            perm.append(
                                (
                                    (g * seq + z * 2 + y) * cores + c,
                                    (tg % groups * seq + tz % pairs * 2 + ty % 2) * cores
                                    + tc % cores,
                                )
                            )
        return lax.ppermute(array, AXES, perm)

    def plane_shift(array, by_group, by_side):
        return permute(array, lambda g, z, y, c: (g + by_group, z, y + by_side, c))

    def line_shift(array, by):
        return permute(array, lambda g, z, y, c: (g, z + by, y, c))

    def core_swap(array):
        return permute(array, lambda g, z, y, c: (g, z, y, c + 1))

    middle = pairs // 2 if pairs % 2 == 0 and pairs > 2 else 0

    def line_near(array):
        return {k: line_shift(array, k) for k in range(1, pairs) if k != middle}

    def line_far(pieces):
        if not middle:
            return []
        up = permute(
            pieces[middle - 1],
            lambda g, z, y, c: (g, z + 1, y, c) if middle <= z + 1 < pairs else None,
        )
        down = permute(
            pieces[middle + 1],
            lambda g, z, y, c: (g, z - 1, y, c) if 0 <= z - 1 < middle else None,
        )
        return [up, down]

    near_shifts = [k for k in range(1, pairs) if k != middle]
    shifts = [0] + near_shifts + ([middle, (middle,)] if middle else [])

    def line_slabs(own, pieces, far):
        return [own] + [pieces[k] for k in near_shifts] + far[::-1]

    lines = [[2 * z + y for z in range(pairs)] for y in range(2)]

    def gather_pairs(array):
        return lax.all_gather(array, "seq", axis=0, tiled=True, axis_index_groups=lines)

    def all_pairs(array):
        return [array] + [line_shift(array, k) for k in range(1, pairs)]

    offsets = [(g, y) for g in range(groups) for y in range(2)]

    part = key_matrix.shape[0] // groups

    def own_part(matrix):
        return lax.dynamic_slice_in_dim(matrix, group * part, part, axis=0)

    key_own = own_part(key_matrix)
    key_near = line_near(key_own)

    index = [(group + g) % groups * 2 + (side + y) % 2 for g, y in offsets]
    vision = after(vision, key_own)
    sends = pack(vision, index[1:], core, groups, pairs, part, "pack_sends")
    received = [plane_shift(send, g, y) for send, (g, y) in zip(sends, offsets[1:])]
    vision = after(vision, *sends)
    near = pack(vision, index[:1], core, groups, pairs, part, "pack_near")
    near = [*near, *received]
    far = pack(vision, index[:1], 1 - core, groups, pairs, part, "pack_far")

    rows_q = queries.shape[0]
    half_q = queries.shape[1] // 2
    heads = half_q // HEAD_SIZE
    queries = after(queries, far[0])
    q_own = lax.dynamic_slice_in_dim(queries, side * half_q, half_q, axis=1)
    q_send = lax.dynamic_slice_in_dim(queries, (1 - side) * half_q, half_q, axis=1)

    key_far = line_far(key_near)
    received = [after(piece, *key_near.values()) for piece in received]
    far = [*far] + [core_swap(piece) for piece in received]
    value_own = after(own_part(value_matrix), *key_far)
    value_near = line_near(value_own)

    def scatter(pieces):
        return [plane_shift(piece, g, y) for piece, (g, y) in zip(pieces[1:], offsets[1:])]

    def sum_up(own, pieces):
        return functools.reduce(lambda a, b: a + b.astype(f32), pieces, own)

    key_slabs = line_slabs(key_own, key_near, key_far)
    key_pieces = project(near, far, shifts, key_slabs, side, place, pairs, f32, "project_keys")
    key_parts = scatter(key_pieces)
    value_near = {k: after(v, *key_pieces) for k, v in value_near.items()}
    value_far = line_far(value_near)
    q_recv = plane_shift(after(q_send, *key_parts), 0, 1)
    keys = norm(sum_up(key_pieces[0], key_parts), key_norm_gain)
    all_keys = all_pairs(keys)
    value_far = [after(v, keys) for v in value_far]
    value_slabs = line_slabs(value_own, value_near, value_far)
    value_pieces = project(
        near, far, shifts, value_slabs, side, place, pairs, bf16, "project_values"
    )
    value_parts = scatter(value_pieces)
    q_recv = after(q_recv, *value_pieces)
    q_pair = jnp.where(
        side == 0,
        jnp.concatenate([q_own, q_recv], axis=0),
        jnp.concatenate([q_recv, q_own], axis=0),
    )
    q_heads = jnp.concatenate(
        [q_pair[:, h * HEAD_SIZE : (h + 1) * HEAD_SIZE] for h in range(heads)], axis=0
    )
    normed = norm(q_heads.astype(f32), query_norm_gain)
    values = sum_up(value_pieces[0], value_parts).astype(bf16)
    all_values = all_pairs(values)
    all_keys = [after(k, values) for k in all_keys]
    weights, denominator = score(normed, all_keys, heads)
    attended = gather_pairs(mix(weights, denominator, all_values, heads))
    other = plane_shift(attended, 0, 1)
    depth = heads * HEAD_SIZE
    weight_own = lax.dynamic_slice_in_dim(out_weight, side * depth, depth, axis=0)
    weight_other = lax.dynamic_slice_in_dim(out_weight, (1 - side) * depth, depth, axis=0)
    projected = jnp.dot(attended, weight_own, preferred_element_type=f32) + jnp.dot(
        other, weight_other, preferred_element_type=f32
    )
    out_rows = residual.shape[0]
    send = lax.dynamic_slice_in_dim(projected, (1 - core) * out_rows, out_rows, axis=0)
    mine = lax.dynamic_slice_in_dim(projected, core * out_rows, out_rows, axis=0)
    mine = mine + core_swap(send.astype(bf16)).astype(f32)
    return (residual.astype(f32) + jnp.tanh(attn_gate[0]) * mine).astype(bf16)


def solution(mesh):
    in_specs = (
        P(("groups", "seq"), "head"),
        P(("groups", "seq"), None),
        P("seq", "head"),
        P("seq", "head"),
        P("head", "seq"),
        P(("groups", "head"), "seq"),
        P(),
        P(),
        P(),
    )
    out_specs = P(("groups", "head"), "seq")
    sizes = tuple(mesh.shape[axis] for axis in AXES)
    return jax.shard_map(
        functools.partial(body, sizes),
        mesh=mesh,
        in_specs=in_specs,
        out_specs=out_specs,
        check_vma=False,
    )
```

time: 136 us -> 138 us (1.015)
  blocking collectives: 87.6 us -> 15.7 us
  waiting for transfers between devices: 10.1 us -> 47.8 us
  starting transfers between devices: 14.2 us -> 42.4 us
  local copies, waits for them, and re-layouts: 2.92 us -> 9.71 us
  Pallas kernels: 12 us -> 13.4 us
    all_gather x5 -> x1, blocking collectives: 87.6 us -> 15.7 us  [gather_pairs(): lax.all_gather(array, 'seq', axis=0, tiled=True, axis_index_groups=lines)]
    ppermute x13 -> x29, waiting for transfers between devices: 10.1 us -> 47.8 us  [permute(): return lax.ppermute(array, AXES, perm)]
    ppermute x13 -> x29, starting transfers between devices: 14.2 us -> 42.4 us  [permute(): return lax.ppermute(array, AXES, perm)]
    unnamed x15 -> x29, local copies, waits for them, and re-layouts: 0.11 us -> 8.05 us
    pallas_call x4 -> x7, Pallas kernels: 12 us -> 13.4 us  [the longest x2 6.45 us: project(): pl.pallas_call(functools.partial(project_kernel, count // 2, pairs, shift...]
  transfers between devices with their start and end apart: 13 -> 29, of which waited for: 3 -> 15; matrix products, arithmetic and copies ran while one was open for 5% -> 3% of each run, Pallas kernels for 1% -> 5%
where the time goes in v3:
time: 138 us
  waiting for transfers between devices  47.8 us (35%)
  starting transfers between devices  42.4 us (31%)
  blocking collectives  15.7 us (11%)
  Pallas kernels  13.4 us (10%)
  local copies, waits for them, and re-layouts  9.71 us (7%)
  matrix products  4.62 us (3%)
  other arithmetic  2.89 us (2%)
    ppermute x29, waiting for transfers between devices, permute(): return lax.ppermute(array, AXES, perm)  47.8 us
    ppermute x29, starting transfers between devices, permute(): return lax.ppermute(array, AXES, perm)  42.4 us
    all_gather x1, blocking collectives, gather_pairs(): lax.all_gather(array, 'seq', axis=0, tiled=True, axis_index_groups=lines)  15.7 us
    unnamed x29, local copies, waits for them, and re-layouts  8.05 us
    pallas_call x2, Pallas kernels, project(): pl.pallas_call(functools.partial(project_kernel, count // 2, pairs, shift...  6.45 us
    pallas_call x3, Pallas kernels, pack(): pl.pallas_call(functools.partial(pack_kernel, groups, pairs, part, count)...  4.22 us
  transfers between devices with their start and end apart: 29, of which 15 were waited for; matrix products, arithmetic and copies ran while one was open for 3% of the time, Pallas kernels for 5%

profile of v3, /device:TPU:0, one launch (start us, length us, event | category | flops | bytes accessed | tf_op | source)
XLA Modules:
  0.0 137.6 jit_solution(13766956006987703503)
XLA Ops:
  0.0 1.0 copy-done
  1.1 0.1 pad_add_fusion.1.index_ref
  1.2 2.1 %copy-done.1 = bf16[256,7680]{1,0:T(8,128)(2,1)S(1)} copy-done((bf16[256,7680]{1,0:T(8,128)(2,1)S(1)}, bf16[256,7680]{1,0:T(8,128)(2,1)}, u32[]{:S(2)}) %copy-start.1) | copy-done | bytes 3932184
  3.3 2.1 %pack_sends.1 = (bf16[128,1920]{1,0:T(8,128)(2,1)S(1)}, bf16[128,1920]{1,0:T(8,128)(2,1)S(1)}, bf16[128,1920]{1,0:T(8,128)(2,1)S(1)}) custom-call(s32[4]{0:T(128)S(1)} %pad_add_fusion.1.index_ref, bf16[256,7680]{1,0:T(8,128)(2,1)S(1)} %copy-done.1), custom_call_target="tpu_custom_call" | custom-call | tf_op jit(solution)/shard_map/pack_sends/pallas_call | solution.py:38
  5.4 3.0 %collective-permute-start = (bf16[128,1920]{1,0:T(8,128)(2,1)S(1)}, bf16[128,1920]{1,0:T(8,128)(2,1)S(1)}, u32[]{:S(2)}, u32[]{:S(2)}) collective-permute-start(bf16[128,1920]{1,0:T(8,128)(2,1)S(1)} %get-tuple-element.36), channel_id=1, source_target_pairs={{0,2},{1,3},{2,0},{3,1},{4,6},{5,7},{6,4},{7,5},{8,10},{9,11},{10,... | collective-permute-start | bytes 1474568 | tf_op jit(solution)/shard_map/ppermute | solution.py:203
  8.4 1.5 %collective-permute-start.1 = (bf16[128,1920]{1,0:T(8,128)(2,1)S(1)}, bf16[128,1920]{1,0:T(8,128)(2,1)S(1)}, u32[]{:S(2)}, u32[]{:S(2)}) collective-permute-start(bf16[128,1920]{1,0:T(8,128)(2,1)S(1)} %get-tuple-element.37), channel_id=1, source_target_pairs={{0,16},{1,17},{2,18},{3,19},{4,20},{5,21},{6,22},{7,23},{8,24},{9,... | collective-permute-start | bytes 1474568 | tf_op jit(solution)/shard_map/ppermute | solution.py:203
  9.9 2.0 %collective-permute-start.3 = (bf16[480,256]{1,0:T(8,128)(2,1)S(1)}, bf16[480,256]{1,0:T(8,128)(2,1)}, u32[]{:S(2)}, u32[]{:S(2)}) collective-permute-start(bf16[480,256]{1,0:T(8,128)(2,1)S(1)} %constant_dynamic-slice_fusion.3.refs_8_), channel_id=1, source_target_pairs={{0,4},{1,5},{2,6},{3,7},{4,8},{5,9},{6,10},{7,11},{8,12},{9,13},{1... | collective-permute-start | bytes 737288 | tf_op jit(solution)/shard_map/ppermute | solution.py:203
  12.0 2.0 %collective-permute-start.4 = (bf16[480,256]{1,0:T(8,128)(2,1)S(1)}, bf16[480,256]{1,0:T(8,128)(2,1)}, u32[]{:S(2)}, u32[]{:S(2)}) collective-permute-start(bf16[480,256]{1,0:T(8,128)(2,1)S(1)} %constant_dynamic-slice_fusion.3.refs_8_), channel_id=1, source_target_pairs={{0,12},{1,13},{2,14},{3,15},{4,0},{5,1},{6,2},{7,3},{8,4},{9,5},{1... | collective-permute-start | bytes 737288 | tf_op jit(solution)/shard_map/ppermute | solution.py:203
  14.0 7.0 %collective-permute-done.3.refs_9_ = bf16[480,256]{1,0:T(8,128)(2,1)} collective-permute-done((bf16[480,256]{1,0:T(8,128)(2,1)S(1)}, bf16[480,256]{1,0:T(8,128)(2,1)}, u32[]{:S(2)}, u32[]{:S(2)}) %collective-permute-start.3) | collective-permute-done | bytes 245792 | tf_op jit(solution)/shard_map/ppermute | solution.py:203
  21.0 2.9 %collective-permute-done.4.refs_10_ = bf16[480,256]{1,0:T(8,128)(2,1)} collective-permute-done((bf16[480,256]{1,0:T(8,128)(2,1)S(1)}, bf16[480,256]{1,0:T(8,128)(2,1)}, u32[]{:S(2)}, u32[]{:S(2)}) %collective-permute-start.4) | collective-permute-done | bytes 245792 | tf_op jit(solution)/shard_map/ppermute | solution.py:203
  23.9 0.5 collective-permute-start.6
  24.4 7.0 %collective-permute-done.2.refs_3_ = bf16[128,1920]{1,0:T(8,128)(2,1)S(1)} collective-permute-done((bf16[128,1920]{1,0:T(8,128)(2,1)S(1)}, bf16[128,1920]{1,0:T(8,128)(2,1)S(1)}, u32[]{:S(2)}, u32[]{:S(2)}) %collective-permute-start.2) | collective-permute-done | bytes 491552 | tf_op jit(solution)/shard_map/ppermute | solution.py:203
  31.4 1.3 collective-permute-start.8
  32.7 1.4 %collective-permute-start.9 = (bf16[480,256]{1,0:T(8,128)(2,1)}, bf16[480,256]{1,0:T(8,128)(2,1)}, u32[]{:S(2)}, u32[]{:S(2)}) collective-permute-start(bf16[480,256]{1,0:T(8,128)(2,1)} %collective-permute-done.3.refs_9_), channel_id=1, source_target_pairs={{4,8},{5,9},{6,10},{7,11},{8,12},{9,13},{10,14},{11,15},{20,24},{2... | collective-permute-start | bytes 737288 | tf_op jit(solution)/shard_map/ppermute | solution.py:203
  34.1 0.1 pad_add_fusion
  34.2 2.1 %copy-done.2 = bf16[256,7680]{1,0:T(8,128)(2,1)S(1)} copy-done((bf16[256,7680]{1,0:T(8,128)(2,1)S(1)}, bf16[256,7680]{1,0:T(8,128)(2,1)}, u32[]{:S(2)}) %copy-start.2) | copy-done | bytes 3932184
  36.3 1.1 pack_far.1.refs_4_
  37.3 1.0 copy-done.3
  38.4 1.1 pack_near.1.refs_0_
  39.5 0.1 pad_add_fusion.2.scalars
  39.6 2.4 %collective-permute-done.8.refs_11_ = bf16[480,256]{1,0:T(8,128)(2,1)} collective-permute-done((bf16[480,256]{1,0:T(8,128)(2,1)}, bf16[480,256]{1,0:T(8,128)(2,1)}, u32[]{:S(2)}, u32[]{:S(2)}) %collective-permute-start.8) | collective-permute-done | bytes 245792 | tf_op jit(solution)/shard_map/ppermute | solution.py:203
  42.0 0.9 copy-done.5
  43.0 3.7 %project_keys.1 = (f32[512,128]{1,0:T(8,128)S(1)}, f32[512,128]{1,0:T(8,128)}, f32[512,128]{1,0:T(8,128)}, f32[512,128]{1,0:T(8,128)}) custom-call(s32[2]{0:T(128)S(1)} %pad_add_fusion.2.scalars, bf16[128,1920]{1,0:T(8,128)(2,1)S(1)} %pack_near.1.refs_0_, bf16[128,1920]{1,0:T(8,128)(2,1)S(1)} %collective-permute-done.refs_1_, ...), custom_call_target="tpu_custom_call" | custom-call | tf_op jit(solution)/shard_map/project_keys/pallas_call | solution.py:89
  46.6 0.7 copy-done.6
  47.3 1.6 %collective-permute-start.10 = (f32[512,128]{1,0:T(8,128)}, f32[512,128]{1,0:T(8,128)}, u32[]{:S(2)}, u32[]{:S(2)}) collective-permute-start(f32[512,128]{1,0:T(8,128)} %get-tuple-element.44), channel_id=1, source_target_pairs={{0,2},{1,3},{2,0},{3,1},{4,6},{5,7},{6,4},{7,5},{8,10},{9,11},{10,... | collective-permute-start | bytes 786440 | tf_op jit(solution)/shard_map/ppermute | solution.py:203
  49.0 1.5 %collective-permute-start.11 = (f32[512,128]{1,0:T(8,128)}, f32[512,128]{1,0:T(8,128)}, u32[]{:S(2)}, u32[]{:S(2)}) collective-permute-start(f32[512,128]{1,0:T(8,128)} %get-tuple-element.45), channel_id=1, source_target_pairs={{0,16},{1,17},{2,18},{3,19},{4,20},{5,21},{6,22},{7,23},{8,24},{9,... | collective-permute-start | bytes 786440 | tf_op jit(solution)/shard_map/ppermute | solution.py:203
  50.5 0.3 collective-permute-start.12
  50.8 0.7 constant_dynamic-slice_fusion.refs_8_
  51.5 3.9 %collective-permute-start.14 = (bf16[480,256]{1,0:T(8,128)(2,1)}, bf16[480,256]{1,0:T(8,128)(2,1)}, u32[]{:S(2)}, u32[]{:S(2)}) collective-permute-start(bf16[480,256]{1,0:T(8,128)(2,1)} %constant_dynamic-slice_fusion.refs_8_), channel_id=1, source_target_pairs={{0,4},{1,5},{2,6},{3,7},{4,8},{5,9},{6,10},{7,11},{8,12},{9,13},{1... | collective-permute-start | bytes 737288 | tf_op jit(solution)/shard_map/ppermute | solution.py:203
  55.5 1.3 collective-permute-start.15
  56.8 0.9 constant_dynamic-slice_fusion.2
  57.7 6.3 %collective-permute-done.14.refs_9_ = bf16[480,256]{1,0:T(8,128)(2,1)} collective-permute-done((bf16[480,256]{1,0:T(8,128)(2,1)}, bf16[480,256]{1,0:T(8,128)(2,1)}, u32[]{:S(2)}, u32[]{:S(2)}) %collective-permute-start.14) | collective-permute-done | bytes 245792 | tf_op jit(solution)/shard_map/ppermute | solution.py:203
  64.0 3.4 %collective-permute-done.15.refs_10_ = bf16[480,256]{1,0:T(8,128)(2,1)} collective-permute-done((bf16[480,256]{1,0:T(8,128)(2,1)}, bf16[480,256]{1,0:T(8,128)(2,1)}, u32[]{:S(2)}, u32[]{:S(2)}) %collective-permute-start.15) | collective-permute-done | bytes 245792 | tf_op jit(solution)/shard_map/ppermute | solution.py:203
  67.4 1.3 collective-permute-start.16
  68.7 0.7 collective-permute-start.17
  69.4 1.6 %collective-permute-start.13 = (bf16[32,1024]{1,0:T(8,128)(2,1)S(1)}, bf16[32,1024]{1,0:T(8,128)(2,1)S(1)}, u32[]{:S(2)}, u32[]{:S(2)}) collective-permute-start(bf16[32,1024]{1,0:T(8,128)(2,1)S(1)} %get-tuple-element.47), channel_id=1, source_target_pairs={{0,2},{1,3},{2,0},{3,1},{4,6},{5,7},{6,4},{7,5},{8,10},{9,11},{10,... | collective-permute-start | bytes 196616 | tf_op jit(solution)/shard_map/ppermute | solution.py:203
  71.0 1.3 multiply_reduce_fusion
  72.3 0.1 multiply_convert_fusion.refs_0_
  72.5 4.5 %collective-permute-start.21 = (bf16[512,128]{1,0:T(8,128)(2,1)S(1)}, bf16[512,128]{1,0:T(8,128)(2,1)S(1)}, u32[]{:S(2)}, u32[]{:S(2)}) collective-permute-start(bf16[512,128]{1,0:T(8,128)(2,1)S(1)} %multiply_convert_fusion.refs_0_), channel_id=1, source_target_pairs={{0,4},{1,5},{2,6},{3,7},{4,8},{5,9},{6,10},{7,11},{8,12},{9,13},{1... | collective-permute-start | bytes 393224 | tf_op jit(solution)/shard_map/ppermute | solution.py:203
  77.0 3.1 %collective-permute-done.16.refs_11_ = bf16[480,256]{1,0:T(8,128)(2,1)S(1)} collective-permute-done((bf16[480,256]{1,0:T(8,128)(2,1)}, bf16[480,256]{1,0:T(8,128)(2,1)S(1)}, u32[]{:S(2)}, u32[]{:S(2)}) %collective-permute-start.16) | collective-permute-done | bytes 245792 | tf_op jit(solution)/shard_map/ppermute | solution.py:203
  80.1 2.8 %project_values.1 = (f32[512,128]{1,0:T(8,128)S(1)}, bf16[512,128]{1,0:T(8,128)(2,1)S(1)}, bf16[512,128]{1,0:T(8,128)(2,1)S(1)}, bf16[512,128]{1,0:T(8,128)(2,1)S(1)}) custom-call(s32[2]{0:T(128)S(1)} %pad_add_fusion.2.scalars, bf16[128,1920]{1,0:T(8,128)(2,1)S(1)} %pack_near.1.refs_0_, bf16[128,1920]{1,0:T(8,128)(2,1)S(1)} %collective-permute-done.refs_1_, ...), custom_call_target="tpu_custom_call" | custom-call | tf_op jit(solution)/shard_map/project_values/pallas_call | solution.py:89
  82.8 2.6 %collective-permute-start.20 = (bf16[512,128]{1,0:T(8,128)(2,1)S(1)}, bf16[512,128]{1,0:T(8,128)(2,1)S(1)}, u32[]{:S(2)}, u32[]{:S(2)}) collective-permute-start(bf16[512,128]{1,0:T(8,128)(2,1)S(1)} %get-tuple-element.57), channel_id=1, source_target_pairs={{0,18},{1,19},{2,16},{3,17},{4,22},{5,23},{6,20},{7,21},{8,26},{9,... | collective-permute-start | bytes 393224 | tf_op jit(solution)/shard_map/ppermute | solution.py:203
  85.4 0.5 collective-permute-start.19
  85.9 0.5 collective-permute-start.18
  86.6 0.1 fusion.7
  86.7 2.9 %collective-permute-done.20 = bf16[512,128]{1,0:T(8,128)(2,1)S(1)} collective-permute-done((bf16[512,128]{1,0:T(8,128)(2,1)S(1)}, bf16[512,128]{1,0:T(8,128)(2,1)S(1)}, u32[]{:S(2)}, u32[]{:S(2)}) %collective-permute-start.20) | collective-permute-done | bytes 131104 | tf_op jit(solution)/shard_map/ppermute | solution.py:203
  89.6 0.8 collective-permute-start.23
  90.5 0.6 collective-permute-done.19
  91.2 4.1 %collective-permute-start.24 = (bf16[512,128]{1,0:T(8,128)(2,1)S(1)}, bf16[512,128]{1,0:T(8,128)(2,1)S(1)}, u32[]{:S(2)}, u32[]{:S(2)}) collective-permute-start(bf16[512,128]{1,0:T(8,128)(2,1)S(1)} %add_convert_fusion.1.refs_0_), channel_id=1, source_target_pairs={{0,4},{1,5},{2,6},{3,7},{4,8},{5,9},{6,10},{7,11},{8,12},{9,13},{1... | collective-permute-start | bytes 393224 | tf_op jit(solution)/shard_map/ppermute | solution.py:203
  95.3 0.8 collective-permute-start.25
  96.1 2.8 %collective-permute-start.26 = (bf16[512,128]{1,0:T(8,128)(2,1)S(1)}, bf16[512,128]{1,0:T(8,128)(2,1)S(1)}, u32[]{:S(2)}, u32[]{:S(2)}) collective-permute-start(bf16[512,128]{1,0:T(8,128)(2,1)S(1)} %add_convert_fusion.1.refs_0_), channel_id=1, source_target_pairs={{0,12},{1,13},{2,14},{3,15},{4,0},{5,1},{6,2},{7,3},{8,4},{9,5},{1... | collective-permute-start | bytes 393224 | tf_op jit(solution)/shard_map/ppermute | solution.py:203
  99.0 0.1 fusion.9.q_ref
  99.1 0.1 collective-permute-done.23.refs_3_
  99.2 2.0 %score.1 = (bf16[512,2048]{1,0:T(8,128)(2,1)S(1)}, f32[512,128]{1,0:T(8,128)S(1)}) custom-call(bf16[512,128]{1,0:T(8,128)(2,1)S(1)} %fusion.9.q_ref, bf16[512,128]{1,0:T(8,128)(2,1)S(1)} %multiply_convert_fusion.refs_0_, bf16[512,128]{1,0:T(8,128)(2,1)S(1)} %collective-permute-done.21.refs_1_, bf16[512,128]{1,0:T(8,128)(2,1)S(1)} %collective-permute-done.22.refs_2_, ...), custom_call_target="tpu_custom_call" | custom-call | tf_op jit(solution)/shard_map/score/pallas_call | solution.py:128
  101.2 0.4 collective-permute-done.24.refs_1_
  101.7 3.2 %collective-permute-done.25.refs_2_ = bf16[512,128]{1,0:T(8,128)(2,1)S(1)} collective-permute-done((bf16[512,128]{1,0:T(8,128)(2,1)S(1)}, bf16[512,128]{1,0:T(8,128)(2,1)S(1)}, u32[]{:S(2)}, u32[]{:S(2)}) %collective-permute-start.25) | collective-permute-done | bytes 131104 | tf_op jit(solution)/shard_map/ppermute | solution.py:203
  104.9 0.7 mix.1
  105.6 15.7 %all_gather.3 = bf16[256,1024]{1,0:T(8,128)(2,1)S(1)} all-gather(bf16[64,1024]{1,0:T(8,128)(2,1)S(1)} %mix.1), channel_id=1, replica_groups={{0,4,8,12},{2,6,10,14},{1,5,9,13},{3,7,11,15},{16,20,24,28},{18,22,26,3..., dimensions={0}, use_global_device_ids=true | all-gather | bytes 655360 | tf_op jit(solution)/shard_map/all_gather | solution.py:241
  121.3 1.7 %collective-permute-start.27 = (bf16[256,1024]{1,0:T(8,128)(2,1)S(1)}, bf16[256,1024]{1,0:T(8,128)(2,1)S(1)}, u32[]{:S(2)}, u32[]{:S(2)}) collective-permute-start(bf16[256,1024]{1,0:T(8,128)(2,1)S(1)} %all_gather.3), channel_id=1, source_target_pairs={{0,2},{1,3},{2,0},{3,1},{4,6},{5,7},{6,4},{7,5},{8,10},{9,11},{10,... | collective-permute-start | bytes 1572872 | tf_op jit(solution)/shard_map/ppermute | solution.py:203
  123.0 7.5 %collective-permute-done.27 = bf16[256,1024]{1,0:T(8,128)(2,1)S(1)} collective-permute-done((bf16[256,1024]{1,0:T(8,128)(2,1)S(1)}, bf16[256,1024]{1,0:T(8,128)(2,1)S(1)}, u32[]{:S(2)}, u32[]{:S(2)}) %collective-permute-start.27) | collective-permute-done | bytes 524320 | tf_op jit(solution)/shard_map/ppermute | solution.py:203
  130.5 2.3 %fusion = f32[256,1024]{1,0:T(8,128)S(1)} fusion(bf16[256,1024]{1,0:T(8,128)(2,1)S(1)} %collective-permute-done.27, bf16[2048,1024]{1,0:T(8,128)(2,1)} %param.13, s32[]{:T(128)S(6)} %select_n.69), kind=kOutput, calls=%fused_computation | convolution fusion | flops 536870912 | bytes 3670020 | tf_op jit(solution)/shard_map/dot_general | solution.py:317
  132.8 2.3 %fusion.4 = f32[256,1024]{1,0:T(8,128)S(1)} fusion(f32[256,1024]{1,0:T(8,128)S(1)} %fusion, bf16[256,1024]{1,0:T(8,128)(2,1)S(1)} %all_gather.3, bf16[2048,1024]{1,0:T(8,128)(2,1)} %param.13, s32[]{:T(128)S(6)} %select_n.68), kind=kOutput, calls=%fused_computation.4 | convolution fusion | flops 537133056 | bytes 4718596 | tf_op jit(solution)/shard_map/dot_general | solution.py:317
  136.0 0.8 collective-permute-done.28
  136.8 0.8 add_convert_fusion
  (50 shorter events, 0.5 us)
Async XLA Ops:
  0.0 1.0 copy-start
  1.1 33.1 %copy-start.4 = (bf16[480,256]{1,0:T(8,128)(2,1)}, bf16[480,256]{1,0:T(8,128)(2,1)S(1)}, u32[]{:S(2)}) copy-start(bf16[480,256]{1,0:T(8,128)(2,1)S(1)} %constant_dynamic-slice_fusion.3.refs_8_) | copy-start | bytes 737284
  1.2 2.1 %copy-start.1 = (bf16[256,7680]{1,0:T(8,128)(2,1)S(1)}, bf16[256,7680]{1,0:T(8,128)(2,1)}, u32[]{:S(2)}) copy-start(bf16[256,7680]{1,0:T(8,128)(2,1)} %rows_ref.2) | copy-start | bytes 11796484
  5.4 18.5 %collective-permute-start = (bf16[128,1920]{1,0:T(8,128)(2,1)S(1)}, bf16[128,1920]{1,0:T(8,128)(2,1)S(1)}, u32[]{:S(2)}, u32[]{:S(2)}) collective-permute-start(bf16[128,1920]{1,0:T(8,128)(2,1)S(1)} %get-tuple-element.36), channel_id=1, source_target_pairs={{0,2},{1,3},{2,0},{3,1},{4,6},{5,7},{6,4},{7,5},{8,10},{9,11},{10,... | collective-permute-start | bytes 1474568 | tf_op jit(solution)/shard_map/ppermute | solution.py:203
  8.4 15.5 %collective-permute-start.1 = (bf16[128,1920]{1,0:T(8,128)(2,1)S(1)}, bf16[128,1920]{1,0:T(8,128)(2,1)S(1)}, u32[]{:S(2)}, u32[]{:S(2)}) collective-permute-start(bf16[128,1920]{1,0:T(8,128)(2,1)S(1)} %get-tuple-element.37), channel_id=1, source_target_pairs={{0,16},{1,17},{2,18},{3,19},{4,20},{5,21},{6,22},{7,23},{8,24},{9,... | collective-permute-start | bytes 1474568 | tf_op jit(solution)/shard_map/ppermute | solution.py:203
  9.9 21.5 %collective-permute-start.2 = (bf16[128,1920]{1,0:T(8,128)(2,1)S(1)}, bf16[128,1920]{1,0:T(8,128)(2,1)S(1)}, u32[]{:S(2)}, u32[]{:S(2)}) collective-permute-start(bf16[128,1920]{1,0:T(8,128)(2,1)S(1)} %get-tuple-element.38), channel_id=1, source_target_pairs={{0,18},{1,19},{2,16},{3,17},{4,22},{5,23},{6,20},{7,21},{8,26},{9,... | collective-permute-start | bytes 1474568 | tf_op jit(solution)/shard_map/ppermute | solution.py:203
  9.9 11.1 %collective-permute-start.3 = (bf16[480,256]{1,0:T(8,128)(2,1)S(1)}, bf16[480,256]{1,0:T(8,128)(2,1)}, u32[]{:S(2)}, u32[]{:S(2)}) collective-permute-start(bf16[480,256]{1,0:T(8,128)(2,1)S(1)} %constant_dynamic-slice_fusion.3.refs_8_), channel_id=1, source_target_pairs={{0,4},{1,5},{2,6},{3,7},{4,8},{5,9},{6,10},{7,11},{8,12},{9,13},{1... | collective-permute-start | bytes 737288 | tf_op jit(solution)/shard_map/ppermute | solution.py:203
  12.0 11.9 %collective-permute-start.4 = (bf16[480,256]{1,0:T(8,128)(2,1)S(1)}, bf16[480,256]{1,0:T(8,128)(2,1)}, u32[]{:S(2)}, u32[]{:S(2)}) collective-permute-start(bf16[480,256]{1,0:T(8,128)(2,1)S(1)} %constant_dynamic-slice_fusion.3.refs_8_), channel_id=1, source_target_pairs={{0,12},{1,13},{2,14},{3,15},{4,0},{5,1},{6,2},{7,3},{8,4},{9,5},{1... | collective-permute-start | bytes 737288 | tf_op jit(solution)/shard_map/ppermute | solution.py:203
  23.9 18.1 %collective-permute-start.5 = (bf16[128,1920]{1,0:T(8,128)(2,1)S(1)}, bf16[128,1920]{1,0:T(8,128)(2,1)S(1)}, u32[]{:S(2)}, u32[]{:S(2)}) collective-permute-start(bf16[128,1920]{1,0:T(8,128)(2,1)S(1)} %collective-permute-done.refs_1_), channel_id=1, source_target_pairs={{0,1},{1,0},{2,3},{3,2},{4,5},{5,4},{6,7},{7,6},{8,9},{9,8},{10,11... | collective-permute-start | bytes 1474568 | tf_op jit(solution)/shard_map/ppermute | solution.py:203
  23.9 18.1 %collective-permute-start.6 = (bf16[128,1920]{1,0:T(8,128)(2,1)S(1)}, bf16[128,1920]{1,0:T(8,128)(2,1)}, u32[]{:S(2)}, u32[]{:S(2)}) collective-permute-start(bf16[128,1920]{1,0:T(8,128)(2,1)S(1)} %collective-permute-done.1.refs_2_), channel_id=1, source_target_pairs={{0,1},{1,0},{2,3},{3,2},{4,5},{5,4},{6,7},{7,6},{8,9},{9,8},{10,11... | collective-permute-start | bytes 1474568 | tf_op jit(solution)/shard_map/ppermute | solution.py:203
  31.4 10.6 %collective-permute-start.7 = (bf16[128,1920]{1,0:T(8,128)(2,1)S(1)}, bf16[128,1920]{1,0:T(8,128)(2,1)}, u32[]{:S(2)}, u32[]{:S(2)}) collective-permute-start(bf16[128,1920]{1,0:T(8,128)(2,1)S(1)} %collective-permute-done.2.refs_3_), channel_id=1, source_target_pairs={{0,1},{1,0},{2,3},{3,2},{4,5},{5,4},{6,7},{7,6},{8,9},{9,8},{10,11... | collective-permute-start | bytes 1474568 | tf_op jit(solution)/shard_map/ppermute | solution.py:203
  31.4 10.6 %collective-permute-start.8 = (bf16[480,256]{1,0:T(8,128)(2,1)}, bf16[480,256]{1,0:T(8,128)(2,1)}, u32[]{:S(2)}, u32[]{:S(2)}) collective-permute-start(bf16[480,256]{1,0:T(8,128)(2,1)} %collective-permute-done.4.refs_10_), channel_id=1, source_target_pairs={{4,0},{5,1},{6,2},{7,3},{8,4},{9,5},{10,6},{11,7},{20,16},{21,17},... | collective-permute-start | bytes 737288 | tf_op jit(solution)/shard_map/ppermute | solution.py:203
  32.7 9.3 %collective-permute-start.9 = (bf16[480,256]{1,0:T(8,128)(2,1)}, bf16[480,256]{1,0:T(8,128)(2,1)}, u32[]{:S(2)}, u32[]{:S(2)}) collective-permute-start(bf16[480,256]{1,0:T(8,128)(2,1)} %collective-permute-done.3.refs_9_), channel_id=1, source_target_pairs={{4,8},{5,9},{6,10},{7,11},{8,12},{9,13},{10,14},{11,15},{20,24},{2... | collective-permute-start | bytes 737288 | tf_op jit(solution)/shard_map/ppermute | solution.py:203
  34.1 2.1 %copy-start.2 = (bf16[256,7680]{1,0:T(8,128)(2,1)S(1)}, bf16[256,7680]{1,0:T(8,128)(2,1)}, u32[]{:S(2)}) copy-start(bf16[256,7680]{1,0:T(8,128)(2,1)} %rows_ref.2) | copy-start | bytes 11796484
  36.3 2.1 %copy-start.3 = (bf16[256,7680]{1,0:T(8,128)(2,1)S(1)}, bf16[256,7680]{1,0:T(8,128)(2,1)}, u32[]{:S(2)}) copy-start(bf16[256,7680]{1,0:T(8,128)(2,1)} %rows_ref.2) | copy-start | bytes 11796484
  39.5 32.8 %copy-start.9 = (f32[128]{0:T(128)S(1)}, f32[128]{0:T(128)}, u32[]{:S(2)}) copy-start(f32[128]{0:T(128)} %param.16) | copy-start | bytes 1540
  42.0 0.9 copy-start.5
  43.0 7.9 %copy-start.8 = (bf16[960,256]{1,0:T(8,128)(2,1)S(1)}, bf16[960,256]{1,0:T(8,128)(2,1)}, u32[]{:S(2)}) copy-start(bf16[960,256]{1,0:T(8,128)(2,1)} %param.12) | copy-start | bytes 1474564
  46.6 0.7 copy-start.6
  47.3 22.0 %collective-permute-start.10 = (f32[512,128]{1,0:T(8,128)}, f32[512,128]{1,0:T(8,128)}, u32[]{:S(2)}, u32[]{:S(2)}) collective-permute-start(f32[512,128]{1,0:T(8,128)} %get-tuple-element.44), channel_id=1, source_target_pairs={{0,2},{1,3},{2,0},{3,1},{4,6},{5,7},{6,4},{7,5},{8,10},{9,11},{10,... | collective-permute-start | bytes 786440 | tf_op jit(solution)/shard_map/ppermute | solution.py:203
  49.0 20.4 %collective-permute-start.11 = (f32[512,128]{1,0:T(8,128)}, f32[512,128]{1,0:T(8,128)}, u32[]{:S(2)}, u32[]{:S(2)}) collective-permute-start(f32[512,128]{1,0:T(8,128)} %get-tuple-element.45), channel_id=1, source_target_pairs={{0,16},{1,17},{2,18},{3,19},{4,20},{5,21},{6,22},{7,23},{8,24},{9,... | collective-permute-start | bytes 786440 | tf_op jit(solution)/shard_map/ppermute | solution.py:203
  50.5 18.9 %collective-permute-start.12 = (f32[512,128]{1,0:T(8,128)}, f32[512,128]{1,0:T(8,128)}, u32[]{:S(2)}, u32[]{:S(2)}) collective-permute-start(f32[512,128]{1,0:T(8,128)} %get-tuple-element.46), channel_id=1, source_target_pairs={{0,18},{1,19},{2,16},{3,17},{4,22},{5,23},{6,20},{7,21},{8,26},{9,... | collective-permute-start | bytes 786440 | tf_op jit(solution)/shard_map/ppermute | solution.py:203
  51.5 12.5 %collective-permute-start.14 = (bf16[480,256]{1,0:T(8,128)(2,1)}, bf16[480,256]{1,0:T(8,128)(2,1)}, u32[]{:S(2)}, u32[]{:S(2)}) collective-permute-start(bf16[480,256]{1,0:T(8,128)(2,1)} %constant_dynamic-slice_fusion.refs_8_), channel_id=1, source_target_pairs={{0,4},{1,5},{2,6},{3,7},{4,8},{5,9},{6,10},{7,11},{8,12},{9,13},{1... | collective-permute-start | bytes 737288 | tf_op jit(solution)/shard_map/ppermute | solution.py:203
  55.5 11.9 %collective-permute-start.15 = (bf16[480,256]{1,0:T(8,128)(2,1)}, bf16[480,256]{1,0:T(8,128)(2,1)}, u32[]{:S(2)}, u32[]{:S(2)}) collective-permute-start(bf16[480,256]{1,0:T(8,128)(2,1)} %constant_dynamic-slice_fusion.refs_8_), channel_id=1, source_target_pairs={{0,12},{1,13},{2,14},{3,15},{4,0},{5,1},{6,2},{7,3},{8,4},{9,5},{1... | collective-permute-start | bytes 737288 | tf_op jit(solution)/shard_map/ppermute | solution.py:203
  67.4 12.7 %collective-permute-start.16 = (bf16[480,256]{1,0:T(8,128)(2,1)}, bf16[480,256]{1,0:T(8,128)(2,1)S(1)}, u32[]{:S(2)}, u32[]{:S(2)}) collective-permute-start(bf16[480,256]{1,0:T(8,128)(2,1)} %collective-permute-done.15.refs_10_), channel_id=1, source_target_pairs={{4,0},{5,1},{6,2},{7,3},{8,4},{9,5},{10,6},{11,7},{20,16},{21,17},... | collective-permute-start | bytes 737288 | tf_op jit(solution)/shard_map/ppermute | solution.py:203
  68.7 11.4 %collective-permute-start.17 = (bf16[480,256]{1,0:T(8,128)(2,1)}, bf16[480,256]{1,0:T(8,128)(2,1)S(1)}, u32[]{:S(2)}, u32[]{:S(2)}) collective-permute-start(bf16[480,256]{1,0:T(8,128)(2,1)} %collective-permute-done.14.refs_9_), channel_id=1, source_target_pairs={{4,8},{5,9},{6,10},{7,11},{8,12},{9,13},{10,14},{11,15},{20,24},{2... | collective-permute-start | bytes 737288 | tf_op jit(solution)/shard_map/ppermute | solution.py:203
  69.4 29.6 %copy-start.10 = (f32[128]{0:T(128)S(1)}, f32[128]{0:T(128)}, u32[]{:S(2)}) copy-start(f32[128]{0:T(128)} %param.15) | copy-start | bytes 1540
  69.4 16.5 %collective-permute-start.13 = (bf16[32,1024]{1,0:T(8,128)(2,1)S(1)}, bf16[32,1024]{1,0:T(8,128)(2,1)S(1)}, u32[]{:S(2)}, u32[]{:S(2)}) collective-permute-start(bf16[32,1024]{1,0:T(8,128)(2,1)S(1)} %get-tuple-element.47), channel_id=1, source_target_pairs={{0,2},{1,3},{2,0},{3,1},{4,6},{5,7},{6,4},{7,5},{8,10},{9,11},{10,... | collective-permute-start | bytes 196616 | tf_op jit(solution)/shard_map/ppermute | solution.py:203
  72.5 23.7 %collective-permute-start.21 = (bf16[512,128]{1,0:T(8,128)(2,1)S(1)}, bf16[512,128]{1,0:T(8,128)(2,1)S(1)}, u32[]{:S(2)}, u32[]{:S(2)}) collective-permute-start(bf16[512,128]{1,0:T(8,128)(2,1)S(1)} %multiply_convert_fusion.refs_0_), channel_id=1, source_target_pairs={{0,4},{1,5},{2,6},{3,7},{4,8},{5,9},{6,10},{7,11},{8,12},{9,13},{1... | collective-permute-start | bytes 393224 | tf_op jit(solution)/shard_map/ppermute | solution.py:203
  77.0 22.1 %collective-permute-start.22 = (bf16[512,128]{1,0:T(8,128)(2,1)S(1)}, bf16[512,128]{1,0:T(8,128)(2,1)S(1)}, u32[]{:S(2)}, u32[]{:S(2)}) collective-permute-start(bf16[512,128]{1,0:T(8,128)(2,1)S(1)} %multiply_convert_fusion.refs_0_), channel_id=1, source_target_pairs={{0,8},{1,9},{2,10},{3,11},{4,12},{5,13},{6,14},{7,15},{8,0},{9,1},... | collective-permute-start | bytes 393224 | tf_op jit(solution)/shard_map/ppermute | solution.py:203
  82.8 6.8 %collective-permute-start.20 = (bf16[512,128]{1,0:T(8,128)(2,1)S(1)}, bf16[512,128]{1,0:T(8,128)(2,1)S(1)}, u32[]{:S(2)}, u32[]{:S(2)}) collective-permute-start(bf16[512,128]{1,0:T(8,128)(2,1)S(1)} %get-tuple-element.57), channel_id=1, source_target_pairs={{0,18},{1,19},{2,16},{3,17},{4,22},{5,23},{6,20},{7,21},{8,26},{9,... | collective-permute-start | bytes 393224 | tf_op jit(solution)/shard_map/ppermute | solution.py:203
  85.4 5.7 %collective-permute-start.19 = (bf16[512,128]{1,0:T(8,128)(2,1)S(1)}, bf16[512,128]{1,0:T(8,128)(2,1)S(1)}, u32[]{:S(2)}, u32[]{:S(2)}) collective-permute-start(bf16[512,128]{1,0:T(8,128)(2,1)S(1)} %get-tuple-element.56), channel_id=1, source_target_pairs={{0,16},{1,17},{2,18},{3,19},{4,20},{5,21},{6,22},{7,23},{8,24},{9,... | collective-permute-start | bytes 393224 | tf_op jit(solution)/shard_map/ppermute | solution.py:203
  85.9 5.3 %collective-permute-start.18 = (bf16[512,128]{1,0:T(8,128)(2,1)S(1)}, bf16[512,128]{1,0:T(8,128)(2,1)S(1)}, u32[]{:S(2)}, u32[]{:S(2)}) collective-permute-start(bf16[512,128]{1,0:T(8,128)(2,1)S(1)} %get-tuple-element.55), channel_id=1, source_target_pairs={{0,2},{1,3},{2,0},{3,1},{4,6},{5,7},{6,4},{7,5},{8,10},{9,11},{10,... | collective-permute-start | bytes 393224 | tf_op jit(solution)/shard_map/ppermute | solution.py:203
  89.6 9.6 %collective-permute-start.23 = (bf16[512,128]{1,0:T(8,128)(2,1)S(1)}, bf16[512,128]{1,0:T(8,128)(2,1)S(1)}, u32[]{:S(2)}, u32[]{:S(2)}) collective-permute-start(bf16[512,128]{1,0:T(8,128)(2,1)S(1)} %multiply_convert_fusion.refs_0_), channel_id=1, source_target_pairs={{0,12},{1,13},{2,14},{3,15},{4,0},{5,1},{6,2},{7,3},{8,4},{9,5},{1... | collective-permute-start | bytes 393224 | tf_op jit(solution)/shard_map/ppermute | solution.py:203
  91.2 10.4 %collective-permute-start.24 = (bf16[512,128]{1,0:T(8,128)(2,1)S(1)}, bf16[512,128]{1,0:T(8,128)(2,1)S(1)}, u32[]{:S(2)}, u32[]{:S(2)}) collective-permute-start(bf16[512,128]{1,0:T(8,128)(2,1)S(1)} %add_convert_fusion.1.refs_0_), channel_id=1, source_target_pairs={{0,4},{1,5},{2,6},{3,7},{4,8},{5,9},{6,10},{7,11},{8,12},{9,13},{1... | collective-permute-start | bytes 393224 | tf_op jit(solution)/shard_map/ppermute | solution.py:203
  95.3 9.6 %collective-permute-start.25 = (bf16[512,128]{1,0:T(8,128)(2,1)S(1)}, bf16[512,128]{1,0:T(8,128)(2,1)S(1)}, u32[]{:S(2)}, u32[]{:S(2)}) collective-permute-start(bf16[512,128]{1,0:T(8,128)(2,1)S(1)} %add_convert_fusion.1.refs_0_), channel_id=1, source_target_pairs={{0,8},{1,9},{2,10},{3,11},{4,12},{5,13},{6,14},{7,15},{8,0},{9,1},... | collective-permute-start | bytes 393224 | tf_op jit(solution)/shard_map/ppermute | solution.py:203
  96.1 8.8 %collective-permute-start.26 = (bf16[512,128]{1,0:T(8,128)(2,1)S(1)}, bf16[512,128]{1,0:T(8,128)(2,1)S(1)}, u32[]{:S(2)}, u32[]{:S(2)}) collective-permute-start(bf16[512,128]{1,0:T(8,128)(2,1)S(1)} %add_convert_fusion.1.refs_0_), channel_id=1, source_target_pairs={{0,12},{1,13},{2,14},{3,15},{4,0},{5,1},{6,2},{7,3},{8,4},{9,5},{1... | collective-permute-start | bytes 393224 | tf_op jit(solution)/shard_map/ppermute | solution.py:203
  121.3 9.2 %collective-permute-start.27 = (bf16[256,1024]{1,0:T(8,128)(2,1)S(1)}, bf16[256,1024]{1,0:T(8,128)(2,1)S(1)}, u32[]{:S(2)}, u32[]{:S(2)}) collective-permute-start(bf16[256,1024]{1,0:T(8,128)(2,1)S(1)} %all_gather.3), channel_id=1, source_target_pairs={{0,2},{1,3},{2,0},{3,1},{4,6},{5,7},{6,4},{7,5},{8,10},{9,11},{10,... | collective-permute-start | bytes 1572872 | tf_op jit(solution)/shard_map/ppermute | solution.py:203
  123.0 13.8 %copy-start.7 = (bf16[128,1024]{1,0:T(8,128)(2,1)S(1)}, bf16[128,1024]{1,0:T(8,128)(2,1)}, u32[]{:S(2)}) copy-start(bf16[128,1024]{1,0:T(8,128)(2,1)} %param.14) | copy-start | bytes 786436
  135.2 1.6 %collective-permute-start.28 = (bf16[128,1024]{1,0:T(8,128)(2,1)S(1)}, bf16[128,1024]{1,0:T(8,128)(2,1)S(1)}, u32[]{:S(2)}, u32[]{:S(2)}) collective-permute-start(bf16[128,1024]{1,0:T(8,128)(2,1)S(1)} %dynamic-slice_convert_fusion), channel_id=1, source_target_pairs={{0,1},{1,0},{2,3},{3,2},{4,5},{5,4},{6,7},{7,6},{8,9},{9,8},{10,11... | collective-permute-start | bytes 786440 | tf_op jit(solution)/shard_map/ppermute | solution.py:203

commit v4 on v3

--- a/solution.py
+++ b/solution.py
@@ -51,8 +51,8 @@
 
 def project_kernel(groups, pairs, shifts, scalars, *refs):
     count = groups * 2
-    near, far, slabs = refs[:count], refs[count : 2 * count], refs[2 * count : -count - 1]
-    outs, placed = refs[-count - 1 : -1], refs[-1]
+    near, far, slabs = refs[:count], refs[count : 2 * count], refs[2 * count : -2 * count - 1]
+    outs, placed = refs[-2 * count - 1 : -1], refs[-1]
     half = near[0].shape[0]
     side, place = scalars[0], scalars[1]
     for shift, slab in zip(shifts, slabs):
@@ -67,35 +67,38 @@
                 placed[lax.rem(place + pairs - shift[0], pairs)] = slab[...]
 
     w = jnp.concatenate([placed[z] for z in range(pairs)], axis=0)
-    swapped = jnp.concatenate([w[:, HEAD_SIZE:], w[:, :HEAD_SIZE]], axis=1)
-    w = jnp.where(side == 0, w, swapped)
     for part, pieces in enumerate((near, far)):
         lhs = jnp.concatenate([ref[...] for ref in pieces], axis=0)
         result = jnp.dot(lhs, w, preferred_element_type=f32)
-        for source in range(count):
-            by_group, by_side = source // 2, source % 2
-            for to in range(2):
-                out = outs[(-by_group) % groups * 2 + to]
-                start = (0 if by_side == to else 2 * half) + part * half
-                out[start : start + half, :] = result[
-                    source * half : (source + 1) * half, to * HEAD_SIZE : (to + 1) * HEAD_SIZE
-                ].astype(out.dtype)
-
-
-def project(near, far, shifts, slabs, side, place, pairs, dtype, name):
+        columns = [result[:, n * HEAD_SIZE : (n + 1) * HEAD_SIZE] for n in range(4)]
+        for matrix in range(2):
+            first, second = columns[2 * matrix : 2 * matrix + 2]
+            heads = jnp.where(side == 0, first, second), jnp.where(side == 0, second, first)
+            for source in range(count):
+                by_group, by_side = source // 2, source % 2
+                for to in range(2):
+                    out = outs[matrix * count + (-by_group) % groups * 2 + to]
+                    start = (0 if by_side == to else 2 * half) + part * half
+                    out[start : start + half, :] = heads[to][
+                        source * half : (source + 1) * half, :
+                    ].astype(out.dtype)
+
+
+def project(near, far, shifts, slabs, side, place, pairs):
     count = len(near)
     half = near[0].shape[0]
     vmem = pl.BlockSpec(memory_space=pltpu.VMEM)
     return pl.pallas_call(
         functools.partial(project_kernel, count // 2, pairs, shifts),
         in_specs=[pl.BlockSpec(memory_space=pltpu.SMEM)] + [vmem] * (2 * count + len(slabs)),
-        out_specs=[vmem] * count,
+        out_specs=[vmem] * (2 * count),
         out_shape=[
-            jax.ShapeDtypeStruct((4 * half, HEAD_SIZE), dtype if k else f32) for k in range(count)
+            jax.ShapeDtypeStruct((4 * half, HEAD_SIZE), bf16 if k > count else f32)
+            for k in range(2 * count)
         ],
         scratch_shapes=[pltpu.VMEM((pairs,) + slabs[0].shape, bf16)],
         compiler_params=pltpu.CompilerParams(vmem_limit_bytes=VMEM_BYTES),
-        name=name,
+        name="project",
     )(jnp.stack([side, place]).astype(jnp.int32), *near, *far, *slabs)
 
 
@@ -156,6 +159,54 @@
     )(weights, denominator, *values)
 
 
+def output_kernel(pairs, last, scalars, *refs):
+    pieces, weight, placed = refs[:pairs], refs[pairs], refs[-1]
+    place, core = scalars[1], scalars[2]
+    for k, piece in enumerate(pieces):
+        placed[lax.rem(place + pairs - k, pairs)] = piece[...]
+    lhs = jnp.concatenate([placed[z] for z in range(pairs)], axis=0)
+    product = jnp.dot(lhs, weight[...], preferred_element_type=f32)
+    if not last:
+        refs[pairs + 1][...] = product
+        return
+    total, mine, send = refs[pairs + 1 : pairs + 4]
+    product = product + total[...]
+    half = mine.shape[0]
+    upper, lower = product[:half], product[half:]
+    mine[...] = jnp.where(core == 0, upper, lower)
+    send[...] = jnp.where(core == 0, lower, upper).astype(bf16)
+
+
+def output(pieces, out_weight, side, place, core, total, name):
+    pairs = len(pieces)
+    text, depth = pieces[0].shape
+    width = out_weight.shape[1]
+    rows = pairs * text
+    whole = lambda *shape: pl.BlockSpec(shape, lambda i, s: (0, 0))
+    last = total is not None
+    shapes = [(rows // 2, width, f32), (rows // 2, width, bf16)] if last else [(rows, width, f32)]
+    return pl.pallas_call(
+        functools.partial(output_kernel, pairs, last),
+        grid_spec=pltpu.PrefetchScalarGridSpec(
+            num_scalar_prefetch=1,
+            grid=(1,),
+            in_specs=[whole(text, depth)] * pairs
+            + [pl.BlockSpec((depth, width), lambda i, s: (s[0], 0))]
+            + ([whole(rows, width)] if last else []),
+            out_specs=[whole(*shape[:2]) for shape in shapes],
+            scratch_shapes=[pltpu.VMEM((pairs, text, depth), bf16)],
+        ),
+        out_shape=[jax.ShapeDtypeStruct(shape[:2], shape[2]) for shape in shapes],
+        compiler_params=pltpu.CompilerParams(vmem_limit_bytes=VMEM_BYTES),
+        name=name,
+    )(
+        jnp.stack([side, place, core]).astype(jnp.int32),
+        *pieces,
+        out_weight,
+        *([total] if last else []),
+    )
+
+
 def after(array, *others):
     return lax.optimization_barrier((array, others))[0]
 
@@ -235,11 +286,6 @@
     def line_slabs(own, pieces, far):
         return [own] + [pieces[k] for k in near_shifts] + far[::-1]
 
-    lines = [[2 * z + y for z in range(pairs)] for y in range(2)]
-
-    def gather_pairs(array):
-        return lax.all_gather(array, "seq", axis=0, tiled=True, axis_index_groups=lines)
-
     def all_pairs(array):
         return [array] + [line_shift(array, k) for k in range(1, pairs)]
 
@@ -250,16 +296,15 @@
     def own_part(matrix):
         return lax.dynamic_slice_in_dim(matrix, group * part, part, axis=0)
 
-    key_own = own_part(key_matrix)
-    key_near = line_near(key_own)
+    slab = jnp.concatenate([own_part(key_matrix), own_part(value_matrix)], axis=1)
+    slab_near = line_near(slab)
 
     index = [(group + g) % groups * 2 + (side + y) % 2 for g, y in offsets]
-    vision = after(vision, key_own)
+    vision = after(vision, slab)
     sends = pack(vision, index[1:], core, groups, pairs, part, "pack_sends")
     received = [plane_shift(send, g, y) for send, (g, y) in zip(sends, offsets[1:])]
     vision = after(vision, *sends)
     near = pack(vision, index[:1], core, groups, pairs, part, "pack_near")
-    near = [*near, *received]
     far = pack(vision, index[:1], 1 - core, groups, pairs, part, "pack_far")
 
     rows_q = queries.shape[0]
@@ -269,11 +314,10 @@
     q_own = lax.dynamic_slice_in_dim(queries, side * half_q, half_q, axis=1)
     q_send = lax.dynamic_slice_in_dim(queries, (1 - side) * half_q, half_q, axis=1)
 
-    key_far = line_far(key_near)
-    received = [after(piece, *key_near.values()) for piece in received]
+    received = [after(piece, near[0], far[0]) for piece in received]
+    near = [*near, *received]
+    slab_far = line_far({k: after(s, near[0], far[0]) for k, s in slab_near.items()})
     far = [*far] + [core_swap(piece) for piece in received]
-    value_own = after(own_part(value_matrix), *key_far)
-    value_near = line_near(value_own)
 
     def scatter(pieces):
         return [plane_shift(piece, g, y) for piece, (g, y) in zip(pieces[1:], offsets[1:])]
@@ -281,21 +325,16 @@
     def sum_up(own, pieces):
         return functools.reduce(lambda a, b: a + b.astype(f32), pieces, own)
 
-    key_slabs = line_slabs(key_own, key_near, key_far)
-    key_pieces = project(near, far, shifts, key_slabs, side, place, pairs, f32, "project_keys")
+    q_recv = plane_shift(after(q_send, *received), 0, 1)
+    far[-1] = after(far[-1], q_recv)
+    slabs = line_slabs(slab, slab_near, slab_far)
+    pieces = project(near, far, shifts, slabs, side, place, pairs)
+    key_pieces, value_pieces = pieces[: len(offsets)], pieces[len(offsets) :]
     key_parts = scatter(key_pieces)
-    value_near = {k: after(v, *key_pieces) for k, v in value_near.items()}
-    value_far = line_far(value_near)
-    q_recv = plane_shift(after(q_send, *key_parts), 0, 1)
+    value_parts = scatter(value_pieces)
     keys = norm(sum_up(key_pieces[0], key_parts), key_norm_gain)
     all_keys = all_pairs(keys)
-    value_far = [after(v, keys) for v in value_far]
-    value_slabs = line_slabs(value_own, value_near, value_far)
-    value_pieces = project(
-        near, far, shifts, value_slabs, side, place, pairs, bf16, "project_values"
-    )
-    value_parts = scatter(value_pieces)
-    q_recv = after(q_recv, *value_pieces)
+    q_recv = after(q_recv, *pieces)
     q_pair = jnp.where(
         side == 0,
         jnp.concatenate([q_own, q_recv], axis=0),
@@ -309,18 +348,19 @@
     all_values = all_pairs(values)
     all_keys = [after(k, values) for k in all_keys]
     weights, denominator = score(normed, all_keys, heads)
-    attended = gather_pairs(mix(weights, denominator, all_values, heads))
-    other = plane_shift(attended, 0, 1)
-    depth = heads * HEAD_SIZE
-    weight_own = lax.dynamic_slice_in_dim(out_weight, side * depth, depth, axis=0)
-    weight_other = lax.dynamic_slice_in_dim(out_weight, (1 - side) * depth, depth, axis=0)
-    projected = jnp.dot(attended, weight_own, preferred_element_type=f32) + jnp.dot(
-        other, weight_other, preferred_element_type=f32
-    )
-    out_rows = residual.shape[0]
-    send = lax.dynamic_slice_in_dim(projected, (1 - core) * out_rows, out_rows, axis=0)
-    mine = lax.dynamic_slice_in_dim(projected, core * out_rows, out_rows, axis=0)
-    mine = mine + core_swap(send.astype(bf16)).astype(f32)
+    attended = mix(weights, denominator, all_values, heads)
+    others = [plane_shift(attended, 0, 1)]
+    own_pieces = [attended]
+    order = sorted(range(1, pairs), key=lambda k: min(k, pairs - k))
+    arrived = {k: line_shift(attended, k) for k in order}
+    for last, k in zip(order, order[1:]):
+        arrived[k] = after(arrived[k], arrived[last])
+    passed = {k: plane_shift(arrived[k], 0, 1) for k in order}
+    own_pieces += [arrived[k] for k in range(1, pairs)]
+    others += [passed[k] for k in range(1, pairs)]
+    (total,) = output(own_pieces, out_weight, side, place, core, None, "output_own")
+    mine, send = output(others, out_weight, 1 - side, place, core, total, "output_other")
+    mine = mine + core_swap(send).astype(f32)
     return (residual.astype(f32) + jnp.tanh(attn_gate[0]) * mine).astype(bf16)
 
 

time: 138 us -> 132 us (0.957)
  blocking collectives: 15.7 us -> 0 us
  waiting for transfers between devices: 47.8 us -> 62.3 us
  matrix products: 4.62 us -> 0 us
  Pallas kernels: 13.4 us -> 16.4 us
  local copies, waits for them, and re-layouts: 9.71 us -> 7.37 us
    all_gather x1 -> x0, blocking collectives: 15.7 us -> none  [gather_pairs(): lax.all_gather(array, 'seq', axis=0, tiled=True, axis_index_groups=lines)]
    ppermute x29 -> x31, waiting for transfers between devices: 47.8 us -> 62.3 us  [permute(): return lax.ppermute(array, AXES, perm)]
    dot_general x2 -> x0, matrix products: 4.62 us -> none  [the longest x1 2.32 us: body(): jnp.dot(attended, weight_own, preferred_element_type=f32)]
    pallas_call x0 -> x2, Pallas kernels: none -> 4.17 us  [output(): pl.pallas_call(functools.partial(output_kernel, pairs, last), grid_spec=p...]
    unnamed x29 -> x21, local copies, waits for them, and re-layouts: 8.05 us -> 5.37 us
    pallas_call x2 -> x1, Pallas kernels: 6.45 us -> 4.25 us  [project(): pl.pallas_call(functools.partial(project_kernel, count // 2, pairs, shift...]
    ppermute x29 -> x31, starting transfers between devices: 42.4 us -> 41.6 us  [permute(): return lax.ppermute(array, AXES, perm)]
  transfers between devices with their start and end apart: 29 -> 31, of which waited for: 15 -> 13; matrix products, arithmetic and copies ran while one was open for 3% -> 2% of each run, Pallas kernels for 5% -> 4%
where the time goes in v4:
time: 132 us
  waiting for transfers between devices  62.3 us (47%)
  starting transfers between devices  41.6 us (32%)
  Pallas kernels  16.4 us (12%)
  local copies, waits for them, and re-layouts  7.37 us (6%)
  other arithmetic  2.81 us (2%)
    ppermute x31, waiting for transfers between devices, permute(): return lax.ppermute(array, AXES, perm)  62.3 us
    ppermute x31, starting transfers between devices, permute(): return lax.ppermute(array, AXES, perm)  41.6 us
    unnamed x21, local copies, waits for them, and re-layouts  5.37 us
    pallas_call x3, Pallas kernels, pack(): pl.pallas_call(functools.partial(pack_kernel, groups, pairs, part, count)...  5.25 us
    pallas_call x1, Pallas kernels, project(): pl.pallas_call(functools.partial(project_kernel, count // 2, pairs, shift...  4.25 us
    pallas_call x2, Pallas kernels, output(): pl.pallas_call(functools.partial(output_kernel, pairs, last), grid_spec=p...  4.17 us
  transfers between devices with their start and end apart: 31, of which 13 were waited for; matrix products, arithmetic and copies ran while one was open for 2% of the time, Pallas kernels for 4%

profile of v4, /device:TPU:0, one launch (start us, length us, event | category | flops | bytes accessed | tf_op | source)
XLA Modules:
  0.0 131.5 jit_solution(1692780968760868771)
XLA Ops:
  0.0 1.1 constant_dynamic-slice_fusion.2
  1.1 0.1 pad_add_fusion.1.index_ref
  1.2 2.1 %copy-done = bf16[256,7680]{1,0:T(8,128)(2,1)S(1)} copy-done((bf16[256,7680]{1,0:T(8,128)(2,1)S(1)}, bf16[256,7680]{1,0:T(8,128)(2,1)}, u32[]{:S(2)}) %copy-start) | copy-done | bytes 3932184
  3.3 3.1 %pack_sends.1 = (bf16[128,1920]{1,0:T(8,128)(2,1)}, bf16[128,1920]{1,0:T(8,128)(2,1)}, bf16[128,1920]{1,0:T(8,128)(2,1)S(1)}) custom-call(s32[4]{0:T(128)S(1)} %pad_add_fusion.1.index_ref, bf16[256,7680]{1,0:T(8,128)(2,1)S(1)} %copy-done), custom_call_target="tpu_custom_call" | custom-call | tf_op jit(solution)/shard_map/pack_sends/pallas_call | solution.py:38
  6.4 3.0 %collective-permute-start = (bf16[128,1920]{1,0:T(8,128)(2,1)}, bf16[128,1920]{1,0:T(8,128)(2,1)S(1)}, u32[]{:S(2)}, u32[]{:S(2)}) collective-permute-start(bf16[128,1920]{1,0:T(8,128)(2,1)} %get-tuple-element.38), channel_id=1, source_target_pairs={{0,2},{1,3},{2,0},{3,1},{4,6},{5,7},{6,4},{7,5},{8,10},{9,11},{10,... | collective-permute-start | bytes 1474568 | tf_op jit(solution)/shard_map/ppermute | solution.py:254
  9.4 1.5 %collective-permute-start.1 = (bf16[128,1920]{1,0:T(8,128)(2,1)}, bf16[128,1920]{1,0:T(8,128)(2,1)S(1)}, u32[]{:S(2)}, u32[]{:S(2)}) collective-permute-start(bf16[128,1920]{1,0:T(8,128)(2,1)} %get-tuple-element.39), channel_id=1, source_target_pairs={{0,16},{1,17},{2,18},{3,19},{4,20},{5,21},{6,22},{7,23},{8,24},{9,... | collective-permute-start | bytes 1474568 | tf_op jit(solution)/shard_map/ppermute | solution.py:254
  10.9 2.0 %collective-permute-start.7 = (bf16[480,512]{1,0:T(8,128)(2,1)S(1)}, bf16[480,512]{1,0:T(8,128)(2,1)}, u32[]{:S(2)}, u32[]{:S(2)}) collective-permute-start(bf16[480,512]{1,0:T(8,128)(2,1)S(1)} %pad_maximum_fusion.refs_8_), channel_id=1, source_target_pairs={{0,4},{1,5},{2,6},{3,7},{4,8},{5,9},{6,10},{7,11},{8,12},{9,13},{1... | collective-permute-start | bytes 1474568 | tf_op jit(solution)/shard_map/ppermute | solution.py:254
  13.0 2.0 %collective-permute-start.8 = (bf16[480,512]{1,0:T(8,128)(2,1)S(1)}, bf16[480,512]{1,0:T(8,128)(2,1)}, u32[]{:S(2)}, u32[]{:S(2)}) collective-permute-start(bf16[480,512]{1,0:T(8,128)(2,1)S(1)} %pad_maximum_fusion.refs_8_), channel_id=1, source_target_pairs={{0,12},{1,13},{2,14},{3,15},{4,0},{5,1},{6,2},{7,3},{8,4},{9,5},{1... | collective-permute-start | bytes 1474568 | tf_op jit(solution)/shard_map/ppermute | solution.py:254
  15.0 0.1 pad_add_fusion
  15.1 2.1 %copy-done.1 = bf16[256,7680]{1,0:T(8,128)(2,1)S(1)} copy-done((bf16[256,7680]{1,0:T(8,128)(2,1)S(1)}, bf16[256,7680]{1,0:T(8,128)(2,1)}, u32[]{:S(2)}) %copy-start.1) | copy-done | bytes 3932184
  17.2 1.1 pack_far.1.refs_4_
  18.3 1.0 copy-done.2
  19.3 1.1 pack_near.1.refs_0_
  20.4 0.9 constant_dynamic-slice_fusion.1
  21.3 2.5 %collective-permute-done.1.refs_2_ = bf16[128,1920]{1,0:T(8,128)(2,1)S(1)} collective-permute-done((bf16[128,1920]{1,0:T(8,128)(2,1)}, bf16[128,1920]{1,0:T(8,128)(2,1)S(1)}, u32[]{:S(2)}, u32[]{:S(2)}) %collective-permute-start.1) | collective-permute-done | bytes 491552 | tf_op jit(solution)/shard_map/ppermute | solution.py:254
  23.8 8.8 %collective-permute-done.2.refs_3_ = bf16[128,1920]{1,0:T(8,128)(2,1)S(1)} collective-permute-done((bf16[128,1920]{1,0:T(8,128)(2,1)S(1)}, bf16[128,1920]{1,0:T(8,128)(2,1)S(1)}, u32[]{:S(2)}, u32[]{:S(2)}) %collective-permute-start.2) | collective-permute-done | bytes 491552 | tf_op jit(solution)/shard_map/ppermute | solution.py:254
  32.5 1.7 %collective-permute-start.3 = (bf16[32,1024]{1,0:T(8,128)(2,1)S(1)}, bf16[32,1024]{1,0:T(8,128)(2,1)}, u32[]{:S(2)}, u32[]{:S(2)}) collective-permute-start(bf16[32,1024]{1,0:T(8,128)(2,1)S(1)} %get-tuple-element.46), channel_id=1, source_target_pairs={{0,2},{1,3},{2,0},{3,1},{4,6},{5,7},{6,4},{7,5},{8,10},{9,11},{10,... | collective-permute-start | bytes 196616 | tf_op jit(solution)/shard_map/ppermute | solution.py:254
  34.3 0.5 collective-permute-start.6
  34.8 0.6 collective-permute-done.8.refs_10_
  35.4 1.3 collective-permute-start.9
  36.7 1.5 %collective-permute-start.10 = (bf16[480,512]{1,0:T(8,128)(2,1)}, bf16[480,512]{1,0:T(8,128)(2,1)}, u32[]{:S(2)}, u32[]{:S(2)}) collective-permute-start(bf16[480,512]{1,0:T(8,128)(2,1)} %collective-permute-done.7.refs_9_), channel_id=1, source_target_pairs={{4,8},{5,9},{6,10},{7,11},{8,12},{9,13},{10,14},{11,15},{20,24},{2... | collective-permute-start | bytes 1474568 | tf_op jit(solution)/shard_map/ppermute | solution.py:254
  38.2 0.1 pad_add_fusion.3.scalars
  38.3 11.9 %collective-permute-done.9.refs_11_ = bf16[480,512]{1,0:T(8,128)(2,1)} collective-permute-done((bf16[480,512]{1,0:T(8,128)(2,1)}, bf16[480,512]{1,0:T(8,128)(2,1)}, u32[]{:S(2)}, u32[]{:S(2)}) %collective-permute-start.9) | collective-permute-done | bytes 491552 | tf_op jit(solution)/shard_map/ppermute | solution.py:254
  50.2 4.3 %project.1 = (f32[512,128]{1,0:T(8,128)S(1)}, f32[512,128]{1,0:T(8,128)S(1)}, f32[512,128]{1,0:T(8,128)S(1)}, f32[512,128]{1,0:T(8,128)S(1)}, f32[512,128]{1,0:T...) custom-call(s32[2]{0:T(128)S(1)} %pad_add_fusion.3.scalars, ...), custom_call_target="tpu_custom_call" | custom-call | tf_op jit(solution)/shard_map/project/pallas_call | solution.py:91
  54.5 1.6 %collective-permute-start.14 = (bf16[512,128]{1,0:T(8,128)(2,1)S(1)}, bf16[512,128]{1,0:T(8,128)(2,1)S(1)}, u32[]{:S(2)}, u32[]{:S(2)}) collective-permute-start(bf16[512,128]{1,0:T(8,128)(2,1)S(1)} %get-tuple-element.55), channel_id=1, source_target_pairs={{0,2},{1,3},{2,0},{3,1},{4,6},{5,7},{6,4},{7,5},{8,10},{9,11},{10,... | collective-permute-start | bytes 393224 | tf_op jit(solution)/shard_map/ppermute | solution.py:254
  56.0 1.5 %collective-permute-start.15 = (bf16[512,128]{1,0:T(8,128)(2,1)S(1)}, bf16[512,128]{1,0:T(8,128)(2,1)S(1)}, u32[]{:S(2)}, u32[]{:S(2)}) collective-permute-start(bf16[512,128]{1,0:T(8,128)(2,1)S(1)} %get-tuple-element.56), channel_id=1, source_target_pairs={{0,16},{1,17},{2,18},{3,19},{4,20},{5,21},{6,22},{7,23},{8,24},{9,... | collective-permute-start | bytes 393224 | tf_op jit(solution)/shard_map/ppermute | solution.py:254
  57.5 0.5 collective-permute-start.11
  58.0 0.5 collective-permute-start.12
  58.6 2.4 %collective-permute-start.13 = (f32[512,128]{1,0:T(8,128)S(1)}, f32[512,128]{1,0:T(8,128)S(1)}, u32[]{:S(2)}, u32[]{:S(2)}) collective-permute-start(f32[512,128]{1,0:T(8,128)S(1)} %get-tuple-element.53), channel_id=1, source_target_pairs={{0,18},{1,19},{2,16},{3,17},{4,22},{5,23},{6,20},{7,21},{8,26},{9,... | collective-permute-start | bytes 786440 | tf_op jit(solution)/shard_map/ppermute | solution.py:254
  61.0 0.9 maximum_select_fusion
  62.1 0.1 fusion
  62.3 3.6 %collective-permute-done.11 = f32[512,128]{1,0:T(8,128)S(1)} collective-permute-done((f32[512,128]{1,0:T(8,128)S(1)}, f32[512,128]{1,0:T(8,128)S(1)}, u32[]{:S(2)}, u32[]{:S(2)}) %collective-permute-start.11) | collective-permute-done | bytes 262176 | tf_op jit(solution)/shard_map/ppermute | solution.py:254
  65.9 2.2 %collective-permute-start.16 = (bf16[512,128]{1,0:T(8,128)(2,1)S(1)}, bf16[512,128]{1,0:T(8,128)(2,1)S(1)}, u32[]{:S(2)}, u32[]{:S(2)}) collective-permute-start(bf16[512,128]{1,0:T(8,128)(2,1)S(1)} %get-tuple-element.57), channel_id=1, source_target_pairs={{0,18},{1,19},{2,16},{3,17},{4,22},{5,23},{6,20},{7,21},{8,26},{9,... | collective-permute-start | bytes 393224 | tf_op jit(solution)/shard_map/ppermute | solution.py:254
  68.1 5.2 %collective-permute-done.13 = f32[512,128]{1,0:T(8,128)S(1)} collective-permute-done((f32[512,128]{1,0:T(8,128)S(1)}, f32[512,128]{1,0:T(8,128)S(1)}, u32[]{:S(2)}, u32[]{:S(2)}) %collective-permute-start.13) | collective-permute-done | bytes 262176 | tf_op jit(solution)/shard_map/ppermute | solution.py:254
  73.3 0.1 multiply_reduce_fusion
  73.5 0.1 multiply_convert_fusion.refs_0_
  73.6 5.7 %collective-permute-start.19 = (bf16[512,128]{1,0:T(8,128)(2,1)S(1)}, bf16[512,128]{1,0:T(8,128)(2,1)S(1)}, u32[]{:S(2)}, u32[]{:S(2)}) collective-permute-start(bf16[512,128]{1,0:T(8,128)(2,1)S(1)} %multiply_convert_fusion.refs_0_), channel_id=1, source_target_pairs={{0,12},{1,13},{2,14},{3,15},{4,0},{5,1},{6,2},{7,3},{8,4},{9,5},{1... | collective-permute-start | bytes 393224 | tf_op jit(solution)/shard_map/ppermute | solution.py:254
  79.4 1.8 %collective-permute-start.22 = (bf16[512,128]{1,0:T(8,128)(2,1)S(1)}, bf16[512,128]{1,0:T(8,128)(2,1)S(1)}, u32[]{:S(2)}, u32[]{:S(2)}) collective-permute-start(bf16[512,128]{1,0:T(8,128)(2,1)S(1)} %add_convert_fusion.1.refs_0_), channel_id=1, source_target_pairs={{0,12},{1,13},{2,14},{3,15},{4,0},{5,1},{6,2},{7,3},{8,4},{9,5},{1... | collective-permute-start | bytes 393224 | tf_op jit(solution)/shard_map/ppermute | solution.py:254
  81.2 1.6 %collective-permute-start.20 = (bf16[512,128]{1,0:T(8,128)(2,1)S(1)}, bf16[512,128]{1,0:T(8,128)(2,1)S(1)}, u32[]{:S(2)}, u32[]{:S(2)}) collective-permute-start(bf16[512,128]{1,0:T(8,128)(2,1)S(1)} %add_convert_fusion.1.refs_0_), channel_id=1, source_target_pairs={{0,4},{1,5},{2,6},{3,7},{4,8},{5,9},{6,10},{7,11},{8,12},{9,13},{1... | collective-permute-start | bytes 393224 | tf_op jit(solution)/shard_map/ppermute | solution.py:254
  82.8 1.6 %collective-permute-start.18 = (bf16[512,128]{1,0:T(8,128)(2,1)S(1)}, bf16[512,128]{1,0:T(8,128)(2,1)S(1)}, u32[]{:S(2)}, u32[]{:S(2)}) collective-permute-start(bf16[512,128]{1,0:T(8,128)(2,1)S(1)} %multiply_convert_fusion.refs_0_), channel_id=1, source_target_pairs={{0,8},{1,9},{2,10},{3,11},{4,12},{5,13},{6,14},{7,15},{8,0},{9,1},... | collective-permute-start | bytes 393224 | tf_op jit(solution)/shard_map/ppermute | solution.py:254
  84.4 1.2 collective-permute-start.17
  85.6 0.1 fusion.2.q_ref
  85.7 15.4 %collective-permute-done.18.refs_2_ = bf16[512,128]{1,0:T(8,128)(2,1)S(1)} collective-permute-done((bf16[512,128]{1,0:T(8,128)(2,1)S(1)}, bf16[512,128]{1,0:T(8,128)(2,1)S(1)}, u32[]{:S(2)}, u32[]{:S(2)}) %collective-permute-start.18) | collective-permute-done | bytes 131104 | tf_op jit(solution)/shard_map/ppermute | solution.py:254
  101.1 2.0 %score.1 = (bf16[512,2048]{1,0:T(8,128)(2,1)S(1)}, f32[512,128]{1,0:T(8,128)S(1)}) custom-call(bf16[512,128]{1,0:T(8,128)(2,1)S(1)} %fusion.2.q_ref, bf16[512,128]{1,0:T(8,128)(2,1)S(1)} %multiply_convert_fusion.refs_0_, bf16[512,128]{1,0:T(8,128)(2,1)S(1)} %collective-permute-done.17.refs_1_, bf16[512,128]{1,0:T(8,128)(2,1)S(1)} %collective-permute-done.18.refs_2_, ...), custom_call_target="tpu_custom_call" | custom-call | tf_op jit(solution)/shard_map/score/pallas_call | solution.py:131
  103.2 0.7 mix.1.refs_0_
  103.9 0.7 collective-permute-start.27
  104.6 1.4 %collective-permute-start.24 = (bf16[64,1024]{1,0:T(8,128)(2,1)S(1)}, bf16[64,1024]{1,0:T(8,128)(2,1)S(1)}, u32[]{:S(2)}, u32[]{:S(2)}) collective-permute-start(bf16[64,1024]{1,0:T(8,128)(2,1)S(1)} %mix.1.refs_0_), channel_id=1, source_target_pairs={{0,4},{1,5},{2,6},{3,7},{4,8},{5,9},{6,10},{7,11},{8,12},{9,13},{1... | collective-permute-start | bytes 393224 | tf_op jit(solution)/shard_map/ppermute | solution.py:254
  106.0 2.4 %collective-permute-start.26 = (bf16[64,1024]{1,0:T(8,128)(2,1)S(1)}, bf16[64,1024]{1,0:T(8,128)(2,1)S(1)}, u32[]{:S(2)}, u32[]{:S(2)}) collective-permute-start(bf16[64,1024]{1,0:T(8,128)(2,1)S(1)} %mix.1.refs_0_), channel_id=1, source_target_pairs={{0,8},{1,9},{2,10},{3,11},{4,12},{5,13},{6,14},{7,15},{8,0},{9,1},... | collective-permute-start | bytes 393224 | tf_op jit(solution)/shard_map/ppermute | solution.py:254
  108.4 0.4 collective-permute-start.23
  108.8 0.2 collective-permute-done.27.refs_3_
  108.9 6.1 %collective-permute-done.24.refs_1_ = bf16[64,1024]{1,0:T(8,128)(2,1)S(1)} collective-permute-done((bf16[64,1024]{1,0:T(8,128)(2,1)S(1)}, bf16[64,1024]{1,0:T(8,128)(2,1)S(1)}, u32[]{:S(2)}, u32[]{:S(2)}) %collective-permute-start.24) | collective-permute-done | bytes 131104 | tf_op jit(solution)/shard_map/ppermute | solution.py:254
  115.1 0.4 collective-permute-start.29
  115.5 3.0 %collective-permute-done.26.refs_2_ = bf16[64,1024]{1,0:T(8,128)(2,1)S(1)} collective-permute-done((bf16[64,1024]{1,0:T(8,128)(2,1)S(1)}, bf16[64,1024]{1,0:T(8,128)(2,1)S(1)}, u32[]{:S(2)}, u32[]{:S(2)}) %collective-permute-start.26) | collective-permute-done | bytes 131104 | tf_op jit(solution)/shard_map/ppermute | solution.py:254
  118.5 0.2 collective-permute-start.28
  118.7 1.8 %collective-permute-start.25 = (bf16[64,1024]{1,0:T(8,128)(2,1)S(1)}, bf16[64,1024]{1,0:T(8,128)(2,1)S(1)}, u32[]{:S(2)}, u32[]{:S(2)}) collective-permute-start(bf16[64,1024]{1,0:T(8,128)(2,1)S(1)} %collective-permute-done.24.refs_1_), channel_id=1, source_target_pairs={{0,2},{1,3},{2,0},{3,1},{4,6},{5,7},{6,4},{7,5},{8,10},{9,11},{10,... | collective-permute-start | bytes 393224 | tf_op jit(solution)/shard_map/ppermute | solution.py:254
  120.5 0.1 add_add_fusion.2.scalars
  120.6 0.1 add_add_fusion.1.scalars
  120.7 1.3 output_own.1.refs_5_
  122.0 2.8 %collective-permute-done.28.refs_2_ = bf16[64,1024]{1,0:T(8,128)(2,1)S(1)} collective-permute-done((bf16[64,1024]{1,0:T(8,128)(2,1)S(1)}, bf16[64,1024]{1,0:T(8,128)(2,1)S(1)}, u32[]{:S(2)}, u32[]{:S(2)}) %collective-permute-start.28) | collective-permute-done | bytes 131104 | tf_op jit(solution)/shard_map/ppermute | solution.py:254
  124.8 1.4 %collective-permute-done.25.refs_1_ = bf16[64,1024]{1,0:T(8,128)(2,1)S(1)} collective-permute-done((bf16[64,1024]{1,0:T(8,128)(2,1)S(1)}, bf16[64,1024]{1,0:T(8,128)(2,1)S(1)}, u32[]{:S(2)}, u32[]{:S(2)}) %collective-permute-start.25) | collective-permute-done | bytes 131104 | tf_op jit(solution)/shard_map/ppermute | solution.py:254
  126.2 2.9 %output_other.1 = (f32[128,1024]{1,0:T(8,128)S(1)}, bf16[128,1024]{1,0:T(8,128)(2,1)S(1)}) custom-call(s32[3]{0:T(128)S(1)} %add_add_fusion.1.scalars, bf16[64,1024]{1,0:T(8,128)(2,1)S(1)} %collective-permute-done.23.refs_0_, bf16[64,1024]{1,0:T(8,128)(2,1)S(1)} %collective-permute-done.25.refs_1_, bf16[64,1024]{1,0:T(8,128)(2,1)S(1)} %collective-permute-done.28.refs_2_, ...), custom_call_target="tpu_custom_call" | custom-call | tf_op jit(solution)/shard_map/output_other/pallas_call | solution.py:188
  129.1 0.1 collective-permute-start.30
  129.8 0.8 collective-permute-done.30
  130.7 0.8 add_convert_fusion
  (45 shorter events, 0.3 us)
Async XLA Ops:
  1.2 2.1 %copy-start = (bf16[256,7680]{1,0:T(8,128)(2,1)S(1)}, bf16[256,7680]{1,0:T(8,128)(2,1)}, u32[]{:S(2)}) copy-start(bf16[256,7680]{1,0:T(8,128)(2,1)} %rows_ref.2) | copy-start | bytes 11796484
  6.4 14.8 %collective-permute-start = (bf16[128,1920]{1,0:T(8,128)(2,1)}, bf16[128,1920]{1,0:T(8,128)(2,1)S(1)}, u32[]{:S(2)}, u32[]{:S(2)}) collective-permute-start(bf16[128,1920]{1,0:T(8,128)(2,1)} %get-tuple-element.38), channel_id=1, source_target_pairs={{0,2},{1,3},{2,0},{3,1},{4,6},{5,7},{6,4},{7,5},{8,10},{9,11},{10,... | collective-permute-start | bytes 1474568 | tf_op jit(solution)/shard_map/ppermute | solution.py:254
  9.4 14.4 %collective-permute-start.1 = (bf16[128,1920]{1,0:T(8,128)(2,1)}, bf16[128,1920]{1,0:T(8,128)(2,1)S(1)}, u32[]{:S(2)}, u32[]{:S(2)}) collective-permute-start(bf16[128,1920]{1,0:T(8,128)(2,1)} %get-tuple-element.39), channel_id=1, source_target_pairs={{0,16},{1,17},{2,18},{3,19},{4,20},{5,21},{6,22},{7,23},{8,24},{9,... | collective-permute-start | bytes 1474568 | tf_op jit(solution)/shard_map/ppermute | solution.py:254
  10.9 21.6 %collective-permute-start.2 = (bf16[128,1920]{1,0:T(8,128)(2,1)S(1)}, bf16[128,1920]{1,0:T(8,128)(2,1)S(1)}, u32[]{:S(2)}, u32[]{:S(2)}) collective-permute-start(bf16[128,1920]{1,0:T(8,128)(2,1)S(1)} %get-tuple-element.40), channel_id=1, source_target_pairs={{0,18},{1,19},{2,16},{3,17},{4,22},{5,23},{6,20},{7,21},{8,26},{9,... | collective-permute-start | bytes 1474568 | tf_op jit(solution)/shard_map/ppermute | solution.py:254
  10.9 23.9 %collective-permute-start.7 = (bf16[480,512]{1,0:T(8,128)(2,1)S(1)}, bf16[480,512]{1,0:T(8,128)(2,1)}, u32[]{:S(2)}, u32[]{:S(2)}) collective-permute-start(bf16[480,512]{1,0:T(8,128)(2,1)S(1)} %pad_maximum_fusion.refs_8_), channel_id=1, source_target_pairs={{0,4},{1,5},{2,6},{3,7},{4,8},{5,9},{6,10},{7,11},{8,12},{9,13},{1... | collective-permute-start | bytes 1474568 | tf_op jit(solution)/shard_map/ppermute | solution.py:254
  13.0 22.5 %collective-permute-start.8 = (bf16[480,512]{1,0:T(8,128)(2,1)S(1)}, bf16[480,512]{1,0:T(8,128)(2,1)}, u32[]{:S(2)}, u32[]{:S(2)}) collective-permute-start(bf16[480,512]{1,0:T(8,128)(2,1)S(1)} %pad_maximum_fusion.refs_8_), channel_id=1, source_target_pairs={{0,12},{1,13},{2,14},{3,15},{4,0},{5,1},{6,2},{7,3},{8,4},{9,5},{1... | collective-permute-start | bytes 1474568 | tf_op jit(solution)/shard_map/ppermute | solution.py:254
  15.1 2.1 %copy-start.1 = (bf16[256,7680]{1,0:T(8,128)(2,1)S(1)}, bf16[256,7680]{1,0:T(8,128)(2,1)}, u32[]{:S(2)}) copy-start(bf16[256,7680]{1,0:T(8,128)(2,1)} %rows_ref.2) | copy-start | bytes 11796484
  17.2 2.1 %copy-start.2 = (bf16[256,7680]{1,0:T(8,128)(2,1)S(1)}, bf16[256,7680]{1,0:T(8,128)(2,1)}, u32[]{:S(2)}) copy-start(bf16[256,7680]{1,0:T(8,128)(2,1)} %rows_ref.2) | copy-start | bytes 11796484
  32.5 5.6 %collective-permute-start.3 = (bf16[32,1024]{1,0:T(8,128)(2,1)S(1)}, bf16[32,1024]{1,0:T(8,128)(2,1)}, u32[]{:S(2)}, u32[]{:S(2)}) collective-permute-start(bf16[32,1024]{1,0:T(8,128)(2,1)S(1)} %get-tuple-element.46), channel_id=1, source_target_pairs={{0,2},{1,3},{2,0},{3,1},{4,6},{5,7},{6,4},{7,5},{8,10},{9,11},{10,... | collective-permute-start | bytes 196616 | tf_op jit(solution)/shard_map/ppermute | solution.py:254
  34.3 15.9 %collective-permute-start.4 = (bf16[128,1920]{1,0:T(8,128)(2,1)S(1)}, bf16[128,1920]{1,0:T(8,128)(2,1)S(1)}, u32[]{:S(2)}, u32[]{:S(2)}) collective-permute-start(bf16[128,1920]{1,0:T(8,128)(2,1)S(1)} %collective-permute-done.refs_1_), channel_id=1, source_target_pairs={{0,1},{1,0},{2,3},{3,2},{4,5},{5,4},{6,7},{7,6},{8,9},{9,8},{10,11... | collective-permute-start | bytes 1474568 | tf_op jit(solution)/shard_map/ppermute | solution.py:254
  34.3 4.0 %collective-permute-start.6 = (bf16[128,1920]{1,0:T(8,128)(2,1)S(1)}, bf16[128,1920]{1,0:T(8,128)(2,1)}, u32[]{:S(2)}, u32[]{:S(2)}) collective-permute-start(bf16[128,1920]{1,0:T(8,128)(2,1)S(1)} %collective-permute-done.2.refs_3_), channel_id=1, source_target_pairs={{0,1},{1,0},{2,3},{3,2},{4,5},{5,4},{6,7},{7,6},{8,9},{9,8},{10,11... | collective-permute-start | bytes 1474568 | tf_op jit(solution)/shard_map/ppermute | solution.py:254
  35.4 14.7 %collective-permute-start.9 = (bf16[480,512]{1,0:T(8,128)(2,1)}, bf16[480,512]{1,0:T(8,128)(2,1)}, u32[]{:S(2)}, u32[]{:S(2)}) collective-permute-start(bf16[480,512]{1,0:T(8,128)(2,1)} %collective-permute-done.8.refs_10_), channel_id=1, source_target_pairs={{4,0},{5,1},{6,2},{7,3},{8,4},{9,5},{10,6},{11,7},{20,16},{21,17},... | collective-permute-start | bytes 1474568 | tf_op jit(solution)/shard_map/ppermute | solution.py:254
  36.7 13.4 %collective-permute-start.10 = (bf16[480,512]{1,0:T(8,128)(2,1)}, bf16[480,512]{1,0:T(8,128)(2,1)}, u32[]{:S(2)}, u32[]{:S(2)}) collective-permute-start(bf16[480,512]{1,0:T(8,128)(2,1)} %collective-permute-done.7.refs_9_), channel_id=1, source_target_pairs={{4,8},{5,9},{6,10},{7,11},{8,12},{9,13},{10,14},{11,15},{20,24},{2... | collective-permute-start | bytes 1474568 | tf_op jit(solution)/shard_map/ppermute | solution.py:254
  38.2 12.0 %collective-permute-start.5 = (bf16[128,1920]{1,0:T(8,128)(2,1)S(1)}, bf16[128,1920]{1,0:T(8,128)(2,1)}, u32[]{:S(2)}, u32[]{:S(2)}) collective-permute-start(bf16[128,1920]{1,0:T(8,128)(2,1)S(1)} %collective-permute-done.1.refs_2_), channel_id=1, source_target_pairs={{0,1},{1,0},{2,3},{3,2},{4,5},{5,4},{6,7},{7,6},{8,9},{9,8},{10,11... | collective-permute-start | bytes 1474568 | tf_op jit(solution)/shard_map/ppermute | solution.py:254
  38.3 35.2 %copy-start.5 = (f32[128]{0:T(128)S(1)}, f32[128]{0:T(128)}, u32[]{:S(2)}) copy-start(f32[128]{0:T(128)} %param.16) | copy-start | bytes 1540
  38.3 47.3 %copy-start.6 = (f32[128]{0:T(128)S(1)}, f32[128]{0:T(128)}, u32[]{:S(2)}) copy-start(f32[128]{0:T(128)} %param.15) | copy-start | bytes 1540
  54.4 66.2 %copy-start.3 = (bf16[2048,1024]{1,0:T(8,128)(2,1)S(1)}, bf16[2048,1024]{1,0:T(8,128)(2,1)}, u32[]{:S(2)}) copy-start(bf16[2048,1024]{1,0:T(8,128)(2,1)} %refs_4_.3) | copy-start | bytes 12582916
  54.5 24.9 %collective-permute-start.14 = (bf16[512,128]{1,0:T(8,128)(2,1)S(1)}, bf16[512,128]{1,0:T(8,128)(2,1)S(1)}, u32[]{:S(2)}, u32[]{:S(2)}) collective-permute-start(bf16[512,128]{1,0:T(8,128)(2,1)S(1)} %get-tuple-element.55), channel_id=1, source_target_pairs={{0,2},{1,3},{2,0},{3,1},{4,6},{5,7},{6,4},{7,5},{8,10},{9,11},{10,... | collective-permute-start | bytes 393224 | tf_op jit(solution)/shard_map/ppermute | solution.py:254
  56.0 23.3 %collective-permute-start.15 = (bf16[512,128]{1,0:T(8,128)(2,1)S(1)}, bf16[512,128]{1,0:T(8,128)(2,1)S(1)}, u32[]{:S(2)}, u32[]{:S(2)}) collective-permute-start(bf16[512,128]{1,0:T(8,128)(2,1)S(1)} %get-tuple-element.56), channel_id=1, source_target_pairs={{0,16},{1,17},{2,18},{3,19},{4,20},{5,21},{6,22},{7,23},{8,24},{9,... | collective-permute-start | bytes 393224 | tf_op jit(solution)/shard_map/ppermute | solution.py:254
  57.5 8.3 %collective-permute-start.11 = (f32[512,128]{1,0:T(8,128)S(1)}, f32[512,128]{1,0:T(8,128)S(1)}, u32[]{:S(2)}, u32[]{:S(2)}) collective-permute-start(f32[512,128]{1,0:T(8,128)S(1)} %get-tuple-element.51), channel_id=1, source_target_pairs={{0,2},{1,3},{2,0},{3,1},{4,6},{5,7},{6,4},{7,5},{8,10},{9,11},{10,... | collective-permute-start | bytes 786440 | tf_op jit(solution)/shard_map/ppermute | solution.py:254
  58.0 10.1 %collective-permute-start.12 = (f32[512,128]{1,0:T(8,128)S(1)}, f32[512,128]{1,0:T(8,128)S(1)}, u32[]{:S(2)}, u32[]{:S(2)}) collective-permute-start(f32[512,128]{1,0:T(8,128)S(1)} %get-tuple-element.52), channel_id=1, source_target_pairs={{0,16},{1,17},{2,18},{3,19},{4,20},{5,21},{6,22},{7,23},{8,24},{9,... | collective-permute-start | bytes 786440 | tf_op jit(solution)/shard_map/ppermute | solution.py:254
  58.6 14.7 %collective-permute-start.13 = (f32[512,128]{1,0:T(8,128)S(1)}, f32[512,128]{1,0:T(8,128)S(1)}, u32[]{:S(2)}, u32[]{:S(2)}) collective-permute-start(f32[512,128]{1,0:T(8,128)S(1)} %get-tuple-element.53), channel_id=1, source_target_pairs={{0,18},{1,19},{2,16},{3,17},{4,22},{5,23},{6,20},{7,21},{8,26},{9,... | collective-permute-start | bytes 786440 | tf_op jit(solution)/shard_map/ppermute | solution.py:254
  65.9 13.5 %collective-permute-start.16 = (bf16[512,128]{1,0:T(8,128)(2,1)S(1)}, bf16[512,128]{1,0:T(8,128)(2,1)S(1)}, u32[]{:S(2)}, u32[]{:S(2)}) collective-permute-start(bf16[512,128]{1,0:T(8,128)(2,1)S(1)} %get-tuple-element.57), channel_id=1, source_target_pairs={{0,18},{1,19},{2,16},{3,17},{4,22},{5,23},{6,20},{7,21},{8,26},{9,... | collective-permute-start | bytes 393224 | tf_op jit(solution)/shard_map/ppermute | solution.py:254
  73.6 10.8 %collective-permute-start.19 = (bf16[512,128]{1,0:T(8,128)(2,1)S(1)}, bf16[512,128]{1,0:T(8,128)(2,1)S(1)}, u32[]{:S(2)}, u32[]{:S(2)}) collective-permute-start(bf16[512,128]{1,0:T(8,128)(2,1)S(1)} %multiply_convert_fusion.refs_0_), channel_id=1, source_target_pairs={{0,12},{1,13},{2,14},{3,15},{4,0},{5,1},{6,2},{7,3},{8,4},{9,5},{1... | collective-permute-start | bytes 393224 | tf_op jit(solution)/shard_map/ppermute | solution.py:254
  79.4 23.8 %collective-permute-start.22 = (bf16[512,128]{1,0:T(8,128)(2,1)S(1)}, bf16[512,128]{1,0:T(8,128)(2,1)S(1)}, u32[]{:S(2)}, u32[]{:S(2)}) collective-permute-start(bf16[512,128]{1,0:T(8,128)(2,1)S(1)} %add_convert_fusion.1.refs_0_), channel_id=1, source_target_pairs={{0,12},{1,13},{2,14},{3,15},{4,0},{5,1},{6,2},{7,3},{8,4},{9,5},{1... | collective-permute-start | bytes 393224 | tf_op jit(solution)/shard_map/ppermute | solution.py:254
  81.2 22.0 %collective-permute-start.21 = (bf16[512,128]{1,0:T(8,128)(2,1)S(1)}, bf16[512,128]{1,0:T(8,128)(2,1)S(1)}, u32[]{:S(2)}, u32[]{:S(2)}) collective-permute-start(bf16[512,128]{1,0:T(8,128)(2,1)S(1)} %add_convert_fusion.1.refs_0_), channel_id=1, source_target_pairs={{0,8},{1,9},{2,10},{3,11},{4,12},{5,13},{6,14},{7,15},{8,0},{9,1},... | collective-permute-start | bytes 393224 | tf_op jit(solution)/shard_map/ppermute | solution.py:254
  81.2 22.0 %collective-permute-start.20 = (bf16[512,128]{1,0:T(8,128)(2,1)S(1)}, bf16[512,128]{1,0:T(8,128)(2,1)S(1)}, u32[]{:S(2)}, u32[]{:S(2)}) collective-permute-start(bf16[512,128]{1,0:T(8,128)(2,1)S(1)} %add_convert_fusion.1.refs_0_), channel_id=1, source_target_pairs={{0,4},{1,5},{2,6},{3,7},{4,8},{5,9},{6,10},{7,11},{8,12},{9,13},{1... | collective-permute-start | bytes 393224 | tf_op jit(solution)/shard_map/ppermute | solution.py:254
  82.8 18.3 %collective-permute-start.18 = (bf16[512,128]{1,0:T(8,128)(2,1)S(1)}, bf16[512,128]{1,0:T(8,128)(2,1)S(1)}, u32[]{:S(2)}, u32[]{:S(2)}) collective-permute-start(bf16[512,128]{1,0:T(8,128)(2,1)S(1)} %multiply_convert_fusion.refs_0_), channel_id=1, source_target_pairs={{0,8},{1,9},{2,10},{3,11},{4,12},{5,13},{6,14},{7,15},{8,0},{9,1},... | collective-permute-start | bytes 393224 | tf_op jit(solution)/shard_map/ppermute | solution.py:254
  84.4 16.7 %collective-permute-start.17 = (bf16[512,128]{1,0:T(8,128)(2,1)S(1)}, bf16[512,128]{1,0:T(8,128)(2,1)S(1)}, u32[]{:S(2)}, u32[]{:S(2)}) collective-permute-start(bf16[512,128]{1,0:T(8,128)(2,1)S(1)} %multiply_convert_fusion.refs_0_), channel_id=1, source_target_pairs={{0,4},{1,5},{2,6},{3,7},{4,8},{5,9},{6,10},{7,11},{8,12},{9,13},{1... | collective-permute-start | bytes 393224 | tf_op jit(solution)/shard_map/ppermute | solution.py:254
  103.9 5.0 %collective-permute-start.27 = (bf16[64,1024]{1,0:T(8,128)(2,1)S(1)}, bf16[64,1024]{1,0:T(8,128)(2,1)S(1)}, u32[]{:S(2)}, u32[]{:S(2)}) collective-permute-start(bf16[64,1024]{1,0:T(8,128)(2,1)S(1)} %mix.1.refs_0_), channel_id=1, source_target_pairs={{0,12},{1,13},{2,14},{3,15},{4,0},{5,1},{6,2},{7,3},{8,4},{9,5},{1... | collective-permute-start | bytes 393224 | tf_op jit(solution)/shard_map/ppermute | solution.py:254
  104.6 10.5 %collective-permute-start.24 = (bf16[64,1024]{1,0:T(8,128)(2,1)S(1)}, bf16[64,1024]{1,0:T(8,128)(2,1)S(1)}, u32[]{:S(2)}, u32[]{:S(2)}) collective-permute-start(bf16[64,1024]{1,0:T(8,128)(2,1)S(1)} %mix.1.refs_0_), channel_id=1, source_target_pairs={{0,4},{1,5},{2,6},{3,7},{4,8},{5,9},{6,10},{7,11},{8,12},{9,13},{1... | collective-permute-start | bytes 393224 | tf_op jit(solution)/shard_map/ppermute | solution.py:254
  106.0 12.5 %collective-permute-start.26 = (bf16[64,1024]{1,0:T(8,128)(2,1)S(1)}, bf16[64,1024]{1,0:T(8,128)(2,1)S(1)}, u32[]{:S(2)}, u32[]{:S(2)}) collective-permute-start(bf16[64,1024]{1,0:T(8,128)(2,1)S(1)} %mix.1.refs_0_), channel_id=1, source_target_pairs={{0,8},{1,9},{2,10},{3,11},{4,12},{5,13},{6,14},{7,15},{8,0},{9,1},... | collective-permute-start | bytes 393224 | tf_op jit(solution)/shard_map/ppermute | solution.py:254
  108.4 13.6 %collective-permute-start.23 = (bf16[64,1024]{1,0:T(8,128)(2,1)S(1)}, bf16[64,1024]{1,0:T(8,128)(2,1)S(1)}, u32[]{:S(2)}, u32[]{:S(2)}) collective-permute-start(bf16[64,1024]{1,0:T(8,128)(2,1)S(1)} %mix.1.refs_0_), channel_id=1, source_target_pairs={{0,2},{1,3},{2,0},{3,1},{4,6},{5,7},{6,4},{7,5},{8,10},{9,11},{10,... | collective-permute-start | bytes 393224 | tf_op jit(solution)/shard_map/ppermute | solution.py:254
  115.1 9.7 %collective-permute-start.29 = (bf16[64,1024]{1,0:T(8,128)(2,1)S(1)}, bf16[64,1024]{1,0:T(8,128)(2,1)S(1)}, u32[]{:S(2)}, u32[]{:S(2)}) collective-permute-start(bf16[64,1024]{1,0:T(8,128)(2,1)S(1)} %collective-permute-done.27.refs_3_), channel_id=1, source_target_pairs={{0,2},{1,3},{2,0},{3,1},{4,6},{5,7},{6,4},{7,5},{8,10},{9,11},{10,... | collective-permute-start | bytes 393224 | tf_op jit(solution)/shard_map/ppermute | solution.py:254
  118.5 6.3 %collective-permute-start.28 = (bf16[64,1024]{1,0:T(8,128)(2,1)S(1)}, bf16[64,1024]{1,0:T(8,128)(2,1)S(1)}, u32[]{:S(2)}, u32[]{:S(2)}) collective-permute-start(bf16[64,1024]{1,0:T(8,128)(2,1)S(1)} %collective-permute-done.26.refs_2_), channel_id=1, source_target_pairs={{0,2},{1,3},{2,0},{3,1},{4,6},{5,7},{6,4},{7,5},{8,10},{9,11},{10,... | collective-permute-start | bytes 393224 | tf_op jit(solution)/shard_map/ppermute | solution.py:254
  118.7 7.5 %collective-permute-start.25 = (bf16[64,1024]{1,0:T(8,128)(2,1)S(1)}, bf16[64,1024]{1,0:T(8,128)(2,1)S(1)}, u32[]{:S(2)}, u32[]{:S(2)}) collective-permute-start(bf16[64,1024]{1,0:T(8,128)(2,1)S(1)} %collective-permute-done.24.refs_1_), channel_id=1, source_target_pairs={{0,2},{1,3},{2,0},{3,1},{4,6},{5,7},{6,4},{7,5},{8,10},{9,11},{10,... | collective-permute-start | bytes 393224 | tf_op jit(solution)/shard_map/ppermute | solution.py:254
  121.9 8.8 %copy-start.4 = (bf16[128,1024]{1,0:T(8,128)(2,1)S(1)}, bf16[128,1024]{1,0:T(8,128)(2,1)}, u32[]{:S(2)}) copy-start(bf16[128,1024]{1,0:T(8,128)(2,1)} %param.14) | copy-start | bytes 786436
  129.1 1.6 %collective-permute-start.30 = (bf16[128,1024]{1,0:T(8,128)(2,1)S(1)}, bf16[128,1024]{1,0:T(8,128)(2,1)S(1)}, u32[]{:S(2)}, u32[]{:S(2)}) collective-permute-start(bf16[128,1024]{1,0:T(8,128)(2,1)S(1)} %get-tuple-element.68), channel_id=1, source_target_pairs={{0,1},{1,0},{2,3},{3,2},{4,5},{5,4},{6,7},{7,6},{8,9},{9,8},{10,11... | collective-permute-start | bytes 786440 | tf_op jit(solution)/shard_map/ppermute | solution.py:254

commit v5 on v4

--- a/solution.py
+++ b/solution.py
@@ -49,56 +49,55 @@
     )(scalars, vision)
 
 
-def project_kernel(groups, pairs, shifts, scalars, *refs):
+def project_kernel(groups, pairs, shifts, matrix, scalars, *refs):
     count = groups * 2
-    near, far, slabs = refs[:count], refs[count : 2 * count], refs[2 * count : -2 * count - 1]
-    outs, placed = refs[-2 * count - 1 : -1], refs[-1]
+    near, far, slabs = refs[:count], refs[count : 2 * count], refs[2 * count : -count - 1]
+    outs, placed = refs[-count - 1 : -1], refs[-1]
+    width = 2 * HEAD_SIZE
+    columns = slice(matrix * width, (matrix + 1) * width)
     half = near[0].shape[0]
     side, place = scalars[0], scalars[1]
     for shift, slab in zip(shifts, slabs):
         if isinstance(shift, tuple):
             continue
-        placed[lax.rem(place + pairs - shift, pairs)] = slab[...]
+        placed[lax.rem(place + pairs - shift, pairs)] = slab[:, columns]
     for shift, slab in zip(shifts, slabs):
         if isinstance(shift, tuple):
 
             @pl.when(place >= pairs // 2)
             def _():
-                placed[lax.rem(place + pairs - shift[0], pairs)] = slab[...]
+                placed[lax.rem(place + pairs - shift[0], pairs)] = slab[:, columns]
 
     w = jnp.concatenate([placed[z] for z in range(pairs)], axis=0)
     for part, pieces in enumerate((near, far)):
         lhs = jnp.concatenate([ref[...] for ref in pieces], axis=0)
         result = jnp.dot(lhs, w, preferred_element_type=f32)
-        columns = [result[:, n * HEAD_SIZE : (n + 1) * HEAD_SIZE] for n in range(4)]
-        for matrix in range(2):
-            first, second = columns[2 * matrix : 2 * matrix + 2]
-            heads = jnp.where(side == 0, first, second), jnp.where(side == 0, second, first)
-            for source in range(count):
-                by_group, by_side = source // 2, source % 2
-                for to in range(2):
-                    out = outs[matrix * count + (-by_group) % groups * 2 + to]
-                    start = (0 if by_side == to else 2 * half) + part * half
-                    out[start : start + half, :] = heads[to][
-                        source * half : (source + 1) * half, :
-                    ].astype(out.dtype)
-
-
-def project(near, far, shifts, slabs, side, place, pairs):
+        first, second = result[:, :HEAD_SIZE], result[:, HEAD_SIZE:]
+        heads = jnp.where(side == 0, first, second), jnp.where(side == 0, second, first)
+        for source in range(count):
+            by_group, by_side = source // 2, source % 2
+            for to in range(2):
+                out = outs[(-by_group) % groups * 2 + to]
+                start = (0 if by_side == to else 2 * half) + part * half
+                out[start : start + half, :] = heads[to][
+                    source * half : (source + 1) * half, :
+                ].astype(out.dtype)
+
+
+def project(near, far, shifts, slabs, side, place, pairs, matrix, dtype, name):
     count = len(near)
     half = near[0].shape[0]
     vmem = pl.BlockSpec(memory_space=pltpu.VMEM)
     return pl.pallas_call(
-        functools.partial(project_kernel, count // 2, pairs, shifts),
+        functools.partial(project_kernel, count // 2, pairs, shifts, matrix),
         in_specs=[pl.BlockSpec(memory_space=pltpu.SMEM)] + [vmem] * (2 * count + len(slabs)),
-        out_specs=[vmem] * (2 * count),
+        out_specs=[vmem] * count,
         out_shape=[
-            jax.ShapeDtypeStruct((4 * half, HEAD_SIZE), bf16 if k > count else f32)
-            for k in range(2 * count)
+            jax.ShapeDtypeStruct((4 * half, HEAD_SIZE), dtype if k else f32) for k in range(count)
         ],
-        scratch_shapes=[pltpu.VMEM((pairs,) + slabs[0].shape, bf16)],
-        compiler_params=pltpu.CompilerParams(vmem_limit_bytes=VMEM_BYTES),
-        name="project",
+        scratch_shapes=[pltpu.VMEM((pairs, slabs[0].shape[0], 2 * HEAD_SIZE), bf16)],
+        compiler_params=pltpu.CompilerParams(vmem_limit_bytes=VMEM_BYTES),
+        name=name,
     )(jnp.stack([side, place]).astype(jnp.int32), *near, *far, *slabs)
 
 
@@ -325,16 +324,15 @@
     def sum_up(own, pieces):
         return functools.reduce(lambda a, b: a + b.astype(f32), pieces, own)
 
-    q_recv = plane_shift(after(q_send, *received), 0, 1)
-    far[-1] = after(far[-1], q_recv)
     slabs = line_slabs(slab, slab_near, slab_far)
-    pieces = project(near, far, shifts, slabs, side, place, pairs)
-    key_pieces, value_pieces = pieces[: len(offsets)], pieces[len(offsets) :]
+    key_pieces = project(near, far, shifts, slabs, side, place, pairs, 0, f32, "project_keys")
     key_parts = scatter(key_pieces)
+    slabs[0] = after(slabs[0], *key_pieces)
+    value_pieces = project(near, far, shifts, slabs, side, place, pairs, 1, bf16, "project_values")
     value_parts = scatter(value_pieces)
     keys = norm(sum_up(key_pieces[0], key_parts), key_norm_gain)
     all_keys = all_pairs(keys)
-    q_recv = after(q_recv, *pieces)
+    q_recv = plane_shift(after(q_send, all_keys[1]), 0, 1)
     q_pair = jnp.where(
         side == 0,
         jnp.concatenate([q_own, q_recv], axis=0),
@@ -344,6 +342,7 @@
         [q_pair[:, h * HEAD_SIZE : (h + 1) * HEAD_SIZE] for h in range(heads)], axis=0
     )
     normed = norm(q_heads.astype(f32), query_norm_gain)
+    value_parts = [after(v, all_keys[1]) for v in value_parts]
     values = sum_up(value_pieces[0], value_parts).astype(bf16)
     all_values = all_pairs(values)
     all_keys = [after(k, values) for k in all_keys]

time: 132 us -> 115 us (0.87)
  waiting for transfers between devices: 62.3 us -> 44.2 us
  Pallas kernels: 16.4 us -> 19.2 us
  starting transfers between devices: 41.6 us -> 39.5 us
    ppermute x31, waiting for transfers between devices: 62.3 us -> 44.2 us  [permute(): return lax.ppermute(array, AXES, perm)]
    pallas_call x1 -> x2, Pallas kernels: 4.25 us -> 7.01 us  [project(): pl.pallas_call(functools.partial(project_kernel, count // 2, pairs, shift...]
    ppermute x31, starting transfers between devices: 41.6 us -> 39.5 us  [permute(): return lax.ppermute(array, AXES, perm)]
    unnamed x21 -> x25, local copies, waits for them, and re-layouts: 5.37 us -> 6.41 us
  transfers between devices with their start and end apart: 31 -> 31, of which waited for: 13 -> 15; matrix products, arithmetic and copies ran while one was open for 2% -> 2% of each run, Pallas kernels for 4% -> 11%
where the time goes in v5:
time: 115 us; the launch traced here: 114 us
  waiting for transfers between devices  44.2 us (38%)
  starting transfers between devices  39.5 us (34%)
  Pallas kernels  19.2 us (17%)
  local copies, waits for them, and re-layouts  8.54 us (7%)
  other arithmetic  1.83 us (2%)
    ppermute x31, waiting for transfers between devices, permute(): return lax.ppermute(array, AXES, perm)  44.2 us
    ppermute x31, starting transfers between devices, permute(): return lax.ppermute(array, AXES, perm)  39.5 us
    pallas_call x2, Pallas kernels, project(): pl.pallas_call(functools.partial(project_kernel, count // 2, pairs, shift...  7.01 us
    unnamed x25, local copies, waits for them, and re-layouts  6.41 us
    pallas_call x3, Pallas kernels, pack(): pl.pallas_call(functools.partial(pack_kernel, groups, pairs, part, count)...  5.33 us
    pallas_call x2, Pallas kernels, output(): pl.pallas_call(functools.partial(output_kernel, pairs, last), grid_spec=p...  4.14 us
  transfers between devices with their start and end apart: 31, of which 15 were waited for; matrix products, arithmetic and copies ran while one was open for 2% of the time, Pallas kernels for 11%

profile of v5, /device:TPU:0, one launch (start us, length us, event | category | flops | bytes accessed | tf_op | source)
XLA Modules:
  0.0 114.3 jit_solution(593036384280980772)
XLA Ops:
  0.0 1.1 constant_dynamic-slice_fusion.2
  1.1 5.1 %collective-permute-start.7 = (bf16[480,512]{1,0:T(8,128)(2,1)S(1)}, bf16[480,512]{1,0:T(8,128)(2,1)S(1)}, u32[]{:S(2)}, u32[]{:S(2)}) collective-permute-start(bf16[480,512]{1,0:T(8,128)(2,1)S(1)} %pad_maximum_fusion.refs_8_), channel_id=1, source_target_pairs={{0,12},{1,13},{2,14},{3,15},{4,0},{5,1},{6,2},{7,3},{8,4},{9,5},{1... | collective-permute-start | bytes 1474568 | tf_op jit(solution)/shard_map/ppermute | solution.py:253
  6.2 0.1 pad_add_fusion.1.index_ref
  6.3 2.1 %copy-done = bf16[256,7680]{1,0:T(8,128)(2,1)S(1)} copy-done((bf16[256,7680]{1,0:T(8,128)(2,1)S(1)}, bf16[256,7680]{1,0:T(8,128)(2,1)}, u32[]{:S(2)}) %copy-start) | copy-done | bytes 3932184
  8.4 3.2 %pack_sends.1 = (bf16[128,1920]{1,0:T(8,128)(2,1)}, bf16[128,1920]{1,0:T(8,128)(2,1)}, bf16[128,1920]{1,0:T(8,128)(2,1)}) custom-call(s32[4]{0:T(128)S(1)} %pad_add_fusion.1.index_ref, bf16[256,7680]{1,0:T(8,128)(2,1)S(1)} %copy-done), custom_call_target="tpu_custom_call" | custom-call | tf_op jit(solution)/shard_map/pack_sends/pallas_call | solution.py:38
  11.6 2.5 %collective-permute-start.2 = (bf16[128,1920]{1,0:T(8,128)(2,1)}, bf16[128,1920]{1,0:T(8,128)(2,1)S(1)}, u32[]{:S(2)}, u32[]{:S(2)}) collective-permute-start(bf16[128,1920]{1,0:T(8,128)(2,1)} %get-tuple-element.42), channel_id=1, source_target_pairs={{0,18},{1,19},{2,16},{3,17},{4,22},{5,23},{6,20},{7,21},{8,26},{9,... | collective-permute-start | bytes 1474568 | tf_op jit(solution)/shard_map/ppermute | solution.py:253
  14.1 0.5 collective-permute-start.1
  14.6 0.5 collective-permute-start
  15.1 0.1 pad_add_fusion
  15.2 2.1 %copy-done.1 = bf16[256,7680]{1,0:T(8,128)(2,1)S(1)} copy-done((bf16[256,7680]{1,0:T(8,128)(2,1)S(1)}, bf16[256,7680]{1,0:T(8,128)(2,1)}, u32[]{:S(2)}) %copy-start.1) | copy-done | bytes 3932184
  17.3 1.1 pack_near.1.refs_0_
  18.4 1.0 copy-done.2
  19.4 1.1 pack_far.1.refs_4_
  20.5 1.3 %collective-permute-start.8 = (bf16[480,512]{1,0:T(8,128)(2,1)S(1)}, bf16[480,512]{1,0:T(8,128)(2,1)}, u32[]{:S(2)}, u32[]{:S(2)}) collective-permute-start(bf16[480,512]{1,0:T(8,128)(2,1)S(1)} %collective-permute-done.7.refs_10_), channel_id=1, source_target_pairs={{4,0},{5,1},{6,2},{7,3},{8,4},{9,5},{10,6},{11,7},{20,16},{21,17},... | collective-permute-start | bytes 1474568 | tf_op jit(solution)/shard_map/ppermute | solution.py:253
  21.8 6.5 %collective-permute-done.6.refs_9_ = bf16[480,512]{1,0:T(8,128)(2,1)S(1)} collective-permute-done((bf16[480,512]{1,0:T(8,128)(2,1)S(1)}, bf16[480,512]{1,0:T(8,128)(2,1)S(1)}, u32[]{:S(2)}, u32[]{:S(2)}) %collective-permute-start.6) | collective-permute-done | bytes 491552 | tf_op jit(solution)/shard_map/ppermute | solution.py:253
  28.3 1.5 %collective-permute-start.9 = (bf16[480,512]{1,0:T(8,128)(2,1)S(1)}, bf16[480,512]{1,0:T(8,128)(2,1)}, u32[]{:S(2)}, u32[]{:S(2)}) collective-permute-start(bf16[480,512]{1,0:T(8,128)(2,1)S(1)} %collective-permute-done.6.refs_9_), channel_id=1, source_target_pairs={{4,8},{5,9},{6,10},{7,11},{8,12},{9,13},{10,14},{11,15},{20,24},{2... | collective-permute-start | bytes 1474568 | tf_op jit(solution)/shard_map/ppermute | solution.py:253
  29.8 6.2 %collective-permute-done.1.refs_2_ = bf16[128,1920]{1,0:T(8,128)(2,1)S(1)} collective-permute-done((bf16[128,1920]{1,0:T(8,128)(2,1)}, bf16[128,1920]{1,0:T(8,128)(2,1)S(1)}, u32[]{:S(2)}, u32[]{:S(2)}) %collective-permute-start.1) | collective-permute-done | bytes 491552 | tf_op jit(solution)/shard_map/ppermute | solution.py:253
  36.1 0.5 collective-permute-start.3
  36.6 0.1 pad_add_fusion.2.scalars
  36.6 2.2 %collective-permute-done.8.refs_11_ = bf16[480,512]{1,0:T(8,128)(2,1)} collective-permute-done((bf16[480,512]{1,0:T(8,128)(2,1)S(1)}, bf16[480,512]{1,0:T(8,128)(2,1)}, u32[]{:S(2)}, u32[]{:S(2)}) %collective-permute-start.8) | collective-permute-done | bytes 491552 | tf_op jit(solution)/shard_map/ppermute | solution.py:253
  39.0 3.2 %project_keys.1 = (f32[512,128]{1,0:T(8,128)S(1)}, f32[512,128]{1,0:T(8,128)S(1)}, f32[512,128]{1,0:T(8,128)S(1)}, f32[512,128]{1,0:T(8,128)S(1)}) custom-call(s32[2]{0:T(128)S(1)} %pad_add_fusion.2.scalars, bf16[128,1920]{1,0:T(8,128)(2,1)S(1)} %pack_near.1.refs_0_, bf16[128,1920]{1,0:T(8,128)(2,1)} %collective-permute-done.refs_1_, ...), custom_call_target="tpu_custom_call" | custom-call | tf_op jit(solution)/shard_map/project_keys/pallas_call | solution.py:91
  42.2 1.5 %collective-permute-start.10 = (f32[512,128]{1,0:T(8,128)S(1)}, f32[512,128]{1,0:T(8,128)S(1)}, u32[]{:S(2)}, u32[]{:S(2)}) collective-permute-start(f32[512,128]{1,0:T(8,128)S(1)} %get-tuple-element.51), channel_id=1, source_target_pairs={{0,2},{1,3},{2,0},{3,1},{4,6},{5,7},{6,4},{7,5},{8,10},{9,11},{10,... | collective-permute-start | bytes 786440 | tf_op jit(solution)/shard_map/ppermute | solution.py:253
  43.8 1.5 %collective-permute-start.11 = (f32[512,128]{1,0:T(8,128)S(1)}, f32[512,128]{1,0:T(8,128)S(1)}, u32[]{:S(2)}, u32[]{:S(2)}) collective-permute-start(f32[512,128]{1,0:T(8,128)S(1)} %get-tuple-element.52), channel_id=1, source_target_pairs={{0,16},{1,17},{2,18},{3,19},{4,20},{5,21},{6,22},{7,23},{8,24},{9,... | collective-permute-start | bytes 786440 | tf_op jit(solution)/shard_map/ppermute | solution.py:253
  45.3 0.5 collective-permute-start.12
  45.8 1.0 copy-done.5
  46.8 3.8 %project_values.1 = (f32[512,128]{1,0:T(8,128)S(1)}, bf16[512,128]{1,0:T(8,128)(2,1)}, bf16[512,128]{1,0:T(8,128)(2,1)}, bf16[512,128]{1,0:T(8,128)(2,1)S(1)}) custom-call(s32[2]{0:T(128)S(1)} %pad_add_fusion.2.scalars, bf16[128,1920]{1,0:T(8,128)(2,1)S(1)} %pack_near.1.refs_0_, bf16[128,1920]{1,0:T(8,128)(2,1)} %collective-permute-done.refs_1_, ...), custom_call_target="tpu_custom_call" | custom-call | tf_op jit(solution)/shard_map/project_values/pallas_call | solution.py:91
  50.6 1.5 %collective-permute-start.15 = (bf16[512,128]{1,0:T(8,128)(2,1)}, bf16[512,128]{1,0:T(8,128)(2,1)S(1)}, u32[]{:S(2)}, u32[]{:S(2)}) collective-permute-start(bf16[512,128]{1,0:T(8,128)(2,1)} %get-tuple-element.57), channel_id=1, source_target_pairs={{0,2},{1,3},{2,0},{3,1},{4,6},{5,7},{6,4},{7,5},{8,10},{9,11},{10,... | collective-permute-start | bytes 393224 | tf_op jit(solution)/shard_map/ppermute | solution.py:253
  52.1 0.9 collective-permute-done.11
  53.0 4.6 %collective-permute-done.12 = f32[512,128]{1,0:T(8,128)S(1)} collective-permute-done((f32[512,128]{1,0:T(8,128)S(1)}, f32[512,128]{1,0:T(8,128)S(1)}, u32[]{:S(2)}, u32[]{:S(2)}) %collective-permute-start.12) | collective-permute-done | bytes 262176 | tf_op jit(solution)/shard_map/ppermute | solution.py:253
  57.6 0.2 multiply_reduce_fusion
  57.7 0.1 multiply_convert_fusion.refs_0_
  57.9 0.3 collective-permute-start.13
  58.2 1.5 %collective-permute-start.16 = (bf16[512,128]{1,0:T(8,128)(2,1)}, bf16[512,128]{1,0:T(8,128)(2,1)S(1)}, u32[]{:S(2)}, u32[]{:S(2)}) collective-permute-start(bf16[512,128]{1,0:T(8,128)(2,1)} %get-tuple-element.59), channel_id=1, source_target_pairs={{0,16},{1,17},{2,18},{3,19},{4,20},{5,21},{6,22},{7,23},{8,24},{9,... | collective-permute-start | bytes 393224 | tf_op jit(solution)/shard_map/ppermute | solution.py:253
  59.7 1.5 %collective-permute-start.17 = (bf16[512,128]{1,0:T(8,128)(2,1)S(1)}, bf16[512,128]{1,0:T(8,128)(2,1)S(1)}, u32[]{:S(2)}, u32[]{:S(2)}) collective-permute-start(bf16[512,128]{1,0:T(8,128)(2,1)S(1)} %get-tuple-element.61), channel_id=1, source_target_pairs={{0,18},{1,19},{2,16},{3,17},{4,22},{5,23},{6,20},{7,21},{8,26},{9,... | collective-permute-start | bytes 393224 | tf_op jit(solution)/shard_map/ppermute | solution.py:253
  61.2 1.0 constant_dynamic-slice_fusion.1
  62.2 3.4 %collective-permute-start.19 = (bf16[512,128]{1,0:T(8,128)(2,1)S(1)}, bf16[512,128]{1,0:T(8,128)(2,1)S(1)}, u32[]{:S(2)}, u32[]{:S(2)}) collective-permute-start(bf16[512,128]{1,0:T(8,128)(2,1)S(1)} %multiply_convert_fusion.refs_0_), channel_id=1, source_target_pairs={{0,12},{1,13},{2,14},{3,15},{4,0},{5,1},{6,2},{7,3},{8,4},{9,5},{1... | collective-permute-start | bytes 393224 | tf_op jit(solution)/shard_map/ppermute | solution.py:253
  65.7 0.6 collective-permute-start.18
  66.2 0.8 collective-permute-start.14
  67.1 2.6 %collective-permute-start.20 = (bf16[512,128]{1,0:T(8,128)(2,1)S(1)}, bf16[512,128]{1,0:T(8,128)(2,1)S(1)}, u32[]{:S(2)}, u32[]{:S(2)}) collective-permute-start(bf16[512,128]{1,0:T(8,128)(2,1)S(1)} %add_convert_fusion.1.refs_0_), channel_id=1, source_target_pairs={{0,4},{1,5},{2,6},{3,7},{4,8},{5,9},{6,10},{7,11},{8,12},{9,13},{1... | collective-permute-start | bytes 393224 | tf_op jit(solution)/shard_map/ppermute | solution.py:253
  69.7 1.5 %collective-permute-start.21 = (bf16[512,128]{1,0:T(8,128)(2,1)S(1)}, bf16[512,128]{1,0:T(8,128)(2,1)S(1)}, u32[]{:S(2)}, u32[]{:S(2)}) collective-permute-start(bf16[512,128]{1,0:T(8,128)(2,1)S(1)} %add_convert_fusion.1.refs_0_), channel_id=1, source_target_pairs={{0,8},{1,9},{2,10},{3,11},{4,12},{5,13},{6,14},{7,15},{8,0},{9,1},... | collective-permute-start | bytes 393224 | tf_op jit(solution)/shard_map/ppermute | solution.py:253
  71.2 2.7 %collective-permute-start.22 = (bf16[512,128]{1,0:T(8,128)(2,1)S(1)}, bf16[512,128]{1,0:T(8,128)(2,1)S(1)}, u32[]{:S(2)}, u32[]{:S(2)}) collective-permute-start(bf16[512,128]{1,0:T(8,128)(2,1)S(1)} %add_convert_fusion.1.refs_0_), channel_id=1, source_target_pairs={{0,12},{1,13},{2,14},{3,15},{4,0},{5,1},{6,2},{7,3},{8,4},{9,5},{1... | collective-permute-start | bytes 393224 | tf_op jit(solution)/shard_map/ppermute | solution.py:253
  73.9 6.5 %collective-permute-done.18.refs_2_ = bf16[512,128]{1,0:T(8,128)(2,1)S(1)} collective-permute-done((bf16[512,128]{1,0:T(8,128)(2,1)S(1)}, bf16[512,128]{1,0:T(8,128)(2,1)S(1)}, u32[]{:S(2)}, u32[]{:S(2)}) %collective-permute-start.18) | collective-permute-done | bytes 131104 | tf_op jit(solution)/shard_map/ppermute | solution.py:253
  80.6 0.1 fusion
  80.7 0.1 fusion.2.q_ref
  80.9 2.0 %score.1 = (bf16[512,2048]{1,0:T(8,128)(2,1)S(1)}, f32[512,128]{1,0:T(8,128)S(1)}) custom-call(bf16[512,128]{1,0:T(8,128)(2,1)S(1)} %fusion.2.q_ref, bf16[512,128]{1,0:T(8,128)(2,1)S(1)} %multiply_convert_fusion.refs_0_, bf16[512,128]{1,0:T(8,128)(2,1)S(1)} %collective-permute-done.13.refs_1_, bf16[512,128]{1,0:T(8,128)(2,1)S(1)} %collective-permute-done.18.refs_2_, ...), custom_call_target="tpu_custom_call" | custom-call | tf_op jit(solution)/shard_map/score/pallas_call | solution.py:130
  83.0 0.7 mix.1.refs_0_
  83.7 2.0 %collective-permute-start.24 = (bf16[64,1024]{1,0:T(8,128)(2,1)S(1)}, bf16[64,1024]{1,0:T(8,128)(2,1)S(1)}, u32[]{:S(2)}, u32[]{:S(2)}) collective-permute-start(bf16[64,1024]{1,0:T(8,128)(2,1)S(1)} %mix.1.refs_0_), channel_id=1, source_target_pairs={{0,4},{1,5},{2,6},{3,7},{4,8},{5,9},{6,10},{7,11},{8,12},{9,13},{1... | collective-permute-start | bytes 393224 | tf_op jit(solution)/shard_map/ppermute | solution.py:253
  85.7 2.0 %collective-permute-start.27 = (bf16[64,1024]{1,0:T(8,128)(2,1)S(1)}, bf16[64,1024]{1,0:T(8,128)(2,1)S(1)}, u32[]{:S(2)}, u32[]{:S(2)}) collective-permute-start(bf16[64,1024]{1,0:T(8,128)(2,1)S(1)} %mix.1.refs_0_), channel_id=1, source_target_pairs={{0,12},{1,13},{2,14},{3,15},{4,0},{5,1},{6,2},{7,3},{8,4},{9,5},{1... | collective-permute-start | bytes 393224 | tf_op jit(solution)/shard_map/ppermute | solution.py:253
  87.7 0.5 collective-permute-start.26
  88.2 0.8 collective-permute-start.23
  89.0 2.9 %collective-permute-done.24.refs_1_ = bf16[64,1024]{1,0:T(8,128)(2,1)S(1)} collective-permute-done((bf16[64,1024]{1,0:T(8,128)(2,1)S(1)}, bf16[64,1024]{1,0:T(8,128)(2,1)S(1)}, u32[]{:S(2)}, u32[]{:S(2)}) %collective-permute-start.24) | collective-permute-done | bytes 131104 | tf_op jit(solution)/shard_map/ppermute | solution.py:253
  92.0 0.3 collective-permute-done.27.refs_3_
  92.3 6.3 %collective-permute-done.26.refs_2_ = bf16[64,1024]{1,0:T(8,128)(2,1)S(1)} collective-permute-done((bf16[64,1024]{1,0:T(8,128)(2,1)S(1)}, bf16[64,1024]{1,0:T(8,128)(2,1)S(1)}, u32[]{:S(2)}, u32[]{:S(2)}) %collective-permute-start.26) | collective-permute-done | bytes 131104 | tf_op jit(solution)/shard_map/ppermute | solution.py:253
  98.6 0.4 collective-permute-start.28
  99.0 1.7 %collective-permute-start.29 = (bf16[64,1024]{1,0:T(8,128)(2,1)S(1)}, bf16[64,1024]{1,0:T(8,128)(2,1)S(1)}, u32[]{:S(2)}, u32[]{:S(2)}) collective-permute-start(bf16[64,1024]{1,0:T(8,128)(2,1)S(1)} %collective-permute-done.27.refs_3_), channel_id=1, source_target_pairs={{0,2},{1,3},{2,0},{3,1},{4,6},{5,7},{6,4},{7,5},{8,10},{9,11},{10,... | collective-permute-start | bytes 393224 | tf_op jit(solution)/shard_map/ppermute | solution.py:253
  100.6 0.4 collective-permute-start.25
  101.0 0.1 add_add_fusion.1
  101.1 1.3 %output_own.1.refs_5_ = f32[256,1024]{1,0:T(8,128)S(1)} custom-call(s32[3]{0:T(128)S(1)} %get-tuple-element.78.scalars, bf16[64,1024]{1,0:T(8,128)(2,1)S(1)} %mix.1.refs_0_, bf16[64,1024]{1,0:T(8,128)(2,1)S(1)} %collective-permute-done.24.refs_1_, bf16[64,1024]{1,0:T(8,128)(2,1)S(1)} %collective-permute-done.26.refs_2_, ...), custom_call_target="tpu_custom_call" | custom-call | tf_op jit(solution)/shard_map/output_own/pallas_call | solution.py:187
  102.4 2.7 %collective-permute-done.28.refs_2_ = bf16[64,1024]{1,0:T(8,128)(2,1)S(1)} collective-permute-done((bf16[64,1024]{1,0:T(8,128)(2,1)S(1)}, bf16[64,1024]{1,0:T(8,128)(2,1)S(1)}, u32[]{:S(2)}, u32[]{:S(2)}) %collective-permute-start.28) | collective-permute-done | bytes 131104 | tf_op jit(solution)/shard_map/ppermute | solution.py:253
  105.0 2.6 %collective-permute-done.29.refs_3_ = bf16[64,1024]{1,0:T(8,128)(2,1)S(1)} collective-permute-done((bf16[64,1024]{1,0:T(8,128)(2,1)S(1)}, bf16[64,1024]{1,0:T(8,128)(2,1)S(1)}, u32[]{:S(2)}, u32[]{:S(2)}) %collective-permute-start.29) | collective-permute-done | bytes 131104 | tf_op jit(solution)/shard_map/ppermute | solution.py:253
  107.6 1.4 %collective-permute-done.25.refs_1_ = bf16[64,1024]{1,0:T(8,128)(2,1)S(1)} collective-permute-done((bf16[64,1024]{1,0:T(8,128)(2,1)S(1)}, bf16[64,1024]{1,0:T(8,128)(2,1)S(1)}, u32[]{:S(2)}, u32[]{:S(2)}) %collective-permute-start.25) | collective-permute-done | bytes 131104 | tf_op jit(solution)/shard_map/ppermute | solution.py:253
  109.0 2.9 %output_other.1 = (f32[128,1024]{1,0:T(8,128)S(1)}, bf16[128,1024]{1,0:T(8,128)(2,1)S(1)}) custom-call(s32[3]{0:T(128)S(1)} %get-tuple-element.77.scalars, bf16[64,1024]{1,0:T(8,128)(2,1)S(1)} %collective-permute-done.23.refs_0_, bf16[64,1024]{1,0:T(8,128)(2,1)S(1)} %collective-permute-done.25.refs_1_, bf16[64,1024]{1,0:T(8,128)(2,1)S(1)} %collective-permute-done.28.refs_2_, ...), custom_call_target="tpu_custom_call" | custom-call | tf_op jit(solution)/shard_map/output_other/pallas_call | solution.py:187
  112.6 0.8 collective-permute-done.30
  113.5 0.8 add_convert_fusion
  (49 shorter events, 0.5 us)
Async XLA Ops:
  1.1 19.4 %collective-permute-start.7 = (bf16[480,512]{1,0:T(8,128)(2,1)S(1)}, bf16[480,512]{1,0:T(8,128)(2,1)S(1)}, u32[]{:S(2)}, u32[]{:S(2)}) collective-permute-start(bf16[480,512]{1,0:T(8,128)(2,1)S(1)} %pad_maximum_fusion.refs_8_), channel_id=1, source_target_pairs={{0,12},{1,13},{2,14},{3,15},{4,0},{5,1},{6,2},{7,3},{8,4},{9,5},{1... | collective-permute-start | bytes 1474568 | tf_op jit(solution)/shard_map/ppermute | solution.py:253
  6.2 22.1 %collective-permute-start.6 = (bf16[480,512]{1,0:T(8,128)(2,1)S(1)}, bf16[480,512]{1,0:T(8,128)(2,1)S(1)}, u32[]{:S(2)}, u32[]{:S(2)}) collective-permute-start(bf16[480,512]{1,0:T(8,128)(2,1)S(1)} %pad_maximum_fusion.refs_8_), channel_id=1, source_target_pairs={{0,4},{1,5},{2,6},{3,7},{4,8},{5,9},{6,10},{7,11},{8,12},{9,13},{1... | collective-permute-start | bytes 1474568 | tf_op jit(solution)/shard_map/ppermute | solution.py:253
  6.3 2.1 %copy-start = (bf16[256,7680]{1,0:T(8,128)(2,1)S(1)}, bf16[256,7680]{1,0:T(8,128)(2,1)}, u32[]{:S(2)}) copy-start(bf16[256,7680]{1,0:T(8,128)(2,1)} %rows_ref.2) | copy-start | bytes 11796484
  11.6 18.2 %collective-permute-start.2 = (bf16[128,1920]{1,0:T(8,128)(2,1)}, bf16[128,1920]{1,0:T(8,128)(2,1)S(1)}, u32[]{:S(2)}, u32[]{:S(2)}) collective-permute-start(bf16[128,1920]{1,0:T(8,128)(2,1)} %get-tuple-element.42), channel_id=1, source_target_pairs={{0,18},{1,19},{2,16},{3,17},{4,22},{5,23},{6,20},{7,21},{8,26},{9,... | collective-permute-start | bytes 1474568 | tf_op jit(solution)/shard_map/ppermute | solution.py:253
  14.1 22.0 %collective-permute-start.1 = (bf16[128,1920]{1,0:T(8,128)(2,1)}, bf16[128,1920]{1,0:T(8,128)(2,1)S(1)}, u32[]{:S(2)}, u32[]{:S(2)}) collective-permute-start(bf16[128,1920]{1,0:T(8,128)(2,1)} %get-tuple-element.41), channel_id=1, source_target_pairs={{0,16},{1,17},{2,18},{3,19},{4,20},{5,21},{6,22},{7,23},{8,24},{9,... | collective-permute-start | bytes 1474568 | tf_op jit(solution)/shard_map/ppermute | solution.py:253
  14.6 21.4 %collective-permute-start = (bf16[128,1920]{1,0:T(8,128)(2,1)}, bf16[128,1920]{1,0:T(8,128)(2,1)}, u32[]{:S(2)}, u32[]{:S(2)}) collective-permute-start(bf16[128,1920]{1,0:T(8,128)(2,1)} %get-tuple-element.40), channel_id=1, source_target_pairs={{0,2},{1,3},{2,0},{3,1},{4,6},{5,7},{6,4},{7,5},{8,10},{9,11},{10,... | collective-permute-start | bytes 1474568 | tf_op jit(solution)/shard_map/ppermute | solution.py:253
  15.2 2.1 %copy-start.1 = (bf16[256,7680]{1,0:T(8,128)(2,1)S(1)}, bf16[256,7680]{1,0:T(8,128)(2,1)}, u32[]{:S(2)}) copy-start(bf16[256,7680]{1,0:T(8,128)(2,1)} %rows_ref.2) | copy-start | bytes 11796484
  17.3 2.1 %copy-start.2 = (bf16[256,7680]{1,0:T(8,128)(2,1)S(1)}, bf16[256,7680]{1,0:T(8,128)(2,1)}, u32[]{:S(2)}) copy-start(bf16[256,7680]{1,0:T(8,128)(2,1)} %rows_ref.2) | copy-start | bytes 11796484
  20.5 18.5 %copy-start.4 = (bf16[480,512]{1,0:T(8,128)(2,1)}, bf16[480,512]{1,0:T(8,128)(2,1)S(1)}, u32[]{:S(2)}) copy-start(bf16[480,512]{1,0:T(8,128)(2,1)S(1)} %collective-permute-done.7.refs_10_) | copy-start | bytes 1474564
  20.5 18.4 %collective-permute-start.8 = (bf16[480,512]{1,0:T(8,128)(2,1)S(1)}, bf16[480,512]{1,0:T(8,128)(2,1)}, u32[]{:S(2)}, u32[]{:S(2)}) collective-permute-start(bf16[480,512]{1,0:T(8,128)(2,1)S(1)} %collective-permute-done.7.refs_10_), channel_id=1, source_target_pairs={{4,0},{5,1},{6,2},{7,3},{8,4},{9,5},{10,6},{11,7},{20,16},{21,17},... | collective-permute-start | bytes 1474568 | tf_op jit(solution)/shard_map/ppermute | solution.py:253
  28.3 10.5 %collective-permute-start.9 = (bf16[480,512]{1,0:T(8,128)(2,1)S(1)}, bf16[480,512]{1,0:T(8,128)(2,1)}, u32[]{:S(2)}, u32[]{:S(2)}) collective-permute-start(bf16[480,512]{1,0:T(8,128)(2,1)S(1)} %collective-permute-done.6.refs_9_), channel_id=1, source_target_pairs={{4,8},{5,9},{6,10},{7,11},{8,12},{9,13},{10,14},{11,15},{20,24},{2... | collective-permute-start | bytes 1474568 | tf_op jit(solution)/shard_map/ppermute | solution.py:253
  29.8 9.1 %collective-permute-start.5 = (bf16[128,1920]{1,0:T(8,128)(2,1)S(1)}, bf16[128,1920]{1,0:T(8,128)(2,1)}, u32[]{:S(2)}, u32[]{:S(2)}) collective-permute-start(bf16[128,1920]{1,0:T(8,128)(2,1)S(1)} %collective-permute-done.2.refs_3_), channel_id=1, source_target_pairs={{0,1},{1,0},{2,3},{3,2},{4,5},{5,4},{6,7},{7,6},{8,9},{9,8},{10,11... | collective-permute-start | bytes 1474568 | tf_op jit(solution)/shard_map/ppermute | solution.py:253
  36.1 2.8 %collective-permute-start.4 = (bf16[128,1920]{1,0:T(8,128)(2,1)S(1)}, bf16[128,1920]{1,0:T(8,128)(2,1)}, u32[]{:S(2)}, u32[]{:S(2)}) collective-permute-start(bf16[128,1920]{1,0:T(8,128)(2,1)S(1)} %collective-permute-done.1.refs_2_), channel_id=1, source_target_pairs={{0,1},{1,0},{2,3},{3,2},{4,5},{5,4},{6,7},{7,6},{8,9},{9,8},{10,11... | collective-permute-start | bytes 1474568 | tf_op jit(solution)/shard_map/ppermute | solution.py:253
  36.1 2.9 %collective-permute-start.3 = (bf16[128,1920]{1,0:T(8,128)(2,1)}, bf16[128,1920]{1,0:T(8,128)(2,1)}, u32[]{:S(2)}, u32[]{:S(2)}) collective-permute-start(bf16[128,1920]{1,0:T(8,128)(2,1)} %collective-permute-done.refs_1_), channel_id=1, source_target_pairs={{0,1},{1,0},{2,3},{3,2},{4,5},{5,4},{6,7},{7,6},{8,9},{9,8},{10,11... | collective-permute-start | bytes 1474568 | tf_op jit(solution)/shard_map/ppermute | solution.py:253
  42.2 15.5 %copy-start.7 = (f32[128]{0:T(128)S(1)}, f32[128]{0:T(128)}, u32[]{:S(2)}) copy-start(f32[128]{0:T(128)} %param.16) | copy-start | bytes 1540
  42.2 9.8 %collective-permute-start.10 = (f32[512,128]{1,0:T(8,128)S(1)}, f32[512,128]{1,0:T(8,128)S(1)}, u32[]{:S(2)}, u32[]{:S(2)}) collective-permute-start(f32[512,128]{1,0:T(8,128)S(1)} %get-tuple-element.51), channel_id=1, source_target_pairs={{0,2},{1,3},{2,0},{3,1},{4,6},{5,7},{6,4},{7,5},{8,10},{9,11},{10,... | collective-permute-start | bytes 786440 | tf_op jit(solution)/shard_map/ppermute | solution.py:253
  43.8 9.2 %collective-permute-start.11 = (f32[512,128]{1,0:T(8,128)S(1)}, f32[512,128]{1,0:T(8,128)S(1)}, u32[]{:S(2)}, u32[]{:S(2)}) collective-permute-start(f32[512,128]{1,0:T(8,128)S(1)} %get-tuple-element.52), channel_id=1, source_target_pairs={{0,16},{1,17},{2,18},{3,19},{4,20},{5,21},{6,22},{7,23},{8,24},{9,... | collective-permute-start | bytes 786440 | tf_op jit(solution)/shard_map/ppermute | solution.py:253
  45.3 12.3 %collective-permute-start.12 = (f32[512,128]{1,0:T(8,128)S(1)}, f32[512,128]{1,0:T(8,128)S(1)}, u32[]{:S(2)}, u32[]{:S(2)}) collective-permute-start(f32[512,128]{1,0:T(8,128)S(1)} %get-tuple-element.53), channel_id=1, source_target_pairs={{0,18},{1,19},{2,16},{3,17},{4,22},{5,23},{6,20},{7,21},{8,26},{9,... | collective-permute-start | bytes 786440 | tf_op jit(solution)/shard_map/ppermute | solution.py:253
  45.8 1.0 copy-start.5
  46.8 33.9 %copy-start.8 = (f32[128]{0:T(128)S(1)}, f32[128]{0:T(128)}, u32[]{:S(2)}) copy-start(f32[128]{0:T(128)} %param.15) | copy-start | bytes 1540
  50.6 15.1 %collective-permute-start.15 = (bf16[512,128]{1,0:T(8,128)(2,1)}, bf16[512,128]{1,0:T(8,128)(2,1)S(1)}, u32[]{:S(2)}, u32[]{:S(2)}) collective-permute-start(bf16[512,128]{1,0:T(8,128)(2,1)} %get-tuple-element.57), channel_id=1, source_target_pairs={{0,2},{1,3},{2,0},{3,1},{4,6},{5,7},{6,4},{7,5},{8,10},{9,11},{10,... | collective-permute-start | bytes 393224 | tf_op jit(solution)/shard_map/ppermute | solution.py:253
  57.9 8.3 %collective-permute-start.13 = (bf16[512,128]{1,0:T(8,128)(2,1)S(1)}, bf16[512,128]{1,0:T(8,128)(2,1)S(1)}, u32[]{:S(2)}, u32[]{:S(2)}) collective-permute-start(bf16[512,128]{1,0:T(8,128)(2,1)S(1)} %multiply_convert_fusion.refs_0_), channel_id=1, source_target_pairs={{0,4},{1,5},{2,6},{3,7},{4,8},{5,9},{6,10},{7,11},{8,12},{9,13},{1... | collective-permute-start | bytes 393224 | tf_op jit(solution)/shard_map/ppermute | solution.py:253
  58.2 8.0 %collective-permute-start.16 = (bf16[512,128]{1,0:T(8,128)(2,1)}, bf16[512,128]{1,0:T(8,128)(2,1)S(1)}, u32[]{:S(2)}, u32[]{:S(2)}) collective-permute-start(bf16[512,128]{1,0:T(8,128)(2,1)} %get-tuple-element.59), channel_id=1, source_target_pairs={{0,16},{1,17},{2,18},{3,19},{4,20},{5,21},{6,22},{7,23},{8,24},{9,... | collective-permute-start | bytes 393224 | tf_op jit(solution)/shard_map/ppermute | solution.py:253
  59.7 6.5 %collective-permute-start.17 = (bf16[512,128]{1,0:T(8,128)(2,1)S(1)}, bf16[512,128]{1,0:T(8,128)(2,1)S(1)}, u32[]{:S(2)}, u32[]{:S(2)}) collective-permute-start(bf16[512,128]{1,0:T(8,128)(2,1)S(1)} %get-tuple-element.61), channel_id=1, source_target_pairs={{0,18},{1,19},{2,16},{3,17},{4,22},{5,23},{6,20},{7,21},{8,26},{9,... | collective-permute-start | bytes 393224 | tf_op jit(solution)/shard_map/ppermute | solution.py:253
  61.2 39.9 %copy-start.3 = (bf16[2048,1024]{1,0:T(8,128)(2,1)S(1)}, bf16[2048,1024]{1,0:T(8,128)(2,1)}, u32[]{:S(2)}) copy-start(bf16[2048,1024]{1,0:T(8,128)(2,1)} %refs_4_.3) | copy-start | bytes 12582916
  62.2 9.0 %collective-permute-start.19 = (bf16[512,128]{1,0:T(8,128)(2,1)S(1)}, bf16[512,128]{1,0:T(8,128)(2,1)S(1)}, u32[]{:S(2)}, u32[]{:S(2)}) collective-permute-start(bf16[512,128]{1,0:T(8,128)(2,1)S(1)} %multiply_convert_fusion.refs_0_), channel_id=1, source_target_pairs={{0,12},{1,13},{2,14},{3,15},{4,0},{5,1},{6,2},{7,3},{8,4},{9,5},{1... | collective-permute-start | bytes 393224 | tf_op jit(solution)/shard_map/ppermute | solution.py:253
  65.7 14.7 %collective-permute-start.18 = (bf16[512,128]{1,0:T(8,128)(2,1)S(1)}, bf16[512,128]{1,0:T(8,128)(2,1)S(1)}, u32[]{:S(2)}, u32[]{:S(2)}) collective-permute-start(bf16[512,128]{1,0:T(8,128)(2,1)S(1)} %multiply_convert_fusion.refs_0_), channel_id=1, source_target_pairs={{0,8},{1,9},{2,10},{3,11},{4,12},{5,13},{6,14},{7,15},{8,0},{9,1},... | collective-permute-start | bytes 393224 | tf_op jit(solution)/shard_map/ppermute | solution.py:253
  66.2 14.2 %collective-permute-start.14 = (bf16[32,1024]{1,0:T(8,128)(2,1)S(1)}, bf16[32,1024]{1,0:T(8,128)(2,1)S(1)}, u32[]{:S(2)}, u32[]{:S(2)}) collective-permute-start(bf16[32,1024]{1,0:T(8,128)(2,1)S(1)} %get-tuple-element.54), channel_id=1, source_target_pairs={{0,2},{1,3},{2,0},{3,1},{4,6},{5,7},{6,4},{7,5},{8,10},{9,11},{10,... | collective-permute-start | bytes 196616 | tf_op jit(solution)/shard_map/ppermute | solution.py:253
  67.1 15.8 %collective-permute-start.20 = (bf16[512,128]{1,0:T(8,128)(2,1)S(1)}, bf16[512,128]{1,0:T(8,128)(2,1)S(1)}, u32[]{:S(2)}, u32[]{:S(2)}) collective-permute-start(bf16[512,128]{1,0:T(8,128)(2,1)S(1)} %add_convert_fusion.1.refs_0_), channel_id=1, source_target_pairs={{0,4},{1,5},{2,6},{3,7},{4,8},{5,9},{6,10},{7,11},{8,12},{9,13},{1... | collective-permute-start | bytes 393224 | tf_op jit(solution)/shard_map/ppermute | solution.py:253
  69.7 13.3 %collective-permute-start.21 = (bf16[512,128]{1,0:T(8,128)(2,1)S(1)}, bf16[512,128]{1,0:T(8,128)(2,1)S(1)}, u32[]{:S(2)}, u32[]{:S(2)}) collective-permute-start(bf16[512,128]{1,0:T(8,128)(2,1)S(1)} %add_convert_fusion.1.refs_0_), channel_id=1, source_target_pairs={{0,8},{1,9},{2,10},{3,11},{4,12},{5,13},{6,14},{7,15},{8,0},{9,1},... | collective-permute-start | bytes 393224 | tf_op jit(solution)/shard_map/ppermute | solution.py:253
  71.2 11.8 %collective-permute-start.22 = (bf16[512,128]{1,0:T(8,128)(2,1)S(1)}, bf16[512,128]{1,0:T(8,128)(2,1)S(1)}, u32[]{:S(2)}, u32[]{:S(2)}) collective-permute-start(bf16[512,128]{1,0:T(8,128)(2,1)S(1)} %add_convert_fusion.1.refs_0_), channel_id=1, source_target_pairs={{0,12},{1,13},{2,14},{3,15},{4,0},{5,1},{6,2},{7,3},{8,4},{9,5},{1... | collective-permute-start | bytes 393224 | tf_op jit(solution)/shard_map/ppermute | solution.py:253
  83.7 8.3 %collective-permute-start.24 = (bf16[64,1024]{1,0:T(8,128)(2,1)S(1)}, bf16[64,1024]{1,0:T(8,128)(2,1)S(1)}, u32[]{:S(2)}, u32[]{:S(2)}) collective-permute-start(bf16[64,1024]{1,0:T(8,128)(2,1)S(1)} %mix.1.refs_0_), channel_id=1, source_target_pairs={{0,4},{1,5},{2,6},{3,7},{4,8},{5,9},{6,10},{7,11},{8,12},{9,13},{1... | collective-permute-start | bytes 393224 | tf_op jit(solution)/shard_map/ppermute | solution.py:253
  85.7 6.6 %collective-permute-start.27 = (bf16[64,1024]{1,0:T(8,128)(2,1)S(1)}, bf16[64,1024]{1,0:T(8,128)(2,1)S(1)}, u32[]{:S(2)}, u32[]{:S(2)}) collective-permute-start(bf16[64,1024]{1,0:T(8,128)(2,1)S(1)} %mix.1.refs_0_), channel_id=1, source_target_pairs={{0,12},{1,13},{2,14},{3,15},{4,0},{5,1},{6,2},{7,3},{8,4},{9,5},{1... | collective-permute-start | bytes 393224 | tf_op jit(solution)/shard_map/ppermute | solution.py:253
  87.7 10.9 %collective-permute-start.26 = (bf16[64,1024]{1,0:T(8,128)(2,1)S(1)}, bf16[64,1024]{1,0:T(8,128)(2,1)S(1)}, u32[]{:S(2)}, u32[]{:S(2)}) collective-permute-start(bf16[64,1024]{1,0:T(8,128)(2,1)S(1)} %mix.1.refs_0_), channel_id=1, source_target_pairs={{0,8},{1,9},{2,10},{3,11},{4,12},{5,13},{6,14},{7,15},{8,0},{9,1},... | collective-permute-start | bytes 393224 | tf_op jit(solution)/shard_map/ppermute | solution.py:253
  88.2 14.1 %collective-permute-start.23 = (bf16[64,1024]{1,0:T(8,128)(2,1)S(1)}, bf16[64,1024]{1,0:T(8,128)(2,1)S(1)}, u32[]{:S(2)}, u32[]{:S(2)}) collective-permute-start(bf16[64,1024]{1,0:T(8,128)(2,1)S(1)} %mix.1.refs_0_), channel_id=1, source_target_pairs={{0,2},{1,3},{2,0},{3,1},{4,6},{5,7},{6,4},{7,5},{8,10},{9,11},{10,... | collective-permute-start | bytes 393224 | tf_op jit(solution)/shard_map/ppermute | solution.py:253
  98.6 6.4 %collective-permute-start.28 = (bf16[64,1024]{1,0:T(8,128)(2,1)S(1)}, bf16[64,1024]{1,0:T(8,128)(2,1)S(1)}, u32[]{:S(2)}, u32[]{:S(2)}) collective-permute-start(bf16[64,1024]{1,0:T(8,128)(2,1)S(1)} %collective-permute-done.26.refs_2_), channel_id=1, source_target_pairs={{0,2},{1,3},{2,0},{3,1},{4,6},{5,7},{6,4},{7,5},{8,10},{9,11},{10,... | collective-permute-start | bytes 393224 | tf_op jit(solution)/shard_map/ppermute | solution.py:253
  99.0 8.6 %collective-permute-start.29 = (bf16[64,1024]{1,0:T(8,128)(2,1)S(1)}, bf16[64,1024]{1,0:T(8,128)(2,1)S(1)}, u32[]{:S(2)}, u32[]{:S(2)}) collective-permute-start(bf16[64,1024]{1,0:T(8,128)(2,1)S(1)} %collective-permute-done.27.refs_3_), channel_id=1, source_target_pairs={{0,2},{1,3},{2,0},{3,1},{4,6},{5,7},{6,4},{7,5},{8,10},{9,11},{10,... | collective-permute-start | bytes 393224 | tf_op jit(solution)/shard_map/ppermute | solution.py:253
  100.6 8.4 %collective-permute-start.25 = (bf16[64,1024]{1,0:T(8,128)(2,1)S(1)}, bf16[64,1024]{1,0:T(8,128)(2,1)S(1)}, u32[]{:S(2)}, u32[]{:S(2)}) collective-permute-start(bf16[64,1024]{1,0:T(8,128)(2,1)S(1)} %collective-permute-done.24.refs_1_), channel_id=1, source_target_pairs={{0,2},{1,3},{2,0},{3,1},{4,6},{5,7},{6,4},{7,5},{8,10},{9,11},{10,... | collective-permute-start | bytes 393224 | tf_op jit(solution)/shard_map/ppermute | solution.py:253
  102.4 11.1 %copy-start.6 = (bf16[128,1024]{1,0:T(8,128)(2,1)S(1)}, bf16[128,1024]{1,0:T(8,128)(2,1)}, u32[]{:S(2)}) copy-start(bf16[128,1024]{1,0:T(8,128)(2,1)} %param.14) | copy-start | bytes 786436
  111.9 1.6 %collective-permute-start.30 = (bf16[128,1024]{1,0:T(8,128)(2,1)S(1)}, bf16[128,1024]{1,0:T(8,128)(2,1)S(1)}, u32[]{:S(2)}, u32[]{:S(2)}) collective-permute-start(bf16[128,1024]{1,0:T(8,128)(2,1)S(1)} %get-tuple-element.72), channel_id=1, source_target_pairs={{0,1},{1,0},{2,3},{3,2},{4,5},{5,4},{6,7},{7,6},{8,9},{9,8},{10,11... | collective-permute-start | bytes 786440 | tf_op jit(solution)/shard_map/ppermute | solution.py:253

commit v6 on v5

--- a/solution.py
+++ b/solution.py
@@ -10,7 +10,7 @@
 HEAD_SIZE = 128
 epsilon = 1e-05
 AXES = ("groups", "seq", "head")
-VMEM_BYTES = 48 * 1024 * 1024
+VMEM_BYTES = 20 * 1024 * 1024
 f32, bf16 = jnp.float32, jnp.bfloat16
 
 
@@ -158,52 +158,69 @@
     )(weights, denominator, *values)
 
 
-def output_kernel(pairs, last, scalars, *refs):
-    pieces, weight, placed = refs[:pairs], refs[pairs], refs[-1]
-    place, core = scalars[1], scalars[2]
+def own_kernel(scalars, *refs):
+    pieces, weight, out = refs[:-2], refs[-2], refs[-1]
+    depth = pieces[0].shape[1]
+    rows = pl.ds(pl.multiple_of(scalars[0] * depth, depth), depth)
+    lhs = jnp.concatenate([piece[...] for piece in pieces], axis=0)
+    out[...] = jnp.dot(lhs, weight[rows, :], preferred_element_type=f32)
+
+
+def own_output(pieces, out_weight, side, name):
+    vmem = pl.BlockSpec(memory_space=pltpu.VMEM)
+    rows = len(pieces) * pieces[0].shape[0]
+    return pl.pallas_call(
+        own_kernel,
+        in_specs=[pl.BlockSpec(memory_space=pltpu.SMEM)] + [vmem] * (len(pieces) + 1),
+        out_specs=vmem,
+        out_shape=jax.ShapeDtypeStruct((rows, out_weight.shape[1]), f32),
+        compiler_params=pltpu.CompilerParams(vmem_limit_bytes=VMEM_BYTES),
+        name=name,
+    )(jnp.stack([side]).astype(jnp.int32), *pieces, out_weight)
+
+
+def other_kernel(shifts, scalars, *refs):
+    pairs = len(shifts)
+    pieces, weight, totals = refs[:pairs], refs[pairs], refs[pairs + 1 : -4]
+    mine, send, placed, summed = refs[-4:]
+    side, place, core = scalars[0], scalars[1], scalars[2]
+    text, depth = pieces[0].shape
     for k, piece in enumerate(pieces):
         placed[lax.rem(place + pairs - k, pairs)] = piece[...]
-    lhs = jnp.concatenate([placed[z] for z in range(pairs)], axis=0)
-    product = jnp.dot(lhs, weight[...], preferred_element_type=f32)
-    if not last:
-        refs[pairs + 1][...] = product
-        return
-    total, mine, send = refs[pairs + 1 : pairs + 4]
-    product = product + total[...]
-    half = mine.shape[0]
-    upper, lower = product[:half], product[half:]
-    mine[...] = jnp.where(core == 0, upper, lower)
-    send[...] = jnp.where(core == 0, lower, upper).astype(bf16)
-
-
-def output(pieces, out_weight, side, place, core, total, name):
+    parts = [(ref, r) for ref in totals for r in range(0, ref.shape[0], text)]
+    for k, (ref, r) in zip(shifts, parts):
+        summed[lax.rem(place + pairs - k, pairs)] = ref[r : r + text, :]
+    rows = pl.ds(pl.multiple_of(side * depth, depth), depth)
+    half = pairs // 2
+    for out, which in ((send, 1 - core), (mine, core)):
+        base = which * half
+        lhs = jnp.concatenate([placed[base + n] for n in range(half)], axis=0)
+        own = jnp.concatenate([summed[base + n] for n in range(half)], axis=0)
+        product = jnp.dot(lhs, weight[rows, :], preferred_element_type=f32)
+        out[...] = (product + own).astype(out.dtype)
+
+
+def other_output(pieces, out_weight, totals, shifts, side, place, core):
+    vmem = pl.BlockSpec(memory_space=pltpu.VMEM)
     pairs = len(pieces)
     text, depth = pieces[0].shape
     width = out_weight.shape[1]
-    rows = pairs * text
-    whole = lambda *shape: pl.BlockSpec(shape, lambda i, s: (0, 0))
-    last = total is not None
-    shapes = [(rows // 2, width, f32), (rows // 2, width, bf16)] if last else [(rows, width, f32)]
-    return pl.pallas_call(
-        functools.partial(output_kernel, pairs, last),
-        grid_spec=pltpu.PrefetchScalarGridSpec(
-            num_scalar_prefetch=1,
-            grid=(1,),
-            in_specs=[whole(text, depth)] * pairs
-            + [pl.BlockSpec((depth, width), lambda i, s: (s[0], 0))]
-            + ([whole(rows, width)] if last else []),
-            out_specs=[whole(*shape[:2]) for shape in shapes],
-            scratch_shapes=[pltpu.VMEM((pairs, text, depth), bf16)],
-        ),
-        out_shape=[jax.ShapeDtypeStruct(shape[:2], shape[2]) for shape in shapes],
-        compiler_params=pltpu.CompilerParams(vmem_limit_bytes=VMEM_BYTES),
-        name=name,
-    )(
-        jnp.stack([side, place, core]).astype(jnp.int32),
-        *pieces,
-        out_weight,
-        *([total] if last else []),
-    )
+    rows = pairs * text // 2
+    return pl.pallas_call(
+        functools.partial(other_kernel, shifts),
+        in_specs=[pl.BlockSpec(memory_space=pltpu.SMEM)] + [vmem] * (pairs + 1 + len(totals)),
+        out_specs=[vmem] * 2,
+        out_shape=[
+            jax.ShapeDtypeStruct((rows, width), f32),
+            jax.ShapeDtypeStruct((rows, width), bf16),
+        ],
+        scratch_shapes=[
+            pltpu.VMEM((pairs, text, depth), bf16),
+            pltpu.VMEM((pairs, text, width), f32),
+        ],
+        compiler_params=pltpu.CompilerParams(vmem_limit_bytes=VMEM_BYTES),
+        name="output_other",
+    )(jnp.stack([side, place, core]).astype(jnp.int32), *pieces, out_weight, *totals)
 
 
 def after(array, *others):
@@ -299,7 +316,6 @@
     slab_near = line_near(slab)
 
     index = [(group + g) % groups * 2 + (side + y) % 2 for g, y in offsets]
-    vision = after(vision, slab)
     sends = pack(vision, index[1:], core, groups, pairs, part, "pack_sends")
     received = [plane_shift(send, g, y) for send, (g, y) in zip(sends, offsets[1:])]
     vision = after(vision, *sends)
@@ -348,17 +364,21 @@
     all_keys = [after(k, values) for k in all_keys]
     weights, denominator = score(normed, all_keys, heads)
     attended = mix(weights, denominator, all_values, heads)
-    others = [plane_shift(attended, 0, 1)]
-    own_pieces = [attended]
-    order = sorted(range(1, pairs), key=lambda k: min(k, pairs - k))
-    arrived = {k: line_shift(attended, k) for k in order}
-    for last, k in zip(order, order[1:]):
-        arrived[k] = after(arrived[k], arrived[last])
-    passed = {k: plane_shift(arrived[k], 0, 1) for k in order}
-    own_pieces += [arrived[k] for k in range(1, pairs)]
-    others += [passed[k] for k in range(1, pairs)]
-    (total,) = output(own_pieces, out_weight, side, place, core, None, "output_own")
-    mine, send = output(others, out_weight, 1 - side, place, core, total, "output_other")
+    passed = {0: plane_shift(attended, 0, 1)}
+    arrived = {k: line_shift(attended, k) for k in range(1, pairs)}
+    for k in near_shifts:
+        passed[k] = plane_shift(after(arrived[k], passed[0]), 0, 1)
+    totals = [
+        own_output([attended, *(arrived[k] for k in near_shifts)], out_weight, side, "output_near")
+    ]
+    order = [0, *near_shifts]
+    if middle:
+        opposite = after(arrived[middle], totals[0], passed[near_shifts[0]])
+        passed[middle] = plane_shift(opposite, 0, 1)
+        totals.append(own_output([opposite], out_weight, side, "output_far"))
+        order.append(middle)
+    others = [passed[k] for k in range(pairs)]
+    mine, send = other_output(others, out_weight, totals, order, 1 - side, place, core)
     mine = mine + core_swap(send).astype(f32)
     return (residual.astype(f32) + jnp.tanh(attn_gate[0]) * mine).astype(bf16)
 

time: 115 us -> 109 us (0.948)
  waiting for transfers between devices: 44.2 us -> 38.3 us
  Pallas kernels: 19.2 us -> 17.3 us
    ppermute x31, waiting for transfers between devices: 44.2 us -> 38.3 us  [permute(): return lax.ppermute(array, AXES, perm)]
    pallas_call x2 -> x3, Pallas kernels: 4.14 us -> 2.38 us  [the longest x1 1.33 us: other_output(): pl.pallas_call(functools.partial(other_kernel, shifts), in_specs=[pl.Bloc...]
    unnamed x25 -> x23, local copies, waits for them, and re-layouts: 6.41 us -> 5.38 us
  transfers between devices with their start and end apart: 31 -> 31, of which waited for: 15 -> 10; matrix products, arithmetic and copies ran while one was open for 2% -> 3% of each run, Pallas kernels for 11% -> 11%
where the time goes in v6:
time: 109 us; the launch traced here: 107 us
  starting transfers between devices  40.5 us (37%)
  waiting for transfers between devices  38.3 us (35%)
  Pallas kernels  17.3 us (16%)
  local copies, waits for them, and re-layouts  7.51 us (7%)
  other arithmetic  2.77 us (3%)
    ppermute x31, starting transfers between devices, permute(): return lax.ppermute(array, AXES, perm)  40.5 us
    ppermute x31, waiting for transfers between devices, permute(): return lax.ppermute(array, AXES, perm)  38.3 us
    pallas_call x2, Pallas kernels, project(): pl.pallas_call(functools.partial(project_kernel, count // 2, pairs, shift...  6.91 us
    unnamed x23, local copies, waits for them, and re-layouts  5.38 us
    pallas_call x3, Pallas kernels, pack(): pl.pallas_call(functools.partial(pack_kernel, groups, pairs, part, count)...  5.29 us
  transfers between devices with their start and end apart: 31, of which 10 were waited for; matrix products, arithmetic and copies ran while one was open for 3% of the time, Pallas kernels for 11%

profile of v6, /device:TPU:0, one launch (start us, length us, event | category | flops | bytes accessed | tf_op | source)
XLA Modules:
  0.0 107.4 jit_solution(3330475523557950968)
XLA Ops:
  0.0 1.1 %constant_dynamic-slice_fusion = (bf16[480,256]{1,0:T(8,128)(2,1)S(1)}, bf16[480,256]{1,0:T(8,128)(2,1)S(1)}) fusion(bf16[960,256]{1,0:T(8,128)(2,1)} %param.12, s32[]{:T(128)S(6)} %select_n.62, bf16[960,256]{1,0:T(8,128)(2,1)} %param.11), kind=kLoop, calls=%fused_computation.22 | loop fusion | bytes 983044 | tf_op jit(solution)/shard_map/dynamic_slice | solution.py:313
  1.1 5.1 %collective-permute-start.7 = (bf16[480,512]{1,0:T(8,128)(2,1)S(1)}, bf16[480,512]{1,0:T(8,128)(2,1)S(1)}, u32[]{:S(2)}, u32[]{:S(2)}) collective-permute-start(bf16[480,512]{1,0:T(8,128)(2,1)S(1)} %pad_maximum_fusion.refs_8_), channel_id=1, source_target_pairs={{0,12},{1,13},{2,14},{3,15},{4,0},{5,1},{6,2},{7,3},{8,4},{9,5},{1... | collective-permute-start | bytes 1474568 | tf_op jit(solution)/shard_map/ppermute | solution.py:270
  6.2 0.1 pad_add_fusion.2.index_ref
  6.3 2.1 %copy-done.1 = bf16[256,7680]{1,0:T(8,128)(2,1)S(1)} copy-done((bf16[256,7680]{1,0:T(8,128)(2,1)S(1)}, bf16[256,7680]{1,0:T(8,128)(2,1)}, u32[]{:S(2)}) %copy-start.1) | copy-done | bytes 3932184
  8.4 3.1 %pack_sends.1 = (bf16[128,1920]{1,0:T(8,128)(2,1)}, bf16[128,1920]{1,0:T(8,128)(2,1)}, bf16[128,1920]{1,0:T(8,128)(2,1)}) custom-call(s32[4]{0:T(128)S(1)} %pad_add_fusion.2.index_ref, bf16[256,7680]{1,0:T(8,128)(2,1)S(1)} %copy-done.1), custom_call_target="tpu_custom_call" | custom-call | tf_op jit(solution)/shard_map/pack_sends/pallas_call | solution.py:38
  11.6 2.5 %collective-permute-start.2 = (bf16[128,1920]{1,0:T(8,128)(2,1)}, bf16[128,1920]{1,0:T(8,128)(2,1)S(1)}, u32[]{:S(2)}, u32[]{:S(2)}) collective-permute-start(bf16[128,1920]{1,0:T(8,128)(2,1)} %get-tuple-element.41), channel_id=1, source_target_pairs={{0,18},{1,19},{2,16},{3,17},{4,22},{5,23},{6,20},{7,21},{8,26},{9,... | collective-permute-start | bytes 1474568 | tf_op jit(solution)/shard_map/ppermute | solution.py:270
  14.0 0.5 collective-permute-start.1
  14.6 0.5 collective-permute-start
  15.1 0.1 pad_add_fusion.1
  15.2 2.1 %copy-done.2 = bf16[256,7680]{1,0:T(8,128)(2,1)S(1)} copy-done((bf16[256,7680]{1,0:T(8,128)(2,1)S(1)}, bf16[256,7680]{1,0:T(8,128)(2,1)}, u32[]{:S(2)}) %copy-start.2) | copy-done | bytes 3932184
  17.3 1.1 pack_near.1.refs_0_
  18.3 1.0 copy-done.3
  19.4 1.1 pack_far.1.refs_4_
  20.5 1.3 %collective-permute-start.8 = (bf16[480,512]{1,0:T(8,128)(2,1)S(1)}, bf16[480,512]{1,0:T(8,128)(2,1)}, u32[]{:S(2)}, u32[]{:S(2)}) collective-permute-start(bf16[480,512]{1,0:T(8,128)(2,1)S(1)} %collective-permute-done.7.refs_10_), channel_id=1, source_target_pairs={{4,0},{5,1},{6,2},{7,3},{8,4},{9,5},{10,6},{11,7},{20,16},{21,17},... | collective-permute-start | bytes 1474568 | tf_op jit(solution)/shard_map/ppermute | solution.py:270
  21.8 6.6 %collective-permute-done.6.refs_9_ = bf16[480,512]{1,0:T(8,128)(2,1)S(1)} collective-permute-done((bf16[480,512]{1,0:T(8,128)(2,1)S(1)}, bf16[480,512]{1,0:T(8,128)(2,1)S(1)}, u32[]{:S(2)}, u32[]{:S(2)}) %collective-permute-start.6) | collective-permute-done | bytes 491552 | tf_op jit(solution)/shard_map/ppermute | solution.py:270
  28.3 1.4 %collective-permute-start.9 = (bf16[480,512]{1,0:T(8,128)(2,1)S(1)}, bf16[480,512]{1,0:T(8,128)(2,1)}, u32[]{:S(2)}, u32[]{:S(2)}) collective-permute-start(bf16[480,512]{1,0:T(8,128)(2,1)S(1)} %collective-permute-done.6.refs_9_), channel_id=1, source_target_pairs={{4,8},{5,9},{6,10},{7,11},{8,12},{9,13},{10,14},{11,15},{20,24},{2... | collective-permute-start | bytes 1474568 | tf_op jit(solution)/shard_map/ppermute | solution.py:270
  29.8 6.2 %collective-permute-done.1.refs_2_ = bf16[128,1920]{1,0:T(8,128)(2,1)S(1)} collective-permute-done((bf16[128,1920]{1,0:T(8,128)(2,1)}, bf16[128,1920]{1,0:T(8,128)(2,1)S(1)}, u32[]{:S(2)}, u32[]{:S(2)}) %collective-permute-start.1) | collective-permute-done | bytes 491552 | tf_op jit(solution)/shard_map/ppermute | solution.py:270
  36.0 0.5 collective-permute-start.3
  36.5 0.1 pad_add_fusion.3.scalars
  36.6 2.3 %collective-permute-done.8.refs_11_ = bf16[480,512]{1,0:T(8,128)(2,1)} collective-permute-done((bf16[480,512]{1,0:T(8,128)(2,1)S(1)}, bf16[480,512]{1,0:T(8,128)(2,1)}, u32[]{:S(2)}, u32[]{:S(2)}) %collective-permute-start.8) | collective-permute-done | bytes 491552 | tf_op jit(solution)/shard_map/ppermute | solution.py:270
  38.9 0.0 collective-permute-done.3.refs_5_
  38.9 3.1 %project_keys.1 = (f32[512,128]{1,0:T(8,128)S(1)}, f32[512,128]{1,0:T(8,128)S(1)}, f32[512,128]{1,0:T(8,128)S(1)}, f32[512,128]{1,0:T(8,128)S(1)}) custom-call(s32[2]{0:T(128)S(1)} %pad_add_fusion.3.scalars, bf16[128,1920]{1,0:T(8,128)(2,1)S(1)} %pack_near.1.refs_0_, bf16[128,1920]{1,0:T(8,128)(2,1)} %collective-permute-done.refs_1_, ...), custom_call_target="tpu_custom_call" | custom-call | tf_op jit(solution)/shard_map/project_keys/pallas_call | solution.py:91
  42.0 1.6 %collective-permute-start.10 = (f32[512,128]{1,0:T(8,128)S(1)}, f32[512,128]{1,0:T(8,128)S(1)}, u32[]{:S(2)}, u32[]{:S(2)}) collective-permute-start(f32[512,128]{1,0:T(8,128)S(1)} %get-tuple-element.50), channel_id=1, source_target_pairs={{0,2},{1,3},{2,0},{3,1},{4,6},{5,7},{6,4},{7,5},{8,10},{9,11},{10,... | collective-permute-start | bytes 786440 | tf_op jit(solution)/shard_map/ppermute | solution.py:270
  43.6 1.5 %collective-permute-start.11 = (f32[512,128]{1,0:T(8,128)S(1)}, f32[512,128]{1,0:T(8,128)S(1)}, u32[]{:S(2)}, u32[]{:S(2)}) collective-permute-start(f32[512,128]{1,0:T(8,128)S(1)} %get-tuple-element.51), channel_id=1, source_target_pairs={{0,16},{1,17},{2,18},{3,19},{4,20},{5,21},{6,22},{7,23},{8,24},{9,... | collective-permute-start | bytes 786440 | tf_op jit(solution)/shard_map/ppermute | solution.py:270
  45.1 0.5 collective-permute-start.12
  45.6 3.8 %project_values.1 = (f32[512,128]{1,0:T(8,128)S(1)}, bf16[512,128]{1,0:T(8,128)(2,1)}, bf16[512,128]{1,0:T(8,128)(2,1)}, bf16[512,128]{1,0:T(8,128)(2,1)}) custom-call(s32[2]{0:T(128)S(1)} %pad_add_fusion.3.scalars, bf16[128,1920]{1,0:T(8,128)(2,1)S(1)} %pack_near.1.refs_0_, bf16[128,1920]{1,0:T(8,128)(2,1)} %collective-permute-done.refs_1_, ...), custom_call_target="tpu_custom_call" | custom-call | tf_op jit(solution)/shard_map/project_values/pallas_call | solution.py:91
  49.4 1.5 %collective-permute-start.15 = (bf16[512,128]{1,0:T(8,128)(2,1)}, bf16[512,128]{1,0:T(8,128)(2,1)S(1)}, u32[]{:S(2)}, u32[]{:S(2)}) collective-permute-start(bf16[512,128]{1,0:T(8,128)(2,1)} %get-tuple-element.56), channel_id=1, source_target_pairs={{0,2},{1,3},{2,0},{3,1},{4,6},{5,7},{6,4},{7,5},{8,10},{9,11},{10,... | collective-permute-start | bytes 393224 | tf_op jit(solution)/shard_map/ppermute | solution.py:270
  50.9 1.9 %collective-permute-done.11 = f32[512,128]{1,0:T(8,128)S(1)} collective-permute-done((f32[512,128]{1,0:T(8,128)S(1)}, f32[512,128]{1,0:T(8,128)S(1)}, u32[]{:S(2)}, u32[]{:S(2)}) %collective-permute-start.11) | collective-permute-done | bytes 262176 | tf_op jit(solution)/shard_map/ppermute | solution.py:270
  52.8 4.5 %collective-permute-done.12 = f32[512,128]{1,0:T(8,128)S(1)} collective-permute-done((f32[512,128]{1,0:T(8,128)S(1)}, f32[512,128]{1,0:T(8,128)S(1)}, u32[]{:S(2)}, u32[]{:S(2)}) %collective-permute-start.12) | collective-permute-done | bytes 262176 | tf_op jit(solution)/shard_map/ppermute | solution.py:270
  57.4 0.2 multiply_reduce_fusion
  57.6 0.1 multiply_convert_fusion.refs_0_
  57.7 0.4 collective-permute-start.13
  58.1 1.5 %collective-permute-start.16 = (bf16[512,128]{1,0:T(8,128)(2,1)}, bf16[512,128]{1,0:T(8,128)(2,1)S(1)}, u32[]{:S(2)}, u32[]{:S(2)}) collective-permute-start(bf16[512,128]{1,0:T(8,128)(2,1)} %get-tuple-element.58), channel_id=1, source_target_pairs={{0,16},{1,17},{2,18},{3,19},{4,20},{5,21},{6,22},{7,23},{8,24},{9,... | collective-permute-start | bytes 393224 | tf_op jit(solution)/shard_map/ppermute | solution.py:270
  59.5 1.5 %collective-permute-start.17 = (bf16[512,128]{1,0:T(8,128)(2,1)}, bf16[512,128]{1,0:T(8,128)(2,1)S(1)}, u32[]{:S(2)}, u32[]{:S(2)}) collective-permute-start(bf16[512,128]{1,0:T(8,128)(2,1)} %get-tuple-element.60), channel_id=1, source_target_pairs={{0,18},{1,19},{2,16},{3,17},{4,22},{5,23},{6,20},{7,21},{8,26},{9,... | collective-permute-start | bytes 393224 | tf_op jit(solution)/shard_map/ppermute | solution.py:270
  61.0 1.0 constant_dynamic-slice_fusion.3
  62.1 3.4 %collective-permute-start.19 = (bf16[512,128]{1,0:T(8,128)(2,1)S(1)}, bf16[512,128]{1,0:T(8,128)(2,1)S(1)}, u32[]{:S(2)}, u32[]{:S(2)}) collective-permute-start(bf16[512,128]{1,0:T(8,128)(2,1)S(1)} %multiply_convert_fusion.refs_0_), channel_id=1, source_target_pairs={{0,12},{1,13},{2,14},{3,15},{4,0},{5,1},{6,2},{7,3},{8,4},{9,5},{1... | collective-permute-start | bytes 393224 | tf_op jit(solution)/shard_map/ppermute | solution.py:270
  65.5 0.6 collective-permute-start.18
  66.1 1.1 collective-permute-start.14
  67.1 1.0 add_convert_fusion.1.refs_0_
  68.2 2.5 %collective-permute-start.20 = (bf16[512,128]{1,0:T(8,128)(2,1)S(1)}, bf16[512,128]{1,0:T(8,128)(2,1)S(1)}, u32[]{:S(2)}, u32[]{:S(2)}) collective-permute-start(bf16[512,128]{1,0:T(8,128)(2,1)S(1)} %add_convert_fusion.1.refs_0_), channel_id=1, source_target_pairs={{0,4},{1,5},{2,6},{3,7},{4,8},{5,9},{6,10},{7,11},{8,12},{9,13},{1... | collective-permute-start | bytes 393224 | tf_op jit(solution)/shard_map/ppermute | solution.py:270
  70.7 1.5 %collective-permute-start.21 = (bf16[512,128]{1,0:T(8,128)(2,1)S(1)}, bf16[512,128]{1,0:T(8,128)(2,1)S(1)}, u32[]{:S(2)}, u32[]{:S(2)}) collective-permute-start(bf16[512,128]{1,0:T(8,128)(2,1)S(1)} %add_convert_fusion.1.refs_0_), channel_id=1, source_target_pairs={{0,8},{1,9},{2,10},{3,11},{4,12},{5,13},{6,14},{7,15},{8,0},{9,1},... | collective-permute-start | bytes 393224 | tf_op jit(solution)/shard_map/ppermute | solution.py:270
  72.2 2.1 %collective-permute-start.22 = (bf16[512,128]{1,0:T(8,128)(2,1)S(1)}, bf16[512,128]{1,0:T(8,128)(2,1)S(1)}, u32[]{:S(2)}, u32[]{:S(2)}) collective-permute-start(bf16[512,128]{1,0:T(8,128)(2,1)S(1)} %add_convert_fusion.1.refs_0_), channel_id=1, source_target_pairs={{0,12},{1,13},{2,14},{3,15},{4,0},{5,1},{6,2},{7,3},{8,4},{9,5},{1... | collective-permute-start | bytes 393224 | tf_op jit(solution)/shard_map/ppermute | solution.py:270
  74.3 6.0 %collective-permute-done.18.refs_2_ = bf16[512,128]{1,0:T(8,128)(2,1)S(1)} collective-permute-done((bf16[512,128]{1,0:T(8,128)(2,1)S(1)}, bf16[512,128]{1,0:T(8,128)(2,1)S(1)}, u32[]{:S(2)}, u32[]{:S(2)}) %collective-permute-start.18) | collective-permute-done | bytes 131104 | tf_op jit(solution)/shard_map/ppermute | solution.py:270
  80.5 0.1 fusion
  80.7 0.1 fusion.2.q_ref
  80.8 2.0 %score.1 = (bf16[512,2048]{1,0:T(8,128)(2,1)S(1)}, f32[512,128]{1,0:T(8,128)S(1)}) custom-call(bf16[512,128]{1,0:T(8,128)(2,1)S(1)} %fusion.2.q_ref, bf16[512,128]{1,0:T(8,128)(2,1)S(1)} %multiply_convert_fusion.refs_0_, bf16[512,128]{1,0:T(8,128)(2,1)S(1)} %collective-permute-done.13.refs_1_, bf16[512,128]{1,0:T(8,128)(2,1)S(1)} %collective-permute-done.18.refs_2_, ...), custom_call_target="tpu_custom_call" | custom-call | tf_op jit(solution)/shard_map/score/pallas_call | solution.py:130
  82.8 0.0 collective-permute-done.21.refs_2_
  82.9 0.7 mix.1.refs_0_
  83.6 1.4 %collective-permute-start.23 = (bf16[64,1024]{1,0:T(8,128)(2,1)S(1)}, bf16[64,1024]{1,0:T(8,128)(2,1)S(1)}, u32[]{:S(2)}, u32[]{:S(2)}) collective-permute-start(bf16[64,1024]{1,0:T(8,128)(2,1)S(1)} %mix.1.refs_0_), channel_id=1, source_target_pairs={{0,2},{1,3},{2,0},{3,1},{4,6},{5,7},{6,4},{7,5},{8,10},{9,11},{10,... | collective-permute-start | bytes 393224 | tf_op jit(solution)/shard_map/ppermute | solution.py:270
  85.0 2.0 %collective-permute-start.24 = (bf16[64,1024]{1,0:T(8,128)(2,1)S(1)}, bf16[64,1024]{1,0:T(8,128)(2,1)S(1)}, u32[]{:S(2)}, u32[]{:S(2)}) collective-permute-start(bf16[64,1024]{1,0:T(8,128)(2,1)S(1)} %mix.1.refs_0_), channel_id=1, source_target_pairs={{0,4},{1,5},{2,6},{3,7},{4,8},{5,9},{6,10},{7,11},{8,12},{9,13},{1... | collective-permute-start | bytes 393224 | tf_op jit(solution)/shard_map/ppermute | solution.py:270
  87.0 1.9 %collective-permute-start.27 = (bf16[64,1024]{1,0:T(8,128)(2,1)S(1)}, bf16[64,1024]{1,0:T(8,128)(2,1)S(1)}, u32[]{:S(2)}, u32[]{:S(2)}) collective-permute-start(bf16[64,1024]{1,0:T(8,128)(2,1)S(1)} %mix.1.refs_0_), channel_id=1, source_target_pairs={{0,12},{1,13},{2,14},{3,15},{4,0},{5,1},{6,2},{7,3},{8,4},{9,5},{1... | collective-permute-start | bytes 393224 | tf_op jit(solution)/shard_map/ppermute | solution.py:270
  88.8 4.4 %collective-permute-done.24.refs_1_ = bf16[64,1024]{1,0:T(8,128)(2,1)S(1)} collective-permute-done((bf16[64,1024]{1,0:T(8,128)(2,1)S(1)}, bf16[64,1024]{1,0:T(8,128)(2,1)S(1)}, u32[]{:S(2)}, u32[]{:S(2)}) %collective-permute-start.24) | collective-permute-done | bytes 131104 | tf_op jit(solution)/shard_map/ppermute | solution.py:270
  93.3 0.6 collective-permute-start.25
  93.8 1.5 %collective-permute-start.29 = (bf16[64,1024]{1,0:T(8,128)(2,1)S(1)}, bf16[64,1024]{1,0:T(8,128)(2,1)S(1)}, u32[]{:S(2)}, u32[]{:S(2)}) collective-permute-start(bf16[64,1024]{1,0:T(8,128)(2,1)S(1)} %collective-permute-done.27.refs_2_), channel_id=1, source_target_pairs={{0,2},{1,3},{2,0},{3,1},{4,6},{5,7},{6,4},{7,5},{8,10},{9,11},{10,... | collective-permute-start | bytes 393224 | tf_op jit(solution)/shard_map/ppermute | solution.py:270
  95.3 0.6 output_near.1.refs_5_
  95.9 2.7 %collective-permute-done.26.refs_0_ = bf16[64,1024]{1,0:T(8,128)(2,1)S(1)} collective-permute-done((bf16[64,1024]{1,0:T(8,128)(2,1)S(1)}, bf16[64,1024]{1,0:T(8,128)(2,1)S(1)}, u32[]{:S(2)}, u32[]{:S(2)}) %collective-permute-start.26) | collective-permute-done | bytes 131104 | tf_op jit(solution)/shard_map/ppermute | solution.py:270
  98.6 1.7 %collective-permute-start.28 = (bf16[64,1024]{1,0:T(8,128)(2,1)S(1)}, bf16[64,1024]{1,0:T(8,128)(2,1)S(1)}, u32[]{:S(2)}, u32[]{:S(2)}) collective-permute-start(bf16[64,1024]{1,0:T(8,128)(2,1)S(1)} %collective-permute-done.26.refs_0_), channel_id=1, source_target_pairs={{0,2},{1,3},{2,0},{3,1},{4,6},{5,7},{6,4},{7,5},{8,10},{9,11},{10,... | collective-permute-start | bytes 393224 | tf_op jit(solution)/shard_map/ppermute | solution.py:270
  100.3 0.1 pad_add_fusion.scalars
  100.4 0.5 output_far.1.refs_6_
  100.9 2.7 %collective-permute-done.28.refs_2_ = bf16[64,1024]{1,0:T(8,128)(2,1)S(1)} collective-permute-done((bf16[64,1024]{1,0:T(8,128)(2,1)S(1)}, bf16[64,1024]{1,0:T(8,128)(2,1)S(1)}, u32[]{:S(2)}, u32[]{:S(2)}) %collective-permute-start.28) | collective-permute-done | bytes 131104 | tf_op jit(solution)/shard_map/ppermute | solution.py:270
  103.6 1.3 %output_other.1 = (f32[128,1024]{1,0:T(8,128)S(1)}, bf16[128,1024]{1,0:T(8,128)(2,1)S(1)}) custom-call(s32[3]{0:T(128)S(1)} %pad_add_fusion.scalars, bf16[64,1024]{1,0:T(8,128)(2,1)S(1)} %collective-permute-done.23.refs_0_, bf16[64,1024]{1,0:T(8,128)(2,1)S(1)} %collective-permute-done.25.refs_1_, bf16[64,1024]{1,0:T(8,128)(2,1)S(1)} %collective-permute-done.28.refs_2_, ...), custom_call_target="tpu_custom_call" | custom-call | tf_op jit(solution)/shard_map/output_other/pallas_call | solution.py:209
  104.9 0.1 collective-permute-start.30
  105.7 0.8 collective-permute-done.30
  106.5 0.8 add_convert_fusion
  (48 shorter events, 0.3 us)
Async XLA Ops:
  1.1 19.3 %collective-permute-start.7 = (bf16[480,512]{1,0:T(8,128)(2,1)S(1)}, bf16[480,512]{1,0:T(8,128)(2,1)S(1)}, u32[]{:S(2)}, u32[]{:S(2)}) collective-permute-start(bf16[480,512]{1,0:T(8,128)(2,1)S(1)} %pad_maximum_fusion.refs_8_), channel_id=1, source_target_pairs={{0,12},{1,13},{2,14},{3,15},{4,0},{5,1},{6,2},{7,3},{8,4},{9,5},{1... | collective-permute-start | bytes 1474568 | tf_op jit(solution)/shard_map/ppermute | solution.py:270
  6.2 22.1 %collective-permute-start.6 = (bf16[480,512]{1,0:T(8,128)(2,1)S(1)}, bf16[480,512]{1,0:T(8,128)(2,1)S(1)}, u32[]{:S(2)}, u32[]{:S(2)}) collective-permute-start(bf16[480,512]{1,0:T(8,128)(2,1)S(1)} %pad_maximum_fusion.refs_8_), channel_id=1, source_target_pairs={{0,4},{1,5},{2,6},{3,7},{4,8},{5,9},{6,10},{7,11},{8,12},{9,13},{1... | collective-permute-start | bytes 1474568 | tf_op jit(solution)/shard_map/ppermute | solution.py:270
  6.3 2.1 %copy-start.1 = (bf16[256,7680]{1,0:T(8,128)(2,1)S(1)}, bf16[256,7680]{1,0:T(8,128)(2,1)}, u32[]{:S(2)}) copy-start(bf16[256,7680]{1,0:T(8,128)(2,1)} %rows_ref.3) | copy-start | bytes 11796484
  11.6 18.2 %collective-permute-start.2 = (bf16[128,1920]{1,0:T(8,128)(2,1)}, bf16[128,1920]{1,0:T(8,128)(2,1)S(1)}, u32[]{:S(2)}, u32[]{:S(2)}) collective-permute-start(bf16[128,1920]{1,0:T(8,128)(2,1)} %get-tuple-element.41), channel_id=1, source_target_pairs={{0,18},{1,19},{2,16},{3,17},{4,22},{5,23},{6,20},{7,21},{8,26},{9,... | collective-permute-start | bytes 1474568 | tf_op jit(solution)/shard_map/ppermute | solution.py:270
  14.0 22.0 %collective-permute-start.1 = (bf16[128,1920]{1,0:T(8,128)(2,1)}, bf16[128,1920]{1,0:T(8,128)(2,1)S(1)}, u32[]{:S(2)}, u32[]{:S(2)}) collective-permute-start(bf16[128,1920]{1,0:T(8,128)(2,1)} %get-tuple-element.40), channel_id=1, source_target_pairs={{0,16},{1,17},{2,18},{3,19},{4,20},{5,21},{6,22},{7,23},{8,24},{9,... | collective-permute-start | bytes 1474568 | tf_op jit(solution)/shard_map/ppermute | solution.py:270
  14.6 21.4 %collective-permute-start = (bf16[128,1920]{1,0:T(8,128)(2,1)}, bf16[128,1920]{1,0:T(8,128)(2,1)}, u32[]{:S(2)}, u32[]{:S(2)}) collective-permute-start(bf16[128,1920]{1,0:T(8,128)(2,1)} %get-tuple-element.39), channel_id=1, source_target_pairs={{0,2},{1,3},{2,0},{3,1},{4,6},{5,7},{6,4},{7,5},{8,10},{9,11},{10,... | collective-permute-start | bytes 1474568 | tf_op jit(solution)/shard_map/ppermute | solution.py:270
  15.2 2.1 %copy-start.2 = (bf16[256,7680]{1,0:T(8,128)(2,1)S(1)}, bf16[256,7680]{1,0:T(8,128)(2,1)}, u32[]{:S(2)}) copy-start(bf16[256,7680]{1,0:T(8,128)(2,1)} %rows_ref.3) | copy-start | bytes 11796484
  17.3 2.1 %copy-start.3 = (bf16[256,7680]{1,0:T(8,128)(2,1)S(1)}, bf16[256,7680]{1,0:T(8,128)(2,1)}, u32[]{:S(2)}) copy-start(bf16[256,7680]{1,0:T(8,128)(2,1)} %rows_ref.3) | copy-start | bytes 11796484
  20.5 18.4 %collective-permute-start.8 = (bf16[480,512]{1,0:T(8,128)(2,1)S(1)}, bf16[480,512]{1,0:T(8,128)(2,1)}, u32[]{:S(2)}, u32[]{:S(2)}) collective-permute-start(bf16[480,512]{1,0:T(8,128)(2,1)S(1)} %collective-permute-done.7.refs_10_), channel_id=1, source_target_pairs={{4,0},{5,1},{6,2},{7,3},{8,4},{9,5},{10,6},{11,7},{20,16},{21,17},... | collective-permute-start | bytes 1474568 | tf_op jit(solution)/shard_map/ppermute | solution.py:270
  28.3 10.5 %collective-permute-start.9 = (bf16[480,512]{1,0:T(8,128)(2,1)S(1)}, bf16[480,512]{1,0:T(8,128)(2,1)}, u32[]{:S(2)}, u32[]{:S(2)}) collective-permute-start(bf16[480,512]{1,0:T(8,128)(2,1)S(1)} %collective-permute-done.6.refs_9_), channel_id=1, source_target_pairs={{4,8},{5,9},{6,10},{7,11},{8,12},{9,13},{10,14},{11,15},{20,24},{2... | collective-permute-start | bytes 1474568 | tf_op jit(solution)/shard_map/ppermute | solution.py:270
  29.8 9.1 %collective-permute-start.5 = (bf16[128,1920]{1,0:T(8,128)(2,1)S(1)}, bf16[128,1920]{1,0:T(8,128)(2,1)}, u32[]{:S(2)}, u32[]{:S(2)}) collective-permute-start(bf16[128,1920]{1,0:T(8,128)(2,1)S(1)} %collective-permute-done.2.refs_3_), channel_id=1, source_target_pairs={{0,1},{1,0},{2,3},{3,2},{4,5},{5,4},{6,7},{7,6},{8,9},{9,8},{10,11... | collective-permute-start | bytes 1474568 | tf_op jit(solution)/shard_map/ppermute | solution.py:270
  36.0 2.9 %collective-permute-start.4 = (bf16[128,1920]{1,0:T(8,128)(2,1)S(1)}, bf16[128,1920]{1,0:T(8,128)(2,1)}, u32[]{:S(2)}, u32[]{:S(2)}) collective-permute-start(bf16[128,1920]{1,0:T(8,128)(2,1)S(1)} %collective-permute-done.1.refs_2_), channel_id=1, source_target_pairs={{0,1},{1,0},{2,3},{3,2},{4,5},{5,4},{6,7},{7,6},{8,9},{9,8},{10,11... | collective-permute-start | bytes 1474568 | tf_op jit(solution)/shard_map/ppermute | solution.py:270
  36.0 2.9 %collective-permute-start.3 = (bf16[128,1920]{1,0:T(8,128)(2,1)}, bf16[128,1920]{1,0:T(8,128)(2,1)}, u32[]{:S(2)}, u32[]{:S(2)}) collective-permute-start(bf16[128,1920]{1,0:T(8,128)(2,1)} %collective-permute-done.refs_1_), channel_id=1, source_target_pairs={{0,1},{1,0},{2,3},{3,2},{4,5},{5,4},{6,7},{7,6},{8,9},{9,8},{10,11... | collective-permute-start | bytes 1474568 | tf_op jit(solution)/shard_map/ppermute | solution.py:270
  42.0 15.5 %copy-start.6 = (f32[128]{0:T(128)S(1)}, f32[128]{0:T(128)}, u32[]{:S(2)}) copy-start(f32[128]{0:T(128)} %param.16) | copy-start | bytes 1540
  42.0 8.9 %collective-permute-start.10 = (f32[512,128]{1,0:T(8,128)S(1)}, f32[512,128]{1,0:T(8,128)S(1)}, u32[]{:S(2)}, u32[]{:S(2)}) collective-permute-start(f32[512,128]{1,0:T(8,128)S(1)} %get-tuple-element.50), channel_id=1, source_target_pairs={{0,2},{1,3},{2,0},{3,1},{4,6},{5,7},{6,4},{7,5},{8,10},{9,11},{10,... | collective-permute-start | bytes 786440 | tf_op jit(solution)/shard_map/ppermute | solution.py:270
  43.6 9.2 %collective-permute-start.11 = (f32[512,128]{1,0:T(8,128)S(1)}, f32[512,128]{1,0:T(8,128)S(1)}, u32[]{:S(2)}, u32[]{:S(2)}) collective-permute-start(f32[512,128]{1,0:T(8,128)S(1)} %get-tuple-element.51), channel_id=1, source_target_pairs={{0,16},{1,17},{2,18},{3,19},{4,20},{5,21},{6,22},{7,23},{8,24},{9,... | collective-permute-start | bytes 786440 | tf_op jit(solution)/shard_map/ppermute | solution.py:270
  45.1 12.2 %collective-permute-start.12 = (f32[512,128]{1,0:T(8,128)S(1)}, f32[512,128]{1,0:T(8,128)S(1)}, u32[]{:S(2)}, u32[]{:S(2)}) collective-permute-start(f32[512,128]{1,0:T(8,128)S(1)} %get-tuple-element.52), channel_id=1, source_target_pairs={{0,18},{1,19},{2,16},{3,17},{4,22},{5,23},{6,20},{7,21},{8,26},{9,... | collective-permute-start | bytes 786440 | tf_op jit(solution)/shard_map/ppermute | solution.py:270
  45.6 35.1 %copy-start.7 = (f32[128]{0:T(128)S(1)}, f32[128]{0:T(128)}, u32[]{:S(2)}) copy-start(f32[128]{0:T(128)} %param.15) | copy-start | bytes 1540
  49.4 8.1 %copy-start.4 = (f32[512,128]{1,0:T(8,128)}, f32[512,128]{1,0:T(8,128)S(1)}, u32[]{:S(2)}) copy-start(f32[512,128]{1,0:T(8,128)S(1)} %get-tuple-element.55) | copy-start | bytes 786436
  49.4 16.1 %collective-permute-start.15 = (bf16[512,128]{1,0:T(8,128)(2,1)}, bf16[512,128]{1,0:T(8,128)(2,1)S(1)}, u32[]{:S(2)}, u32[]{:S(2)}) collective-permute-start(bf16[512,128]{1,0:T(8,128)(2,1)} %get-tuple-element.56), channel_id=1, source_target_pairs={{0,2},{1,3},{2,0},{3,1},{4,6},{5,7},{6,4},{7,5},{8,10},{9,11},{10,... | collective-permute-start | bytes 393224 | tf_op jit(solution)/shard_map/ppermute | solution.py:270
  57.7 8.4 %collective-permute-start.13 = (bf16[512,128]{1,0:T(8,128)(2,1)S(1)}, bf16[512,128]{1,0:T(8,128)(2,1)S(1)}, u32[]{:S(2)}, u32[]{:S(2)}) collective-permute-start(bf16[512,128]{1,0:T(8,128)(2,1)S(1)} %multiply_convert_fusion.refs_0_), channel_id=1, source_target_pairs={{0,4},{1,5},{2,6},{3,7},{4,8},{5,9},{6,10},{7,11},{8,12},{9,13},{1... | collective-permute-start | bytes 393224 | tf_op jit(solution)/shard_map/ppermute | solution.py:270
  58.1 8.0 %collective-permute-start.16 = (bf16[512,128]{1,0:T(8,128)(2,1)}, bf16[512,128]{1,0:T(8,128)(2,1)S(1)}, u32[]{:S(2)}, u32[]{:S(2)}) collective-permute-start(bf16[512,128]{1,0:T(8,128)(2,1)} %get-tuple-element.58), channel_id=1, source_target_pairs={{0,16},{1,17},{2,18},{3,19},{4,20},{5,21},{6,22},{7,23},{8,24},{9,... | collective-permute-start | bytes 393224 | tf_op jit(solution)/shard_map/ppermute | solution.py:270
  59.5 6.5 %collective-permute-start.17 = (bf16[512,128]{1,0:T(8,128)(2,1)}, bf16[512,128]{1,0:T(8,128)(2,1)S(1)}, u32[]{:S(2)}, u32[]{:S(2)}) collective-permute-start(bf16[512,128]{1,0:T(8,128)(2,1)} %get-tuple-element.60), channel_id=1, source_target_pairs={{0,18},{1,19},{2,16},{3,17},{4,22},{5,23},{6,20},{7,21},{8,26},{9,... | collective-permute-start | bytes 393224 | tf_op jit(solution)/shard_map/ppermute | solution.py:270
  61.0 34.3 %copy-start = (bf16[2048,1024]{1,0:T(8,128)(2,1)S(1)}, bf16[2048,1024]{1,0:T(8,128)(2,1)}, u32[]{:S(2)}) copy-start(bf16[2048,1024]{1,0:T(8,128)(2,1)} %refs_4_.1) | copy-start | bytes 12582916
  62.1 10.2 %collective-permute-start.19 = (bf16[512,128]{1,0:T(8,128)(2,1)S(1)}, bf16[512,128]{1,0:T(8,128)(2,1)S(1)}, u32[]{:S(2)}, u32[]{:S(2)}) collective-permute-start(bf16[512,128]{1,0:T(8,128)(2,1)S(1)} %multiply_convert_fusion.refs_0_), channel_id=1, source_target_pairs={{0,12},{1,13},{2,14},{3,15},{4,0},{5,1},{6,2},{7,3},{8,4},{9,5},{1... | collective-permute-start | bytes 393224 | tf_op jit(solution)/shard_map/ppermute | solution.py:270
  65.5 14.8 %collective-permute-start.18 = (bf16[512,128]{1,0:T(8,128)(2,1)S(1)}, bf16[512,128]{1,0:T(8,128)(2,1)S(1)}, u32[]{:S(2)}, u32[]{:S(2)}) collective-permute-start(bf16[512,128]{1,0:T(8,128)(2,1)S(1)} %multiply_convert_fusion.refs_0_), channel_id=1, source_target_pairs={{0,8},{1,9},{2,10},{3,11},{4,12},{5,13},{6,14},{7,15},{8,0},{9,1},... | collective-permute-start | bytes 393224 | tf_op jit(solution)/shard_map/ppermute | solution.py:270
  66.1 14.2 %collective-permute-start.14 = (bf16[32,1024]{1,0:T(8,128)(2,1)S(1)}, bf16[32,1024]{1,0:T(8,128)(2,1)S(1)}, u32[]{:S(2)}, u32[]{:S(2)}) collective-permute-start(bf16[32,1024]{1,0:T(8,128)(2,1)S(1)} %get-tuple-element.53), channel_id=1, source_target_pairs={{0,2},{1,3},{2,0},{3,1},{4,6},{5,7},{6,4},{7,5},{8,10},{9,11},{10,... | collective-permute-start | bytes 196616 | tf_op jit(solution)/shard_map/ppermute | solution.py:270
  68.2 14.7 %collective-permute-start.20 = (bf16[512,128]{1,0:T(8,128)(2,1)S(1)}, bf16[512,128]{1,0:T(8,128)(2,1)S(1)}, u32[]{:S(2)}, u32[]{:S(2)}) collective-permute-start(bf16[512,128]{1,0:T(8,128)(2,1)S(1)} %add_convert_fusion.1.refs_0_), channel_id=1, source_target_pairs={{0,4},{1,5},{2,6},{3,7},{4,8},{5,9},{6,10},{7,11},{8,12},{9,13},{1... | collective-permute-start | bytes 393224 | tf_op jit(solution)/shard_map/ppermute | solution.py:270
  70.7 12.2 %collective-permute-start.21 = (bf16[512,128]{1,0:T(8,128)(2,1)S(1)}, bf16[512,128]{1,0:T(8,128)(2,1)S(1)}, u32[]{:S(2)}, u32[]{:S(2)}) collective-permute-start(bf16[512,128]{1,0:T(8,128)(2,1)S(1)} %add_convert_fusion.1.refs_0_), channel_id=1, source_target_pairs={{0,8},{1,9},{2,10},{3,11},{4,12},{5,13},{6,14},{7,15},{8,0},{9,1},... | collective-permute-start | bytes 393224 | tf_op jit(solution)/shard_map/ppermute | solution.py:270
  72.2 10.6 %collective-permute-start.22 = (bf16[512,128]{1,0:T(8,128)(2,1)S(1)}, bf16[512,128]{1,0:T(8,128)(2,1)S(1)}, u32[]{:S(2)}, u32[]{:S(2)}) collective-permute-start(bf16[512,128]{1,0:T(8,128)(2,1)S(1)} %add_convert_fusion.1.refs_0_), channel_id=1, source_target_pairs={{0,12},{1,13},{2,14},{3,15},{4,0},{5,1},{6,2},{7,3},{8,4},{9,5},{1... | collective-permute-start | bytes 393224 | tf_op jit(solution)/shard_map/ppermute | solution.py:270
  83.6 5.3 %collective-permute-start.23 = (bf16[64,1024]{1,0:T(8,128)(2,1)S(1)}, bf16[64,1024]{1,0:T(8,128)(2,1)S(1)}, u32[]{:S(2)}, u32[]{:S(2)}) collective-permute-start(bf16[64,1024]{1,0:T(8,128)(2,1)S(1)} %mix.1.refs_0_), channel_id=1, source_target_pairs={{0,2},{1,3},{2,0},{3,1},{4,6},{5,7},{6,4},{7,5},{8,10},{9,11},{10,... | collective-permute-start | bytes 393224 | tf_op jit(solution)/shard_map/ppermute | solution.py:270
  85.0 8.3 %collective-permute-start.24 = (bf16[64,1024]{1,0:T(8,128)(2,1)S(1)}, bf16[64,1024]{1,0:T(8,128)(2,1)S(1)}, u32[]{:S(2)}, u32[]{:S(2)}) collective-permute-start(bf16[64,1024]{1,0:T(8,128)(2,1)S(1)} %mix.1.refs_0_), channel_id=1, source_target_pairs={{0,4},{1,5},{2,6},{3,7},{4,8},{5,9},{6,10},{7,11},{8,12},{9,13},{1... | collective-permute-start | bytes 393224 | tf_op jit(solution)/shard_map/ppermute | solution.py:270
  87.0 6.9 %collective-permute-start.27 = (bf16[64,1024]{1,0:T(8,128)(2,1)S(1)}, bf16[64,1024]{1,0:T(8,128)(2,1)S(1)}, u32[]{:S(2)}, u32[]{:S(2)}) collective-permute-start(bf16[64,1024]{1,0:T(8,128)(2,1)S(1)} %mix.1.refs_0_), channel_id=1, source_target_pairs={{0,12},{1,13},{2,14},{3,15},{4,0},{5,1},{6,2},{7,3},{8,4},{9,5},{1... | collective-permute-start | bytes 393224 | tf_op jit(solution)/shard_map/ppermute | solution.py:270
  88.8 9.8 %collective-permute-start.26 = (bf16[64,1024]{1,0:T(8,128)(2,1)S(1)}, bf16[64,1024]{1,0:T(8,128)(2,1)S(1)}, u32[]{:S(2)}, u32[]{:S(2)}) collective-permute-start(bf16[64,1024]{1,0:T(8,128)(2,1)S(1)} %mix.1.refs_0_), channel_id=1, source_target_pairs={{0,8},{1,9},{2,10},{3,11},{4,12},{5,13},{6,14},{7,15},{8,0},{9,1},... | collective-permute-start | bytes 393224 | tf_op jit(solution)/shard_map/ppermute | solution.py:270
  93.3 5.4 %collective-permute-start.25 = (bf16[64,1024]{1,0:T(8,128)(2,1)S(1)}, bf16[64,1024]{1,0:T(8,128)(2,1)S(1)}, u32[]{:S(2)}, u32[]{:S(2)}) collective-permute-start(bf16[64,1024]{1,0:T(8,128)(2,1)S(1)} %collective-permute-done.24.refs_1_), channel_id=1, source_target_pairs={{0,2},{1,3},{2,0},{3,1},{4,6},{5,7},{6,4},{7,5},{8,10},{9,11},{10,... | collective-permute-start | bytes 393224 | tf_op jit(solution)/shard_map/ppermute | solution.py:270
  93.8 7.0 %collective-permute-start.29 = (bf16[64,1024]{1,0:T(8,128)(2,1)S(1)}, bf16[64,1024]{1,0:T(8,128)(2,1)S(1)}, u32[]{:S(2)}, u32[]{:S(2)}) collective-permute-start(bf16[64,1024]{1,0:T(8,128)(2,1)S(1)} %collective-permute-done.27.refs_2_), channel_id=1, source_target_pairs={{0,2},{1,3},{2,0},{3,1},{4,6},{5,7},{6,4},{7,5},{8,10},{9,11},{10,... | collective-permute-start | bytes 393224 | tf_op jit(solution)/shard_map/ppermute | solution.py:270
  98.6 5.0 %collective-permute-start.28 = (bf16[64,1024]{1,0:T(8,128)(2,1)S(1)}, bf16[64,1024]{1,0:T(8,128)(2,1)S(1)}, u32[]{:S(2)}, u32[]{:S(2)}) collective-permute-start(bf16[64,1024]{1,0:T(8,128)(2,1)S(1)} %collective-permute-done.26.refs_0_), channel_id=1, source_target_pairs={{0,2},{1,3},{2,0},{3,1},{4,6},{5,7},{6,4},{7,5},{8,10},{9,11},{10,... | collective-permute-start | bytes 393224 | tf_op jit(solution)/shard_map/ppermute | solution.py:270
  100.9 5.7 %copy-start.5 = (bf16[128,1024]{1,0:T(8,128)(2,1)S(1)}, bf16[128,1024]{1,0:T(8,128)(2,1)}, u32[]{:S(2)}) copy-start(bf16[128,1024]{1,0:T(8,128)(2,1)} %param.14) | copy-start | bytes 786436
  104.9 1.6 %collective-permute-start.30 = (bf16[128,1024]{1,0:T(8,128)(2,1)S(1)}, bf16[128,1024]{1,0:T(8,128)(2,1)S(1)}, u32[]{:S(2)}, u32[]{:S(2)}) collective-permute-start(bf16[128,1024]{1,0:T(8,128)(2,1)S(1)} %get-tuple-element.72), channel_id=1, source_target_pairs={{0,1},{1,0},{2,3},{3,2},{4,5},{5,4},{6,7},{7,6},{8,9},{9,8},{10,11... | collective-permute-start | bytes 786440 | tf_op jit(solution)/shard_map/ppermute | solution.py:270

commit v7 on v6

--- a/solution.py
+++ b/solution.py
@@ -51,7 +51,7 @@
 
 def project_kernel(groups, pairs, shifts, matrix, scalars, *refs):
     count = groups * 2
-    near, far, slabs = refs[:count], refs[count : 2 * count], refs[2 * count : -count - 1]
+    slabs, near, far = refs[: -3 * count - 1], refs[-3 * count - 1 : -2 * count - 1], refs[-2 * count - 1 : -count - 1]
     outs, placed = refs[-count - 1 : -1], refs[-1]
     width = 2 * HEAD_SIZE
     columns = slice(matrix * width, (matrix + 1) * width)
@@ -98,7 +98,7 @@
         scratch_shapes=[pltpu.VMEM((pairs, slabs[0].shape[0], 2 * HEAD_SIZE), bf16)],
         compiler_params=pltpu.CompilerParams(vmem_limit_bytes=VMEM_BYTES),
         name=name,
-    )(jnp.stack([side, place]).astype(jnp.int32), *near, *far, *slabs)
+    )(jnp.stack([side, place]).astype(jnp.int32), *slabs, *near, *far)
 
 
 def score_kernel(heads, q_ref, *refs):
@@ -341,14 +341,15 @@
         return functools.reduce(lambda a, b: a + b.astype(f32), pieces, own)
 
     slabs = line_slabs(slab, slab_near, slab_far)
+    value_pieces = project(near, far, shifts, slabs, side, place, pairs, 1, bf16, "project_values")
+    value_parts = scatter(value_pieces)
+    slabs[0] = after(slabs[0], *value_pieces)
     key_pieces = project(near, far, shifts, slabs, side, place, pairs, 0, f32, "project_keys")
     key_parts = scatter(key_pieces)
-    slabs[0] = after(slabs[0], *key_pieces)
-    value_pieces = project(near, far, shifts, slabs, side, place, pairs, 1, bf16, "project_values")
-    value_parts = scatter(value_pieces)
-    keys = norm(sum_up(key_pieces[0], key_parts), key_norm_gain)
-    all_keys = all_pairs(keys)
-    q_recv = plane_shift(after(q_send, all_keys[1]), 0, 1)
+    values = sum_up(value_pieces[0], value_parts).astype(bf16)
+    all_values = all_pairs(values)
+    key_parts = [after(k, all_values[1]) for k in key_parts]
+    q_recv = plane_shift(after(q_send, all_values[1]), 0, 1)
     q_pair = jnp.where(
         side == 0,
         jnp.concatenate([q_own, q_recv], axis=0),
@@ -358,10 +359,8 @@
         [q_pair[:, h * HEAD_SIZE : (h + 1) * HEAD_SIZE] for h in range(heads)], axis=0
     )
     normed = norm(q_heads.astype(f32), query_norm_gain)
-    value_parts = [after(v, all_keys[1]) for v in value_parts]
-    values = sum_up(value_pieces[0], value_parts).astype(bf16)
-    all_values = all_pairs(values)
-    all_keys = [after(k, values) for k in all_keys]
+    keys = norm(sum_up(key_pieces[0], key_parts), key_norm_gain)
+    all_keys = all_pairs(keys)
     weights, denominator = score(normed, all_keys, heads)
     attended = mix(weights, denominator, all_values, heads)
     passed = {0: plane_shift(attended, 0, 1)}

time: 109 us -> 112 us (1.028)
  starting transfers between devices: 40.5 us -> 42.5 us
    ppermute x31, starting transfers between devices: 40.5 us -> 42.5 us  [permute(): return lax.ppermute(array, AXES, perm)]
  transfers between devices with their start and end apart: 31 -> 31, of which waited for: 10 -> 12; matrix products, arithmetic and copies ran while one was open for 3% -> 3% of each run, Pallas kernels for 11% -> 11%
where the time goes in v7:
time: 112 us; the launch traced here: 110 us
  starting transfers between devices  42.5 us (38%)
  waiting for transfers between devices  38.4 us (34%)
  Pallas kernels  17.5 us (16%)
  local copies, waits for them, and re-layouts  8.2 us (7%)
  other arithmetic  2.77 us (2%)
    ppermute x31, starting transfers between devices, permute(): return lax.ppermute(array, AXES, perm)  42.5 us
    ppermute x31, waiting for transfers between devices, permute(): return lax.ppermute(array, AXES, perm)  38.4 us
    pallas_call x2, Pallas kernels, project(): pl.pallas_call(functools.partial(project_kernel, count // 2, pairs, shift...  7.07 us
    unnamed x23, local copies, waits for them, and re-layouts  6.06 us
    pallas_call x3, Pallas kernels, pack(): pl.pallas_call(functools.partial(pack_kernel, groups, pairs, part, count)...  5.29 us
  transfers between devices with their start and end apart: 31, of which 12 were waited for; matrix products, arithmetic and copies ran while one was open for 3% of the time, Pallas kernels for 11%

profile of v7, /device:TPU:0, one launch (start us, length us, event | category | flops | bytes accessed | tf_op | source)
XLA Modules:
  0.0 110.4 jit_solution(4463181198680832769)
XLA Ops:
  0.0 1.1 constant_dynamic-slice_fusion
  1.1 3.1 %collective-permute-start = (bf16[480,512]{1,0:T(8,128)(2,1)S(1)}, bf16[480,512]{1,0:T(8,128)(2,1)S(1)}, u32[]{:S(2)}, u32[]{:S(2)}) collective-permute-start(bf16[480,512]{1,0:T(8,128)(2,1)S(1)} %pad_maximum_fusion.refs_0_), channel_id=1, source_target_pairs={{0,4},{1,5},{2,6},{3,7},{4,8},{5,9},{6,10},{7,11},{8,12},{9,13},{1... | collective-permute-start | bytes 1474568 | tf_op jit(solution)/shard_map/ppermute | solution.py:270
  4.2 2.1 %collective-permute-start.1 = (bf16[480,512]{1,0:T(8,128)(2,1)S(1)}, bf16[480,512]{1,0:T(8,128)(2,1)S(1)}, u32[]{:S(2)}, u32[]{:S(2)}) collective-permute-start(bf16[480,512]{1,0:T(8,128)(2,1)S(1)} %pad_maximum_fusion.refs_0_), channel_id=1, source_target_pairs={{0,12},{1,13},{2,14},{3,15},{4,0},{5,1},{6,2},{7,3},{8,4},{9,5},{1... | collective-permute-start | bytes 1474568 | tf_op jit(solution)/shard_map/ppermute | solution.py:270
  6.3 0.1 pad_add_fusion.2.index_ref
  6.4 2.1 %copy-done.1 = bf16[256,7680]{1,0:T(8,128)(2,1)S(1)} copy-done((bf16[256,7680]{1,0:T(8,128)(2,1)S(1)}, bf16[256,7680]{1,0:T(8,128)(2,1)}, u32[]{:S(2)}) %copy-start.1) | copy-done | bytes 3932184
  8.5 3.1 %pack_sends.1 = (bf16[128,1920]{1,0:T(8,128)(2,1)}, bf16[128,1920]{1,0:T(8,128)(2,1)}, bf16[128,1920]{1,0:T(8,128)(2,1)}) custom-call(s32[4]{0:T(128)S(1)} %pad_add_fusion.2.index_ref, bf16[256,7680]{1,0:T(8,128)(2,1)S(1)} %copy-done.1), custom_call_target="tpu_custom_call" | custom-call | tf_op jit(solution)/shard_map/pack_sends/pallas_call | solution.py:38
  11.6 1.7 %collective-permute-start.4 = (bf16[128,1920]{1,0:T(8,128)(2,1)}, bf16[128,1920]{1,0:T(8,128)(2,1)S(1)}, u32[]{:S(2)}, u32[]{:S(2)}) collective-permute-start(bf16[128,1920]{1,0:T(8,128)(2,1)} %get-tuple-element.35), channel_id=1, source_target_pairs={{0,2},{1,3},{2,0},{3,1},{4,6},{5,7},{6,4},{7,5},{8,10},{9,11},{10,... | collective-permute-start | bytes 1474568 | tf_op jit(solution)/shard_map/ppermute | solution.py:270
  13.3 1.5 %collective-permute-start.5 = (bf16[128,1920]{1,0:T(8,128)(2,1)}, bf16[128,1920]{1,0:T(8,128)(2,1)S(1)}, u32[]{:S(2)}, u32[]{:S(2)}) collective-permute-start(bf16[128,1920]{1,0:T(8,128)(2,1)} %get-tuple-element.36), channel_id=1, source_target_pairs={{0,16},{1,17},{2,18},{3,19},{4,20},{5,21},{6,22},{7,23},{8,24},{9,... | collective-permute-start | bytes 1474568 | tf_op jit(solution)/shard_map/ppermute | solution.py:270
  14.8 0.3 collective-permute-start.6
  15.1 0.1 pad_add_fusion.1
  15.2 2.1 %copy-done.2 = bf16[256,7680]{1,0:T(8,128)(2,1)S(1)} copy-done((bf16[256,7680]{1,0:T(8,128)(2,1)S(1)}, bf16[256,7680]{1,0:T(8,128)(2,1)}, u32[]{:S(2)}) %copy-start.2) | copy-done | bytes 3932184
  17.3 1.1 pack_far.1.refs_9_
  18.4 1.0 copy-done.3
  19.4 1.1 pack_near.1.refs_5_
  20.5 6.9 %collective-permute-done.1.refs_2_ = bf16[480,512]{1,0:T(8,128)(2,1)S(1)} collective-permute-done((bf16[480,512]{1,0:T(8,128)(2,1)S(1)}, bf16[480,512]{1,0:T(8,128)(2,1)S(1)}, u32[]{:S(2)}, u32[]{:S(2)}) %collective-permute-start.1) | collective-permute-done | bytes 491552 | tf_op jit(solution)/shard_map/ppermute | solution.py:270
  27.4 1.3 %collective-permute-start.2 = (bf16[480,512]{1,0:T(8,128)(2,1)S(1)}, bf16[480,512]{1,0:T(8,128)(2,1)}, u32[]{:S(2)}, u32[]{:S(2)}) collective-permute-start(bf16[480,512]{1,0:T(8,128)(2,1)S(1)} %collective-permute-done.1.refs_2_), channel_id=1, source_target_pairs={{4,0},{5,1},{6,2},{7,3},{8,4},{9,5},{10,6},{11,7},{20,16},{21,17},... | collective-permute-start | bytes 1474568 | tf_op jit(solution)/shard_map/ppermute | solution.py:270
  28.7 1.4 %collective-permute-start.3 = (bf16[480,512]{1,0:T(8,128)(2,1)S(1)}, bf16[480,512]{1,0:T(8,128)(2,1)}, u32[]{:S(2)}, u32[]{:S(2)}) collective-permute-start(bf16[480,512]{1,0:T(8,128)(2,1)S(1)} %collective-permute-done.refs_1_), channel_id=1, source_target_pairs={{4,8},{5,9},{6,10},{7,11},{8,12},{9,13},{10,14},{11,15},{20,24},{2... | collective-permute-start | bytes 1474568 | tf_op jit(solution)/shard_map/ppermute | solution.py:270
  30.2 6.2 %collective-permute-done.6.refs_8_ = bf16[128,1920]{1,0:T(8,128)(2,1)} collective-permute-done((bf16[128,1920]{1,0:T(8,128)(2,1)}, bf16[128,1920]{1,0:T(8,128)(2,1)}, u32[]{:S(2)}, u32[]{:S(2)}) %collective-permute-start.6) | collective-permute-done | bytes 491552 | tf_op jit(solution)/shard_map/ppermute | solution.py:270
  36.4 0.5 collective-permute-start.8
  36.9 0.1 pad_add_fusion.3.scalars
  37.0 5.1 %collective-permute-done.2.refs_3_ = bf16[480,512]{1,0:T(8,128)(2,1)} collective-permute-done((bf16[480,512]{1,0:T(8,128)(2,1)S(1)}, bf16[480,512]{1,0:T(8,128)(2,1)}, u32[]{:S(2)}, u32[]{:S(2)}) %collective-permute-start.2) | collective-permute-done | bytes 491552 | tf_op jit(solution)/shard_map/ppermute | solution.py:270
  42.1 3.1 %project_values.1 = (f32[512,128]{1,0:T(8,128)S(1)}, bf16[512,128]{1,0:T(8,128)(2,1)S(1)}, bf16[512,128]{1,0:T(8,128)(2,1)S(1)}, bf16[512,128]{1,0:T(8,128)(2,1)S(1)}) custom-call(s32[2]{0:T(128)S(1)} %pad_add_fusion.3.scalars, bf16[480,512]{1,0:T(8,128)(2,1)S(1)} %pad_maximum_fusion.refs_0_, bf16[480,512]{1,0:T(8,128)(2,1)S(1)} %collective-permute-done.refs_1_, ...), custom_call_target="tpu_custom_call" | custom-call | tf_op jit(solution)/shard_map/project_values/pallas_call | solution.py:91
  45.2 2.5 %collective-permute-start.12 = (bf16[512,128]{1,0:T(8,128)(2,1)S(1)}, bf16[512,128]{1,0:T(8,128)(2,1)S(1)}, u32[]{:S(2)}, u32[]{:S(2)}) collective-permute-start(bf16[512,128]{1,0:T(8,128)(2,1)S(1)} %get-tuple-element.48), channel_id=1, source_target_pairs={{0,18},{1,19},{2,16},{3,17},{4,22},{5,23},{6,20},{7,21},{8,26},{9,... | collective-permute-start | bytes 393224 | tf_op jit(solution)/shard_map/ppermute | solution.py:270
  47.7 0.5 collective-permute-start.11
  48.2 0.5 collective-permute-start.10
  48.8 4.0 %project_keys.1 = (f32[512,128]{1,0:T(8,128)S(1)}, f32[512,128]{1,0:T(8,128)}, f32[512,128]{1,0:T(8,128)}, f32[512,128]{1,0:T(8,128)}) custom-call(s32[2]{0:T(128)S(1)} %pad_add_fusion.3.scalars, bf16[480,512]{1,0:T(8,128)(2,1)S(1)} %pad_maximum_fusion.refs_0_, bf16[480,512]{1,0:T(8,128)(2,1)S(1)} %collective-permute-done.refs_1_, ...), custom_call_target="tpu_custom_call" | custom-call | tf_op jit(solution)/shard_map/project_keys/pallas_call | solution.py:91
  52.7 0.7 copy-done.4
  53.4 2.4 %collective-permute-start.17 = (f32[512,128]{1,0:T(8,128)}, f32[512,128]{1,0:T(8,128)S(1)}, u32[]{:S(2)}, u32[]{:S(2)}) collective-permute-start(f32[512,128]{1,0:T(8,128)} %get-tuple-element.56), channel_id=1, source_target_pairs={{0,18},{1,19},{2,16},{3,17},{4,22},{5,23},{6,20},{7,21},{8,26},{9,... | collective-permute-start | bytes 786440 | tf_op jit(solution)/shard_map/ppermute | solution.py:270
  55.9 0.5 collective-permute-start.16
  56.4 0.5 collective-permute-start.15
  57.0 3.6 %collective-permute-start.13 = (bf16[512,128]{1,0:T(8,128)(2,1)S(1)}, bf16[512,128]{1,0:T(8,128)(2,1)S(1)}, u32[]{:S(2)}, u32[]{:S(2)}) collective-permute-start(bf16[512,128]{1,0:T(8,128)(2,1)S(1)} %add_convert_fusion.1.refs_0_), channel_id=1, source_target_pairs={{0,4},{1,5},{2,6},{3,7},{4,8},{5,9},{6,10},{7,11},{8,12},{9,13},{1... | collective-permute-start | bytes 393224 | tf_op jit(solution)/shard_map/ppermute | solution.py:270
  60.6 1.0 constant_dynamic-slice_fusion.3
  61.7 2.4 %collective-permute-start.21 = (bf16[512,128]{1,0:T(8,128)(2,1)S(1)}, bf16[512,128]{1,0:T(8,128)(2,1)S(1)}, u32[]{:S(2)}, u32[]{:S(2)}) collective-permute-start(bf16[512,128]{1,0:T(8,128)(2,1)S(1)} %add_convert_fusion.1.refs_0_), channel_id=1, source_target_pairs={{0,8},{1,9},{2,10},{3,11},{4,12},{5,13},{6,14},{7,15},{8,0},{9,1},... | collective-permute-start | bytes 393224 | tf_op jit(solution)/shard_map/ppermute | solution.py:270
  64.1 2.5 %collective-permute-done.13.refs_1_ = bf16[512,128]{1,0:T(8,128)(2,1)S(1)} collective-permute-done((bf16[512,128]{1,0:T(8,128)(2,1)S(1)}, bf16[512,128]{1,0:T(8,128)(2,1)S(1)}, u32[]{:S(2)}, u32[]{:S(2)}) %collective-permute-start.13) | collective-permute-done | bytes 131104 | tf_op jit(solution)/shard_map/ppermute | solution.py:270
  66.5 1.2 %collective-permute-start.22 = (bf16[512,128]{1,0:T(8,128)(2,1)S(1)}, bf16[512,128]{1,0:T(8,128)(2,1)S(1)}, u32[]{:S(2)}, u32[]{:S(2)}) collective-permute-start(bf16[512,128]{1,0:T(8,128)(2,1)S(1)} %add_convert_fusion.1.refs_0_), channel_id=1, source_target_pairs={{0,12},{1,13},{2,14},{3,15},{4,0},{5,1},{6,2},{7,3},{8,4},{9,5},{1... | collective-permute-start | bytes 393224 | tf_op jit(solution)/shard_map/ppermute | solution.py:270
  67.8 1.5 %collective-permute-start.14 = (bf16[32,1024]{1,0:T(8,128)(2,1)S(1)}, bf16[32,1024]{1,0:T(8,128)(2,1)S(1)}, u32[]{:S(2)}, u32[]{:S(2)}) collective-permute-start(bf16[32,1024]{1,0:T(8,128)(2,1)S(1)} %get-tuple-element.49), channel_id=1, source_target_pairs={{0,2},{1,3},{2,0},{3,1},{4,6},{5,7},{6,4},{7,5},{8,10},{9,11},{10,... | collective-permute-start | bytes 196616 | tf_op jit(solution)/shard_map/ppermute | solution.py:270
  69.3 1.1 multiply_reduce_fusion
  70.4 0.1 multiply_convert_fusion.refs_0_
  70.5 1.5 %collective-permute-start.18 = (bf16[512,128]{1,0:T(8,128)(2,1)S(1)}, bf16[512,128]{1,0:T(8,128)(2,1)S(1)}, u32[]{:S(2)}, u32[]{:S(2)}) collective-permute-start(bf16[512,128]{1,0:T(8,128)(2,1)S(1)} %multiply_convert_fusion.refs_0_), channel_id=1, source_target_pairs={{0,4},{1,5},{2,6},{3,7},{4,8},{5,9},{6,10},{7,11},{8,12},{9,13},{1... | collective-permute-start | bytes 393224 | tf_op jit(solution)/shard_map/ppermute | solution.py:270
  72.1 3.9 %collective-permute-start.19 = (bf16[512,128]{1,0:T(8,128)(2,1)S(1)}, bf16[512,128]{1,0:T(8,128)(2,1)S(1)}, u32[]{:S(2)}, u32[]{:S(2)}) collective-permute-start(bf16[512,128]{1,0:T(8,128)(2,1)S(1)} %multiply_convert_fusion.refs_0_), channel_id=1, source_target_pairs={{0,8},{1,9},{2,10},{3,11},{4,12},{5,13},{6,14},{7,15},{8,0},{9,1},... | collective-permute-start | bytes 393224 | tf_op jit(solution)/shard_map/ppermute | solution.py:270
  76.0 1.1 collective-permute-start.20
  77.2 0.1 fusion
  77.4 0.1 fusion.2.q_ref
  77.6 2.3 %collective-permute-done.18.refs_1_ = bf16[512,128]{1,0:T(8,128)(2,1)S(1)} collective-permute-done((bf16[512,128]{1,0:T(8,128)(2,1)S(1)}, bf16[512,128]{1,0:T(8,128)(2,1)S(1)}, u32[]{:S(2)}, u32[]{:S(2)}) %collective-permute-start.18) | collective-permute-done | bytes 131104 | tf_op jit(solution)/shard_map/ppermute | solution.py:270
  79.8 3.6 %collective-permute-done.19.refs_2_ = bf16[512,128]{1,0:T(8,128)(2,1)S(1)} collective-permute-done((bf16[512,128]{1,0:T(8,128)(2,1)S(1)}, bf16[512,128]{1,0:T(8,128)(2,1)S(1)}, u32[]{:S(2)}, u32[]{:S(2)}) %collective-permute-start.19) | collective-permute-done | bytes 131104 | tf_op jit(solution)/shard_map/ppermute | solution.py:270
  83.5 2.0 %score.1 = (bf16[512,2048]{1,0:T(8,128)(2,1)S(1)}, f32[512,128]{1,0:T(8,128)S(1)}) custom-call(bf16[512,128]{1,0:T(8,128)(2,1)S(1)} %fusion.2.q_ref, bf16[512,128]{1,0:T(8,128)(2,1)S(1)} %multiply_convert_fusion.refs_0_, bf16[512,128]{1,0:T(8,128)(2,1)S(1)} %collective-permute-done.18.refs_1_, bf16[512,128]{1,0:T(8,128)(2,1)S(1)} %collective-permute-done.19.refs_2_, ...), custom_call_target="tpu_custom_call" | custom-call | tf_op jit(solution)/shard_map/score/pallas_call | solution.py:130
  85.6 0.7 mix.1.refs_0_
  86.3 1.9 %collective-permute-start.23 = (bf16[64,1024]{1,0:T(8,128)(2,1)S(1)}, bf16[64,1024]{1,0:T(8,128)(2,1)S(1)}, u32[]{:S(2)}, u32[]{:S(2)}) collective-permute-start(bf16[64,1024]{1,0:T(8,128)(2,1)S(1)} %mix.1.refs_0_), channel_id=1, source_target_pairs={{0,2},{1,3},{2,0},{3,1},{4,6},{5,7},{6,4},{7,5},{8,10},{9,11},{10,... | collective-permute-start | bytes 393224 | tf_op jit(solution)/shard_map/ppermute | solution.py:270
  88.2 2.3 %collective-permute-start.24 = (bf16[64,1024]{1,0:T(8,128)(2,1)S(1)}, bf16[64,1024]{1,0:T(8,128)(2,1)S(1)}, u32[]{:S(2)}, u32[]{:S(2)}) collective-permute-start(bf16[64,1024]{1,0:T(8,128)(2,1)S(1)} %mix.1.refs_0_), channel_id=1, source_target_pairs={{0,4},{1,5},{2,6},{3,7},{4,8},{5,9},{6,10},{7,11},{8,12},{9,13},{1... | collective-permute-start | bytes 393224 | tf_op jit(solution)/shard_map/ppermute | solution.py:270
  90.5 1.5 %collective-permute-start.27 = (bf16[64,1024]{1,0:T(8,128)(2,1)S(1)}, bf16[64,1024]{1,0:T(8,128)(2,1)S(1)}, u32[]{:S(2)}, u32[]{:S(2)}) collective-permute-start(bf16[64,1024]{1,0:T(8,128)(2,1)S(1)} %mix.1.refs_0_), channel_id=1, source_target_pairs={{0,12},{1,13},{2,14},{3,15},{4,0},{5,1},{6,2},{7,3},{8,4},{9,5},{1... | collective-permute-start | bytes 393224 | tf_op jit(solution)/shard_map/ppermute | solution.py:270
  92.0 0.5 collective-permute-start.26
  92.5 3.9 %collective-permute-done.24.refs_1_ = bf16[64,1024]{1,0:T(8,128)(2,1)S(1)} collective-permute-done((bf16[64,1024]{1,0:T(8,128)(2,1)S(1)}, bf16[64,1024]{1,0:T(8,128)(2,1)S(1)}, u32[]{:S(2)}, u32[]{:S(2)}) %collective-permute-start.24) | collective-permute-done | bytes 131104 | tf_op jit(solution)/shard_map/ppermute | solution.py:270
  96.4 0.4 collective-permute-done.27.refs_2_
  96.8 1.6 %collective-permute-start.29 = (bf16[64,1024]{1,0:T(8,128)(2,1)S(1)}, bf16[64,1024]{1,0:T(8,128)(2,1)S(1)}, u32[]{:S(2)}, u32[]{:S(2)}) collective-permute-start(bf16[64,1024]{1,0:T(8,128)(2,1)S(1)} %collective-permute-done.27.refs_2_), channel_id=1, source_target_pairs={{0,2},{1,3},{2,0},{3,1},{4,6},{5,7},{6,4},{7,5},{8,10},{9,11},{10,... | collective-permute-start | bytes 393224 | tf_op jit(solution)/shard_map/ppermute | solution.py:270
  98.4 0.6 output_near.1.refs_5_
  99.0 2.6 %collective-permute-done.26.refs_0_ = bf16[64,1024]{1,0:T(8,128)(2,1)S(1)} collective-permute-done((bf16[64,1024]{1,0:T(8,128)(2,1)S(1)}, bf16[64,1024]{1,0:T(8,128)(2,1)S(1)}, u32[]{:S(2)}, u32[]{:S(2)}) %collective-permute-start.26) | collective-permute-done | bytes 131104 | tf_op jit(solution)/shard_map/ppermute | solution.py:270
  101.7 0.3 collective-permute-start.28
  102.0 0.1 pad_add_fusion.scalars
  102.1 0.5 output_far.1.refs_6_
  102.6 0.7 collective-permute-done.29.refs_3_
  103.3 3.3 %collective-permute-done.28.refs_2_ = bf16[64,1024]{1,0:T(8,128)(2,1)S(1)} collective-permute-done((bf16[64,1024]{1,0:T(8,128)(2,1)S(1)}, bf16[64,1024]{1,0:T(8,128)(2,1)S(1)}, u32[]{:S(2)}, u32[]{:S(2)}) %collective-permute-start.28) | collective-permute-done | bytes 131104 | tf_op jit(solution)/shard_map/ppermute | solution.py:270
  106.6 1.3 %output_other.1 = (f32[128,1024]{1,0:T(8,128)S(1)}, bf16[128,1024]{1,0:T(8,128)(2,1)S(1)}) custom-call(s32[3]{0:T(128)S(1)} %pad_add_fusion.scalars, bf16[64,1024]{1,0:T(8,128)(2,1)S(1)} %collective-permute-done.23.refs_0_, bf16[64,1024]{1,0:T(8,128)(2,1)S(1)} %collective-permute-done.25.refs_1_, bf16[64,1024]{1,0:T(8,128)(2,1)S(1)} %collective-permute-done.28.refs_2_, ...), custom_call_target="tpu_custom_call" | custom-call | tf_op jit(solution)/shard_map/output_other/pallas_call | solution.py:209
  108.7 0.8 collective-permute-done.30
  109.6 0.8 add_convert_fusion
  (48 shorter events, 0.4 us)
Async XLA Ops:
  1.1 27.6 %collective-permute-start = (bf16[480,512]{1,0:T(8,128)(2,1)S(1)}, bf16[480,512]{1,0:T(8,128)(2,1)S(1)}, u32[]{:S(2)}, u32[]{:S(2)}) collective-permute-start(bf16[480,512]{1,0:T(8,128)(2,1)S(1)} %pad_maximum_fusion.refs_0_), channel_id=1, source_target_pairs={{0,4},{1,5},{2,6},{3,7},{4,8},{5,9},{6,10},{7,11},{8,12},{9,13},{1... | collective-permute-start | bytes 1474568 | tf_op jit(solution)/shard_map/ppermute | solution.py:270
  4.2 23.2 %collective-permute-start.1 = (bf16[480,512]{1,0:T(8,128)(2,1)S(1)}, bf16[480,512]{1,0:T(8,128)(2,1)S(1)}, u32[]{:S(2)}, u32[]{:S(2)}) collective-permute-start(bf16[480,512]{1,0:T(8,128)(2,1)S(1)} %pad_maximum_fusion.refs_0_), channel_id=1, source_target_pairs={{0,12},{1,13},{2,14},{3,15},{4,0},{5,1},{6,2},{7,3},{8,4},{9,5},{1... | collective-permute-start | bytes 1474568 | tf_op jit(solution)/shard_map/ppermute | solution.py:270
  6.4 2.1 %copy-start.1 = (bf16[256,7680]{1,0:T(8,128)(2,1)S(1)}, bf16[256,7680]{1,0:T(8,128)(2,1)}, u32[]{:S(2)}) copy-start(bf16[256,7680]{1,0:T(8,128)(2,1)} %rows_ref.3) | copy-start | bytes 11796484
  11.6 18.5 %collective-permute-start.4 = (bf16[128,1920]{1,0:T(8,128)(2,1)}, bf16[128,1920]{1,0:T(8,128)(2,1)S(1)}, u32[]{:S(2)}, u32[]{:S(2)}) collective-permute-start(bf16[128,1920]{1,0:T(8,128)(2,1)} %get-tuple-element.35), channel_id=1, source_target_pairs={{0,2},{1,3},{2,0},{3,1},{4,6},{5,7},{6,4},{7,5},{8,10},{9,11},{10,... | collective-permute-start | bytes 1474568 | tf_op jit(solution)/shard_map/ppermute | solution.py:270
  13.3 16.9 %collective-permute-start.5 = (bf16[128,1920]{1,0:T(8,128)(2,1)}, bf16[128,1920]{1,0:T(8,128)(2,1)S(1)}, u32[]{:S(2)}, u32[]{:S(2)}) collective-permute-start(bf16[128,1920]{1,0:T(8,128)(2,1)} %get-tuple-element.36), channel_id=1, source_target_pairs={{0,16},{1,17},{2,18},{3,19},{4,20},{5,21},{6,22},{7,23},{8,24},{9,... | collective-permute-start | bytes 1474568 | tf_op jit(solution)/shard_map/ppermute | solution.py:270
  14.8 21.5 %collective-permute-start.6 = (bf16[128,1920]{1,0:T(8,128)(2,1)}, bf16[128,1920]{1,0:T(8,128)(2,1)}, u32[]{:S(2)}, u32[]{:S(2)}) collective-permute-start(bf16[128,1920]{1,0:T(8,128)(2,1)} %get-tuple-element.37), channel_id=1, source_target_pairs={{0,18},{1,19},{2,16},{3,17},{4,22},{5,23},{6,20},{7,21},{8,26},{9,... | collective-permute-start | bytes 1474568 | tf_op jit(solution)/shard_map/ppermute | solution.py:270
  15.2 2.1 %copy-start.2 = (bf16[256,7680]{1,0:T(8,128)(2,1)S(1)}, bf16[256,7680]{1,0:T(8,128)(2,1)}, u32[]{:S(2)}) copy-start(bf16[256,7680]{1,0:T(8,128)(2,1)} %rows_ref.3) | copy-start | bytes 11796484
  17.3 2.1 %copy-start.3 = (bf16[256,7680]{1,0:T(8,128)(2,1)S(1)}, bf16[256,7680]{1,0:T(8,128)(2,1)}, u32[]{:S(2)}) copy-start(bf16[256,7680]{1,0:T(8,128)(2,1)} %rows_ref.3) | copy-start | bytes 11796484
  27.4 14.6 %collective-permute-start.2 = (bf16[480,512]{1,0:T(8,128)(2,1)S(1)}, bf16[480,512]{1,0:T(8,128)(2,1)}, u32[]{:S(2)}, u32[]{:S(2)}) collective-permute-start(bf16[480,512]{1,0:T(8,128)(2,1)S(1)} %collective-permute-done.1.refs_2_), channel_id=1, source_target_pairs={{4,0},{5,1},{6,2},{7,3},{8,4},{9,5},{10,6},{11,7},{20,16},{21,17},... | collective-permute-start | bytes 1474568 | tf_op jit(solution)/shard_map/ppermute | solution.py:270
  28.7 13.3 %collective-permute-start.3 = (bf16[480,512]{1,0:T(8,128)(2,1)S(1)}, bf16[480,512]{1,0:T(8,128)(2,1)}, u32[]{:S(2)}, u32[]{:S(2)}) collective-permute-start(bf16[480,512]{1,0:T(8,128)(2,1)S(1)} %collective-permute-done.refs_1_), channel_id=1, source_target_pairs={{4,8},{5,9},{6,10},{7,11},{8,12},{9,13},{10,14},{11,15},{20,24},{2... | collective-permute-start | bytes 1474568 | tf_op jit(solution)/shard_map/ppermute | solution.py:270
  36.4 5.7 %collective-permute-start.7 = (bf16[128,1920]{1,0:T(8,128)(2,1)S(1)}, bf16[128,1920]{1,0:T(8,128)(2,1)}, u32[]{:S(2)}, u32[]{:S(2)}) collective-permute-start(bf16[128,1920]{1,0:T(8,128)(2,1)S(1)} %collective-permute-done.4.refs_6_), channel_id=1, source_target_pairs={{0,1},{1,0},{2,3},{3,2},{4,5},{5,4},{6,7},{7,6},{8,9},{9,8},{10,11... | collective-permute-start | bytes 1474568 | tf_op jit(solution)/shard_map/ppermute | solution.py:270
  36.4 5.7 %collective-permute-start.8 = (bf16[128,1920]{1,0:T(8,128)(2,1)S(1)}, bf16[128,1920]{1,0:T(8,128)(2,1)}, u32[]{:S(2)}, u32[]{:S(2)}) collective-permute-start(bf16[128,1920]{1,0:T(8,128)(2,1)S(1)} %collective-permute-done.5.refs_7_), channel_id=1, source_target_pairs={{0,1},{1,0},{2,3},{3,2},{4,5},{5,4},{6,7},{7,6},{8,9},{9,8},{10,11... | collective-permute-start | bytes 1474568 | tf_op jit(solution)/shard_map/ppermute | solution.py:270
  36.9 5.2 %collective-permute-start.9 = (bf16[128,1920]{1,0:T(8,128)(2,1)}, bf16[128,1920]{1,0:T(8,128)(2,1)}, u32[]{:S(2)}, u32[]{:S(2)}) collective-permute-start(bf16[128,1920]{1,0:T(8,128)(2,1)} %collective-permute-done.6.refs_8_), channel_id=1, source_target_pairs={{0,1},{1,0},{2,3},{3,2},{4,5},{5,4},{6,7},{7,6},{8,9},{9,8},{10,11... | collective-permute-start | bytes 1474568 | tf_op jit(solution)/shard_map/ppermute | solution.py:270
  45.2 11.2 %collective-permute-start.12 = (bf16[512,128]{1,0:T(8,128)(2,1)S(1)}, bf16[512,128]{1,0:T(8,128)(2,1)S(1)}, u32[]{:S(2)}, u32[]{:S(2)}) collective-permute-start(bf16[512,128]{1,0:T(8,128)(2,1)S(1)} %get-tuple-element.48), channel_id=1, source_target_pairs={{0,18},{1,19},{2,16},{3,17},{4,22},{5,23},{6,20},{7,21},{8,26},{9,... | collective-permute-start | bytes 393224 | tf_op jit(solution)/shard_map/ppermute | solution.py:270
  47.7 9.2 %collective-permute-start.11 = (bf16[512,128]{1,0:T(8,128)(2,1)S(1)}, bf16[512,128]{1,0:T(8,128)(2,1)S(1)}, u32[]{:S(2)}, u32[]{:S(2)}) collective-permute-start(bf16[512,128]{1,0:T(8,128)(2,1)S(1)} %get-tuple-element.47), channel_id=1, source_target_pairs={{0,16},{1,17},{2,18},{3,19},{4,20},{5,21},{6,22},{7,23},{8,24},{9,... | collective-permute-start | bytes 393224 | tf_op jit(solution)/shard_map/ppermute | solution.py:270
  48.2 8.7 %collective-permute-start.10 = (bf16[512,128]{1,0:T(8,128)(2,1)S(1)}, bf16[512,128]{1,0:T(8,128)(2,1)S(1)}, u32[]{:S(2)}, u32[]{:S(2)}) collective-permute-start(bf16[512,128]{1,0:T(8,128)(2,1)S(1)} %get-tuple-element.46), channel_id=1, source_target_pairs={{0,2},{1,3},{2,0},{3,1},{4,6},{5,7},{6,4},{7,5},{8,10},{9,11},{10,... | collective-permute-start | bytes 393224 | tf_op jit(solution)/shard_map/ppermute | solution.py:270
  48.8 21.6 %copy-start.6 = (f32[128]{0:T(128)S(1)}, f32[128]{0:T(128)}, u32[]{:S(2)}) copy-start(f32[128]{0:T(128)} %param.16) | copy-start | bytes 1540
  48.8 28.6 %copy-start.7 = (f32[128]{0:T(128)S(1)}, f32[128]{0:T(128)}, u32[]{:S(2)}) copy-start(f32[128]{0:T(128)} %param.15) | copy-start | bytes 1540
  52.7 0.7 copy-start.4
  53.4 14.3 %collective-permute-start.17 = (f32[512,128]{1,0:T(8,128)}, f32[512,128]{1,0:T(8,128)S(1)}, u32[]{:S(2)}, u32[]{:S(2)}) collective-permute-start(f32[512,128]{1,0:T(8,128)} %get-tuple-element.56), channel_id=1, source_target_pairs={{0,18},{1,19},{2,16},{3,17},{4,22},{5,23},{6,20},{7,21},{8,26},{9,... | collective-permute-start | bytes 786440 | tf_op jit(solution)/shard_map/ppermute | solution.py:270
  55.9 13.4 %collective-permute-start.16 = (f32[512,128]{1,0:T(8,128)}, f32[512,128]{1,0:T(8,128)S(1)}, u32[]{:S(2)}, u32[]{:S(2)}) collective-permute-start(f32[512,128]{1,0:T(8,128)} %get-tuple-element.54), channel_id=1, source_target_pairs={{0,16},{1,17},{2,18},{3,19},{4,20},{5,21},{6,22},{7,23},{8,24},{9,... | collective-permute-start | bytes 786440 | tf_op jit(solution)/shard_map/ppermute | solution.py:270
  56.4 12.9 %collective-permute-start.15 = (f32[512,128]{1,0:T(8,128)}, f32[512,128]{1,0:T(8,128)S(1)}, u32[]{:S(2)}, u32[]{:S(2)}) collective-permute-start(f32[512,128]{1,0:T(8,128)} %get-tuple-element.52), channel_id=1, source_target_pairs={{0,2},{1,3},{2,0},{3,1},{4,6},{5,7},{6,4},{7,5},{8,10},{9,11},{10,... | collective-permute-start | bytes 786440 | tf_op jit(solution)/shard_map/ppermute | solution.py:270
  57.0 9.5 %collective-permute-start.13 = (bf16[512,128]{1,0:T(8,128)(2,1)S(1)}, bf16[512,128]{1,0:T(8,128)(2,1)S(1)}, u32[]{:S(2)}, u32[]{:S(2)}) collective-permute-start(bf16[512,128]{1,0:T(8,128)(2,1)S(1)} %add_convert_fusion.1.refs_0_), channel_id=1, source_target_pairs={{0,4},{1,5},{2,6},{3,7},{4,8},{5,9},{6,10},{7,11},{8,12},{9,13},{1... | collective-permute-start | bytes 393224 | tf_op jit(solution)/shard_map/ppermute | solution.py:270
  60.6 37.8 %copy-start = (bf16[2048,1024]{1,0:T(8,128)(2,1)S(1)}, bf16[2048,1024]{1,0:T(8,128)(2,1)}, u32[]{:S(2)}) copy-start(bf16[2048,1024]{1,0:T(8,128)(2,1)} %refs_4_.1) | copy-start | bytes 12582916
  61.7 23.9 %collective-permute-start.21 = (bf16[512,128]{1,0:T(8,128)(2,1)S(1)}, bf16[512,128]{1,0:T(8,128)(2,1)S(1)}, u32[]{:S(2)}, u32[]{:S(2)}) collective-permute-start(bf16[512,128]{1,0:T(8,128)(2,1)S(1)} %add_convert_fusion.1.refs_0_), channel_id=1, source_target_pairs={{0,8},{1,9},{2,10},{3,11},{4,12},{5,13},{6,14},{7,15},{8,0},{9,1},... | collective-permute-start | bytes 393224 | tf_op jit(solution)/shard_map/ppermute | solution.py:270
  66.5 19.0 %collective-permute-start.22 = (bf16[512,128]{1,0:T(8,128)(2,1)S(1)}, bf16[512,128]{1,0:T(8,128)(2,1)S(1)}, u32[]{:S(2)}, u32[]{:S(2)}) collective-permute-start(bf16[512,128]{1,0:T(8,128)(2,1)S(1)} %add_convert_fusion.1.refs_0_), channel_id=1, source_target_pairs={{0,12},{1,13},{2,14},{3,15},{4,0},{5,1},{6,2},{7,3},{8,4},{9,5},{1... | collective-permute-start | bytes 393224 | tf_op jit(solution)/shard_map/ppermute | solution.py:270
  67.8 8.2 %collective-permute-start.14 = (bf16[32,1024]{1,0:T(8,128)(2,1)S(1)}, bf16[32,1024]{1,0:T(8,128)(2,1)S(1)}, u32[]{:S(2)}, u32[]{:S(2)}) collective-permute-start(bf16[32,1024]{1,0:T(8,128)(2,1)S(1)} %get-tuple-element.49), channel_id=1, source_target_pairs={{0,2},{1,3},{2,0},{3,1},{4,6},{5,7},{6,4},{7,5},{8,10},{9,11},{10,... | collective-permute-start | bytes 196616 | tf_op jit(solution)/shard_map/ppermute | solution.py:270
  70.5 9.3 %collective-permute-start.18 = (bf16[512,128]{1,0:T(8,128)(2,1)S(1)}, bf16[512,128]{1,0:T(8,128)(2,1)S(1)}, u32[]{:S(2)}, u32[]{:S(2)}) collective-permute-start(bf16[512,128]{1,0:T(8,128)(2,1)S(1)} %multiply_convert_fusion.refs_0_), channel_id=1, source_target_pairs={{0,4},{1,5},{2,6},{3,7},{4,8},{5,9},{6,10},{7,11},{8,12},{9,13},{1... | collective-permute-start | bytes 393224 | tf_op jit(solution)/shard_map/ppermute | solution.py:270
  72.1 11.4 %collective-permute-start.19 = (bf16[512,128]{1,0:T(8,128)(2,1)S(1)}, bf16[512,128]{1,0:T(8,128)(2,1)S(1)}, u32[]{:S(2)}, u32[]{:S(2)}) collective-permute-start(bf16[512,128]{1,0:T(8,128)(2,1)S(1)} %multiply_convert_fusion.refs_0_), channel_id=1, source_target_pairs={{0,8},{1,9},{2,10},{3,11},{4,12},{5,13},{6,14},{7,15},{8,0},{9,1},... | collective-permute-start | bytes 393224 | tf_op jit(solution)/shard_map/ppermute | solution.py:270
  76.0 7.5 %collective-permute-start.20 = (bf16[512,128]{1,0:T(8,128)(2,1)S(1)}, bf16[512,128]{1,0:T(8,128)(2,1)S(1)}, u32[]{:S(2)}, u32[]{:S(2)}) collective-permute-start(bf16[512,128]{1,0:T(8,128)(2,1)S(1)} %multiply_convert_fusion.refs_0_), channel_id=1, source_target_pairs={{0,12},{1,13},{2,14},{3,15},{4,0},{5,1},{6,2},{7,3},{8,4},{9,5},{1... | collective-permute-start | bytes 393224 | tf_op jit(solution)/shard_map/ppermute | solution.py:270
  86.3 6.3 %collective-permute-start.23 = (bf16[64,1024]{1,0:T(8,128)(2,1)S(1)}, bf16[64,1024]{1,0:T(8,128)(2,1)S(1)}, u32[]{:S(2)}, u32[]{:S(2)}) collective-permute-start(bf16[64,1024]{1,0:T(8,128)(2,1)S(1)} %mix.1.refs_0_), channel_id=1, source_target_pairs={{0,2},{1,3},{2,0},{3,1},{4,6},{5,7},{6,4},{7,5},{8,10},{9,11},{10,... | collective-permute-start | bytes 393224 | tf_op jit(solution)/shard_map/ppermute | solution.py:270
  88.2 8.2 %collective-permute-start.24 = (bf16[64,1024]{1,0:T(8,128)(2,1)S(1)}, bf16[64,1024]{1,0:T(8,128)(2,1)S(1)}, u32[]{:S(2)}, u32[]{:S(2)}) collective-permute-start(bf16[64,1024]{1,0:T(8,128)(2,1)S(1)} %mix.1.refs_0_), channel_id=1, source_target_pairs={{0,4},{1,5},{2,6},{3,7},{4,8},{5,9},{6,10},{7,11},{8,12},{9,13},{1... | collective-permute-start | bytes 393224 | tf_op jit(solution)/shard_map/ppermute | solution.py:270
  90.5 6.4 %collective-permute-start.27 = (bf16[64,1024]{1,0:T(8,128)(2,1)S(1)}, bf16[64,1024]{1,0:T(8,128)(2,1)S(1)}, u32[]{:S(2)}, u32[]{:S(2)}) collective-permute-start(bf16[64,1024]{1,0:T(8,128)(2,1)S(1)} %mix.1.refs_0_), channel_id=1, source_target_pairs={{0,12},{1,13},{2,14},{3,15},{4,0},{5,1},{6,2},{7,3},{8,4},{9,5},{1... | collective-permute-start | bytes 393224 | tf_op jit(solution)/shard_map/ppermute | solution.py:270
  92.0 9.7 %collective-permute-start.26 = (bf16[64,1024]{1,0:T(8,128)(2,1)S(1)}, bf16[64,1024]{1,0:T(8,128)(2,1)S(1)}, u32[]{:S(2)}, u32[]{:S(2)}) collective-permute-start(bf16[64,1024]{1,0:T(8,128)(2,1)S(1)} %mix.1.refs_0_), channel_id=1, source_target_pairs={{0,8},{1,9},{2,10},{3,11},{4,12},{5,13},{6,14},{7,15},{8,0},{9,1},... | collective-permute-start | bytes 393224 | tf_op jit(solution)/shard_map/ppermute | solution.py:270
  96.4 5.3 %collective-permute-start.25 = (bf16[64,1024]{1,0:T(8,128)(2,1)S(1)}, bf16[64,1024]{1,0:T(8,128)(2,1)S(1)}, u32[]{:S(2)}, u32[]{:S(2)}) collective-permute-start(bf16[64,1024]{1,0:T(8,128)(2,1)S(1)} %collective-permute-done.24.refs_1_), channel_id=1, source_target_pairs={{0,2},{1,3},{2,0},{3,1},{4,6},{5,7},{6,4},{7,5},{8,10},{9,11},{10,... | collective-permute-start | bytes 393224 | tf_op jit(solution)/shard_map/ppermute | solution.py:270
  96.8 6.5 %collective-permute-start.29 = (bf16[64,1024]{1,0:T(8,128)(2,1)S(1)}, bf16[64,1024]{1,0:T(8,128)(2,1)S(1)}, u32[]{:S(2)}, u32[]{:S(2)}) collective-permute-start(bf16[64,1024]{1,0:T(8,128)(2,1)S(1)} %collective-permute-done.27.refs_2_), channel_id=1, source_target_pairs={{0,2},{1,3},{2,0},{3,1},{4,6},{5,7},{6,4},{7,5},{8,10},{9,11},{10,... | collective-permute-start | bytes 393224 | tf_op jit(solution)/shard_map/ppermute | solution.py:270
  101.7 5.0 %collective-permute-start.28 = (bf16[64,1024]{1,0:T(8,128)(2,1)S(1)}, bf16[64,1024]{1,0:T(8,128)(2,1)S(1)}, u32[]{:S(2)}, u32[]{:S(2)}) collective-permute-start(bf16[64,1024]{1,0:T(8,128)(2,1)S(1)} %collective-permute-done.26.refs_0_), channel_id=1, source_target_pairs={{0,2},{1,3},{2,0},{3,1},{4,6},{5,7},{6,4},{7,5},{8,10},{9,11},{10,... | collective-permute-start | bytes 393224 | tf_op jit(solution)/shard_map/ppermute | solution.py:270
  102.6 7.0 %copy-start.5 = (bf16[128,1024]{1,0:T(8,128)(2,1)S(1)}, bf16[128,1024]{1,0:T(8,128)(2,1)}, u32[]{:S(2)}) copy-start(bf16[128,1024]{1,0:T(8,128)(2,1)} %param.14) | copy-start | bytes 786436
  108.0 1.6 %collective-permute-start.30 = (bf16[128,1024]{1,0:T(8,128)(2,1)S(1)}, bf16[128,1024]{1,0:T(8,128)(2,1)S(1)}, u32[]{:S(2)}, u32[]{:S(2)}) collective-permute-start(bf16[128,1024]{1,0:T(8,128)(2,1)S(1)} %get-tuple-element.64), channel_id=1, source_target_pairs={{0,1},{1,0},{2,3},{3,2},{4,5},{5,4},{6,7},{7,6},{8,9},{9,8},{10,11... | collective-permute-start | bytes 786440 | tf_op jit(solution)/shard_map/ppermute | solution.py:270

commit v8 on v7

--- a/solution.py
+++ b/solution.py
@@ -49,56 +49,57 @@
     )(scalars, vision)
 
 
-def project_kernel(groups, pairs, shifts, matrix, scalars, *refs):
+def project_kernel(groups, pairs, shifts, scalars, *refs):
     count = groups * 2
-    slabs, near, far = refs[: -3 * count - 1], refs[-3 * count - 1 : -2 * count - 1], refs[-2 * count - 1 : -count - 1]
-    outs, placed = refs[-count - 1 : -1], refs[-1]
-    width = 2 * HEAD_SIZE
-    columns = slice(matrix * width, (matrix + 1) * width)
+    near, far, slabs = refs[:count], refs[count : 2 * count], refs[2 * count : -2 * count - 1]
+    outs, placed = refs[-2 * count - 1 : -1], refs[-1]
     half = near[0].shape[0]
     side, place = scalars[0], scalars[1]
     for shift, slab in zip(shifts, slabs):
         if isinstance(shift, tuple):
             continue
-        placed[lax.rem(place + pairs - shift, pairs)] = slab[:, columns]
+        placed[lax.rem(place + pairs - shift, pairs)] = slab[...]
     for shift, slab in zip(shifts, slabs):
         if isinstance(shift, tuple):
 
             @pl.when(place >= pairs // 2)
             def _():
-                placed[lax.rem(place + pairs - shift[0], pairs)] = slab[:, columns]
+                placed[lax.rem(place + pairs - shift[0], pairs)] = slab[...]
 
     w = jnp.concatenate([placed[z] for z in range(pairs)], axis=0)
     for part, pieces in enumerate((near, far)):
         lhs = jnp.concatenate([ref[...] for ref in pieces], axis=0)
         result = jnp.dot(lhs, w, preferred_element_type=f32)
-        first, second = result[:, :HEAD_SIZE], result[:, HEAD_SIZE:]
-        heads = jnp.where(side == 0, first, second), jnp.where(side == 0, second, first)
-        for source in range(count):
-            by_group, by_side = source // 2, source % 2
-            for to in range(2):
-                out = outs[(-by_group) % groups * 2 + to]
-                start = (0 if by_side == to else 2 * half) + part * half
-                out[start : start + half, :] = heads[to][
-                    source * half : (source + 1) * half, :
-                ].astype(out.dtype)
-
-
-def project(near, far, shifts, slabs, side, place, pairs, matrix, dtype, name):
+        columns = [result[:, n * HEAD_SIZE : (n + 1) * HEAD_SIZE] for n in range(4)]
+        for matrix in range(2):
+            first, second = columns[2 * matrix : 2 * matrix + 2]
+            heads = jnp.where(side == 0, first, second), jnp.where(side == 0, second, first)
+            for source in range(count):
+                by_group, by_side = source // 2, source % 2
+                for to in range(2):
+                    out = outs[matrix * count + (-by_group) % groups * 2 + to]
+                    start = (0 if by_side == to else 2 * half) + part * half
+                    out[start : start + half, :] = heads[to][
+                        source * half : (source + 1) * half, :
+                    ].astype(out.dtype)
+
+
+def project(near, far, shifts, slabs, side, place, pairs):
     count = len(near)
     half = near[0].shape[0]
     vmem = pl.BlockSpec(memory_space=pltpu.VMEM)
     return pl.pallas_call(
-        functools.partial(project_kernel, count // 2, pairs, shifts, matrix),
+        functools.partial(project_kernel, count // 2, pairs, shifts),
         in_specs=[pl.BlockSpec(memory_space=pltpu.SMEM)] + [vmem] * (2 * count + len(slabs)),
-        out_specs=[vmem] * count,
+        out_specs=[vmem] * (2 * count),
         out_shape=[
-            jax.ShapeDtypeStruct((4 * half, HEAD_SIZE), dtype if k else f32) for k in range(count)
+            jax.ShapeDtypeStruct((4 * half, HEAD_SIZE), bf16 if k > count else f32)
+            for k in range(2 * count)
         ],
-        scratch_shapes=[pltpu.VMEM((pairs, slabs[0].shape[0], 2 * HEAD_SIZE), bf16)],
-        compiler_params=pltpu.CompilerParams(vmem_limit_bytes=VMEM_BYTES),
-        name=name,
-    )(jnp.stack([side, place]).astype(jnp.int32), *slabs, *near, *far)
+        scratch_shapes=[pltpu.VMEM((pairs,) + slabs[0].shape, bf16)],
+        compiler_params=pltpu.CompilerParams(vmem_limit_bytes=VMEM_BYTES),
+        name="project",
+    )(jnp.stack([side, place]).astype(jnp.int32), *near, *far, *slabs)
 
 
 def score_kernel(heads, q_ref, *refs):
@@ -341,10 +342,9 @@
         return functools.reduce(lambda a, b: a + b.astype(f32), pieces, own)
 
     slabs = line_slabs(slab, slab_near, slab_far)
-    value_pieces = project(near, far, shifts, slabs, side, place, pairs, 1, bf16, "project_values")
+    pieces = project(near, far, shifts, slabs, side, place, pairs)
+    key_pieces, value_pieces = pieces[: len(offsets)], pieces[len(offsets) :]
     value_parts = scatter(value_pieces)
-    slabs[0] = after(slabs[0], *value_pieces)
-    key_pieces = project(near, far, shifts, slabs, side, place, pairs, 0, f32, "project_keys")
     key_parts = scatter(key_pieces)
     values = sum_up(value_pieces[0], value_parts).astype(bf16)
     all_values = all_pairs(values)

time: 112 us -> 107 us (0.955)
  waiting for transfers between devices: 38.4 us -> 36 us
  Pallas kernels: 17.5 us -> 15.5 us
    ppermute x31, waiting for transfers between devices: 38.4 us -> 36 us  [permute(): return lax.ppermute(array, AXES, perm)]
    pallas_call x2 -> x1, Pallas kernels: 7.07 us -> 5.07 us  [project(): pl.pallas_call(functools.partial(project_kernel, count // 2, pairs, shift...]
  transfers between devices with their start and end apart: 31 -> 31, of which waited for: 12 -> 12; matrix products, arithmetic and copies ran while one was open for 3% -> 3% of each run, Pallas kernels for 11% -> 8%
where the time goes in v8:
time: 107 us; the launch traced here: 106 us
  starting transfers between devices  43 us (40%)
  waiting for transfers between devices  36 us (34%)
  Pallas kernels  15.5 us (14%)
  local copies, waits for them, and re-layouts  8.21 us (8%)
  other arithmetic  2.76 us (3%)
    ppermute x31, starting transfers between devices, permute(): return lax.ppermute(array, AXES, perm)  43 us
    ppermute x31, waiting for transfers between devices, permute(): return lax.ppermute(array, AXES, perm)  36 us
    unnamed x23, local copies, waits for them, and re-layouts  6.07 us
    pallas_call x3, Pallas kernels, pack(): pl.pallas_call(functools.partial(pack_kernel, groups, pairs, part, count)...  5.32 us
    pallas_call x1, Pallas kernels, project(): pl.pallas_call(functools.partial(project_kernel, count // 2, pairs, shift...  5.07 us
  transfers between devices with their start and end apart: 31, of which 12 were waited for; matrix products, arithmetic and copies ran while one was open for 3% of the time, Pallas kernels for 8%

profile of v8, /device:TPU:0, one launch (start us, length us, event | category | flops | bytes accessed | tf_op | source)
XLA Modules:
  0.0 106.4 jit_solution(5452065565299412862)
XLA Ops:
  0.0 1.1 %constant_dynamic-slice_fusion = (bf16[480,256]{1,0:T(8,128)(2,1)S(1)}, bf16[480,256]{1,0:T(8,128)(2,1)S(1)}) fusion(bf16[960,256]{1,0:T(8,128)(2,1)} %param.12, s32[]{:T(128)S(6)} %select_n.62, bf16[960,256]{1,0:T(8,128)(2,1)} %param.11), kind=kLoop, calls=%fused_computation.22 | loop fusion | bytes 983044 | tf_op jit(solution)/shard_map/dynamic_slice | solution.py:314
  1.1 5.1 %collective-permute-start.7 = (bf16[480,512]{1,0:T(8,128)(2,1)S(1)}, bf16[480,512]{1,0:T(8,128)(2,1)S(1)}, u32[]{:S(2)}, u32[]{:S(2)}) collective-permute-start(bf16[480,512]{1,0:T(8,128)(2,1)S(1)} %pad_maximum_fusion.refs_8_), channel_id=1, source_target_pairs={{0,12},{1,13},{2,14},{3,15},{4,0},{5,1},{6,2},{7,3},{8,4},{9,5},{1... | collective-permute-start | bytes 1474568 | tf_op jit(solution)/shard_map/ppermute | solution.py:271
  6.2 0.1 pad_add_fusion.2.index_ref
  6.3 2.1 %copy-done.1 = bf16[256,7680]{1,0:T(8,128)(2,1)S(1)} copy-done((bf16[256,7680]{1,0:T(8,128)(2,1)S(1)}, bf16[256,7680]{1,0:T(8,128)(2,1)}, u32[]{:S(2)}) %copy-start.1) | copy-done | bytes 3932184
  8.4 3.2 %pack_sends.1 = (bf16[128,1920]{1,0:T(8,128)(2,1)}, bf16[128,1920]{1,0:T(8,128)(2,1)}, bf16[128,1920]{1,0:T(8,128)(2,1)}) custom-call(s32[4]{0:T(128)S(1)} %pad_add_fusion.2.index_ref, bf16[256,7680]{1,0:T(8,128)(2,1)S(1)} %copy-done.1), custom_call_target="tpu_custom_call" | custom-call | tf_op jit(solution)/shard_map/pack_sends/pallas_call | solution.py:38
  11.6 2.5 %collective-permute-start.2 = (bf16[128,1920]{1,0:T(8,128)(2,1)}, bf16[128,1920]{1,0:T(8,128)(2,1)S(1)}, u32[]{:S(2)}, u32[]{:S(2)}) collective-permute-start(bf16[128,1920]{1,0:T(8,128)(2,1)} %get-tuple-element.36), channel_id=1, source_target_pairs={{0,18},{1,19},{2,16},{3,17},{4,22},{5,23},{6,20},{7,21},{8,26},{9,... | collective-permute-start | bytes 1474568 | tf_op jit(solution)/shard_map/ppermute | solution.py:271
  14.1 0.5 collective-permute-start.1
  14.6 0.5 collective-permute-start
  15.1 0.1 pad_add_fusion.1
  15.2 2.1 %copy-done.2 = bf16[256,7680]{1,0:T(8,128)(2,1)S(1)} copy-done((bf16[256,7680]{1,0:T(8,128)(2,1)S(1)}, bf16[256,7680]{1,0:T(8,128)(2,1)}, u32[]{:S(2)}) %copy-start.2) | copy-done | bytes 3932184
  17.3 1.1 %pack_near.1.refs_0_ = bf16[128,1920]{1,0:T(8,128)(2,1)S(1)} custom-call(s32[2]{0:T(128)S(1)} %get-tuple-element.68.index_ref, bf16[256,7680]{1,0:T(8,128)(2,1)S(1)} %copy-done.2), custom_call_target="tpu_custom_call" | custom-call | tf_op jit(solution)/shard_map/pack_near/pallas_call | solution.py:38
  18.4 1.0 copy-done.3
  19.4 1.1 %pack_far.1.refs_4_ = bf16[128,1920]{1,0:T(8,128)(2,1)S(1)} custom-call(s32[2]{0:T(128)S(1)} %get-tuple-element.67.index_ref, bf16[256,7680]{1,0:T(8,128)(2,1)S(1)} %copy-done.3), custom_call_target="tpu_custom_call" | custom-call | tf_op jit(solution)/shard_map/pack_far/pallas_call | solution.py:38
  20.5 1.3 %collective-permute-start.8 = (bf16[480,512]{1,0:T(8,128)(2,1)S(1)}, bf16[480,512]{1,0:T(8,128)(2,1)}, u32[]{:S(2)}, u32[]{:S(2)}) collective-permute-start(bf16[480,512]{1,0:T(8,128)(2,1)S(1)} %collective-permute-done.7.refs_10_), channel_id=1, source_target_pairs={{4,0},{5,1},{6,2},{7,3},{8,4},{9,5},{10,6},{11,7},{20,16},{21,17},... | collective-permute-start | bytes 1474568 | tf_op jit(solution)/shard_map/ppermute | solution.py:271
  21.8 6.5 %collective-permute-done.6.refs_9_ = bf16[480,512]{1,0:T(8,128)(2,1)S(1)} collective-permute-done((bf16[480,512]{1,0:T(8,128)(2,1)S(1)}, bf16[480,512]{1,0:T(8,128)(2,1)S(1)}, u32[]{:S(2)}, u32[]{:S(2)}) %collective-permute-start.6) | collective-permute-done | bytes 491552 | tf_op jit(solution)/shard_map/ppermute | solution.py:271
  28.3 1.4 %collective-permute-start.9 = (bf16[480,512]{1,0:T(8,128)(2,1)S(1)}, bf16[480,512]{1,0:T(8,128)(2,1)}, u32[]{:S(2)}, u32[]{:S(2)}) collective-permute-start(bf16[480,512]{1,0:T(8,128)(2,1)S(1)} %collective-permute-done.6.refs_9_), channel_id=1, source_target_pairs={{4,8},{5,9},{6,10},{7,11},{8,12},{9,13},{10,14},{11,15},{20,24},{2... | collective-permute-start | bytes 1474568 | tf_op jit(solution)/shard_map/ppermute | solution.py:271
  29.8 6.3 %collective-permute-done.1.refs_2_ = bf16[128,1920]{1,0:T(8,128)(2,1)S(1)} collective-permute-done((bf16[128,1920]{1,0:T(8,128)(2,1)}, bf16[128,1920]{1,0:T(8,128)(2,1)S(1)}, u32[]{:S(2)}, u32[]{:S(2)}) %collective-permute-start.1) | collective-permute-done | bytes 491552 | tf_op jit(solution)/shard_map/ppermute | solution.py:271
  36.0 0.5 collective-permute-start.3
  36.6 0.1 pad_add_fusion.3.scalars
  36.6 2.2 %collective-permute-done.8.refs_11_ = bf16[480,512]{1,0:T(8,128)(2,1)} collective-permute-done((bf16[480,512]{1,0:T(8,128)(2,1)S(1)}, bf16[480,512]{1,0:T(8,128)(2,1)}, u32[]{:S(2)}, u32[]{:S(2)}) %collective-permute-start.8) | collective-permute-done | bytes 491552 | tf_op jit(solution)/shard_map/ppermute | solution.py:271
  38.9 0.1 collective-permute-done.3.refs_5_
  39.0 5.1 %project.1 = (f32[512,128]{1,0:T(8,128)S(1)}, f32[512,128]{1,0:T(8,128)}, f32[512,128]{1,0:T(8,128)}, f32[512,128]{1,0:T(8,128)}, f32[512,128]{1,0:T(8,128)S(1)}...) custom-call(s32[2]{0:T(128)S(1)} %pad_add_fusion.3.scalars, ...), custom_call_target="tpu_custom_call" | custom-call | tf_op jit(solution)/shard_map/project/pallas_call | solution.py:91
  44.0 0.7 copy-done.4
  44.7 1.5 %collective-permute-start.10 = (bf16[512,128]{1,0:T(8,128)(2,1)S(1)}, bf16[512,128]{1,0:T(8,128)(2,1)S(1)}, u32[]{:S(2)}, u32[]{:S(2)}) collective-permute-start(bf16[512,128]{1,0:T(8,128)(2,1)S(1)} %get-tuple-element.45), channel_id=1, source_target_pairs={{0,2},{1,3},{2,0},{3,1},{4,6},{5,7},{6,4},{7,5},{8,10},{9,11},{10,... | collective-permute-start | bytes 393224 | tf_op jit(solution)/shard_map/ppermute | solution.py:271
  46.2 1.5 %collective-permute-start.11 = (bf16[512,128]{1,0:T(8,128)(2,1)S(1)}, bf16[512,128]{1,0:T(8,128)(2,1)S(1)}, u32[]{:S(2)}, u32[]{:S(2)}) collective-permute-start(bf16[512,128]{1,0:T(8,128)(2,1)S(1)} %get-tuple-element.46), channel_id=1, source_target_pairs={{0,16},{1,17},{2,18},{3,19},{4,20},{5,21},{6,22},{7,23},{8,24},{9,... | collective-permute-start | bytes 393224 | tf_op jit(solution)/shard_map/ppermute | solution.py:271
  47.7 0.5 collective-permute-start.12
  48.2 1.5 %collective-permute-start.15 = (f32[512,128]{1,0:T(8,128)}, f32[512,128]{1,0:T(8,128)S(1)}, u32[]{:S(2)}, u32[]{:S(2)}) collective-permute-start(f32[512,128]{1,0:T(8,128)} %get-tuple-element.50), channel_id=1, source_target_pairs={{0,2},{1,3},{2,0},{3,1},{4,6},{5,7},{6,4},{7,5},{8,10},{9,11},{10,... | collective-permute-start | bytes 786440 | tf_op jit(solution)/shard_map/ppermute | solution.py:271
  49.7 1.5 %collective-permute-start.16 = (f32[512,128]{1,0:T(8,128)}, f32[512,128]{1,0:T(8,128)S(1)}, u32[]{:S(2)}, u32[]{:S(2)}) collective-permute-start(f32[512,128]{1,0:T(8,128)} %get-tuple-element.52), channel_id=1, source_target_pairs={{0,16},{1,17},{2,18},{3,19},{4,20},{5,21},{6,22},{7,23},{8,24},{9,... | collective-permute-start | bytes 786440 | tf_op jit(solution)/shard_map/ppermute | solution.py:271
  51.2 1.4 %collective-permute-start.17 = (f32[512,128]{1,0:T(8,128)}, f32[512,128]{1,0:T(8,128)S(1)}, u32[]{:S(2)}, u32[]{:S(2)}) collective-permute-start(f32[512,128]{1,0:T(8,128)} %get-tuple-element.54), channel_id=1, source_target_pairs={{0,18},{1,19},{2,16},{3,17},{4,22},{5,23},{6,20},{7,21},{8,26},{9,... | collective-permute-start | bytes 786440 | tf_op jit(solution)/shard_map/ppermute | solution.py:271
  52.6 2.4 %collective-permute-done.12 = bf16[512,128]{1,0:T(8,128)(2,1)S(1)} collective-permute-done((bf16[512,128]{1,0:T(8,128)(2,1)S(1)}, bf16[512,128]{1,0:T(8,128)(2,1)S(1)}, u32[]{:S(2)}, u32[]{:S(2)}) %collective-permute-start.12) | collective-permute-done | bytes 131104 | tf_op jit(solution)/shard_map/ppermute | solution.py:271
  55.1 0.1 add_convert_fusion.1.refs_0_
  55.1 2.5 %collective-permute-start.13 = (bf16[512,128]{1,0:T(8,128)(2,1)S(1)}, bf16[512,128]{1,0:T(8,128)(2,1)S(1)}, u32[]{:S(2)}, u32[]{:S(2)}) collective-permute-start(bf16[512,128]{1,0:T(8,128)(2,1)S(1)} %add_convert_fusion.1.refs_0_), channel_id=1, source_target_pairs={{0,4},{1,5},{2,6},{3,7},{4,8},{5,9},{6,10},{7,11},{8,12},{9,13},{1... | collective-permute-start | bytes 393224 | tf_op jit(solution)/shard_map/ppermute | solution.py:271
  57.6 1.0 constant_dynamic-slice_fusion.3
  58.7 3.4 %collective-permute-start.21 = (bf16[512,128]{1,0:T(8,128)(2,1)S(1)}, bf16[512,128]{1,0:T(8,128)(2,1)S(1)}, u32[]{:S(2)}, u32[]{:S(2)}) collective-permute-start(bf16[512,128]{1,0:T(8,128)(2,1)S(1)} %add_convert_fusion.1.refs_0_), channel_id=1, source_target_pairs={{0,8},{1,9},{2,10},{3,11},{4,12},{5,13},{6,14},{7,15},{8,0},{9,1},... | collective-permute-start | bytes 393224 | tf_op jit(solution)/shard_map/ppermute | solution.py:271
  62.0 1.9 %collective-permute-done.13.refs_1_ = bf16[512,128]{1,0:T(8,128)(2,1)S(1)} collective-permute-done((bf16[512,128]{1,0:T(8,128)(2,1)S(1)}, bf16[512,128]{1,0:T(8,128)(2,1)S(1)}, u32[]{:S(2)}, u32[]{:S(2)}) %collective-permute-start.13) | collective-permute-done | bytes 131104 | tf_op jit(solution)/shard_map/ppermute | solution.py:271
  64.0 2.9 %collective-permute-start.22 = (bf16[512,128]{1,0:T(8,128)(2,1)S(1)}, bf16[512,128]{1,0:T(8,128)(2,1)S(1)}, u32[]{:S(2)}, u32[]{:S(2)}) collective-permute-start(bf16[512,128]{1,0:T(8,128)(2,1)S(1)} %add_convert_fusion.1.refs_0_), channel_id=1, source_target_pairs={{0,12},{1,13},{2,14},{3,15},{4,0},{5,1},{6,2},{7,3},{8,4},{9,5},{1... | collective-permute-start | bytes 393224 | tf_op jit(solution)/shard_map/ppermute | solution.py:271
  66.9 1.1 %collective-permute-start.14 = (bf16[32,1024]{1,0:T(8,128)(2,1)S(1)}, bf16[32,1024]{1,0:T(8,128)(2,1)S(1)}, u32[]{:S(2)}, u32[]{:S(2)}) collective-permute-start(bf16[32,1024]{1,0:T(8,128)(2,1)S(1)} %get-tuple-element.48), channel_id=1, source_target_pairs={{0,2},{1,3},{2,0},{3,1},{4,6},{5,7},{6,4},{7,5},{8,10},{9,11},{10,... | collective-permute-start | bytes 196616 | tf_op jit(solution)/shard_map/ppermute | solution.py:271
  68.1 1.1 %multiply_reduce_fusion = (f32[512]{0:T(512)S(1)}, f32[512,128]{1,0:T(8,128)S(1)}) fusion(f32[512,128]{1,0:T(8,128)S(1)} %collective-permute-done.17, f32[512,128]{1,0:T(8,128)S(1)} %collective-permute-done.16, f32[512,128]{1,0:T(8,128)} %copy-done.4, f32[512,128]{1,0:T(8,128)S(1)} %collective-permute-done.15), kind=kLoop, calls=%fused_computation.8 | loop fusion | flops 327168 | bytes 1312768 | tf_op jit(solution)/shard_map/reduce_sum | solution.py:232
  69.2 0.1 multiply_convert_fusion.refs_0_
  69.4 1.8 %collective-permute-start.19 = (bf16[512,128]{1,0:T(8,128)(2,1)S(1)}, bf16[512,128]{1,0:T(8,128)(2,1)S(1)}, u32[]{:S(2)}, u32[]{:S(2)}) collective-permute-start(bf16[512,128]{1,0:T(8,128)(2,1)S(1)} %multiply_convert_fusion.refs_0_), channel_id=1, source_target_pairs={{0,8},{1,9},{2,10},{3,11},{4,12},{5,13},{6,14},{7,15},{8,0},{9,1},... | collective-permute-start | bytes 393224 | tf_op jit(solution)/shard_map/ppermute | solution.py:271
  71.2 2.0 %collective-permute-start.20 = (bf16[512,128]{1,0:T(8,128)(2,1)S(1)}, bf16[512,128]{1,0:T(8,128)(2,1)S(1)}, u32[]{:S(2)}, u32[]{:S(2)}) collective-permute-start(bf16[512,128]{1,0:T(8,128)(2,1)S(1)} %multiply_convert_fusion.refs_0_), channel_id=1, source_target_pairs={{0,12},{1,13},{2,14},{3,15},{4,0},{5,1},{6,2},{7,3},{8,4},{9,5},{1... | collective-permute-start | bytes 393224 | tf_op jit(solution)/shard_map/ppermute | solution.py:271
  73.4 0.1 fusion
  73.5 0.1 fusion.2.q_ref
  73.7 2.7 %collective-permute-done.18.refs_1_ = bf16[512,128]{1,0:T(8,128)(2,1)S(1)} collective-permute-done((bf16[512,128]{1,0:T(8,128)(2,1)S(1)}, bf16[512,128]{1,0:T(8,128)(2,1)S(1)}, u32[]{:S(2)}, u32[]{:S(2)}) %collective-permute-start.18) | collective-permute-done | bytes 131104 | tf_op jit(solution)/shard_map/ppermute | solution.py:271
  76.4 3.1 %collective-permute-done.19.refs_2_ = bf16[512,128]{1,0:T(8,128)(2,1)S(1)} collective-permute-done((bf16[512,128]{1,0:T(8,128)(2,1)S(1)}, bf16[512,128]{1,0:T(8,128)(2,1)S(1)}, u32[]{:S(2)}, u32[]{:S(2)}) %collective-permute-start.19) | collective-permute-done | bytes 131104 | tf_op jit(solution)/shard_map/ppermute | solution.py:271
  79.5 2.0 %score.1 = (bf16[512,2048]{1,0:T(8,128)(2,1)S(1)}, f32[512,128]{1,0:T(8,128)S(1)}) custom-call(bf16[512,128]{1,0:T(8,128)(2,1)S(1)} %fusion.2.q_ref, bf16[512,128]{1,0:T(8,128)(2,1)S(1)} %multiply_convert_fusion.refs_0_, bf16[512,128]{1,0:T(8,128)(2,1)S(1)} %collective-permute-done.18.refs_1_, bf16[512,128]{1,0:T(8,128)(2,1)S(1)} %collective-permute-done.19.refs_2_, ...), custom_call_target="tpu_custom_call" | custom-call | tf_op jit(solution)/shard_map/score/pallas_call | solution.py:131
  81.6 0.7 mix.1.refs_0_
  82.3 1.0 collective-permute-start.23
  83.3 2.0 %collective-permute-start.24 = (bf16[64,1024]{1,0:T(8,128)(2,1)S(1)}, bf16[64,1024]{1,0:T(8,128)(2,1)S(1)}, u32[]{:S(2)}, u32[]{:S(2)}) collective-permute-start(bf16[64,1024]{1,0:T(8,128)(2,1)S(1)} %mix.1.refs_0_), channel_id=1, source_target_pairs={{0,4},{1,5},{2,6},{3,7},{4,8},{5,9},{6,10},{7,11},{8,12},{9,13},{1... | collective-permute-start | bytes 393224 | tf_op jit(solution)/shard_map/ppermute | solution.py:271
  85.3 2.2 %collective-permute-start.27 = (bf16[64,1024]{1,0:T(8,128)(2,1)S(1)}, bf16[64,1024]{1,0:T(8,128)(2,1)S(1)}, u32[]{:S(2)}, u32[]{:S(2)}) collective-permute-start(bf16[64,1024]{1,0:T(8,128)(2,1)S(1)} %mix.1.refs_0_), channel_id=1, source_target_pairs={{0,12},{1,13},{2,14},{3,15},{4,0},{5,1},{6,2},{7,3},{8,4},{9,5},{1... | collective-permute-start | bytes 393224 | tf_op jit(solution)/shard_map/ppermute | solution.py:271
  87.5 0.6 collective-permute-start.26
  88.1 3.9 %collective-permute-done.24.refs_1_ = bf16[64,1024]{1,0:T(8,128)(2,1)S(1)} collective-permute-done((bf16[64,1024]{1,0:T(8,128)(2,1)S(1)}, bf16[64,1024]{1,0:T(8,128)(2,1)S(1)}, u32[]{:S(2)}, u32[]{:S(2)}) %collective-permute-start.24) | collective-permute-done | bytes 131104 | tf_op jit(solution)/shard_map/ppermute | solution.py:271
  92.0 1.1 %collective-permute-start.25 = (bf16[64,1024]{1,0:T(8,128)(2,1)S(1)}, bf16[64,1024]{1,0:T(8,128)(2,1)S(1)}, u32[]{:S(2)}, u32[]{:S(2)}) collective-permute-start(bf16[64,1024]{1,0:T(8,128)(2,1)S(1)} %collective-permute-done.24.refs_1_), channel_id=1, source_target_pairs={{0,2},{1,3},{2,0},{3,1},{4,6},{5,7},{6,4},{7,5},{8,10},{9,11},{10,... | collective-permute-start | bytes 393224 | tf_op jit(solution)/shard_map/ppermute | solution.py:271
  93.0 0.9 collective-permute-start.29
  94.0 0.6 output_near.1.refs_5_
  94.6 3.1 %collective-permute-done.26.refs_0_ = bf16[64,1024]{1,0:T(8,128)(2,1)S(1)} collective-permute-done((bf16[64,1024]{1,0:T(8,128)(2,1)S(1)}, bf16[64,1024]{1,0:T(8,128)(2,1)S(1)}, u32[]{:S(2)}, u32[]{:S(2)}) %collective-permute-start.26) | collective-permute-done | bytes 131104 | tf_op jit(solution)/shard_map/ppermute | solution.py:271
  97.7 1.7 %collective-permute-start.28 = (bf16[64,1024]{1,0:T(8,128)(2,1)S(1)}, bf16[64,1024]{1,0:T(8,128)(2,1)S(1)}, u32[]{:S(2)}, u32[]{:S(2)}) collective-permute-start(bf16[64,1024]{1,0:T(8,128)(2,1)S(1)} %collective-permute-done.26.refs_0_), channel_id=1, source_target_pairs={{0,2},{1,3},{2,0},{3,1},{4,6},{5,7},{6,4},{7,5},{8,10},{9,11},{10,... | collective-permute-start | bytes 393224 | tf_op jit(solution)/shard_map/ppermute | solution.py:271
  99.4 0.1 pad_add_fusion.scalars
  99.4 0.5 output_far.1.refs_6_
  100.0 2.7 %collective-permute-done.28.refs_2_ = bf16[64,1024]{1,0:T(8,128)(2,1)S(1)} collective-permute-done((bf16[64,1024]{1,0:T(8,128)(2,1)S(1)}, bf16[64,1024]{1,0:T(8,128)(2,1)S(1)}, u32[]{:S(2)}, u32[]{:S(2)}) %collective-permute-start.28) | collective-permute-done | bytes 131104 | tf_op jit(solution)/shard_map/ppermute | solution.py:271
  102.7 1.3 %output_other.1 = (f32[128,1024]{1,0:T(8,128)S(1)}, bf16[128,1024]{1,0:T(8,128)(2,1)S(1)}) custom-call(s32[3]{0:T(128)S(1)} %pad_add_fusion.scalars, bf16[64,1024]{1,0:T(8,128)(2,1)S(1)} %collective-permute-done.23.refs_0_, bf16[64,1024]{1,0:T(8,128)(2,1)S(1)} %collective-permute-done.25.refs_1_, bf16[64,1024]{1,0:T(8,128)(2,1)S(1)} %collective-permute-done.28.refs_2_, ...), custom_call_target="tpu_custom_call" | custom-call | tf_op jit(solution)/shard_map/output_other/pallas_call | solution.py:210
  104.0 0.1 collective-permute-start.30
  104.8 0.8 collective-permute-done.30
  105.6 0.8 add_convert_fusion
  (47 shorter events, 0.4 us)
Async XLA Ops:
  1.1 19.4 %collective-permute-start.7 = (bf16[480,512]{1,0:T(8,128)(2,1)S(1)}, bf16[480,512]{1,0:T(8,128)(2,1)S(1)}, u32[]{:S(2)}, u32[]{:S(2)}) collective-permute-start(bf16[480,512]{1,0:T(8,128)(2,1)S(1)} %pad_maximum_fusion.refs_8_), channel_id=1, source_target_pairs={{0,12},{1,13},{2,14},{3,15},{4,0},{5,1},{6,2},{7,3},{8,4},{9,5},{1... | collective-permute-start | bytes 1474568 | tf_op jit(solution)/shard_map/ppermute | solution.py:271
  6.2 22.1 %collective-permute-start.6 = (bf16[480,512]{1,0:T(8,128)(2,1)S(1)}, bf16[480,512]{1,0:T(8,128)(2,1)S(1)}, u32[]{:S(2)}, u32[]{:S(2)}) collective-permute-start(bf16[480,512]{1,0:T(8,128)(2,1)S(1)} %pad_maximum_fusion.refs_8_), channel_id=1, source_target_pairs={{0,4},{1,5},{2,6},{3,7},{4,8},{5,9},{6,10},{7,11},{8,12},{9,13},{1... | collective-permute-start | bytes 1474568 | tf_op jit(solution)/shard_map/ppermute | solution.py:271
  6.3 2.1 %copy-start.1 = (bf16[256,7680]{1,0:T(8,128)(2,1)S(1)}, bf16[256,7680]{1,0:T(8,128)(2,1)}, u32[]{:S(2)}) copy-start(bf16[256,7680]{1,0:T(8,128)(2,1)} %rows_ref.3) | copy-start | bytes 11796484
  11.6 18.2 %collective-permute-start.2 = (bf16[128,1920]{1,0:T(8,128)(2,1)}, bf16[128,1920]{1,0:T(8,128)(2,1)S(1)}, u32[]{:S(2)}, u32[]{:S(2)}) collective-permute-start(bf16[128,1920]{1,0:T(8,128)(2,1)} %get-tuple-element.36), channel_id=1, source_target_pairs={{0,18},{1,19},{2,16},{3,17},{4,22},{5,23},{6,20},{7,21},{8,26},{9,... | collective-permute-start | bytes 1474568 | tf_op jit(solution)/shard_map/ppermute | solution.py:271
  14.1 22.0 %collective-permute-start.1 = (bf16[128,1920]{1,0:T(8,128)(2,1)}, bf16[128,1920]{1,0:T(8,128)(2,1)S(1)}, u32[]{:S(2)}, u32[]{:S(2)}) collective-permute-start(bf16[128,1920]{1,0:T(8,128)(2,1)} %get-tuple-element.35), channel_id=1, source_target_pairs={{0,16},{1,17},{2,18},{3,19},{4,20},{5,21},{6,22},{7,23},{8,24},{9,... | collective-permute-start | bytes 1474568 | tf_op jit(solution)/shard_map/ppermute | solution.py:271
  14.6 21.4 %collective-permute-start = (bf16[128,1920]{1,0:T(8,128)(2,1)}, bf16[128,1920]{1,0:T(8,128)(2,1)}, u32[]{:S(2)}, u32[]{:S(2)}) collective-permute-start(bf16[128,1920]{1,0:T(8,128)(2,1)} %get-tuple-element.34), channel_id=1, source_target_pairs={{0,2},{1,3},{2,0},{3,1},{4,6},{5,7},{6,4},{7,5},{8,10},{9,11},{10,... | collective-permute-start | bytes 1474568 | tf_op jit(solution)/shard_map/ppermute | solution.py:271
  15.2 2.1 %copy-start.2 = (bf16[256,7680]{1,0:T(8,128)(2,1)S(1)}, bf16[256,7680]{1,0:T(8,128)(2,1)}, u32[]{:S(2)}) copy-start(bf16[256,7680]{1,0:T(8,128)(2,1)} %rows_ref.3) | copy-start | bytes 11796484
  17.3 2.1 %copy-start.3 = (bf16[256,7680]{1,0:T(8,128)(2,1)S(1)}, bf16[256,7680]{1,0:T(8,128)(2,1)}, u32[]{:S(2)}) copy-start(bf16[256,7680]{1,0:T(8,128)(2,1)} %rows_ref.3) | copy-start | bytes 11796484
  20.5 18.4 %collective-permute-start.8 = (bf16[480,512]{1,0:T(8,128)(2,1)S(1)}, bf16[480,512]{1,0:T(8,128)(2,1)}, u32[]{:S(2)}, u32[]{:S(2)}) collective-permute-start(bf16[480,512]{1,0:T(8,128)(2,1)S(1)} %collective-permute-done.7.refs_10_), channel_id=1, source_target_pairs={{4,0},{5,1},{6,2},{7,3},{8,4},{9,5},{10,6},{11,7},{20,16},{21,17},... | collective-permute-start | bytes 1474568 | tf_op jit(solution)/shard_map/ppermute | solution.py:271
  28.3 10.5 %collective-permute-start.9 = (bf16[480,512]{1,0:T(8,128)(2,1)S(1)}, bf16[480,512]{1,0:T(8,128)(2,1)}, u32[]{:S(2)}, u32[]{:S(2)}) collective-permute-start(bf16[480,512]{1,0:T(8,128)(2,1)S(1)} %collective-permute-done.6.refs_9_), channel_id=1, source_target_pairs={{4,8},{5,9},{6,10},{7,11},{8,12},{9,13},{10,14},{11,15},{20,24},{2... | collective-permute-start | bytes 1474568 | tf_op jit(solution)/shard_map/ppermute | solution.py:271
  29.8 9.1 %collective-permute-start.5 = (bf16[128,1920]{1,0:T(8,128)(2,1)S(1)}, bf16[128,1920]{1,0:T(8,128)(2,1)}, u32[]{:S(2)}, u32[]{:S(2)}) collective-permute-start(bf16[128,1920]{1,0:T(8,128)(2,1)S(1)} %collective-permute-done.2.refs_3_), channel_id=1, source_target_pairs={{0,1},{1,0},{2,3},{3,2},{4,5},{5,4},{6,7},{7,6},{8,9},{9,8},{10,11... | collective-permute-start | bytes 1474568 | tf_op jit(solution)/shard_map/ppermute | solution.py:271
  36.0 2.8 %collective-permute-start.4 = (bf16[128,1920]{1,0:T(8,128)(2,1)S(1)}, bf16[128,1920]{1,0:T(8,128)(2,1)}, u32[]{:S(2)}, u32[]{:S(2)}) collective-permute-start(bf16[128,1920]{1,0:T(8,128)(2,1)S(1)} %collective-permute-done.1.refs_2_), channel_id=1, source_target_pairs={{0,1},{1,0},{2,3},{3,2},{4,5},{5,4},{6,7},{7,6},{8,9},{9,8},{10,11... | collective-permute-start | bytes 1474568 | tf_op jit(solution)/shard_map/ppermute | solution.py:271
  36.0 2.9 %collective-permute-start.3 = (bf16[128,1920]{1,0:T(8,128)(2,1)}, bf16[128,1920]{1,0:T(8,128)(2,1)}, u32[]{:S(2)}, u32[]{:S(2)}) collective-permute-start(bf16[128,1920]{1,0:T(8,128)(2,1)} %collective-permute-done.refs_1_), channel_id=1, source_target_pairs={{0,1},{1,0},{2,3},{3,2},{4,5},{5,4},{6,7},{7,6},{8,9},{9,8},{10,11... | collective-permute-start | bytes 1474568 | tf_op jit(solution)/shard_map/ppermute | solution.py:271
  36.6 32.5 %copy-start.6 = (f32[128]{0:T(128)S(1)}, f32[128]{0:T(128)}, u32[]{:S(2)}) copy-start(f32[128]{0:T(128)} %param.16) | copy-start | bytes 1540
  36.6 36.9 %copy-start.7 = (f32[128]{0:T(128)S(1)}, f32[128]{0:T(128)}, u32[]{:S(2)}) copy-start(f32[128]{0:T(128)} %param.15) | copy-start | bytes 1540
  44.0 0.7 copy-start.4
  44.7 6.5 %collective-permute-start.10 = (bf16[512,128]{1,0:T(8,128)(2,1)S(1)}, bf16[512,128]{1,0:T(8,128)(2,1)S(1)}, u32[]{:S(2)}, u32[]{:S(2)}) collective-permute-start(bf16[512,128]{1,0:T(8,128)(2,1)S(1)} %get-tuple-element.45), channel_id=1, source_target_pairs={{0,2},{1,3},{2,0},{3,1},{4,6},{5,7},{6,4},{7,5},{8,10},{9,11},{10,... | collective-permute-start | bytes 393224 | tf_op jit(solution)/shard_map/ppermute | solution.py:271
  46.2 6.4 %collective-permute-start.11 = (bf16[512,128]{1,0:T(8,128)(2,1)S(1)}, bf16[512,128]{1,0:T(8,128)(2,1)S(1)}, u32[]{:S(2)}, u32[]{:S(2)}) collective-permute-start(bf16[512,128]{1,0:T(8,128)(2,1)S(1)} %get-tuple-element.46), channel_id=1, source_target_pairs={{0,16},{1,17},{2,18},{3,19},{4,20},{5,21},{6,22},{7,23},{8,24},{9,... | collective-permute-start | bytes 393224 | tf_op jit(solution)/shard_map/ppermute | solution.py:271
  47.7 7.4 %collective-permute-start.12 = (bf16[512,128]{1,0:T(8,128)(2,1)S(1)}, bf16[512,128]{1,0:T(8,128)(2,1)S(1)}, u32[]{:S(2)}, u32[]{:S(2)}) collective-permute-start(bf16[512,128]{1,0:T(8,128)(2,1)S(1)} %get-tuple-element.47), channel_id=1, source_target_pairs={{0,18},{1,19},{2,16},{3,17},{4,22},{5,23},{6,20},{7,21},{8,26},{9,... | collective-permute-start | bytes 393224 | tf_op jit(solution)/shard_map/ppermute | solution.py:271
  48.2 18.7 %collective-permute-start.15 = (f32[512,128]{1,0:T(8,128)}, f32[512,128]{1,0:T(8,128)S(1)}, u32[]{:S(2)}, u32[]{:S(2)}) collective-permute-start(f32[512,128]{1,0:T(8,128)} %get-tuple-element.50), channel_id=1, source_target_pairs={{0,2},{1,3},{2,0},{3,1},{4,6},{5,7},{6,4},{7,5},{8,10},{9,11},{10,... | collective-permute-start | bytes 786440 | tf_op jit(solution)/shard_map/ppermute | solution.py:271
  49.7 18.4 %collective-permute-start.16 = (f32[512,128]{1,0:T(8,128)}, f32[512,128]{1,0:T(8,128)S(1)}, u32[]{:S(2)}, u32[]{:S(2)}) collective-permute-start(f32[512,128]{1,0:T(8,128)} %get-tuple-element.52), channel_id=1, source_target_pairs={{0,16},{1,17},{2,18},{3,19},{4,20},{5,21},{6,22},{7,23},{8,24},{9,... | collective-permute-start | bytes 786440 | tf_op jit(solution)/shard_map/ppermute | solution.py:271
  51.2 16.9 %collective-permute-start.17 = (f32[512,128]{1,0:T(8,128)}, f32[512,128]{1,0:T(8,128)S(1)}, u32[]{:S(2)}, u32[]{:S(2)}) collective-permute-start(f32[512,128]{1,0:T(8,128)} %get-tuple-element.54), channel_id=1, source_target_pairs={{0,18},{1,19},{2,16},{3,17},{4,22},{5,23},{6,20},{7,21},{8,26},{9,... | collective-permute-start | bytes 786440 | tf_op jit(solution)/shard_map/ppermute | solution.py:271
  55.1 8.8 %collective-permute-start.13 = (bf16[512,128]{1,0:T(8,128)(2,1)S(1)}, bf16[512,128]{1,0:T(8,128)(2,1)S(1)}, u32[]{:S(2)}, u32[]{:S(2)}) collective-permute-start(bf16[512,128]{1,0:T(8,128)(2,1)S(1)} %add_convert_fusion.1.refs_0_), channel_id=1, source_target_pairs={{0,4},{1,5},{2,6},{3,7},{4,8},{5,9},{6,10},{7,11},{8,12},{9,13},{1... | collective-permute-start | bytes 393224 | tf_op jit(solution)/shard_map/ppermute | solution.py:271
  57.6 36.4 %copy-start = (bf16[2048,1024]{1,0:T(8,128)(2,1)S(1)}, bf16[2048,1024]{1,0:T(8,128)(2,1)}, u32[]{:S(2)}) copy-start(bf16[2048,1024]{1,0:T(8,128)(2,1)} %refs_4_.1) | copy-start | bytes 12582916
  58.7 22.9 %collective-permute-start.21 = (bf16[512,128]{1,0:T(8,128)(2,1)S(1)}, bf16[512,128]{1,0:T(8,128)(2,1)S(1)}, u32[]{:S(2)}, u32[]{:S(2)}) collective-permute-start(bf16[512,128]{1,0:T(8,128)(2,1)S(1)} %add_convert_fusion.1.refs_0_), channel_id=1, source_target_pairs={{0,8},{1,9},{2,10},{3,11},{4,12},{5,13},{6,14},{7,15},{8,0},{9,1},... | collective-permute-start | bytes 393224 | tf_op jit(solution)/shard_map/ppermute | solution.py:271
  64.0 17.6 %collective-permute-start.22 = (bf16[512,128]{1,0:T(8,128)(2,1)S(1)}, bf16[512,128]{1,0:T(8,128)(2,1)S(1)}, u32[]{:S(2)}, u32[]{:S(2)}) collective-permute-start(bf16[512,128]{1,0:T(8,128)(2,1)S(1)} %add_convert_fusion.1.refs_0_), channel_id=1, source_target_pairs={{0,12},{1,13},{2,14},{3,15},{4,0},{5,1},{6,2},{7,3},{8,4},{9,5},{1... | collective-permute-start | bytes 393224 | tf_op jit(solution)/shard_map/ppermute | solution.py:271
  66.9 4.3 %collective-permute-start.14 = (bf16[32,1024]{1,0:T(8,128)(2,1)S(1)}, bf16[32,1024]{1,0:T(8,128)(2,1)S(1)}, u32[]{:S(2)}, u32[]{:S(2)}) collective-permute-start(bf16[32,1024]{1,0:T(8,128)(2,1)S(1)} %get-tuple-element.48), channel_id=1, source_target_pairs={{0,2},{1,3},{2,0},{3,1},{4,6},{5,7},{6,4},{7,5},{8,10},{9,11},{10,... | collective-permute-start | bytes 196616 | tf_op jit(solution)/shard_map/ppermute | solution.py:271
  69.3 7.1 %collective-permute-start.18 = (bf16[512,128]{1,0:T(8,128)(2,1)S(1)}, bf16[512,128]{1,0:T(8,128)(2,1)S(1)}, u32[]{:S(2)}, u32[]{:S(2)}) collective-permute-start(bf16[512,128]{1,0:T(8,128)(2,1)S(1)} %multiply_convert_fusion.refs_0_), channel_id=1, source_target_pairs={{0,4},{1,5},{2,6},{3,7},{4,8},{5,9},{6,10},{7,11},{8,12},{9,13},{1... | collective-permute-start | bytes 393224 | tf_op jit(solution)/shard_map/ppermute | solution.py:271
  69.4 10.2 %collective-permute-start.19 = (bf16[512,128]{1,0:T(8,128)(2,1)S(1)}, bf16[512,128]{1,0:T(8,128)(2,1)S(1)}, u32[]{:S(2)}, u32[]{:S(2)}) collective-permute-start(bf16[512,128]{1,0:T(8,128)(2,1)S(1)} %multiply_convert_fusion.refs_0_), channel_id=1, source_target_pairs={{0,8},{1,9},{2,10},{3,11},{4,12},{5,13},{6,14},{7,15},{8,0},{9,1},... | collective-permute-start | bytes 393224 | tf_op jit(solution)/shard_map/ppermute | solution.py:271
  71.2 8.4 %collective-permute-start.20 = (bf16[512,128]{1,0:T(8,128)(2,1)S(1)}, bf16[512,128]{1,0:T(8,128)(2,1)S(1)}, u32[]{:S(2)}, u32[]{:S(2)}) collective-permute-start(bf16[512,128]{1,0:T(8,128)(2,1)S(1)} %multiply_convert_fusion.refs_0_), channel_id=1, source_target_pairs={{0,12},{1,13},{2,14},{3,15},{4,0},{5,1},{6,2},{7,3},{8,4},{9,5},{1... | collective-permute-start | bytes 393224 | tf_op jit(solution)/shard_map/ppermute | solution.py:271
  82.3 5.7 %collective-permute-start.23 = (bf16[64,1024]{1,0:T(8,128)(2,1)S(1)}, bf16[64,1024]{1,0:T(8,128)(2,1)S(1)}, u32[]{:S(2)}, u32[]{:S(2)}) collective-permute-start(bf16[64,1024]{1,0:T(8,128)(2,1)S(1)} %mix.1.refs_0_), channel_id=1, source_target_pairs={{0,2},{1,3},{2,0},{3,1},{4,6},{5,7},{6,4},{7,5},{8,10},{9,11},{10,... | collective-permute-start | bytes 393224 | tf_op jit(solution)/shard_map/ppermute | solution.py:271
  83.3 8.6 %collective-permute-start.24 = (bf16[64,1024]{1,0:T(8,128)(2,1)S(1)}, bf16[64,1024]{1,0:T(8,128)(2,1)S(1)}, u32[]{:S(2)}, u32[]{:S(2)}) collective-permute-start(bf16[64,1024]{1,0:T(8,128)(2,1)S(1)} %mix.1.refs_0_), channel_id=1, source_target_pairs={{0,4},{1,5},{2,6},{3,7},{4,8},{5,9},{6,10},{7,11},{8,12},{9,13},{1... | collective-permute-start | bytes 393224 | tf_op jit(solution)/shard_map/ppermute | solution.py:271
  85.3 7.8 %collective-permute-start.27 = (bf16[64,1024]{1,0:T(8,128)(2,1)S(1)}, bf16[64,1024]{1,0:T(8,128)(2,1)S(1)}, u32[]{:S(2)}, u32[]{:S(2)}) collective-permute-start(bf16[64,1024]{1,0:T(8,128)(2,1)S(1)} %mix.1.refs_0_), channel_id=1, source_target_pairs={{0,12},{1,13},{2,14},{3,15},{4,0},{5,1},{6,2},{7,3},{8,4},{9,5},{1... | collective-permute-start | bytes 393224 | tf_op jit(solution)/shard_map/ppermute | solution.py:271
  87.5 10.2 %collective-permute-start.26 = (bf16[64,1024]{1,0:T(8,128)(2,1)S(1)}, bf16[64,1024]{1,0:T(8,128)(2,1)S(1)}, u32[]{:S(2)}, u32[]{:S(2)}) collective-permute-start(bf16[64,1024]{1,0:T(8,128)(2,1)S(1)} %mix.1.refs_0_), channel_id=1, source_target_pairs={{0,8},{1,9},{2,10},{3,11},{4,12},{5,13},{6,14},{7,15},{8,0},{9,1},... | collective-permute-start | bytes 393224 | tf_op jit(solution)/shard_map/ppermute | solution.py:271
  92.0 5.7 %collective-permute-start.25 = (bf16[64,1024]{1,0:T(8,128)(2,1)S(1)}, bf16[64,1024]{1,0:T(8,128)(2,1)S(1)}, u32[]{:S(2)}, u32[]{:S(2)}) collective-permute-start(bf16[64,1024]{1,0:T(8,128)(2,1)S(1)} %collective-permute-done.24.refs_1_), channel_id=1, source_target_pairs={{0,2},{1,3},{2,0},{3,1},{4,6},{5,7},{6,4},{7,5},{8,10},{9,11},{10,... | collective-permute-start | bytes 393224 | tf_op jit(solution)/shard_map/ppermute | solution.py:271
  93.0 6.9 %collective-permute-start.29 = (bf16[64,1024]{1,0:T(8,128)(2,1)S(1)}, bf16[64,1024]{1,0:T(8,128)(2,1)S(1)}, u32[]{:S(2)}, u32[]{:S(2)}) collective-permute-start(bf16[64,1024]{1,0:T(8,128)(2,1)S(1)} %collective-permute-done.27.refs_2_), channel_id=1, source_target_pairs={{0,2},{1,3},{2,0},{3,1},{4,6},{5,7},{6,4},{7,5},{8,10},{9,11},{10,... | collective-permute-start | bytes 393224 | tf_op jit(solution)/shard_map/ppermute | solution.py:271
  97.7 5.0 %collective-permute-start.28 = (bf16[64,1024]{1,0:T(8,128)(2,1)S(1)}, bf16[64,1024]{1,0:T(8,128)(2,1)S(1)}, u32[]{:S(2)}, u32[]{:S(2)}) collective-permute-start(bf16[64,1024]{1,0:T(8,128)(2,1)S(1)} %collective-permute-done.26.refs_0_), channel_id=1, source_target_pairs={{0,2},{1,3},{2,0},{3,1},{4,6},{5,7},{6,4},{7,5},{8,10},{9,11},{10,... | collective-permute-start | bytes 393224 | tf_op jit(solution)/shard_map/ppermute | solution.py:271
  99.9 5.7 %copy-start.5 = (bf16[128,1024]{1,0:T(8,128)(2,1)S(1)}, bf16[128,1024]{1,0:T(8,128)(2,1)}, u32[]{:S(2)}) copy-start(bf16[128,1024]{1,0:T(8,128)(2,1)} %param.14) | copy-start | bytes 786436
  104.0 1.6 %collective-permute-start.30 = (bf16[128,1024]{1,0:T(8,128)(2,1)S(1)}, bf16[128,1024]{1,0:T(8,128)(2,1)S(1)}, u32[]{:S(2)}, u32[]{:S(2)}) collective-permute-start(bf16[128,1024]{1,0:T(8,128)(2,1)S(1)} %get-tuple-element.62), channel_id=1, source_target_pairs={{0,1},{1,0},{2,3},{3,2},{4,5},{5,4},{6,7},{7,6},{8,9},{9,8},{10,11... | collective-permute-start | bytes 786440 | tf_op jit(solution)/shard_map/ppermute | solution.py:271

commit v9 on v8

--- a/solution.py
+++ b/solution.py
@@ -347,7 +347,7 @@
     value_parts = scatter(value_pieces)
     key_parts = scatter(key_pieces)
     values = sum_up(value_pieces[0], value_parts).astype(bf16)
-    all_values = all_pairs(values)
+    all_values = {k: line_shift(values, k) for k in near_shifts}
     key_parts = [after(k, all_values[1]) for k in key_parts]
     q_recv = plane_shift(after(q_send, all_values[1]), 0, 1)
     q_pair = jnp.where(
@@ -361,6 +361,9 @@
     normed = norm(q_heads.astype(f32), query_norm_gain)
     keys = norm(sum_up(key_pieces[0], key_parts), key_norm_gain)
     all_keys = all_pairs(keys)
+    if middle:
+        all_values[middle] = line_shift(after(values, keys), middle)
+    all_values = [values, *(all_values[k] for k in range(1, pairs))]
     weights, denominator = score(normed, all_keys, heads)
     attended = mix(weights, denominator, all_values, heads)
     passed = {0: plane_shift(attended, 0, 1)}

time: 107 us -> 111 us (1.037)
  waiting for transfers between devices: 36 us -> 42.2 us
  starting transfers between devices: 43 us -> 40.7 us
    ppermute x31, waiting for transfers between devices: 36 us -> 42.2 us  [permute(): return lax.ppermute(array, AXES, perm)]
    ppermute x31, starting transfers between devices: 43 us -> 40.7 us  [permute(): return lax.ppermute(array, AXES, perm)]
  transfers between devices with their start and end apart: 31 -> 31, of which waited for: 12 -> 16; matrix products, arithmetic and copies ran while one was open for 3% -> 3% of each run, Pallas kernels for 8% -> 8%
where the time goes in v9:
time: 111 us; the launch traced here: 110 us
  waiting for transfers between devices  42.2 us (38%)
  starting transfers between devices  40.7 us (37%)
  Pallas kernels  15.5 us (14%)
  local copies, waits for them, and re-layouts  8.21 us (7%)
  other arithmetic  2.76 us (2%)
    ppermute x31, waiting for transfers between devices, permute(): return lax.ppermute(array, AXES, perm)  42.2 us
    ppermute x31, starting transfers between devices, permute(): return lax.ppermute(array, AXES, perm)  40.7 us
    unnamed x23, local copies, waits for them, and re-layouts  6.07 us
    pallas_call x3, Pallas kernels, pack(): pl.pallas_call(functools.partial(pack_kernel, groups, pairs, part, count)...  5.32 us
    pallas_call x1, Pallas kernels, project(): pl.pallas_call(functools.partial(project_kernel, count // 2, pairs, shift...  5.07 us
  transfers between devices with their start and end apart: 31, of which 16 were waited for; matrix products, arithmetic and copies ran while one was open for 3% of the time, Pallas kernels for 8%

profile of v9, /device:TPU:0, one launch (start us, length us, event | category | flops | bytes accessed | tf_op | source)
XLA Modules:
  0.0 110.3 jit_solution(3340255469018061536)
XLA Ops:
  0.0 1.1 constant_dynamic-slice_fusion
  1.1 5.1 %collective-permute-start.7 = (bf16[480,512]{1,0:T(8,128)(2,1)S(1)}, bf16[480,512]{1,0:T(8,128)(2,1)S(1)}, u32[]{:S(2)}, u32[]{:S(2)}) collective-permute-start(bf16[480,512]{1,0:T(8,128)(2,1)S(1)} %pad_maximum_fusion.refs_8_), channel_id=1, source_target_pairs={{0,12},{1,13},{2,14},{3,15},{4,0},{5,1},{6,2},{7,3},{8,4},{9,5},{1... | collective-permute-start | bytes 1474568 | tf_op jit(solution)/shard_map/ppermute | solution.py:271
  6.2 0.1 pad_add_fusion.2.index_ref
  6.3 2.1 %copy-done.1 = bf16[256,7680]{1,0:T(8,128)(2,1)S(1)} copy-done((bf16[256,7680]{1,0:T(8,128)(2,1)S(1)}, bf16[256,7680]{1,0:T(8,128)(2,1)}, u32[]{:S(2)}) %copy-start.1) | copy-done | bytes 3932184
  8.4 3.2 %pack_sends.1 = (bf16[128,1920]{1,0:T(8,128)(2,1)}, bf16[128,1920]{1,0:T(8,128)(2,1)}, bf16[128,1920]{1,0:T(8,128)(2,1)}) custom-call(s32[4]{0:T(128)S(1)} %pad_add_fusion.2.index_ref, bf16[256,7680]{1,0:T(8,128)(2,1)S(1)} %copy-done.1), custom_call_target="tpu_custom_call" | custom-call | tf_op jit(solution)/shard_map/pack_sends/pallas_call | solution.py:38
  11.6 2.5 %collective-permute-start.2 = (bf16[128,1920]{1,0:T(8,128)(2,1)}, bf16[128,1920]{1,0:T(8,128)(2,1)S(1)}, u32[]{:S(2)}, u32[]{:S(2)}) collective-permute-start(bf16[128,1920]{1,0:T(8,128)(2,1)} %get-tuple-element.37), channel_id=1, source_target_pairs={{0,18},{1,19},{2,16},{3,17},{4,22},{5,23},{6,20},{7,21},{8,26},{9,... | collective-permute-start | bytes 1474568 | tf_op jit(solution)/shard_map/ppermute | solution.py:271
  14.1 0.5 collective-permute-start.1
  14.6 0.5 collective-permute-start
  15.1 0.1 pad_add_fusion.1
  15.2 2.1 %copy-done.2 = bf16[256,7680]{1,0:T(8,128)(2,1)S(1)} copy-done((bf16[256,7680]{1,0:T(8,128)(2,1)S(1)}, bf16[256,7680]{1,0:T(8,128)(2,1)}, u32[]{:S(2)}) %copy-start.2) | copy-done | bytes 3932184
  17.3 1.1 pack_near.1.refs_0_
  18.4 1.0 copy-done.3
  19.4 1.1 pack_far.1.refs_4_
  20.5 1.3 %collective-permute-start.8 = (bf16[480,512]{1,0:T(8,128)(2,1)S(1)}, bf16[480,512]{1,0:T(8,128)(2,1)}, u32[]{:S(2)}, u32[]{:S(2)}) collective-permute-start(bf16[480,512]{1,0:T(8,128)(2,1)S(1)} %collective-permute-done.7.refs_10_), channel_id=1, source_target_pairs={{4,0},{5,1},{6,2},{7,3},{8,4},{9,5},{10,6},{11,7},{20,16},{21,17},... | collective-permute-start | bytes 1474568 | tf_op jit(solution)/shard_map/ppermute | solution.py:271
  21.8 6.5 %collective-permute-done.6.refs_9_ = bf16[480,512]{1,0:T(8,128)(2,1)S(1)} collective-permute-done((bf16[480,512]{1,0:T(8,128)(2,1)S(1)}, bf16[480,512]{1,0:T(8,128)(2,1)S(1)}, u32[]{:S(2)}, u32[]{:S(2)}) %collective-permute-start.6) | collective-permute-done | bytes 491552 | tf_op jit(solution)/shard_map/ppermute | solution.py:271
  28.3 1.4 %collective-permute-start.9 = (bf16[480,512]{1,0:T(8,128)(2,1)S(1)}, bf16[480,512]{1,0:T(8,128)(2,1)}, u32[]{:S(2)}, u32[]{:S(2)}) collective-permute-start(bf16[480,512]{1,0:T(8,128)(2,1)S(1)} %collective-permute-done.6.refs_9_), channel_id=1, source_target_pairs={{4,8},{5,9},{6,10},{7,11},{8,12},{9,13},{10,14},{11,15},{20,24},{2... | collective-permute-start | bytes 1474568 | tf_op jit(solution)/shard_map/ppermute | solution.py:271
  29.8 6.3 %collective-permute-done.1.refs_2_ = bf16[128,1920]{1,0:T(8,128)(2,1)S(1)} collective-permute-done((bf16[128,1920]{1,0:T(8,128)(2,1)}, bf16[128,1920]{1,0:T(8,128)(2,1)S(1)}, u32[]{:S(2)}, u32[]{:S(2)}) %collective-permute-start.1) | collective-permute-done | bytes 491552 | tf_op jit(solution)/shard_map/ppermute | solution.py:271
  36.0 0.5 collective-permute-start.3
  36.6 0.1 pad_add_fusion.3.scalars
  36.6 2.2 %collective-permute-done.8.refs_11_ = bf16[480,512]{1,0:T(8,128)(2,1)} collective-permute-done((bf16[480,512]{1,0:T(8,128)(2,1)S(1)}, bf16[480,512]{1,0:T(8,128)(2,1)}, u32[]{:S(2)}, u32[]{:S(2)}) %collective-permute-start.8) | collective-permute-done | bytes 491552 | tf_op jit(solution)/shard_map/ppermute | solution.py:271
  39.0 5.1 %project.1 = (f32[512,128]{1,0:T(8,128)S(1)}, f32[512,128]{1,0:T(8,128)}, f32[512,128]{1,0:T(8,128)}, f32[512,128]{1,0:T(8,128)}, f32[512,128]{1,0:T(8,128)S(1)}...) custom-call(s32[2]{0:T(128)S(1)} %pad_add_fusion.3.scalars, ...), custom_call_target="tpu_custom_call" | custom-call | tf_op jit(solution)/shard_map/project/pallas_call | solution.py:91
  44.0 0.7 copy-done.4
  44.7 1.5 %collective-permute-start.10 = (bf16[512,128]{1,0:T(8,128)(2,1)S(1)}, bf16[512,128]{1,0:T(8,128)(2,1)S(1)}, u32[]{:S(2)}, u32[]{:S(2)}) collective-permute-start(bf16[512,128]{1,0:T(8,128)(2,1)S(1)} %get-tuple-element.46), channel_id=1, source_target_pairs={{0,2},{1,3},{2,0},{3,1},{4,6},{5,7},{6,4},{7,5},{8,10},{9,11},{10,... | collective-permute-start | bytes 393224 | tf_op jit(solution)/shard_map/ppermute | solution.py:271
  46.2 1.5 %collective-permute-start.11 = (bf16[512,128]{1,0:T(8,128)(2,1)S(1)}, bf16[512,128]{1,0:T(8,128)(2,1)S(1)}, u32[]{:S(2)}, u32[]{:S(2)}) collective-permute-start(bf16[512,128]{1,0:T(8,128)(2,1)S(1)} %get-tuple-element.47), channel_id=1, source_target_pairs={{0,16},{1,17},{2,18},{3,19},{4,20},{5,21},{6,22},{7,23},{8,24},{9,... | collective-permute-start | bytes 393224 | tf_op jit(solution)/shard_map/ppermute | solution.py:271
  47.7 0.5 collective-permute-start.12
  48.2 1.5 %collective-permute-start.15 = (f32[512,128]{1,0:T(8,128)}, f32[512,128]{1,0:T(8,128)S(1)}, u32[]{:S(2)}, u32[]{:S(2)}) collective-permute-start(f32[512,128]{1,0:T(8,128)} %get-tuple-element.51), channel_id=1, source_target_pairs={{0,2},{1,3},{2,0},{3,1},{4,6},{5,7},{6,4},{7,5},{8,10},{9,11},{10,... | collective-permute-start | bytes 786440 | tf_op jit(solution)/shard_map/ppermute | solution.py:271
  49.7 1.5 %collective-permute-start.16 = (f32[512,128]{1,0:T(8,128)}, f32[512,128]{1,0:T(8,128)S(1)}, u32[]{:S(2)}, u32[]{:S(2)}) collective-permute-start(f32[512,128]{1,0:T(8,128)} %get-tuple-element.53), channel_id=1, source_target_pairs={{0,16},{1,17},{2,18},{3,19},{4,20},{5,21},{6,22},{7,23},{8,24},{9,... | collective-permute-start | bytes 786440 | tf_op jit(solution)/shard_map/ppermute | solution.py:271
  51.2 1.4 %collective-permute-start.17 = (f32[512,128]{1,0:T(8,128)}, f32[512,128]{1,0:T(8,128)S(1)}, u32[]{:S(2)}, u32[]{:S(2)}) collective-permute-start(f32[512,128]{1,0:T(8,128)} %get-tuple-element.55), channel_id=1, source_target_pairs={{0,18},{1,19},{2,16},{3,17},{4,22},{5,23},{6,20},{7,21},{8,26},{9,... | collective-permute-start | bytes 786440 | tf_op jit(solution)/shard_map/ppermute | solution.py:271
  52.6 2.4 %collective-permute-done.12 = bf16[512,128]{1,0:T(8,128)(2,1)S(1)} collective-permute-done((bf16[512,128]{1,0:T(8,128)(2,1)S(1)}, bf16[512,128]{1,0:T(8,128)(2,1)S(1)}, u32[]{:S(2)}, u32[]{:S(2)}) %collective-permute-start.12) | collective-permute-done | bytes 131104 | tf_op jit(solution)/shard_map/ppermute | solution.py:271
  55.1 2.5 %collective-permute-start.13 = (bf16[512,128]{1,0:T(8,128)(2,1)S(1)}, bf16[512,128]{1,0:T(8,128)(2,1)S(1)}, u32[]{:S(2)}, u32[]{:S(2)}) collective-permute-start(bf16[512,128]{1,0:T(8,128)(2,1)S(1)} %add_convert_fusion.1.refs_0_), channel_id=1, source_target_pairs={{0,4},{1,5},{2,6},{3,7},{4,8},{5,9},{6,10},{7,11},{8,12},{9,13},{1... | collective-permute-start | bytes 393224 | tf_op jit(solution)/shard_map/ppermute | solution.py:271
  57.6 1.0 constant_dynamic-slice_fusion.3
  58.7 2.9 %collective-permute-start.22 = (bf16[512,128]{1,0:T(8,128)(2,1)S(1)}, bf16[512,128]{1,0:T(8,128)(2,1)S(1)}, u32[]{:S(2)}, u32[]{:S(2)}) collective-permute-start(bf16[512,128]{1,0:T(8,128)(2,1)S(1)} %add_convert_fusion.1.refs_0_), channel_id=1, source_target_pairs={{0,12},{1,13},{2,14},{3,15},{4,0},{5,1},{6,2},{7,3},{8,4},{9,5},{1... | collective-permute-start | bytes 393224 | tf_op jit(solution)/shard_map/ppermute | solution.py:271
  61.5 1.9 %collective-permute-done.13.refs_1_ = bf16[512,128]{1,0:T(8,128)(2,1)S(1)} collective-permute-done((bf16[512,128]{1,0:T(8,128)(2,1)S(1)}, bf16[512,128]{1,0:T(8,128)(2,1)S(1)}, u32[]{:S(2)}, u32[]{:S(2)}) %collective-permute-start.13) | collective-permute-done | bytes 131104 | tf_op jit(solution)/shard_map/ppermute | solution.py:271
  63.4 1.5 %collective-permute-start.14 = (bf16[32,1024]{1,0:T(8,128)(2,1)S(1)}, bf16[32,1024]{1,0:T(8,128)(2,1)S(1)}, u32[]{:S(2)}, u32[]{:S(2)}) collective-permute-start(bf16[32,1024]{1,0:T(8,128)(2,1)S(1)} %get-tuple-element.49), channel_id=1, source_target_pairs={{0,2},{1,3},{2,0},{3,1},{4,6},{5,7},{6,4},{7,5},{8,10},{9,11},{10,... | collective-permute-start | bytes 196616 | tf_op jit(solution)/shard_map/ppermute | solution.py:271
  64.9 0.7 collective-permute-done.17
  65.6 1.1 multiply_reduce_fusion
  66.7 0.1 multiply_convert_fusion.refs_0_
  66.9 1.1 collective-permute-start.18
  67.9 3.3 %collective-permute-start.19 = (bf16[512,128]{1,0:T(8,128)(2,1)S(1)}, bf16[512,128]{1,0:T(8,128)(2,1)S(1)}, u32[]{:S(2)}, u32[]{:S(2)}) collective-permute-start(bf16[512,128]{1,0:T(8,128)(2,1)S(1)} %multiply_convert_fusion.refs_0_), channel_id=1, source_target_pairs={{0,8},{1,9},{2,10},{3,11},{4,12},{5,13},{6,14},{7,15},{8,0},{9,1},... | collective-permute-start | bytes 393224 | tf_op jit(solution)/shard_map/ppermute | solution.py:271
  71.2 1.7 %collective-permute-start.20 = (bf16[512,128]{1,0:T(8,128)(2,1)S(1)}, bf16[512,128]{1,0:T(8,128)(2,1)S(1)}, u32[]{:S(2)}, u32[]{:S(2)}) collective-permute-start(bf16[512,128]{1,0:T(8,128)(2,1)S(1)} %multiply_convert_fusion.refs_0_), channel_id=1, source_target_pairs={{0,12},{1,13},{2,14},{3,15},{4,0},{5,1},{6,2},{7,3},{8,4},{9,5},{1... | collective-permute-start | bytes 393224 | tf_op jit(solution)/shard_map/ppermute | solution.py:271
  73.1 0.1 fusion
  73.3 0.1 fusion.2.q_ref
  73.4 1.8 %collective-permute-done.18.refs_1_ = bf16[512,128]{1,0:T(8,128)(2,1)S(1)} collective-permute-done((bf16[512,128]{1,0:T(8,128)(2,1)S(1)}, bf16[512,128]{1,0:T(8,128)(2,1)S(1)}, u32[]{:S(2)}, u32[]{:S(2)}) %collective-permute-start.18) | collective-permute-done | bytes 131104 | tf_op jit(solution)/shard_map/ppermute | solution.py:271
  75.2 6.8 %collective-permute-done.19.refs_2_ = bf16[512,128]{1,0:T(8,128)(2,1)S(1)} collective-permute-done((bf16[512,128]{1,0:T(8,128)(2,1)S(1)}, bf16[512,128]{1,0:T(8,128)(2,1)S(1)}, u32[]{:S(2)}, u32[]{:S(2)}) %collective-permute-start.19) | collective-permute-done | bytes 131104 | tf_op jit(solution)/shard_map/ppermute | solution.py:271
  81.9 2.0 %score.1 = (bf16[512,2048]{1,0:T(8,128)(2,1)S(1)}, f32[512,128]{1,0:T(8,128)S(1)}) custom-call(bf16[512,128]{1,0:T(8,128)(2,1)S(1)} %fusion.2.q_ref, bf16[512,128]{1,0:T(8,128)(2,1)S(1)} %multiply_convert_fusion.refs_0_, bf16[512,128]{1,0:T(8,128)(2,1)S(1)} %collective-permute-done.18.refs_1_, bf16[512,128]{1,0:T(8,128)(2,1)S(1)} %collective-permute-done.19.refs_2_, ...), custom_call_target="tpu_custom_call" | custom-call | tf_op jit(solution)/shard_map/score/pallas_call | solution.py:131
  84.0 2.6 %collective-permute-done.21.refs_2_ = bf16[512,128]{1,0:T(8,128)(2,1)S(1)} collective-permute-done((bf16[512,128]{1,0:T(8,128)(2,1)S(1)}, bf16[512,128]{1,0:T(8,128)(2,1)S(1)}, u32[]{:S(2)}, u32[]{:S(2)}) %collective-permute-start.21) | collective-permute-done | bytes 131104 | tf_op jit(solution)/shard_map/ppermute | solution.py:271
  86.6 0.7 mix.1.refs_0_
  87.3 1.0 collective-permute-start.23
  88.3 0.8 collective-permute-start.24
  89.1 3.0 %collective-permute-start.27 = (bf16[64,1024]{1,0:T(8,128)(2,1)S(1)}, bf16[64,1024]{1,0:T(8,128)(2,1)S(1)}, u32[]{:S(2)}, u32[]{:S(2)}) collective-permute-start(bf16[64,1024]{1,0:T(8,128)(2,1)S(1)} %mix.1.refs_0_), channel_id=1, source_target_pairs={{0,12},{1,13},{2,14},{3,15},{4,0},{5,1},{6,2},{7,3},{8,4},{9,5},{1... | collective-permute-start | bytes 393224 | tf_op jit(solution)/shard_map/ppermute | solution.py:271
  92.1 0.2 collective-permute-done.23.refs_0_
  92.3 4.3 %collective-permute-done.24.refs_1_ = bf16[64,1024]{1,0:T(8,128)(2,1)S(1)} collective-permute-done((bf16[64,1024]{1,0:T(8,128)(2,1)S(1)}, bf16[64,1024]{1,0:T(8,128)(2,1)S(1)}, u32[]{:S(2)}, u32[]{:S(2)}) %collective-permute-start.24) | collective-permute-done | bytes 131104 | tf_op jit(solution)/shard_map/ppermute | solution.py:271
  96.6 1.1 %collective-permute-start.25 = (bf16[64,1024]{1,0:T(8,128)(2,1)S(1)}, bf16[64,1024]{1,0:T(8,128)(2,1)S(1)}, u32[]{:S(2)}, u32[]{:S(2)}) collective-permute-start(bf16[64,1024]{1,0:T(8,128)(2,1)S(1)} %collective-permute-done.24.refs_1_), channel_id=1, source_target_pairs={{0,2},{1,3},{2,0},{3,1},{4,6},{5,7},{6,4},{7,5},{8,10},{9,11},{10,... | collective-permute-start | bytes 393224 | tf_op jit(solution)/shard_map/ppermute | solution.py:271
  97.7 0.9 collective-permute-start.29
  98.6 0.6 output_near.1.refs_5_
  99.2 2.1 %collective-permute-done.26.refs_0_ = bf16[64,1024]{1,0:T(8,128)(2,1)S(1)} collective-permute-done((bf16[64,1024]{1,0:T(8,128)(2,1)S(1)}, bf16[64,1024]{1,0:T(8,128)(2,1)S(1)}, u32[]{:S(2)}, u32[]{:S(2)}) %collective-permute-start.26) | collective-permute-done | bytes 131104 | tf_op jit(solution)/shard_map/ppermute | solution.py:271
  101.3 0.2 collective-permute-done.25.refs_1_
  101.6 1.1 %collective-permute-start.28 = (bf16[64,1024]{1,0:T(8,128)(2,1)S(1)}, bf16[64,1024]{1,0:T(8,128)(2,1)S(1)}, u32[]{:S(2)}, u32[]{:S(2)}) collective-permute-start(bf16[64,1024]{1,0:T(8,128)(2,1)S(1)} %collective-permute-done.26.refs_0_), channel_id=1, source_target_pairs={{0,2},{1,3},{2,0},{3,1},{4,6},{5,7},{6,4},{7,5},{8,10},{9,11},{10,... | collective-permute-start | bytes 393224 | tf_op jit(solution)/shard_map/ppermute | solution.py:271
  102.7 0.1 pad_add_fusion.scalars
  102.8 0.5 output_far.1.refs_6_
  103.3 3.3 %collective-permute-done.28.refs_2_ = bf16[64,1024]{1,0:T(8,128)(2,1)S(1)} collective-permute-done((bf16[64,1024]{1,0:T(8,128)(2,1)S(1)}, bf16[64,1024]{1,0:T(8,128)(2,1)S(1)}, u32[]{:S(2)}, u32[]{:S(2)}) %collective-permute-start.28) | collective-permute-done | bytes 131104 | tf_op jit(solution)/shard_map/ppermute | solution.py:271
  106.5 1.3 %output_other.1 = (f32[128,1024]{1,0:T(8,128)S(1)}, bf16[128,1024]{1,0:T(8,128)(2,1)S(1)}) custom-call(s32[3]{0:T(128)S(1)} %pad_add_fusion.scalars, bf16[64,1024]{1,0:T(8,128)(2,1)S(1)} %collective-permute-done.23.refs_0_, bf16[64,1024]{1,0:T(8,128)(2,1)S(1)} %collective-permute-done.25.refs_1_, bf16[64,1024]{1,0:T(8,128)(2,1)S(1)} %collective-permute-done.28.refs_2_, ...), custom_call_target="tpu_custom_call" | custom-call | tf_op jit(solution)/shard_map/output_other/pallas_call | solution.py:210
  108.6 0.8 collective-permute-done.30
  109.5 0.8 add_convert_fusion
  (47 shorter events, 0.5 us)
Async XLA Ops:
  1.1 19.4 %collective-permute-start.7 = (bf16[480,512]{1,0:T(8,128)(2,1)S(1)}, bf16[480,512]{1,0:T(8,128)(2,1)S(1)}, u32[]{:S(2)}, u32[]{:S(2)}) collective-permute-start(bf16[480,512]{1,0:T(8,128)(2,1)S(1)} %pad_maximum_fusion.refs_8_), channel_id=1, source_target_pairs={{0,12},{1,13},{2,14},{3,15},{4,0},{5,1},{6,2},{7,3},{8,4},{9,5},{1... | collective-permute-start | bytes 1474568 | tf_op jit(solution)/shard_map/ppermute | solution.py:271
  6.2 22.1 %collective-permute-start.6 = (bf16[480,512]{1,0:T(8,128)(2,1)S(1)}, bf16[480,512]{1,0:T(8,128)(2,1)S(1)}, u32[]{:S(2)}, u32[]{:S(2)}) collective-permute-start(bf16[480,512]{1,0:T(8,128)(2,1)S(1)} %pad_maximum_fusion.refs_8_), channel_id=1, source_target_pairs={{0,4},{1,5},{2,6},{3,7},{4,8},{5,9},{6,10},{7,11},{8,12},{9,13},{1... | collective-permute-start | bytes 1474568 | tf_op jit(solution)/shard_map/ppermute | solution.py:271
  6.3 2.1 %copy-start.1 = (bf16[256,7680]{1,0:T(8,128)(2,1)S(1)}, bf16[256,7680]{1,0:T(8,128)(2,1)}, u32[]{:S(2)}) copy-start(bf16[256,7680]{1,0:T(8,128)(2,1)} %rows_ref.3) | copy-start | bytes 11796484
  11.6 18.2 %collective-permute-start.2 = (bf16[128,1920]{1,0:T(8,128)(2,1)}, bf16[128,1920]{1,0:T(8,128)(2,1)S(1)}, u32[]{:S(2)}, u32[]{:S(2)}) collective-permute-start(bf16[128,1920]{1,0:T(8,128)(2,1)} %get-tuple-element.37), channel_id=1, source_target_pairs={{0,18},{1,19},{2,16},{3,17},{4,22},{5,23},{6,20},{7,21},{8,26},{9,... | collective-permute-start | bytes 1474568 | tf_op jit(solution)/shard_map/ppermute | solution.py:271
  14.1 22.0 %collective-permute-start.1 = (bf16[128,1920]{1,0:T(8,128)(2,1)}, bf16[128,1920]{1,0:T(8,128)(2,1)S(1)}, u32[]{:S(2)}, u32[]{:S(2)}) collective-permute-start(bf16[128,1920]{1,0:T(8,128)(2,1)} %get-tuple-element.36), channel_id=1, source_target_pairs={{0,16},{1,17},{2,18},{3,19},{4,20},{5,21},{6,22},{7,23},{8,24},{9,... | collective-permute-start | bytes 1474568 | tf_op jit(solution)/shard_map/ppermute | solution.py:271
  14.6 21.4 %collective-permute-start = (bf16[128,1920]{1,0:T(8,128)(2,1)}, bf16[128,1920]{1,0:T(8,128)(2,1)}, u32[]{:S(2)}, u32[]{:S(2)}) collective-permute-start(bf16[128,1920]{1,0:T(8,128)(2,1)} %get-tuple-element.35), channel_id=1, source_target_pairs={{0,2},{1,3},{2,0},{3,1},{4,6},{5,7},{6,4},{7,5},{8,10},{9,11},{10,... | collective-permute-start | bytes 1474568 | tf_op jit(solution)/shard_map/ppermute | solution.py:271
  15.2 2.1 %copy-start.2 = (bf16[256,7680]{1,0:T(8,128)(2,1)S(1)}, bf16[256,7680]{1,0:T(8,128)(2,1)}, u32[]{:S(2)}) copy-start(bf16[256,7680]{1,0:T(8,128)(2,1)} %rows_ref.3) | copy-start | bytes 11796484
  17.3 2.1 %copy-start.3 = (bf16[256,7680]{1,0:T(8,128)(2,1)S(1)}, bf16[256,7680]{1,0:T(8,128)(2,1)}, u32[]{:S(2)}) copy-start(bf16[256,7680]{1,0:T(8,128)(2,1)} %rows_ref.3) | copy-start | bytes 11796484
  20.5 18.4 %collective-permute-start.8 = (bf16[480,512]{1,0:T(8,128)(2,1)S(1)}, bf16[480,512]{1,0:T(8,128)(2,1)}, u32[]{:S(2)}, u32[]{:S(2)}) collective-permute-start(bf16[480,512]{1,0:T(8,128)(2,1)S(1)} %collective-permute-done.7.refs_10_), channel_id=1, source_target_pairs={{4,0},{5,1},{6,2},{7,3},{8,4},{9,5},{10,6},{11,7},{20,16},{21,17},... | collective-permute-start | bytes 1474568 | tf_op jit(solution)/shard_map/ppermute | solution.py:271
  28.3 10.5 %collective-permute-start.9 = (bf16[480,512]{1,0:T(8,128)(2,1)S(1)}, bf16[480,512]{1,0:T(8,128)(2,1)}, u32[]{:S(2)}, u32[]{:S(2)}) collective-permute-start(bf16[480,512]{1,0:T(8,128)(2,1)S(1)} %collective-permute-done.6.refs_9_), channel_id=1, source_target_pairs={{4,8},{5,9},{6,10},{7,11},{8,12},{9,13},{10,14},{11,15},{20,24},{2... | collective-permute-start | bytes 1474568 | tf_op jit(solution)/shard_map/ppermute | solution.py:271
  29.8 9.1 %collective-permute-start.5 = (bf16[128,1920]{1,0:T(8,128)(2,1)S(1)}, bf16[128,1920]{1,0:T(8,128)(2,1)}, u32[]{:S(2)}, u32[]{:S(2)}) collective-permute-start(bf16[128,1920]{1,0:T(8,128)(2,1)S(1)} %collective-permute-done.2.refs_3_), channel_id=1, source_target_pairs={{0,1},{1,0},{2,3},{3,2},{4,5},{5,4},{6,7},{7,6},{8,9},{9,8},{10,11... | collective-permute-start | bytes 1474568 | tf_op jit(solution)/shard_map/ppermute | solution.py:271
  36.0 2.8 %collective-permute-start.4 = (bf16[128,1920]{1,0:T(8,128)(2,1)S(1)}, bf16[128,1920]{1,0:T(8,128)(2,1)}, u32[]{:S(2)}, u32[]{:S(2)}) collective-permute-start(bf16[128,1920]{1,0:T(8,128)(2,1)S(1)} %collective-permute-done.1.refs_2_), channel_id=1, source_target_pairs={{0,1},{1,0},{2,3},{3,2},{4,5},{5,4},{6,7},{7,6},{8,9},{9,8},{10,11... | collective-permute-start | bytes 1474568 | tf_op jit(solution)/shard_map/ppermute | solution.py:271
  36.0 2.9 %collective-permute-start.3 = (bf16[128,1920]{1,0:T(8,128)(2,1)}, bf16[128,1920]{1,0:T(8,128)(2,1)}, u32[]{:S(2)}, u32[]{:S(2)}) collective-permute-start(bf16[128,1920]{1,0:T(8,128)(2,1)} %collective-permute-done.refs_1_), channel_id=1, source_target_pairs={{0,1},{1,0},{2,3},{3,2},{4,5},{5,4},{6,7},{7,6},{8,9},{9,8},{10,11... | collective-permute-start | bytes 1474568 | tf_op jit(solution)/shard_map/ppermute | solution.py:271
  36.6 30.1 %copy-start.6 = (f32[128]{0:T(128)S(1)}, f32[128]{0:T(128)}, u32[]{:S(2)}) copy-start(f32[128]{0:T(128)} %param.16) | copy-start | bytes 1540
  36.6 36.6 %copy-start.7 = (f32[128]{0:T(128)S(1)}, f32[128]{0:T(128)}, u32[]{:S(2)}) copy-start(f32[128]{0:T(128)} %param.15) | copy-start | bytes 1540
  44.0 0.7 copy-start.4
  44.7 6.5 %collective-permute-start.10 = (bf16[512,128]{1,0:T(8,128)(2,1)S(1)}, bf16[512,128]{1,0:T(8,128)(2,1)S(1)}, u32[]{:S(2)}, u32[]{:S(2)}) collective-permute-start(bf16[512,128]{1,0:T(8,128)(2,1)S(1)} %get-tuple-element.46), channel_id=1, source_target_pairs={{0,2},{1,3},{2,0},{3,1},{4,6},{5,7},{6,4},{7,5},{8,10},{9,11},{10,... | collective-permute-start | bytes 393224 | tf_op jit(solution)/shard_map/ppermute | solution.py:271
  46.2 6.4 %collective-permute-start.11 = (bf16[512,128]{1,0:T(8,128)(2,1)S(1)}, bf16[512,128]{1,0:T(8,128)(2,1)S(1)}, u32[]{:S(2)}, u32[]{:S(2)}) collective-permute-start(bf16[512,128]{1,0:T(8,128)(2,1)S(1)} %get-tuple-element.47), channel_id=1, source_target_pairs={{0,16},{1,17},{2,18},{3,19},{4,20},{5,21},{6,22},{7,23},{8,24},{9,... | collective-permute-start | bytes 393224 | tf_op jit(solution)/shard_map/ppermute | solution.py:271
  47.7 7.4 %collective-permute-start.12 = (bf16[512,128]{1,0:T(8,128)(2,1)S(1)}, bf16[512,128]{1,0:T(8,128)(2,1)S(1)}, u32[]{:S(2)}, u32[]{:S(2)}) collective-permute-start(bf16[512,128]{1,0:T(8,128)(2,1)S(1)} %get-tuple-element.48), channel_id=1, source_target_pairs={{0,18},{1,19},{2,16},{3,17},{4,22},{5,23},{6,20},{7,21},{8,26},{9,... | collective-permute-start | bytes 393224 | tf_op jit(solution)/shard_map/ppermute | solution.py:271
  48.2 16.7 %collective-permute-start.15 = (f32[512,128]{1,0:T(8,128)}, f32[512,128]{1,0:T(8,128)S(1)}, u32[]{:S(2)}, u32[]{:S(2)}) collective-permute-start(f32[512,128]{1,0:T(8,128)} %get-tuple-element.51), channel_id=1, source_target_pairs={{0,2},{1,3},{2,0},{3,1},{4,6},{5,7},{6,4},{7,5},{8,10},{9,11},{10,... | collective-permute-start | bytes 786440 | tf_op jit(solution)/shard_map/ppermute | solution.py:271
  49.7 15.2 %collective-permute-start.16 = (f32[512,128]{1,0:T(8,128)}, f32[512,128]{1,0:T(8,128)S(1)}, u32[]{:S(2)}, u32[]{:S(2)}) collective-permute-start(f32[512,128]{1,0:T(8,128)} %get-tuple-element.53), channel_id=1, source_target_pairs={{0,16},{1,17},{2,18},{3,19},{4,20},{5,21},{6,22},{7,23},{8,24},{9,... | collective-permute-start | bytes 786440 | tf_op jit(solution)/shard_map/ppermute | solution.py:271
  51.2 14.4 %collective-permute-start.17 = (f32[512,128]{1,0:T(8,128)}, f32[512,128]{1,0:T(8,128)S(1)}, u32[]{:S(2)}, u32[]{:S(2)}) collective-permute-start(f32[512,128]{1,0:T(8,128)} %get-tuple-element.55), channel_id=1, source_target_pairs={{0,18},{1,19},{2,16},{3,17},{4,22},{5,23},{6,20},{7,21},{8,26},{9,... | collective-permute-start | bytes 786440 | tf_op jit(solution)/shard_map/ppermute | solution.py:271
  55.1 8.2 %collective-permute-start.13 = (bf16[512,128]{1,0:T(8,128)(2,1)S(1)}, bf16[512,128]{1,0:T(8,128)(2,1)S(1)}, u32[]{:S(2)}, u32[]{:S(2)}) collective-permute-start(bf16[512,128]{1,0:T(8,128)(2,1)S(1)} %add_convert_fusion.1.refs_0_), channel_id=1, source_target_pairs={{0,4},{1,5},{2,6},{3,7},{4,8},{5,9},{6,10},{7,11},{8,12},{9,13},{1... | collective-permute-start | bytes 393224 | tf_op jit(solution)/shard_map/ppermute | solution.py:271
  57.6 41.0 %copy-start = (bf16[2048,1024]{1,0:T(8,128)(2,1)S(1)}, bf16[2048,1024]{1,0:T(8,128)(2,1)}, u32[]{:S(2)}) copy-start(bf16[2048,1024]{1,0:T(8,128)(2,1)} %refs_4_.1) | copy-start | bytes 12582916
  58.7 25.3 %collective-permute-start.22 = (bf16[512,128]{1,0:T(8,128)(2,1)S(1)}, bf16[512,128]{1,0:T(8,128)(2,1)S(1)}, u32[]{:S(2)}, u32[]{:S(2)}) collective-permute-start(bf16[512,128]{1,0:T(8,128)(2,1)S(1)} %add_convert_fusion.1.refs_0_), channel_id=1, source_target_pairs={{0,12},{1,13},{2,14},{3,15},{4,0},{5,1},{6,2},{7,3},{8,4},{9,5},{1... | collective-permute-start | bytes 393224 | tf_op jit(solution)/shard_map/ppermute | solution.py:271
  63.4 9.5 %collective-permute-start.14 = (bf16[32,1024]{1,0:T(8,128)(2,1)S(1)}, bf16[32,1024]{1,0:T(8,128)(2,1)S(1)}, u32[]{:S(2)}, u32[]{:S(2)}) collective-permute-start(bf16[32,1024]{1,0:T(8,128)(2,1)S(1)} %get-tuple-element.49), channel_id=1, source_target_pairs={{0,2},{1,3},{2,0},{3,1},{4,6},{5,7},{6,4},{7,5},{8,10},{9,11},{10,... | collective-permute-start | bytes 196616 | tf_op jit(solution)/shard_map/ppermute | solution.py:271
  66.9 8.3 %collective-permute-start.18 = (bf16[512,128]{1,0:T(8,128)(2,1)S(1)}, bf16[512,128]{1,0:T(8,128)(2,1)S(1)}, u32[]{:S(2)}, u32[]{:S(2)}) collective-permute-start(bf16[512,128]{1,0:T(8,128)(2,1)S(1)} %multiply_convert_fusion.refs_0_), channel_id=1, source_target_pairs={{0,4},{1,5},{2,6},{3,7},{4,8},{5,9},{6,10},{7,11},{8,12},{9,13},{1... | collective-permute-start | bytes 393224 | tf_op jit(solution)/shard_map/ppermute | solution.py:271
  67.9 14.0 %collective-permute-start.19 = (bf16[512,128]{1,0:T(8,128)(2,1)S(1)}, bf16[512,128]{1,0:T(8,128)(2,1)S(1)}, u32[]{:S(2)}, u32[]{:S(2)}) collective-permute-start(bf16[512,128]{1,0:T(8,128)(2,1)S(1)} %multiply_convert_fusion.refs_0_), channel_id=1, source_target_pairs={{0,8},{1,9},{2,10},{3,11},{4,12},{5,13},{6,14},{7,15},{8,0},{9,1},... | collective-permute-start | bytes 393224 | tf_op jit(solution)/shard_map/ppermute | solution.py:271
  71.2 10.7 %collective-permute-start.20 = (bf16[512,128]{1,0:T(8,128)(2,1)S(1)}, bf16[512,128]{1,0:T(8,128)(2,1)S(1)}, u32[]{:S(2)}, u32[]{:S(2)}) collective-permute-start(bf16[512,128]{1,0:T(8,128)(2,1)S(1)} %multiply_convert_fusion.refs_0_), channel_id=1, source_target_pairs={{0,12},{1,13},{2,14},{3,15},{4,0},{5,1},{6,2},{7,3},{8,4},{9,5},{1... | collective-permute-start | bytes 393224 | tf_op jit(solution)/shard_map/ppermute | solution.py:271
  72.9 13.7 %collective-permute-start.21 = (bf16[512,128]{1,0:T(8,128)(2,1)S(1)}, bf16[512,128]{1,0:T(8,128)(2,1)S(1)}, u32[]{:S(2)}, u32[]{:S(2)}) collective-permute-start(bf16[512,128]{1,0:T(8,128)(2,1)S(1)} %add_convert_fusion.1.refs_0_), channel_id=1, source_target_pairs={{0,8},{1,9},{2,10},{3,11},{4,12},{5,13},{6,14},{7,15},{8,0},{9,1},... | collective-permute-start | bytes 393224 | tf_op jit(solution)/shard_map/ppermute | solution.py:271
  87.3 5.0 %collective-permute-start.23 = (bf16[64,1024]{1,0:T(8,128)(2,1)S(1)}, bf16[64,1024]{1,0:T(8,128)(2,1)S(1)}, u32[]{:S(2)}, u32[]{:S(2)}) collective-permute-start(bf16[64,1024]{1,0:T(8,128)(2,1)S(1)} %mix.1.refs_0_), channel_id=1, source_target_pairs={{0,2},{1,3},{2,0},{3,1},{4,6},{5,7},{6,4},{7,5},{8,10},{9,11},{10,... | collective-permute-start | bytes 393224 | tf_op jit(solution)/shard_map/ppermute | solution.py:271
  88.3 8.3 %collective-permute-start.24 = (bf16[64,1024]{1,0:T(8,128)(2,1)S(1)}, bf16[64,1024]{1,0:T(8,128)(2,1)S(1)}, u32[]{:S(2)}, u32[]{:S(2)}) collective-permute-start(bf16[64,1024]{1,0:T(8,128)(2,1)S(1)} %mix.1.refs_0_), channel_id=1, source_target_pairs={{0,4},{1,5},{2,6},{3,7},{4,8},{5,9},{6,10},{7,11},{8,12},{9,13},{1... | collective-permute-start | bytes 393224 | tf_op jit(solution)/shard_map/ppermute | solution.py:271
  89.1 8.6 %collective-permute-start.27 = (bf16[64,1024]{1,0:T(8,128)(2,1)S(1)}, bf16[64,1024]{1,0:T(8,128)(2,1)S(1)}, u32[]{:S(2)}, u32[]{:S(2)}) collective-permute-start(bf16[64,1024]{1,0:T(8,128)(2,1)S(1)} %mix.1.refs_0_), channel_id=1, source_target_pairs={{0,12},{1,13},{2,14},{3,15},{4,0},{5,1},{6,2},{7,3},{8,4},{9,5},{1... | collective-permute-start | bytes 393224 | tf_op jit(solution)/shard_map/ppermute | solution.py:271
  92.1 9.2 %collective-permute-start.26 = (bf16[64,1024]{1,0:T(8,128)(2,1)S(1)}, bf16[64,1024]{1,0:T(8,128)(2,1)S(1)}, u32[]{:S(2)}, u32[]{:S(2)}) collective-permute-start(bf16[64,1024]{1,0:T(8,128)(2,1)S(1)} %mix.1.refs_0_), channel_id=1, source_target_pairs={{0,8},{1,9},{2,10},{3,11},{4,12},{5,13},{6,14},{7,15},{8,0},{9,1},... | collective-permute-start | bytes 393224 | tf_op jit(solution)/shard_map/ppermute | solution.py:271
  96.6 5.0 %collective-permute-start.25 = (bf16[64,1024]{1,0:T(8,128)(2,1)S(1)}, bf16[64,1024]{1,0:T(8,128)(2,1)S(1)}, u32[]{:S(2)}, u32[]{:S(2)}) collective-permute-start(bf16[64,1024]{1,0:T(8,128)(2,1)S(1)} %collective-permute-done.24.refs_1_), channel_id=1, source_target_pairs={{0,2},{1,3},{2,0},{3,1},{4,6},{5,7},{6,4},{7,5},{8,10},{9,11},{10,... | collective-permute-start | bytes 393224 | tf_op jit(solution)/shard_map/ppermute | solution.py:271
  97.7 5.5 %collective-permute-start.29 = (bf16[64,1024]{1,0:T(8,128)(2,1)S(1)}, bf16[64,1024]{1,0:T(8,128)(2,1)S(1)}, u32[]{:S(2)}, u32[]{:S(2)}) collective-permute-start(bf16[64,1024]{1,0:T(8,128)(2,1)S(1)} %collective-permute-done.27.refs_2_), channel_id=1, source_target_pairs={{0,2},{1,3},{2,0},{3,1},{4,6},{5,7},{6,4},{7,5},{8,10},{9,11},{10,... | collective-permute-start | bytes 393224 | tf_op jit(solution)/shard_map/ppermute | solution.py:271
  101.6 5.0 %collective-permute-start.28 = (bf16[64,1024]{1,0:T(8,128)(2,1)S(1)}, bf16[64,1024]{1,0:T(8,128)(2,1)S(1)}, u32[]{:S(2)}, u32[]{:S(2)}) collective-permute-start(bf16[64,1024]{1,0:T(8,128)(2,1)S(1)} %collective-permute-done.26.refs_0_), channel_id=1, source_target_pairs={{0,2},{1,3},{2,0},{3,1},{4,6},{5,7},{6,4},{7,5},{8,10},{9,11},{10,... | collective-permute-start | bytes 393224 | tf_op jit(solution)/shard_map/ppermute | solution.py:271
  103.2 6.2 %copy-start.5 = (bf16[128,1024]{1,0:T(8,128)(2,1)S(1)}, bf16[128,1024]{1,0:T(8,128)(2,1)}, u32[]{:S(2)}) copy-start(bf16[128,1024]{1,0:T(8,128)(2,1)} %param.14) | copy-start | bytes 786436
  107.9 1.6 %collective-permute-start.30 = (bf16[128,1024]{1,0:T(8,128)(2,1)S(1)}, bf16[128,1024]{1,0:T(8,128)(2,1)S(1)}, u32[]{:S(2)}, u32[]{:S(2)}) collective-permute-start(bf16[128,1024]{1,0:T(8,128)(2,1)S(1)} %get-tuple-element.64), channel_id=1, source_target_pairs={{0,1},{1,0},{2,3},{3,2},{4,5},{5,4},{6,7},{7,6},{8,9},{9,8},{10,11... | collective-permute-start | bytes 786440 | tf_op jit(solution)/shard_map/ppermute | solution.py:271

commit v10 on v8

--- a/solution.py
+++ b/solution.py
@@ -51,8 +51,13 @@
 
 def project_kernel(groups, pairs, shifts, scalars, *refs):
     count = groups * 2
-    near, far, slabs = refs[:count], refs[count : 2 * count], refs[2 * count : -2 * count - 1]
-    outs, placed = refs[-2 * count - 1 : -1], refs[-1]
+    near, far, slabs = refs[:count], refs[count : 2 * count], refs[2 * count : -2 * count - 3]
+    outs, placed, held, arrived = refs[-2 * count - 3 : -3], *refs[-3:]
+    copies = [
+        pltpu.make_async_copy(ref, held.at[n], arrived.at[n]) for n, ref in enumerate(far)
+    ]
+    for copy in copies:
+        copy.start()
     half = near[0].shape[0]
     side, place = scalars[0], scalars[1]
     for shift, slab in zip(shifts, slabs):
@@ -67,8 +72,12 @@
                 placed[lax.rem(place + pairs - shift[0], pairs)] = slab[...]
 
     w = jnp.concatenate([placed[z] for z in range(pairs)], axis=0)
-    for part, pieces in enumerate((near, far)):
-        lhs = jnp.concatenate([ref[...] for ref in pieces], axis=0)
+    for part in range(2):
+        if part:
+            for copy in copies:
+                copy.wait()
+        pieces = [held[n] for n in range(count)] if part else [ref[...] for ref in near]
+        lhs = jnp.concatenate(pieces, axis=0)
         result = jnp.dot(lhs, w, preferred_element_type=f32)
         columns = [result[:, n * HEAD_SIZE : (n + 1) * HEAD_SIZE] for n in range(4)]
         for matrix in range(2):
@@ -90,13 +99,19 @@
     vmem = pl.BlockSpec(memory_space=pltpu.VMEM)
     return pl.pallas_call(
         functools.partial(project_kernel, count // 2, pairs, shifts),
-        in_specs=[pl.BlockSpec(memory_space=pltpu.SMEM)] + [vmem] * (2 * count + len(slabs)),
+        in_specs=[pl.BlockSpec(memory_space=pltpu.SMEM)] + [vmem] * count
+        + [pl.BlockSpec(memory_space=pl.ANY)] * count
+        + [vmem] * len(slabs),
         out_specs=[vmem] * (2 * count),
         out_shape=[
             jax.ShapeDtypeStruct((4 * half, HEAD_SIZE), bf16 if k > count else f32)
             for k in range(2 * count)
         ],
-        scratch_shapes=[pltpu.VMEM((pairs,) + slabs[0].shape, bf16)],
+        scratch_shapes=[
+            pltpu.VMEM((pairs,) + slabs[0].shape, bf16),
+            pltpu.VMEM((count,) + near[0].shape, bf16),
+            pltpu.SemaphoreType.DMA((count,)),
+        ],
         compiler_params=pltpu.CompilerParams(vmem_limit_bytes=VMEM_BYTES),
         name="project",
     )(jnp.stack([side, place]).astype(jnp.int32), *near, *far, *slabs)

time: 107 us -> 107 us (level)
  no operation moved by 1% of the time
where the time goes in v10:
time: 107 us
  starting transfers between devices  42.9 us (40%)
  waiting for transfers between devices  36 us (34%)
  Pallas kernels  15.7 us (15%)
  local copies, waits for them, and re-layouts  8.21 us (8%)
  other arithmetic  2.76 us (3%)
    ppermute x31, starting transfers between devices, permute(): return lax.ppermute(array, AXES, perm)  42.9 us
    ppermute x31, waiting for transfers between devices, permute(): return lax.ppermute(array, AXES, perm)  36 us
    unnamed x23, local copies, waits for them, and re-layouts  6.07 us
    pallas_call x3, Pallas kernels, pack(): pl.pallas_call(functools.partial(pack_kernel, groups, pairs, part, count)...  5.32 us
    pallas_call x1, Pallas kernels, project(): pl.pallas_call(functools.partial(project_kernel, count // 2, pairs, shift...  5.23 us
  transfers between devices with their start and end apart: 31, of which 12 were waited for; matrix products, arithmetic and copies ran while one was open for 3% of the time, Pallas kernels for 8%

profile of v10, /device:TPU:0, one launch (start us, length us, event | category | flops | bytes accessed | tf_op | source)
XLA Modules:
  0.0 106.6 jit_solution(12167071199914943480)
XLA Ops:
  0.0 1.1 %constant_dynamic-slice_fusion = (bf16[480,256]{1,0:T(8,128)(2,1)S(1)}, bf16[480,256]{1,0:T(8,128)(2,1)S(1)}) fusion(bf16[960,256]{1,0:T(8,128)(2,1)} %param.12, s32[]{:T(128)S(6)} %select_n.62, bf16[960,256]{1,0:T(8,128)(2,1)} %param.11), kind=kLoop, calls=%fused_computation.22 | loop fusion | bytes 983044 | tf_op jit(solution)/shard_map/dynamic_slice | solution.py:329
  1.1 5.1 %collective-permute-start.7 = (bf16[480,512]{1,0:T(8,128)(2,1)S(1)}, bf16[480,512]{1,0:T(8,128)(2,1)S(1)}, u32[]{:S(2)}, u32[]{:S(2)}) collective-permute-start(bf16[480,512]{1,0:T(8,128)(2,1)S(1)} %pad_maximum_fusion.refs_8_), channel_id=1, source_target_pairs={{0,12},{1,13},{2,14},{3,15},{4,0},{5,1},{6,2},{7,3},{8,4},{9,5},{1... | collective-permute-start | bytes 1474568 | tf_op jit(solution)/shard_map/ppermute | solution.py:286
  6.2 0.1 pad_add_fusion.2.index_ref
  6.3 2.1 %copy-done.1 = bf16[256,7680]{1,0:T(8,128)(2,1)S(1)} copy-done((bf16[256,7680]{1,0:T(8,128)(2,1)S(1)}, bf16[256,7680]{1,0:T(8,128)(2,1)}, u32[]{:S(2)}) %copy-start.1) | copy-done | bytes 3932184
  8.4 3.2 %pack_sends.1 = (bf16[128,1920]{1,0:T(8,128)(2,1)}, bf16[128,1920]{1,0:T(8,128)(2,1)}, bf16[128,1920]{1,0:T(8,128)(2,1)}) custom-call(s32[4]{0:T(128)S(1)} %pad_add_fusion.2.index_ref, bf16[256,7680]{1,0:T(8,128)(2,1)S(1)} %copy-done.1), custom_call_target="tpu_custom_call" | custom-call | tf_op jit(solution)/shard_map/pack_sends/pallas_call | solution.py:38
  11.6 2.5 %collective-permute-start.2 = (bf16[128,1920]{1,0:T(8,128)(2,1)}, bf16[128,1920]{1,0:T(8,128)(2,1)S(1)}, u32[]{:S(2)}, u32[]{:S(2)}) collective-permute-start(bf16[128,1920]{1,0:T(8,128)(2,1)} %get-tuple-element.36), channel_id=1, source_target_pairs={{0,18},{1,19},{2,16},{3,17},{4,22},{5,23},{6,20},{7,21},{8,26},{9,... | collective-permute-start | bytes 1474568 | tf_op jit(solution)/shard_map/ppermute | solution.py:286
  14.1 0.5 collective-permute-start.1
  14.6 0.5 collective-permute-start
  15.1 0.1 pad_add_fusion.1
  15.2 2.1 %copy-done.2 = bf16[256,7680]{1,0:T(8,128)(2,1)S(1)} copy-done((bf16[256,7680]{1,0:T(8,128)(2,1)S(1)}, bf16[256,7680]{1,0:T(8,128)(2,1)}, u32[]{:S(2)}) %copy-start.2) | copy-done | bytes 3932184
  17.3 1.1 %pack_near.1.refs_0_ = bf16[128,1920]{1,0:T(8,128)(2,1)S(1)} custom-call(s32[2]{0:T(128)S(1)} %get-tuple-element.68.index_ref, bf16[256,7680]{1,0:T(8,128)(2,1)S(1)} %copy-done.2), custom_call_target="tpu_custom_call" | custom-call | tf_op jit(solution)/shard_map/pack_near/pallas_call | solution.py:38
  18.4 1.0 copy-done.3
  19.4 1.1 %pack_far.1.refs_4_ = bf16[128,1920]{1,0:T(8,128)(2,1)S(1)} custom-call(s32[2]{0:T(128)S(1)} %get-tuple-element.67.index_ref, bf16[256,7680]{1,0:T(8,128)(2,1)S(1)} %copy-done.3), custom_call_target="tpu_custom_call" | custom-call | tf_op jit(solution)/shard_map/pack_far/pallas_call | solution.py:38
  20.5 1.3 %collective-permute-start.8 = (bf16[480,512]{1,0:T(8,128)(2,1)S(1)}, bf16[480,512]{1,0:T(8,128)(2,1)}, u32[]{:S(2)}, u32[]{:S(2)}) collective-permute-start(bf16[480,512]{1,0:T(8,128)(2,1)S(1)} %collective-permute-done.7.refs_10_), channel_id=1, source_target_pairs={{4,0},{5,1},{6,2},{7,3},{8,4},{9,5},{10,6},{11,7},{20,16},{21,17},... | collective-permute-start | bytes 1474568 | tf_op jit(solution)/shard_map/ppermute | solution.py:286
  21.8 6.5 %collective-permute-done.6.refs_9_ = bf16[480,512]{1,0:T(8,128)(2,1)S(1)} collective-permute-done((bf16[480,512]{1,0:T(8,128)(2,1)S(1)}, bf16[480,512]{1,0:T(8,128)(2,1)S(1)}, u32[]{:S(2)}, u32[]{:S(2)}) %collective-permute-start.6) | collective-permute-done | bytes 491552 | tf_op jit(solution)/shard_map/ppermute | solution.py:286
  28.3 1.4 %collective-permute-start.9 = (bf16[480,512]{1,0:T(8,128)(2,1)S(1)}, bf16[480,512]{1,0:T(8,128)(2,1)}, u32[]{:S(2)}, u32[]{:S(2)}) collective-permute-start(bf16[480,512]{1,0:T(8,128)(2,1)S(1)} %collective-permute-done.6.refs_9_), channel_id=1, source_target_pairs={{4,8},{5,9},{6,10},{7,11},{8,12},{9,13},{10,14},{11,15},{20,24},{2... | collective-permute-start | bytes 1474568 | tf_op jit(solution)/shard_map/ppermute | solution.py:286
  29.8 6.3 %collective-permute-done.1.refs_2_ = bf16[128,1920]{1,0:T(8,128)(2,1)S(1)} collective-permute-done((bf16[128,1920]{1,0:T(8,128)(2,1)}, bf16[128,1920]{1,0:T(8,128)(2,1)S(1)}, u32[]{:S(2)}, u32[]{:S(2)}) %collective-permute-start.1) | collective-permute-done | bytes 491552 | tf_op jit(solution)/shard_map/ppermute | solution.py:286
  36.0 0.5 collective-permute-start.3
  36.6 0.1 pad_add_fusion.3.scalars
  36.6 2.2 %collective-permute-done.8.refs_11_ = bf16[480,512]{1,0:T(8,128)(2,1)} collective-permute-done((bf16[480,512]{1,0:T(8,128)(2,1)S(1)}, bf16[480,512]{1,0:T(8,128)(2,1)}, u32[]{:S(2)}, u32[]{:S(2)}) %collective-permute-start.8) | collective-permute-done | bytes 491552 | tf_op jit(solution)/shard_map/ppermute | solution.py:286
  38.9 0.1 collective-permute-done.3.refs_5_
  39.0 5.2 %project.1 = (f32[512,128]{1,0:T(8,128)S(1)}, f32[512,128]{1,0:T(8,128)}, f32[512,128]{1,0:T(8,128)}, f32[512,128]{1,0:T(8,128)}, f32[512,128]{1,0:T(8,128)S(1)}...) custom-call(s32[2]{0:T(128)S(1)} %pad_add_fusion.3.scalars, ...), custom_call_target="tpu_custom_call" | custom-call | tf_op jit(solution)/shard_map/project/pallas_call | solution.py:100
  44.2 0.7 copy-done.4
  44.9 1.5 %collective-permute-start.10 = (bf16[512,128]{1,0:T(8,128)(2,1)S(1)}, bf16[512,128]{1,0:T(8,128)(2,1)S(1)}, u32[]{:S(2)}, u32[]{:S(2)}) collective-permute-start(bf16[512,128]{1,0:T(8,128)(2,1)S(1)} %get-tuple-element.45), channel_id=1, source_target_pairs={{0,2},{1,3},{2,0},{3,1},{4,6},{5,7},{6,4},{7,5},{8,10},{9,11},{10,... | collective-permute-start | bytes 393224 | tf_op jit(solution)/shard_map/ppermute | solution.py:286
  46.4 1.5 %collective-permute-start.11 = (bf16[512,128]{1,0:T(8,128)(2,1)S(1)}, bf16[512,128]{1,0:T(8,128)(2,1)S(1)}, u32[]{:S(2)}, u32[]{:S(2)}) collective-permute-start(bf16[512,128]{1,0:T(8,128)(2,1)S(1)} %get-tuple-element.46), channel_id=1, source_target_pairs={{0,16},{1,17},{2,18},{3,19},{4,20},{5,21},{6,22},{7,23},{8,24},{9,... | collective-permute-start | bytes 393224 | tf_op jit(solution)/shard_map/ppermute | solution.py:286
  47.9 0.5 collective-permute-start.12
  48.4 1.5 %collective-permute-start.15 = (f32[512,128]{1,0:T(8,128)}, f32[512,128]{1,0:T(8,128)S(1)}, u32[]{:S(2)}, u32[]{:S(2)}) collective-permute-start(f32[512,128]{1,0:T(8,128)} %get-tuple-element.50), channel_id=1, source_target_pairs={{0,2},{1,3},{2,0},{3,1},{4,6},{5,7},{6,4},{7,5},{8,10},{9,11},{10,... | collective-permute-start | bytes 786440 | tf_op jit(solution)/shard_map/ppermute | solution.py:286
  49.9 1.5 %collective-permute-start.16 = (f32[512,128]{1,0:T(8,128)}, f32[512,128]{1,0:T(8,128)S(1)}, u32[]{:S(2)}, u32[]{:S(2)}) collective-permute-start(f32[512,128]{1,0:T(8,128)} %get-tuple-element.52), channel_id=1, source_target_pairs={{0,16},{1,17},{2,18},{3,19},{4,20},{5,21},{6,22},{7,23},{8,24},{9,... | collective-permute-start | bytes 786440 | tf_op jit(solution)/shard_map/ppermute | solution.py:286
  51.4 1.4 %collective-permute-start.17 = (f32[512,128]{1,0:T(8,128)}, f32[512,128]{1,0:T(8,128)S(1)}, u32[]{:S(2)}, u32[]{:S(2)}) collective-permute-start(f32[512,128]{1,0:T(8,128)} %get-tuple-element.54), channel_id=1, source_target_pairs={{0,18},{1,19},{2,16},{3,17},{4,22},{5,23},{6,20},{7,21},{8,26},{9,... | collective-permute-start | bytes 786440 | tf_op jit(solution)/shard_map/ppermute | solution.py:286
  52.8 2.4 %collective-permute-done.12 = bf16[512,128]{1,0:T(8,128)(2,1)S(1)} collective-permute-done((bf16[512,128]{1,0:T(8,128)(2,1)S(1)}, bf16[512,128]{1,0:T(8,128)(2,1)S(1)}, u32[]{:S(2)}, u32[]{:S(2)}) %collective-permute-start.12) | collective-permute-done | bytes 131104 | tf_op jit(solution)/shard_map/ppermute | solution.py:286
  55.2 0.1 add_convert_fusion.1.refs_0_
  55.3 2.5 %collective-permute-start.13 = (bf16[512,128]{1,0:T(8,128)(2,1)S(1)}, bf16[512,128]{1,0:T(8,128)(2,1)S(1)}, u32[]{:S(2)}, u32[]{:S(2)}) collective-permute-start(bf16[512,128]{1,0:T(8,128)(2,1)S(1)} %add_convert_fusion.1.refs_0_), channel_id=1, source_target_pairs={{0,4},{1,5},{2,6},{3,7},{4,8},{5,9},{6,10},{7,11},{8,12},{9,13},{1... | collective-permute-start | bytes 393224 | tf_op jit(solution)/shard_map/ppermute | solution.py:286
  57.8 1.0 constant_dynamic-slice_fusion.3
  58.8 3.4 %collective-permute-start.21 = (bf16[512,128]{1,0:T(8,128)(2,1)S(1)}, bf16[512,128]{1,0:T(8,128)(2,1)S(1)}, u32[]{:S(2)}, u32[]{:S(2)}) collective-permute-start(bf16[512,128]{1,0:T(8,128)(2,1)S(1)} %add_convert_fusion.1.refs_0_), channel_id=1, source_target_pairs={{0,8},{1,9},{2,10},{3,11},{4,12},{5,13},{6,14},{7,15},{8,0},{9,1},... | collective-permute-start | bytes 393224 | tf_op jit(solution)/shard_map/ppermute | solution.py:286
  62.2 1.9 %collective-permute-done.13.refs_1_ = bf16[512,128]{1,0:T(8,128)(2,1)S(1)} collective-permute-done((bf16[512,128]{1,0:T(8,128)(2,1)S(1)}, bf16[512,128]{1,0:T(8,128)(2,1)S(1)}, u32[]{:S(2)}, u32[]{:S(2)}) %collective-permute-start.13) | collective-permute-done | bytes 131104 | tf_op jit(solution)/shard_map/ppermute | solution.py:286
  64.1 2.9 %collective-permute-start.22 = (bf16[512,128]{1,0:T(8,128)(2,1)S(1)}, bf16[512,128]{1,0:T(8,128)(2,1)S(1)}, u32[]{:S(2)}, u32[]{:S(2)}) collective-permute-start(bf16[512,128]{1,0:T(8,128)(2,1)S(1)} %add_convert_fusion.1.refs_0_), channel_id=1, source_target_pairs={{0,12},{1,13},{2,14},{3,15},{4,0},{5,1},{6,2},{7,3},{8,4},{9,5},{1... | collective-permute-start | bytes 393224 | tf_op jit(solution)/shard_map/ppermute | solution.py:286
  67.1 1.1 %collective-permute-start.14 = (bf16[32,1024]{1,0:T(8,128)(2,1)S(1)}, bf16[32,1024]{1,0:T(8,128)(2,1)S(1)}, u32[]{:S(2)}, u32[]{:S(2)}) collective-permute-start(bf16[32,1024]{1,0:T(8,128)(2,1)S(1)} %get-tuple-element.48), channel_id=1, source_target_pairs={{0,2},{1,3},{2,0},{3,1},{4,6},{5,7},{6,4},{7,5},{8,10},{9,11},{10,... | collective-permute-start | bytes 196616 | tf_op jit(solution)/shard_map/ppermute | solution.py:286
  68.2 1.1 %multiply_reduce_fusion = (f32[512]{0:T(512)S(1)}, f32[512,128]{1,0:T(8,128)S(1)}) fusion(f32[512,128]{1,0:T(8,128)S(1)} %collective-permute-done.17, f32[512,128]{1,0:T(8,128)S(1)} %collective-permute-done.16, f32[512,128]{1,0:T(8,128)} %copy-done.4, f32[512,128]{1,0:T(8,128)S(1)} %collective-permute-done.15), kind=kLoop, calls=%fused_computation.8 | loop fusion | flops 327168 | bytes 1312768 | tf_op jit(solution)/shard_map/reduce_sum | solution.py:247
  69.3 0.1 multiply_convert_fusion.refs_0_
  69.5 1.8 %collective-permute-start.19 = (bf16[512,128]{1,0:T(8,128)(2,1)S(1)}, bf16[512,128]{1,0:T(8,128)(2,1)S(1)}, u32[]{:S(2)}, u32[]{:S(2)}) collective-permute-start(bf16[512,128]{1,0:T(8,128)(2,1)S(1)} %multiply_convert_fusion.refs_0_), channel_id=1, source_target_pairs={{0,8},{1,9},{2,10},{3,11},{4,12},{5,13},{6,14},{7,15},{8,0},{9,1},... | collective-permute-start | bytes 393224 | tf_op jit(solution)/shard_map/ppermute | solution.py:286
  71.3 2.0 %collective-permute-start.20 = (bf16[512,128]{1,0:T(8,128)(2,1)S(1)}, bf16[512,128]{1,0:T(8,128)(2,1)S(1)}, u32[]{:S(2)}, u32[]{:S(2)}) collective-permute-start(bf16[512,128]{1,0:T(8,128)(2,1)S(1)} %multiply_convert_fusion.refs_0_), channel_id=1, source_target_pairs={{0,12},{1,13},{2,14},{3,15},{4,0},{5,1},{6,2},{7,3},{8,4},{9,5},{1... | collective-permute-start | bytes 393224 | tf_op jit(solution)/shard_map/ppermute | solution.py:286
  73.5 0.1 fusion
  73.7 0.1 fusion.2.q_ref
  73.8 2.8 %collective-permute-done.18.refs_1_ = bf16[512,128]{1,0:T(8,128)(2,1)S(1)} collective-permute-done((bf16[512,128]{1,0:T(8,128)(2,1)S(1)}, bf16[512,128]{1,0:T(8,128)(2,1)S(1)}, u32[]{:S(2)}, u32[]{:S(2)}) %collective-permute-start.18) | collective-permute-done | bytes 131104 | tf_op jit(solution)/shard_map/ppermute | solution.py:286
  76.6 3.1 %collective-permute-done.19.refs_2_ = bf16[512,128]{1,0:T(8,128)(2,1)S(1)} collective-permute-done((bf16[512,128]{1,0:T(8,128)(2,1)S(1)}, bf16[512,128]{1,0:T(8,128)(2,1)S(1)}, u32[]{:S(2)}, u32[]{:S(2)}) %collective-permute-start.19) | collective-permute-done | bytes 131104 | tf_op jit(solution)/shard_map/ppermute | solution.py:286
  79.7 2.0 %score.1 = (bf16[512,2048]{1,0:T(8,128)(2,1)S(1)}, f32[512,128]{1,0:T(8,128)S(1)}) custom-call(bf16[512,128]{1,0:T(8,128)(2,1)S(1)} %fusion.2.q_ref, bf16[512,128]{1,0:T(8,128)(2,1)S(1)} %multiply_convert_fusion.refs_0_, bf16[512,128]{1,0:T(8,128)(2,1)S(1)} %collective-permute-done.18.refs_1_, bf16[512,128]{1,0:T(8,128)(2,1)S(1)} %collective-permute-done.19.refs_2_, ...), custom_call_target="tpu_custom_call" | custom-call | tf_op jit(solution)/shard_map/score/pallas_call | solution.py:146
  81.8 0.7 mix.1.refs_0_
  82.5 1.0 collective-permute-start.23
  83.5 2.0 %collective-permute-start.24 = (bf16[64,1024]{1,0:T(8,128)(2,1)S(1)}, bf16[64,1024]{1,0:T(8,128)(2,1)S(1)}, u32[]{:S(2)}, u32[]{:S(2)}) collective-permute-start(bf16[64,1024]{1,0:T(8,128)(2,1)S(1)} %mix.1.refs_0_), channel_id=1, source_target_pairs={{0,4},{1,5},{2,6},{3,7},{4,8},{5,9},{6,10},{7,11},{8,12},{9,13},{1... | collective-permute-start | bytes 393224 | tf_op jit(solution)/shard_map/ppermute | solution.py:286
  85.5 2.1 %collective-permute-start.27 = (bf16[64,1024]{1,0:T(8,128)(2,1)S(1)}, bf16[64,1024]{1,0:T(8,128)(2,1)S(1)}, u32[]{:S(2)}, u32[]{:S(2)}) collective-permute-start(bf16[64,1024]{1,0:T(8,128)(2,1)S(1)} %mix.1.refs_0_), channel_id=1, source_target_pairs={{0,12},{1,13},{2,14},{3,15},{4,0},{5,1},{6,2},{7,3},{8,4},{9,5},{1... | collective-permute-start | bytes 393224 | tf_op jit(solution)/shard_map/ppermute | solution.py:286
  87.6 0.6 collective-permute-start.26
  88.2 3.9 %collective-permute-done.24.refs_1_ = bf16[64,1024]{1,0:T(8,128)(2,1)S(1)} collective-permute-done((bf16[64,1024]{1,0:T(8,128)(2,1)S(1)}, bf16[64,1024]{1,0:T(8,128)(2,1)S(1)}, u32[]{:S(2)}, u32[]{:S(2)}) %collective-permute-start.24) | collective-permute-done | bytes 131104 | tf_op jit(solution)/shard_map/ppermute | solution.py:286
  92.1 1.1 %collective-permute-start.25 = (bf16[64,1024]{1,0:T(8,128)(2,1)S(1)}, bf16[64,1024]{1,0:T(8,128)(2,1)S(1)}, u32[]{:S(2)}, u32[]{:S(2)}) collective-permute-start(bf16[64,1024]{1,0:T(8,128)(2,1)S(1)} %collective-permute-done.24.refs_1_), channel_id=1, source_target_pairs={{0,2},{1,3},{2,0},{3,1},{4,6},{5,7},{6,4},{7,5},{8,10},{9,11},{10,... | collective-permute-start | bytes 393224 | tf_op jit(solution)/shard_map/ppermute | solution.py:286
  93.2 0.9 collective-permute-start.29
  94.1 0.6 output_near.1.refs_5_
  94.7 3.1 %collective-permute-done.26.refs_0_ = bf16[64,1024]{1,0:T(8,128)(2,1)S(1)} collective-permute-done((bf16[64,1024]{1,0:T(8,128)(2,1)S(1)}, bf16[64,1024]{1,0:T(8,128)(2,1)S(1)}, u32[]{:S(2)}, u32[]{:S(2)}) %collective-permute-start.26) | collective-permute-done | bytes 131104 | tf_op jit(solution)/shard_map/ppermute | solution.py:286
  97.8 1.7 %collective-permute-start.28 = (bf16[64,1024]{1,0:T(8,128)(2,1)S(1)}, bf16[64,1024]{1,0:T(8,128)(2,1)S(1)}, u32[]{:S(2)}, u32[]{:S(2)}) collective-permute-start(bf16[64,1024]{1,0:T(8,128)(2,1)S(1)} %collective-permute-done.26.refs_0_), channel_id=1, source_target_pairs={{0,2},{1,3},{2,0},{3,1},{4,6},{5,7},{6,4},{7,5},{8,10},{9,11},{10,... | collective-permute-start | bytes 393224 | tf_op jit(solution)/shard_map/ppermute | solution.py:286
  99.5 0.1 pad_add_fusion.scalars
  99.6 0.5 output_far.1.refs_6_
  100.1 2.7 %collective-permute-done.28.refs_2_ = bf16[64,1024]{1,0:T(8,128)(2,1)S(1)} collective-permute-done((bf16[64,1024]{1,0:T(8,128)(2,1)S(1)}, bf16[64,1024]{1,0:T(8,128)(2,1)S(1)}, u32[]{:S(2)}, u32[]{:S(2)}) %collective-permute-start.28) | collective-permute-done | bytes 131104 | tf_op jit(solution)/shard_map/ppermute | solution.py:286
  102.8 1.3 %output_other.1 = (f32[128,1024]{1,0:T(8,128)S(1)}, bf16[128,1024]{1,0:T(8,128)(2,1)S(1)}) custom-call(s32[3]{0:T(128)S(1)} %pad_add_fusion.scalars, bf16[64,1024]{1,0:T(8,128)(2,1)S(1)} %collective-permute-done.23.refs_0_, bf16[64,1024]{1,0:T(8,128)(2,1)S(1)} %collective-permute-done.25.refs_1_, bf16[64,1024]{1,0:T(8,128)(2,1)S(1)} %collective-permute-done.28.refs_2_, ...), custom_call_target="tpu_custom_call" | custom-call | tf_op jit(solution)/shard_map/output_other/pallas_call | solution.py:225
  104.2 0.1 collective-permute-start.30
  104.9 0.8 collective-permute-done.30
  105.8 0.8 add_convert_fusion
  (47 shorter events, 0.4 us)
Async XLA Ops:
  1.1 19.4 %collective-permute-start.7 = (bf16[480,512]{1,0:T(8,128)(2,1)S(1)}, bf16[480,512]{1,0:T(8,128)(2,1)S(1)}, u32[]{:S(2)}, u32[]{:S(2)}) collective-permute-start(bf16[480,512]{1,0:T(8,128)(2,1)S(1)} %pad_maximum_fusion.refs_8_), channel_id=1, source_target_pairs={{0,12},{1,13},{2,14},{3,15},{4,0},{5,1},{6,2},{7,3},{8,4},{9,5},{1... | collective-permute-start | bytes 1474568 | tf_op jit(solution)/shard_map/ppermute | solution.py:286
  6.2 22.1 %collective-permute-start.6 = (bf16[480,512]{1,0:T(8,128)(2,1)S(1)}, bf16[480,512]{1,0:T(8,128)(2,1)S(1)}, u32[]{:S(2)}, u32[]{:S(2)}) collective-permute-start(bf16[480,512]{1,0:T(8,128)(2,1)S(1)} %pad_maximum_fusion.refs_8_), channel_id=1, source_target_pairs={{0,4},{1,5},{2,6},{3,7},{4,8},{5,9},{6,10},{7,11},{8,12},{9,13},{1... | collective-permute-start | bytes 1474568 | tf_op jit(solution)/shard_map/ppermute | solution.py:286
  6.3 2.1 %copy-start.1 = (bf16[256,7680]{1,0:T(8,128)(2,1)S(1)}, bf16[256,7680]{1,0:T(8,128)(2,1)}, u32[]{:S(2)}) copy-start(bf16[256,7680]{1,0:T(8,128)(2,1)} %rows_ref.3) | copy-start | bytes 11796484
  11.6 18.2 %collective-permute-start.2 = (bf16[128,1920]{1,0:T(8,128)(2,1)}, bf16[128,1920]{1,0:T(8,128)(2,1)S(1)}, u32[]{:S(2)}, u32[]{:S(2)}) collective-permute-start(bf16[128,1920]{1,0:T(8,128)(2,1)} %get-tuple-element.36), channel_id=1, source_target_pairs={{0,18},{1,19},{2,16},{3,17},{4,22},{5,23},{6,20},{7,21},{8,26},{9,... | collective-permute-start | bytes 1474568 | tf_op jit(solution)/shard_map/ppermute | solution.py:286
  14.1 22.0 %collective-permute-start.1 = (bf16[128,1920]{1,0:T(8,128)(2,1)}, bf16[128,1920]{1,0:T(8,128)(2,1)S(1)}, u32[]{:S(2)}, u32[]{:S(2)}) collective-permute-start(bf16[128,1920]{1,0:T(8,128)(2,1)} %get-tuple-element.35), channel_id=1, source_target_pairs={{0,16},{1,17},{2,18},{3,19},{4,20},{5,21},{6,22},{7,23},{8,24},{9,... | collective-permute-start | bytes 1474568 | tf_op jit(solution)/shard_map/ppermute | solution.py:286
  14.6 21.4 %collective-permute-start = (bf16[128,1920]{1,0:T(8,128)(2,1)}, bf16[128,1920]{1,0:T(8,128)(2,1)}, u32[]{:S(2)}, u32[]{:S(2)}) collective-permute-start(bf16[128,1920]{1,0:T(8,128)(2,1)} %get-tuple-element.34), channel_id=1, source_target_pairs={{0,2},{1,3},{2,0},{3,1},{4,6},{5,7},{6,4},{7,5},{8,10},{9,11},{10,... | collective-permute-start | bytes 1474568 | tf_op jit(solution)/shard_map/ppermute | solution.py:286
  15.2 2.1 %copy-start.2 = (bf16[256,7680]{1,0:T(8,128)(2,1)S(1)}, bf16[256,7680]{1,0:T(8,128)(2,1)}, u32[]{:S(2)}) copy-start(bf16[256,7680]{1,0:T(8,128)(2,1)} %rows_ref.3) | copy-start | bytes 11796484
  17.3 2.1 %copy-start.3 = (bf16[256,7680]{1,0:T(8,128)(2,1)S(1)}, bf16[256,7680]{1,0:T(8,128)(2,1)}, u32[]{:S(2)}) copy-start(bf16[256,7680]{1,0:T(8,128)(2,1)} %rows_ref.3) | copy-start | bytes 11796484
  20.5 18.4 %collective-permute-start.8 = (bf16[480,512]{1,0:T(8,128)(2,1)S(1)}, bf16[480,512]{1,0:T(8,128)(2,1)}, u32[]{:S(2)}, u32[]{:S(2)}) collective-permute-start(bf16[480,512]{1,0:T(8,128)(2,1)S(1)} %collective-permute-done.7.refs_10_), channel_id=1, source_target_pairs={{4,0},{5,1},{6,2},{7,3},{8,4},{9,5},{10,6},{11,7},{20,16},{21,17},... | collective-permute-start | bytes 1474568 | tf_op jit(solution)/shard_map/ppermute | solution.py:286
  28.3 10.5 %collective-permute-start.9 = (bf16[480,512]{1,0:T(8,128)(2,1)S(1)}, bf16[480,512]{1,0:T(8,128)(2,1)}, u32[]{:S(2)}, u32[]{:S(2)}) collective-permute-start(bf16[480,512]{1,0:T(8,128)(2,1)S(1)} %collective-permute-done.6.refs_9_), channel_id=1, source_target_pairs={{4,8},{5,9},{6,10},{7,11},{8,12},{9,13},{10,14},{11,15},{20,24},{2... | collective-permute-start | bytes 1474568 | tf_op jit(solution)/shard_map/ppermute | solution.py:286
  29.8 9.1 %collective-permute-start.5 = (bf16[128,1920]{1,0:T(8,128)(2,1)S(1)}, bf16[128,1920]{1,0:T(8,128)(2,1)}, u32[]{:S(2)}, u32[]{:S(2)}) collective-permute-start(bf16[128,1920]{1,0:T(8,128)(2,1)S(1)} %collective-permute-done.2.refs_3_), channel_id=1, source_target_pairs={{0,1},{1,0},{2,3},{3,2},{4,5},{5,4},{6,7},{7,6},{8,9},{9,8},{10,11... | collective-permute-start | bytes 1474568 | tf_op jit(solution)/shard_map/ppermute | solution.py:286
  36.0 2.8 %collective-permute-start.4 = (bf16[128,1920]{1,0:T(8,128)(2,1)S(1)}, bf16[128,1920]{1,0:T(8,128)(2,1)}, u32[]{:S(2)}, u32[]{:S(2)}) collective-permute-start(bf16[128,1920]{1,0:T(8,128)(2,1)S(1)} %collective-permute-done.1.refs_2_), channel_id=1, source_target_pairs={{0,1},{1,0},{2,3},{3,2},{4,5},{5,4},{6,7},{7,6},{8,9},{9,8},{10,11... | collective-permute-start | bytes 1474568 | tf_op jit(solution)/shard_map/ppermute | solution.py:286
  36.0 2.9 %collective-permute-start.3 = (bf16[128,1920]{1,0:T(8,128)(2,1)}, bf16[128,1920]{1,0:T(8,128)(2,1)}, u32[]{:S(2)}, u32[]{:S(2)}) collective-permute-start(bf16[128,1920]{1,0:T(8,128)(2,1)} %collective-permute-done.refs_1_), channel_id=1, source_target_pairs={{0,1},{1,0},{2,3},{3,2},{4,5},{5,4},{6,7},{7,6},{8,9},{9,8},{10,11... | collective-permute-start | bytes 1474568 | tf_op jit(solution)/shard_map/ppermute | solution.py:286
  36.6 32.7 %copy-start.6 = (f32[128]{0:T(128)S(1)}, f32[128]{0:T(128)}, u32[]{:S(2)}) copy-start(f32[128]{0:T(128)} %param.16) | copy-start | bytes 1540
  36.6 37.0 %copy-start.7 = (f32[128]{0:T(128)S(1)}, f32[128]{0:T(128)}, u32[]{:S(2)}) copy-start(f32[128]{0:T(128)} %param.15) | copy-start | bytes 1540
  44.2 0.7 copy-start.4
  44.9 6.5 %collective-permute-start.10 = (bf16[512,128]{1,0:T(8,128)(2,1)S(1)}, bf16[512,128]{1,0:T(8,128)(2,1)S(1)}, u32[]{:S(2)}, u32[]{:S(2)}) collective-permute-start(bf16[512,128]{1,0:T(8,128)(2,1)S(1)} %get-tuple-element.45), channel_id=1, source_target_pairs={{0,2},{1,3},{2,0},{3,1},{4,6},{5,7},{6,4},{7,5},{8,10},{9,11},{10,... | collective-permute-start | bytes 393224 | tf_op jit(solution)/shard_map/ppermute | solution.py:286
  46.4 6.4 %collective-permute-start.11 = (bf16[512,128]{1,0:T(8,128)(2,1)S(1)}, bf16[512,128]{1,0:T(8,128)(2,1)S(1)}, u32[]{:S(2)}, u32[]{:S(2)}) collective-permute-start(bf16[512,128]{1,0:T(8,128)(2,1)S(1)} %get-tuple-element.46), channel_id=1, source_target_pairs={{0,16},{1,17},{2,18},{3,19},{4,20},{5,21},{6,22},{7,23},{8,24},{9,... | collective-permute-start | bytes 393224 | tf_op jit(solution)/shard_map/ppermute | solution.py:286
  47.9 7.4 %collective-permute-start.12 = (bf16[512,128]{1,0:T(8,128)(2,1)S(1)}, bf16[512,128]{1,0:T(8,128)(2,1)S(1)}, u32[]{:S(2)}, u32[]{:S(2)}) collective-permute-start(bf16[512,128]{1,0:T(8,128)(2,1)S(1)} %get-tuple-element.47), channel_id=1, source_target_pairs={{0,18},{1,19},{2,16},{3,17},{4,22},{5,23},{6,20},{7,21},{8,26},{9,... | collective-permute-start | bytes 393224 | tf_op jit(solution)/shard_map/ppermute | solution.py:286
  48.4 18.7 %collective-permute-start.15 = (f32[512,128]{1,0:T(8,128)}, f32[512,128]{1,0:T(8,128)S(1)}, u32[]{:S(2)}, u32[]{:S(2)}) collective-permute-start(f32[512,128]{1,0:T(8,128)} %get-tuple-element.50), channel_id=1, source_target_pairs={{0,2},{1,3},{2,0},{3,1},{4,6},{5,7},{6,4},{7,5},{8,10},{9,11},{10,... | collective-permute-start | bytes 786440 | tf_op jit(solution)/shard_map/ppermute | solution.py:286
  49.9 18.3 %collective-permute-start.16 = (f32[512,128]{1,0:T(8,128)}, f32[512,128]{1,0:T(8,128)S(1)}, u32[]{:S(2)}, u32[]{:S(2)}) collective-permute-start(f32[512,128]{1,0:T(8,128)} %get-tuple-element.52), channel_id=1, source_target_pairs={{0,16},{1,17},{2,18},{3,19},{4,20},{5,21},{6,22},{7,23},{8,24},{9,... | collective-permute-start | bytes 786440 | tf_op jit(solution)/shard_map/ppermute | solution.py:286
  51.4 16.8 %collective-permute-start.17 = (f32[512,128]{1,0:T(8,128)}, f32[512,128]{1,0:T(8,128)S(1)}, u32[]{:S(2)}, u32[]{:S(2)}) collective-permute-start(f32[512,128]{1,0:T(8,128)} %get-tuple-element.54), channel_id=1, source_target_pairs={{0,18},{1,19},{2,16},{3,17},{4,22},{5,23},{6,20},{7,21},{8,26},{9,... | collective-permute-start | bytes 786440 | tf_op jit(solution)/shard_map/ppermute | solution.py:286
  55.3 8.8 %collective-permute-start.13 = (bf16[512,128]{1,0:T(8,128)(2,1)S(1)}, bf16[512,128]{1,0:T(8,128)(2,1)S(1)}, u32[]{:S(2)}, u32[]{:S(2)}) collective-permute-start(bf16[512,128]{1,0:T(8,128)(2,1)S(1)} %add_convert_fusion.1.refs_0_), channel_id=1, source_target_pairs={{0,4},{1,5},{2,6},{3,7},{4,8},{5,9},{6,10},{7,11},{8,12},{9,13},{1... | collective-permute-start | bytes 393224 | tf_op jit(solution)/shard_map/ppermute | solution.py:286
  57.8 36.3 %copy-start = (bf16[2048,1024]{1,0:T(8,128)(2,1)S(1)}, bf16[2048,1024]{1,0:T(8,128)(2,1)}, u32[]{:S(2)}) copy-start(bf16[2048,1024]{1,0:T(8,128)(2,1)} %refs_4_.1) | copy-start | bytes 12582916
  58.8 22.9 %collective-permute-start.21 = (bf16[512,128]{1,0:T(8,128)(2,1)S(1)}, bf16[512,128]{1,0:T(8,128)(2,1)S(1)}, u32[]{:S(2)}, u32[]{:S(2)}) collective-permute-start(bf16[512,128]{1,0:T(8,128)(2,1)S(1)} %add_convert_fusion.1.refs_0_), channel_id=1, source_target_pairs={{0,8},{1,9},{2,10},{3,11},{4,12},{5,13},{6,14},{7,15},{8,0},{9,1},... | collective-permute-start | bytes 393224 | tf_op jit(solution)/shard_map/ppermute | solution.py:286
  64.1 17.6 %collective-permute-start.22 = (bf16[512,128]{1,0:T(8,128)(2,1)S(1)}, bf16[512,128]{1,0:T(8,128)(2,1)S(1)}, u32[]{:S(2)}, u32[]{:S(2)}) collective-permute-start(bf16[512,128]{1,0:T(8,128)(2,1)S(1)} %add_convert_fusion.1.refs_0_), channel_id=1, source_target_pairs={{0,12},{1,13},{2,14},{3,15},{4,0},{5,1},{6,2},{7,3},{8,4},{9,5},{1... | collective-permute-start | bytes 393224 | tf_op jit(solution)/shard_map/ppermute | solution.py:286
  67.1 4.3 %collective-permute-start.14 = (bf16[32,1024]{1,0:T(8,128)(2,1)S(1)}, bf16[32,1024]{1,0:T(8,128)(2,1)S(1)}, u32[]{:S(2)}, u32[]{:S(2)}) collective-permute-start(bf16[32,1024]{1,0:T(8,128)(2,1)S(1)} %get-tuple-element.48), channel_id=1, source_target_pairs={{0,2},{1,3},{2,0},{3,1},{4,6},{5,7},{6,4},{7,5},{8,10},{9,11},{10,... | collective-permute-start | bytes 196616 | tf_op jit(solution)/shard_map/ppermute | solution.py:286
  69.4 7.1 %collective-permute-start.18 = (bf16[512,128]{1,0:T(8,128)(2,1)S(1)}, bf16[512,128]{1,0:T(8,128)(2,1)S(1)}, u32[]{:S(2)}, u32[]{:S(2)}) collective-permute-start(bf16[512,128]{1,0:T(8,128)(2,1)S(1)} %multiply_convert_fusion.refs_0_), channel_id=1, source_target_pairs={{0,4},{1,5},{2,6},{3,7},{4,8},{5,9},{6,10},{7,11},{8,12},{9,13},{1... | collective-permute-start | bytes 393224 | tf_op jit(solution)/shard_map/ppermute | solution.py:286
  69.5 10.2 %collective-permute-start.19 = (bf16[512,128]{1,0:T(8,128)(2,1)S(1)}, bf16[512,128]{1,0:T(8,128)(2,1)S(1)}, u32[]{:S(2)}, u32[]{:S(2)}) collective-permute-start(bf16[512,128]{1,0:T(8,128)(2,1)S(1)} %multiply_convert_fusion.refs_0_), channel_id=1, source_target_pairs={{0,8},{1,9},{2,10},{3,11},{4,12},{5,13},{6,14},{7,15},{8,0},{9,1},... | collective-permute-start | bytes 393224 | tf_op jit(solution)/shard_map/ppermute | solution.py:286
  71.3 8.4 %collective-permute-start.20 = (bf16[512,128]{1,0:T(8,128)(2,1)S(1)}, bf16[512,128]{1,0:T(8,128)(2,1)S(1)}, u32[]{:S(2)}, u32[]{:S(2)}) collective-permute-start(bf16[512,128]{1,0:T(8,128)(2,1)S(1)} %multiply_convert_fusion.refs_0_), channel_id=1, source_target_pairs={{0,12},{1,13},{2,14},{3,15},{4,0},{5,1},{6,2},{7,3},{8,4},{9,5},{1... | collective-permute-start | bytes 393224 | tf_op jit(solution)/shard_map/ppermute | solution.py:286
  82.5 5.7 %collective-permute-start.23 = (bf16[64,1024]{1,0:T(8,128)(2,1)S(1)}, bf16[64,1024]{1,0:T(8,128)(2,1)S(1)}, u32[]{:S(2)}, u32[]{:S(2)}) collective-permute-start(bf16[64,1024]{1,0:T(8,128)(2,1)S(1)} %mix.1.refs_0_), channel_id=1, source_target_pairs={{0,2},{1,3},{2,0},{3,1},{4,6},{5,7},{6,4},{7,5},{8,10},{9,11},{10,... | collective-permute-start | bytes 393224 | tf_op jit(solution)/shard_map/ppermute | solution.py:286
  83.5 8.6 %collective-permute-start.24 = (bf16[64,1024]{1,0:T(8,128)(2,1)S(1)}, bf16[64,1024]{1,0:T(8,128)(2,1)S(1)}, u32[]{:S(2)}, u32[]{:S(2)}) collective-permute-start(bf16[64,1024]{1,0:T(8,128)(2,1)S(1)} %mix.1.refs_0_), channel_id=1, source_target_pairs={{0,4},{1,5},{2,6},{3,7},{4,8},{5,9},{6,10},{7,11},{8,12},{9,13},{1... | collective-permute-start | bytes 393224 | tf_op jit(solution)/shard_map/ppermute | solution.py:286
  85.5 7.7 %collective-permute-start.27 = (bf16[64,1024]{1,0:T(8,128)(2,1)S(1)}, bf16[64,1024]{1,0:T(8,128)(2,1)S(1)}, u32[]{:S(2)}, u32[]{:S(2)}) collective-permute-start(bf16[64,1024]{1,0:T(8,128)(2,1)S(1)} %mix.1.refs_0_), channel_id=1, source_target_pairs={{0,12},{1,13},{2,14},{3,15},{4,0},{5,1},{6,2},{7,3},{8,4},{9,5},{1... | collective-permute-start | bytes 393224 | tf_op jit(solution)/shard_map/ppermute | solution.py:286
  87.6 10.2 %collective-permute-start.26 = (bf16[64,1024]{1,0:T(8,128)(2,1)S(1)}, bf16[64,1024]{1,0:T(8,128)(2,1)S(1)}, u32[]{:S(2)}, u32[]{:S(2)}) collective-permute-start(bf16[64,1024]{1,0:T(8,128)(2,1)S(1)} %mix.1.refs_0_), channel_id=1, source_target_pairs={{0,8},{1,9},{2,10},{3,11},{4,12},{5,13},{6,14},{7,15},{8,0},{9,1},... | collective-permute-start | bytes 393224 | tf_op jit(solution)/shard_map/ppermute | solution.py:286
  92.1 5.8 %collective-permute-start.25 = (bf16[64,1024]{1,0:T(8,128)(2,1)S(1)}, bf16[64,1024]{1,0:T(8,128)(2,1)S(1)}, u32[]{:S(2)}, u32[]{:S(2)}) collective-permute-start(bf16[64,1024]{1,0:T(8,128)(2,1)S(1)} %collective-permute-done.24.refs_1_), channel_id=1, source_target_pairs={{0,2},{1,3},{2,0},{3,1},{4,6},{5,7},{6,4},{7,5},{8,10},{9,11},{10,... | collective-permute-start | bytes 393224 | tf_op jit(solution)/shard_map/ppermute | solution.py:286
  93.2 6.9 %collective-permute-start.29 = (bf16[64,1024]{1,0:T(8,128)(2,1)S(1)}, bf16[64,1024]{1,0:T(8,128)(2,1)S(1)}, u32[]{:S(2)}, u32[]{:S(2)}) collective-permute-start(bf16[64,1024]{1,0:T(8,128)(2,1)S(1)} %collective-permute-done.27.refs_2_), channel_id=1, source_target_pairs={{0,2},{1,3},{2,0},{3,1},{4,6},{5,7},{6,4},{7,5},{8,10},{9,11},{10,... | collective-permute-start | bytes 393224 | tf_op jit(solution)/shard_map/ppermute | solution.py:286
  97.8 5.0 %collective-permute-start.28 = (bf16[64,1024]{1,0:T(8,128)(2,1)S(1)}, bf16[64,1024]{1,0:T(8,128)(2,1)S(1)}, u32[]{:S(2)}, u32[]{:S(2)}) collective-permute-start(bf16[64,1024]{1,0:T(8,128)(2,1)S(1)} %collective-permute-done.26.refs_0_), channel_id=1, source_target_pairs={{0,2},{1,3},{2,0},{3,1},{4,6},{5,7},{6,4},{7,5},{8,10},{9,11},{10,... | collective-permute-start | bytes 393224 | tf_op jit(solution)/shard_map/ppermute | solution.py:286
  100.1 5.7 %copy-start.5 = (bf16[128,1024]{1,0:T(8,128)(2,1)S(1)}, bf16[128,1024]{1,0:T(8,128)(2,1)}, u32[]{:S(2)}) copy-start(bf16[128,1024]{1,0:T(8,128)(2,1)} %param.14) | copy-start | bytes 786436
  104.2 1.6 %collective-permute-start.30 = (bf16[128,1024]{1,0:T(8,128)(2,1)S(1)}, bf16[128,1024]{1,0:T(8,128)(2,1)S(1)}, u32[]{:S(2)}, u32[]{:S(2)}) collective-permute-start(bf16[128,1024]{1,0:T(8,128)(2,1)S(1)} %get-tuple-element.62), channel_id=1, source_target_pairs={{0,1},{1,0},{2,3},{3,2},{4,5},{5,4},{6,7},{7,6},{8,9},{9,8},{10,11... | collective-permute-start | bytes 786440 | tf_op jit(solution)/shard_map/ppermute | solution.py:286

commit v11 on v8

--- a/solution.py
+++ b/solution.py
@@ -348,7 +348,7 @@
     key_parts = scatter(key_pieces)
     values = sum_up(value_pieces[0], value_parts).astype(bf16)
     all_values = all_pairs(values)
-    key_parts = [after(k, all_values[1]) for k in key_parts]
+    key_parts = [after(k, all_values[1], all_values[-1]) for k in key_parts]
     q_recv = plane_shift(after(q_send, all_values[1]), 0, 1)
     q_pair = jnp.where(
         side == 0,

time: 107 us -> 108 us (level)
  waiting for transfers between devices: 36 us -> 38.3 us
  starting transfers between devices: 43 us -> 41.7 us
    ppermute x31, waiting for transfers between devices: 36 us -> 38.3 us  [permute(): return lax.ppermute(array, AXES, perm)]
    ppermute x31, starting transfers between devices: 43 us -> 41.7 us  [permute(): return lax.ppermute(array, AXES, perm)]
  transfers between devices with their start and end apart: 31 -> 31, of which waited for: 12 -> 14; matrix products, arithmetic and copies ran while one was open for 3% -> 3% of each run, Pallas kernels for 8% -> 8%
where the time goes in v11:
time: 108 us; the launch traced here: 107 us
  starting transfers between devices  41.7 us (39%)
  waiting for transfers between devices  38.3 us (35%)
  Pallas kernels  15.5 us (14%)
  local copies, waits for them, and re-layouts  7.51 us (7%)
  other arithmetic  2.76 us (3%)
    ppermute x31, starting transfers between devices, permute(): return lax.ppermute(array, AXES, perm)  41.7 us
    ppermute x31, waiting for transfers between devices, permute(): return lax.ppermute(array, AXES, perm)  38.3 us
    unnamed x23, local copies, waits for them, and re-layouts  5.37 us
    pallas_call x3, Pallas kernels, pack(): pl.pallas_call(functools.partial(pack_kernel, groups, pairs, part, count)...  5.32 us
    pallas_call x1, Pallas kernels, project(): pl.pallas_call(functools.partial(project_kernel, count // 2, pairs, shift...  5.07 us
  transfers between devices with their start and end apart: 31, of which 14 were waited for; matrix products, arithmetic and copies ran while one was open for 3% of the time, Pallas kernels for 8%

profile of v11, /device:TPU:0, one launch (start us, length us, event | category | flops | bytes accessed | tf_op | source)
XLA Modules:
  0.0 106.8 jit_solution(4677803074199771053)
XLA Ops:
  0.0 1.1 %constant_dynamic-slice_fusion = (bf16[480,256]{1,0:T(8,128)(2,1)S(1)}, bf16[480,256]{1,0:T(8,128)(2,1)S(1)}) fusion(bf16[960,256]{1,0:T(8,128)(2,1)} %param.12, s32[]{:T(128)S(6)} %select_n.62, bf16[960,256]{1,0:T(8,128)(2,1)} %param.11), kind=kLoop, calls=%fused_computation.22 | loop fusion | bytes 983044 | tf_op jit(solution)/shard_map/dynamic_slice | solution.py:314
  1.1 5.1 %collective-permute-start.7 = (bf16[480,512]{1,0:T(8,128)(2,1)S(1)}, bf16[480,512]{1,0:T(8,128)(2,1)S(1)}, u32[]{:S(2)}, u32[]{:S(2)}) collective-permute-start(bf16[480,512]{1,0:T(8,128)(2,1)S(1)} %pad_maximum_fusion.refs_8_), channel_id=1, source_target_pairs={{0,12},{1,13},{2,14},{3,15},{4,0},{5,1},{6,2},{7,3},{8,4},{9,5},{1... | collective-permute-start | bytes 1474568 | tf_op jit(solution)/shard_map/ppermute | solution.py:271
  6.2 0.1 pad_add_fusion.2.index_ref
  6.3 2.1 %copy-done.1 = bf16[256,7680]{1,0:T(8,128)(2,1)S(1)} copy-done((bf16[256,7680]{1,0:T(8,128)(2,1)S(1)}, bf16[256,7680]{1,0:T(8,128)(2,1)}, u32[]{:S(2)}) %copy-start.1) | copy-done | bytes 3932184
  8.4 3.2 %pack_sends.1 = (bf16[128,1920]{1,0:T(8,128)(2,1)}, bf16[128,1920]{1,0:T(8,128)(2,1)}, bf16[128,1920]{1,0:T(8,128)(2,1)}) custom-call(s32[4]{0:T(128)S(1)} %pad_add_fusion.2.index_ref, bf16[256,7680]{1,0:T(8,128)(2,1)S(1)} %copy-done.1), custom_call_target="tpu_custom_call" | custom-call | tf_op jit(solution)/shard_map/pack_sends/pallas_call | solution.py:38
  11.6 2.5 %collective-permute-start.2 = (bf16[128,1920]{1,0:T(8,128)(2,1)}, bf16[128,1920]{1,0:T(8,128)(2,1)S(1)}, u32[]{:S(2)}, u32[]{:S(2)}) collective-permute-start(bf16[128,1920]{1,0:T(8,128)(2,1)} %get-tuple-element.36), channel_id=1, source_target_pairs={{0,18},{1,19},{2,16},{3,17},{4,22},{5,23},{6,20},{7,21},{8,26},{9,... | collective-permute-start | bytes 1474568 | tf_op jit(solution)/shard_map/ppermute | solution.py:271
  14.1 0.5 collective-permute-start.1
  14.6 0.5 collective-permute-start
  15.1 0.1 pad_add_fusion.1
  15.2 2.1 %copy-done.2 = bf16[256,7680]{1,0:T(8,128)(2,1)S(1)} copy-done((bf16[256,7680]{1,0:T(8,128)(2,1)S(1)}, bf16[256,7680]{1,0:T(8,128)(2,1)}, u32[]{:S(2)}) %copy-start.2) | copy-done | bytes 3932184
  17.3 1.1 %pack_near.1.refs_0_ = bf16[128,1920]{1,0:T(8,128)(2,1)S(1)} custom-call(s32[2]{0:T(128)S(1)} %get-tuple-element.68.index_ref, bf16[256,7680]{1,0:T(8,128)(2,1)S(1)} %copy-done.2), custom_call_target="tpu_custom_call" | custom-call | tf_op jit(solution)/shard_map/pack_near/pallas_call | solution.py:38
  18.4 1.0 copy-done.3
  19.4 1.1 %pack_far.1.refs_4_ = bf16[128,1920]{1,0:T(8,128)(2,1)S(1)} custom-call(s32[2]{0:T(128)S(1)} %get-tuple-element.67.index_ref, bf16[256,7680]{1,0:T(8,128)(2,1)S(1)} %copy-done.3), custom_call_target="tpu_custom_call" | custom-call | tf_op jit(solution)/shard_map/pack_far/pallas_call | solution.py:38
  20.5 1.3 %collective-permute-start.8 = (bf16[480,512]{1,0:T(8,128)(2,1)S(1)}, bf16[480,512]{1,0:T(8,128)(2,1)}, u32[]{:S(2)}, u32[]{:S(2)}) collective-permute-start(bf16[480,512]{1,0:T(8,128)(2,1)S(1)} %collective-permute-done.7.refs_10_), channel_id=1, source_target_pairs={{4,0},{5,1},{6,2},{7,3},{8,4},{9,5},{10,6},{11,7},{20,16},{21,17},... | collective-permute-start | bytes 1474568 | tf_op jit(solution)/shard_map/ppermute | solution.py:271
  21.8 6.5 %collective-permute-done.6.refs_9_ = bf16[480,512]{1,0:T(8,128)(2,1)S(1)} collective-permute-done((bf16[480,512]{1,0:T(8,128)(2,1)S(1)}, bf16[480,512]{1,0:T(8,128)(2,1)S(1)}, u32[]{:S(2)}, u32[]{:S(2)}) %collective-permute-start.6) | collective-permute-done | bytes 491552 | tf_op jit(solution)/shard_map/ppermute | solution.py:271
  28.3 1.4 %collective-permute-start.9 = (bf16[480,512]{1,0:T(8,128)(2,1)S(1)}, bf16[480,512]{1,0:T(8,128)(2,1)}, u32[]{:S(2)}, u32[]{:S(2)}) collective-permute-start(bf16[480,512]{1,0:T(8,128)(2,1)S(1)} %collective-permute-done.6.refs_9_), channel_id=1, source_target_pairs={{4,8},{5,9},{6,10},{7,11},{8,12},{9,13},{10,14},{11,15},{20,24},{2... | collective-permute-start | bytes 1474568 | tf_op jit(solution)/shard_map/ppermute | solution.py:271
  29.8 6.3 %collective-permute-done.1.refs_2_ = bf16[128,1920]{1,0:T(8,128)(2,1)S(1)} collective-permute-done((bf16[128,1920]{1,0:T(8,128)(2,1)}, bf16[128,1920]{1,0:T(8,128)(2,1)S(1)}, u32[]{:S(2)}, u32[]{:S(2)}) %collective-permute-start.1) | collective-permute-done | bytes 491552 | tf_op jit(solution)/shard_map/ppermute | solution.py:271
  36.0 0.5 collective-permute-start.3
  36.6 0.1 pad_add_fusion.3.scalars
  36.6 2.2 %collective-permute-done.8.refs_11_ = bf16[480,512]{1,0:T(8,128)(2,1)} collective-permute-done((bf16[480,512]{1,0:T(8,128)(2,1)S(1)}, bf16[480,512]{1,0:T(8,128)(2,1)}, u32[]{:S(2)}, u32[]{:S(2)}) %collective-permute-start.8) | collective-permute-done | bytes 491552 | tf_op jit(solution)/shard_map/ppermute | solution.py:271
  38.9 0.1 collective-permute-done.3.refs_5_
  39.0 5.1 %project.1 = (f32[512,128]{1,0:T(8,128)S(1)}, f32[512,128]{1,0:T(8,128)}, f32[512,128]{1,0:T(8,128)}, f32[512,128]{1,0:T(8,128)}, f32[512,128]{1,0:T(8,128)S(1)}...) custom-call(s32[2]{0:T(128)S(1)} %pad_add_fusion.3.scalars, ...), custom_call_target="tpu_custom_call" | custom-call | tf_op jit(solution)/shard_map/project/pallas_call | solution.py:91
  44.0 1.5 %collective-permute-start.10 = (bf16[512,128]{1,0:T(8,128)(2,1)S(1)}, bf16[512,128]{1,0:T(8,128)(2,1)S(1)}, u32[]{:S(2)}, u32[]{:S(2)}) collective-permute-start(bf16[512,128]{1,0:T(8,128)(2,1)S(1)} %get-tuple-element.45), channel_id=1, source_target_pairs={{0,2},{1,3},{2,0},{3,1},{4,6},{5,7},{6,4},{7,5},{8,10},{9,11},{10,... | collective-permute-start | bytes 393224 | tf_op jit(solution)/shard_map/ppermute | solution.py:271
  45.5 1.5 %collective-permute-start.11 = (bf16[512,128]{1,0:T(8,128)(2,1)S(1)}, bf16[512,128]{1,0:T(8,128)(2,1)S(1)}, u32[]{:S(2)}, u32[]{:S(2)}) collective-permute-start(bf16[512,128]{1,0:T(8,128)(2,1)S(1)} %get-tuple-element.46), channel_id=1, source_target_pairs={{0,16},{1,17},{2,18},{3,19},{4,20},{5,21},{6,22},{7,23},{8,24},{9,... | collective-permute-start | bytes 393224 | tf_op jit(solution)/shard_map/ppermute | solution.py:271
  47.0 0.5 collective-permute-start.12
  47.5 1.5 %collective-permute-start.15 = (f32[512,128]{1,0:T(8,128)}, f32[512,128]{1,0:T(8,128)S(1)}, u32[]{:S(2)}, u32[]{:S(2)}) collective-permute-start(f32[512,128]{1,0:T(8,128)} %get-tuple-element.50), channel_id=1, source_target_pairs={{0,2},{1,3},{2,0},{3,1},{4,6},{5,7},{6,4},{7,5},{8,10},{9,11},{10,... | collective-permute-start | bytes 786440 | tf_op jit(solution)/shard_map/ppermute | solution.py:271
  49.0 1.5 %collective-permute-start.17 = (f32[512,128]{1,0:T(8,128)}, f32[512,128]{1,0:T(8,128)S(1)}, u32[]{:S(2)}, u32[]{:S(2)}) collective-permute-start(f32[512,128]{1,0:T(8,128)} %get-tuple-element.52), channel_id=1, source_target_pairs={{0,16},{1,17},{2,18},{3,19},{4,20},{5,21},{6,22},{7,23},{8,24},{9,... | collective-permute-start | bytes 786440 | tf_op jit(solution)/shard_map/ppermute | solution.py:271
  50.5 1.4 %collective-permute-start.18 = (f32[512,128]{1,0:T(8,128)}, f32[512,128]{1,0:T(8,128)S(1)}, u32[]{:S(2)}, u32[]{:S(2)}) collective-permute-start(f32[512,128]{1,0:T(8,128)} %get-tuple-element.54), channel_id=1, source_target_pairs={{0,18},{1,19},{2,16},{3,17},{4,22},{5,23},{6,20},{7,21},{8,26},{9,... | collective-permute-start | bytes 786440 | tf_op jit(solution)/shard_map/ppermute | solution.py:271
  51.9 2.4 %collective-permute-done.12 = bf16[512,128]{1,0:T(8,128)(2,1)S(1)} collective-permute-done((bf16[512,128]{1,0:T(8,128)(2,1)S(1)}, bf16[512,128]{1,0:T(8,128)(2,1)S(1)}, u32[]{:S(2)}, u32[]{:S(2)}) %collective-permute-start.12) | collective-permute-done | bytes 131104 | tf_op jit(solution)/shard_map/ppermute | solution.py:271
  54.4 0.1 add_convert_fusion.1.refs_0_
  54.4 2.5 %collective-permute-start.13 = (bf16[512,128]{1,0:T(8,128)(2,1)S(1)}, bf16[512,128]{1,0:T(8,128)(2,1)S(1)}, u32[]{:S(2)}, u32[]{:S(2)}) collective-permute-start(bf16[512,128]{1,0:T(8,128)(2,1)S(1)} %add_convert_fusion.1.refs_0_), channel_id=1, source_target_pairs={{0,4},{1,5},{2,6},{3,7},{4,8},{5,9},{6,10},{7,11},{8,12},{9,13},{1... | collective-permute-start | bytes 393224 | tf_op jit(solution)/shard_map/ppermute | solution.py:271
  56.9 2.8 %collective-permute-start.16 = (bf16[512,128]{1,0:T(8,128)(2,1)S(1)}, bf16[512,128]{1,0:T(8,128)(2,1)S(1)}, u32[]{:S(2)}, u32[]{:S(2)}) collective-permute-start(bf16[512,128]{1,0:T(8,128)(2,1)S(1)} %add_convert_fusion.1.refs_0_), channel_id=1, source_target_pairs={{0,12},{1,13},{2,14},{3,15},{4,0},{5,1},{6,2},{7,3},{8,4},{9,5},{1... | collective-permute-start | bytes 393224 | tf_op jit(solution)/shard_map/ppermute | solution.py:271
  59.7 1.0 constant_dynamic-slice_fusion.3
  60.8 2.5 %collective-permute-done.13.refs_1_ = bf16[512,128]{1,0:T(8,128)(2,1)S(1)} collective-permute-done((bf16[512,128]{1,0:T(8,128)(2,1)S(1)}, bf16[512,128]{1,0:T(8,128)(2,1)S(1)}, u32[]{:S(2)}, u32[]{:S(2)}) %collective-permute-start.13) | collective-permute-done | bytes 131104 | tf_op jit(solution)/shard_map/ppermute | solution.py:271
  63.3 3.9 %collective-permute-start.22 = (bf16[512,128]{1,0:T(8,128)(2,1)S(1)}, bf16[512,128]{1,0:T(8,128)(2,1)S(1)}, u32[]{:S(2)}, u32[]{:S(2)}) collective-permute-start(bf16[512,128]{1,0:T(8,128)(2,1)S(1)} %add_convert_fusion.1.refs_0_), channel_id=1, source_target_pairs={{0,8},{1,9},{2,10},{3,11},{4,12},{5,13},{6,14},{7,15},{8,0},{9,1},... | collective-permute-start | bytes 393224 | tf_op jit(solution)/shard_map/ppermute | solution.py:271
  67.1 0.9 collective-permute-start.14
  68.1 1.1 %multiply_reduce_fusion = (f32[512]{0:T(512)S(1)}, f32[512,128]{1,0:T(8,128)S(1)}) fusion(f32[512,128]{1,0:T(8,128)S(1)} %collective-permute-done.18, f32[512,128]{1,0:T(8,128)S(1)} %collective-permute-done.17, f32[512,128]{1,0:T(8,128)} %copy-done.4, f32[512,128]{1,0:T(8,128)S(1)} %collective-permute-done.15), kind=kLoop, calls=%fused_computation.8 | loop fusion | flops 327168 | bytes 1312768 | tf_op jit(solution)/shard_map/reduce_sum | solution.py:232
  69.2 0.1 multiply_convert_fusion.refs_0_
  69.4 1.0 collective-permute-start.20
  70.4 2.8 %collective-permute-start.21 = (bf16[512,128]{1,0:T(8,128)(2,1)S(1)}, bf16[512,128]{1,0:T(8,128)(2,1)S(1)}, u32[]{:S(2)}, u32[]{:S(2)}) collective-permute-start(bf16[512,128]{1,0:T(8,128)(2,1)S(1)} %multiply_convert_fusion.refs_0_), channel_id=1, source_target_pairs={{0,12},{1,13},{2,14},{3,15},{4,0},{5,1},{6,2},{7,3},{8,4},{9,5},{1... | collective-permute-start | bytes 393224 | tf_op jit(solution)/shard_map/ppermute | solution.py:271
  73.4 0.1 fusion
  73.6 0.1 fusion.2.q_ref
  73.7 2.7 %collective-permute-done.19.refs_1_ = bf16[512,128]{1,0:T(8,128)(2,1)S(1)} collective-permute-done((bf16[512,128]{1,0:T(8,128)(2,1)S(1)}, bf16[512,128]{1,0:T(8,128)(2,1)S(1)}, u32[]{:S(2)}, u32[]{:S(2)}) %collective-permute-start.19) | collective-permute-done | bytes 131104 | tf_op jit(solution)/shard_map/ppermute | solution.py:271
  76.4 4.6 %collective-permute-done.20.refs_2_ = bf16[512,128]{1,0:T(8,128)(2,1)S(1)} collective-permute-done((bf16[512,128]{1,0:T(8,128)(2,1)S(1)}, bf16[512,128]{1,0:T(8,128)(2,1)S(1)}, u32[]{:S(2)}, u32[]{:S(2)}) %collective-permute-start.20) | collective-permute-done | bytes 131104 | tf_op jit(solution)/shard_map/ppermute | solution.py:271
  81.0 2.0 %score.1 = (bf16[512,2048]{1,0:T(8,128)(2,1)S(1)}, f32[512,128]{1,0:T(8,128)S(1)}) custom-call(bf16[512,128]{1,0:T(8,128)(2,1)S(1)} %fusion.2.q_ref, bf16[512,128]{1,0:T(8,128)(2,1)S(1)} %multiply_convert_fusion.refs_0_, bf16[512,128]{1,0:T(8,128)(2,1)S(1)} %collective-permute-done.19.refs_1_, bf16[512,128]{1,0:T(8,128)(2,1)S(1)} %collective-permute-done.20.refs_2_, ...), custom_call_target="tpu_custom_call" | custom-call | tf_op jit(solution)/shard_map/score/pallas_call | solution.py:131
  83.1 0.7 mix.1.refs_0_
  83.8 1.0 collective-permute-start.23
  84.8 2.3 %collective-permute-start.24 = (bf16[64,1024]{1,0:T(8,128)(2,1)S(1)}, bf16[64,1024]{1,0:T(8,128)(2,1)S(1)}, u32[]{:S(2)}, u32[]{:S(2)}) collective-permute-start(bf16[64,1024]{1,0:T(8,128)(2,1)S(1)} %mix.1.refs_0_), channel_id=1, source_target_pairs={{0,4},{1,5},{2,6},{3,7},{4,8},{5,9},{6,10},{7,11},{8,12},{9,13},{1... | collective-permute-start | bytes 393224 | tf_op jit(solution)/shard_map/ppermute | solution.py:271
  87.1 1.5 %collective-permute-start.27 = (bf16[64,1024]{1,0:T(8,128)(2,1)S(1)}, bf16[64,1024]{1,0:T(8,128)(2,1)S(1)}, u32[]{:S(2)}, u32[]{:S(2)}) collective-permute-start(bf16[64,1024]{1,0:T(8,128)(2,1)S(1)} %mix.1.refs_0_), channel_id=1, source_target_pairs={{0,12},{1,13},{2,14},{3,15},{4,0},{5,1},{6,2},{7,3},{8,4},{9,5},{1... | collective-permute-start | bytes 393224 | tf_op jit(solution)/shard_map/ppermute | solution.py:271
  88.6 0.2 collective-permute-done.23.refs_0_
  88.8 4.2 %collective-permute-done.24.refs_1_ = bf16[64,1024]{1,0:T(8,128)(2,1)S(1)} collective-permute-done((bf16[64,1024]{1,0:T(8,128)(2,1)S(1)}, bf16[64,1024]{1,0:T(8,128)(2,1)S(1)}, u32[]{:S(2)}, u32[]{:S(2)}) %collective-permute-start.24) | collective-permute-done | bytes 131104 | tf_op jit(solution)/shard_map/ppermute | solution.py:271
  93.0 1.1 %collective-permute-start.25 = (bf16[64,1024]{1,0:T(8,128)(2,1)S(1)}, bf16[64,1024]{1,0:T(8,128)(2,1)S(1)}, u32[]{:S(2)}, u32[]{:S(2)}) collective-permute-start(bf16[64,1024]{1,0:T(8,128)(2,1)S(1)} %collective-permute-done.24.refs_1_), channel_id=1, source_target_pairs={{0,2},{1,3},{2,0},{3,1},{4,6},{5,7},{6,4},{7,5},{8,10},{9,11},{10,... | collective-permute-start | bytes 393224 | tf_op jit(solution)/shard_map/ppermute | solution.py:271
  94.1 0.9 collective-permute-start.29
  95.0 0.6 output_near.1.refs_5_
  95.6 2.5 %collective-permute-done.26.refs_0_ = bf16[64,1024]{1,0:T(8,128)(2,1)S(1)} collective-permute-done((bf16[64,1024]{1,0:T(8,128)(2,1)S(1)}, bf16[64,1024]{1,0:T(8,128)(2,1)S(1)}, u32[]{:S(2)}, u32[]{:S(2)}) %collective-permute-start.26) | collective-permute-done | bytes 131104 | tf_op jit(solution)/shard_map/ppermute | solution.py:271
  98.1 1.1 %collective-permute-start.28 = (bf16[64,1024]{1,0:T(8,128)(2,1)S(1)}, bf16[64,1024]{1,0:T(8,128)(2,1)S(1)}, u32[]{:S(2)}, u32[]{:S(2)}) collective-permute-start(bf16[64,1024]{1,0:T(8,128)(2,1)S(1)} %collective-permute-done.26.refs_0_), channel_id=1, source_target_pairs={{0,2},{1,3},{2,0},{3,1},{4,6},{5,7},{6,4},{7,5},{8,10},{9,11},{10,... | collective-permute-start | bytes 393224 | tf_op jit(solution)/shard_map/ppermute | solution.py:271
  99.2 0.1 pad_add_fusion.scalars
  99.3 0.5 output_far.1.refs_6_
  99.7 0.3 collective-permute-done.29.refs_3_
  100.0 3.0 %collective-permute-done.28.refs_2_ = bf16[64,1024]{1,0:T(8,128)(2,1)S(1)} collective-permute-done((bf16[64,1024]{1,0:T(8,128)(2,1)S(1)}, bf16[64,1024]{1,0:T(8,128)(2,1)S(1)}, u32[]{:S(2)}, u32[]{:S(2)}) %collective-permute-start.28) | collective-permute-done | bytes 131104 | tf_op jit(solution)/shard_map/ppermute | solution.py:271
  103.0 1.3 %output_other.1 = (f32[128,1024]{1,0:T(8,128)S(1)}, bf16[128,1024]{1,0:T(8,128)(2,1)S(1)}) custom-call(s32[3]{0:T(128)S(1)} %pad_add_fusion.scalars, bf16[64,1024]{1,0:T(8,128)(2,1)S(1)} %collective-permute-done.23.refs_0_, bf16[64,1024]{1,0:T(8,128)(2,1)S(1)} %collective-permute-done.25.refs_1_, bf16[64,1024]{1,0:T(8,128)(2,1)S(1)} %collective-permute-done.28.refs_2_, ...), custom_call_target="tpu_custom_call" | custom-call | tf_op jit(solution)/shard_map/output_other/pallas_call | solution.py:210
  104.4 0.1 collective-permute-start.30
  105.1 0.8 collective-permute-done.30
  106.0 0.8 add_convert_fusion
  (47 shorter events, 0.3 us)
Async XLA Ops:
  1.1 19.4 %collective-permute-start.7 = (bf16[480,512]{1,0:T(8,128)(2,1)S(1)}, bf16[480,512]{1,0:T(8,128)(2,1)S(1)}, u32[]{:S(2)}, u32[]{:S(2)}) collective-permute-start(bf16[480,512]{1,0:T(8,128)(2,1)S(1)} %pad_maximum_fusion.refs_8_), channel_id=1, source_target_pairs={{0,12},{1,13},{2,14},{3,15},{4,0},{5,1},{6,2},{7,3},{8,4},{9,5},{1... | collective-permute-start | bytes 1474568 | tf_op jit(solution)/shard_map/ppermute | solution.py:271
  6.2 22.1 %collective-permute-start.6 = (bf16[480,512]{1,0:T(8,128)(2,1)S(1)}, bf16[480,512]{1,0:T(8,128)(2,1)S(1)}, u32[]{:S(2)}, u32[]{:S(2)}) collective-permute-start(bf16[480,512]{1,0:T(8,128)(2,1)S(1)} %pad_maximum_fusion.refs_8_), channel_id=1, source_target_pairs={{0,4},{1,5},{2,6},{3,7},{4,8},{5,9},{6,10},{7,11},{8,12},{9,13},{1... | collective-permute-start | bytes 1474568 | tf_op jit(solution)/shard_map/ppermute | solution.py:271
  6.3 2.1 %copy-start.1 = (bf16[256,7680]{1,0:T(8,128)(2,1)S(1)}, bf16[256,7680]{1,0:T(8,128)(2,1)}, u32[]{:S(2)}) copy-start(bf16[256,7680]{1,0:T(8,128)(2,1)} %rows_ref.3) | copy-start | bytes 11796484
  11.6 18.2 %collective-permute-start.2 = (bf16[128,1920]{1,0:T(8,128)(2,1)}, bf16[128,1920]{1,0:T(8,128)(2,1)S(1)}, u32[]{:S(2)}, u32[]{:S(2)}) collective-permute-start(bf16[128,1920]{1,0:T(8,128)(2,1)} %get-tuple-element.36), channel_id=1, source_target_pairs={{0,18},{1,19},{2,16},{3,17},{4,22},{5,23},{6,20},{7,21},{8,26},{9,... | collective-permute-start | bytes 1474568 | tf_op jit(solution)/shard_map/ppermute | solution.py:271
  14.1 22.0 %collective-permute-start.1 = (bf16[128,1920]{1,0:T(8,128)(2,1)}, bf16[128,1920]{1,0:T(8,128)(2,1)S(1)}, u32[]{:S(2)}, u32[]{:S(2)}) collective-permute-start(bf16[128,1920]{1,0:T(8,128)(2,1)} %get-tuple-element.35), channel_id=1, source_target_pairs={{0,16},{1,17},{2,18},{3,19},{4,20},{5,21},{6,22},{7,23},{8,24},{9,... | collective-permute-start | bytes 1474568 | tf_op jit(solution)/shard_map/ppermute | solution.py:271
  14.6 21.4 %collective-permute-start = (bf16[128,1920]{1,0:T(8,128)(2,1)}, bf16[128,1920]{1,0:T(8,128)(2,1)}, u32[]{:S(2)}, u32[]{:S(2)}) collective-permute-start(bf16[128,1920]{1,0:T(8,128)(2,1)} %get-tuple-element.34), channel_id=1, source_target_pairs={{0,2},{1,3},{2,0},{3,1},{4,6},{5,7},{6,4},{7,5},{8,10},{9,11},{10,... | collective-permute-start | bytes 1474568 | tf_op jit(solution)/shard_map/ppermute | solution.py:271
  15.2 2.1 %copy-start.2 = (bf16[256,7680]{1,0:T(8,128)(2,1)S(1)}, bf16[256,7680]{1,0:T(8,128)(2,1)}, u32[]{:S(2)}) copy-start(bf16[256,7680]{1,0:T(8,128)(2,1)} %rows_ref.3) | copy-start | bytes 11796484
  17.3 2.1 %copy-start.3 = (bf16[256,7680]{1,0:T(8,128)(2,1)S(1)}, bf16[256,7680]{1,0:T(8,128)(2,1)}, u32[]{:S(2)}) copy-start(bf16[256,7680]{1,0:T(8,128)(2,1)} %rows_ref.3) | copy-start | bytes 11796484
  20.5 18.4 %collective-permute-start.8 = (bf16[480,512]{1,0:T(8,128)(2,1)S(1)}, bf16[480,512]{1,0:T(8,128)(2,1)}, u32[]{:S(2)}, u32[]{:S(2)}) collective-permute-start(bf16[480,512]{1,0:T(8,128)(2,1)S(1)} %collective-permute-done.7.refs_10_), channel_id=1, source_target_pairs={{4,0},{5,1},{6,2},{7,3},{8,4},{9,5},{10,6},{11,7},{20,16},{21,17},... | collective-permute-start | bytes 1474568 | tf_op jit(solution)/shard_map/ppermute | solution.py:271
  28.3 10.5 %collective-permute-start.9 = (bf16[480,512]{1,0:T(8,128)(2,1)S(1)}, bf16[480,512]{1,0:T(8,128)(2,1)}, u32[]{:S(2)}, u32[]{:S(2)}) collective-permute-start(bf16[480,512]{1,0:T(8,128)(2,1)S(1)} %collective-permute-done.6.refs_9_), channel_id=1, source_target_pairs={{4,8},{5,9},{6,10},{7,11},{8,12},{9,13},{10,14},{11,15},{20,24},{2... | collective-permute-start | bytes 1474568 | tf_op jit(solution)/shard_map/ppermute | solution.py:271
  29.8 9.1 %collective-permute-start.5 = (bf16[128,1920]{1,0:T(8,128)(2,1)S(1)}, bf16[128,1920]{1,0:T(8,128)(2,1)}, u32[]{:S(2)}, u32[]{:S(2)}) collective-permute-start(bf16[128,1920]{1,0:T(8,128)(2,1)S(1)} %collective-permute-done.2.refs_3_), channel_id=1, source_target_pairs={{0,1},{1,0},{2,3},{3,2},{4,5},{5,4},{6,7},{7,6},{8,9},{9,8},{10,11... | collective-permute-start | bytes 1474568 | tf_op jit(solution)/shard_map/ppermute | solution.py:271
  36.0 2.8 %collective-permute-start.4 = (bf16[128,1920]{1,0:T(8,128)(2,1)S(1)}, bf16[128,1920]{1,0:T(8,128)(2,1)}, u32[]{:S(2)}, u32[]{:S(2)}) collective-permute-start(bf16[128,1920]{1,0:T(8,128)(2,1)S(1)} %collective-permute-done.1.refs_2_), channel_id=1, source_target_pairs={{0,1},{1,0},{2,3},{3,2},{4,5},{5,4},{6,7},{7,6},{8,9},{9,8},{10,11... | collective-permute-start | bytes 1474568 | tf_op jit(solution)/shard_map/ppermute | solution.py:271
  36.0 2.9 %collective-permute-start.3 = (bf16[128,1920]{1,0:T(8,128)(2,1)}, bf16[128,1920]{1,0:T(8,128)(2,1)}, u32[]{:S(2)}, u32[]{:S(2)}) collective-permute-start(bf16[128,1920]{1,0:T(8,128)(2,1)} %collective-permute-done.refs_1_), channel_id=1, source_target_pairs={{0,1},{1,0},{2,3},{3,2},{4,5},{5,4},{6,7},{7,6},{8,9},{9,8},{10,11... | collective-permute-start | bytes 1474568 | tf_op jit(solution)/shard_map/ppermute | solution.py:271
  36.6 32.6 %copy-start.6 = (f32[128]{0:T(128)S(1)}, f32[128]{0:T(128)}, u32[]{:S(2)}) copy-start(f32[128]{0:T(128)} %param.16) | copy-start | bytes 1540
  36.6 36.9 %copy-start.7 = (f32[128]{0:T(128)S(1)}, f32[128]{0:T(128)}, u32[]{:S(2)}) copy-start(f32[128]{0:T(128)} %param.15) | copy-start | bytes 1540
  44.0 10.4 %copy-start.4 = (f32[512,128]{1,0:T(8,128)}, f32[512,128]{1,0:T(8,128)S(1)}, u32[]{:S(2)}) copy-start(f32[512,128]{1,0:T(8,128)S(1)} %get-tuple-element.49) | copy-start | bytes 786436
  44.0 6.5 %collective-permute-start.10 = (bf16[512,128]{1,0:T(8,128)(2,1)S(1)}, bf16[512,128]{1,0:T(8,128)(2,1)S(1)}, u32[]{:S(2)}, u32[]{:S(2)}) collective-permute-start(bf16[512,128]{1,0:T(8,128)(2,1)S(1)} %get-tuple-element.45), channel_id=1, source_target_pairs={{0,2},{1,3},{2,0},{3,1},{4,6},{5,7},{6,4},{7,5},{8,10},{9,11},{10,... | collective-permute-start | bytes 393224 | tf_op jit(solution)/shard_map/ppermute | solution.py:271
  45.5 6.4 %collective-permute-start.11 = (bf16[512,128]{1,0:T(8,128)(2,1)S(1)}, bf16[512,128]{1,0:T(8,128)(2,1)S(1)}, u32[]{:S(2)}, u32[]{:S(2)}) collective-permute-start(bf16[512,128]{1,0:T(8,128)(2,1)S(1)} %get-tuple-element.46), channel_id=1, source_target_pairs={{0,16},{1,17},{2,18},{3,19},{4,20},{5,21},{6,22},{7,23},{8,24},{9,... | collective-permute-start | bytes 393224 | tf_op jit(solution)/shard_map/ppermute | solution.py:271
  47.0 7.4 %collective-permute-start.12 = (bf16[512,128]{1,0:T(8,128)(2,1)S(1)}, bf16[512,128]{1,0:T(8,128)(2,1)S(1)}, u32[]{:S(2)}, u32[]{:S(2)}) collective-permute-start(bf16[512,128]{1,0:T(8,128)(2,1)S(1)} %get-tuple-element.47), channel_id=1, source_target_pairs={{0,18},{1,19},{2,16},{3,17},{4,22},{5,23},{6,20},{7,21},{8,26},{9,... | collective-permute-start | bytes 393224 | tf_op jit(solution)/shard_map/ppermute | solution.py:271
  47.5 20.6 %collective-permute-start.15 = (f32[512,128]{1,0:T(8,128)}, f32[512,128]{1,0:T(8,128)S(1)}, u32[]{:S(2)}, u32[]{:S(2)}) collective-permute-start(f32[512,128]{1,0:T(8,128)} %get-tuple-element.50), channel_id=1, source_target_pairs={{0,2},{1,3},{2,0},{3,1},{4,6},{5,7},{6,4},{7,5},{8,10},{9,11},{10,... | collective-permute-start | bytes 786440 | tf_op jit(solution)/shard_map/ppermute | solution.py:271
  49.0 19.1 %collective-permute-start.17 = (f32[512,128]{1,0:T(8,128)}, f32[512,128]{1,0:T(8,128)S(1)}, u32[]{:S(2)}, u32[]{:S(2)}) collective-permute-start(f32[512,128]{1,0:T(8,128)} %get-tuple-element.52), channel_id=1, source_target_pairs={{0,16},{1,17},{2,18},{3,19},{4,20},{5,21},{6,22},{7,23},{8,24},{9,... | collective-permute-start | bytes 786440 | tf_op jit(solution)/shard_map/ppermute | solution.py:271
  50.5 17.6 %collective-permute-start.18 = (f32[512,128]{1,0:T(8,128)}, f32[512,128]{1,0:T(8,128)S(1)}, u32[]{:S(2)}, u32[]{:S(2)}) collective-permute-start(f32[512,128]{1,0:T(8,128)} %get-tuple-element.54), channel_id=1, source_target_pairs={{0,18},{1,19},{2,16},{3,17},{4,22},{5,23},{6,20},{7,21},{8,26},{9,... | collective-permute-start | bytes 786440 | tf_op jit(solution)/shard_map/ppermute | solution.py:271
  54.4 8.8 %collective-permute-start.13 = (bf16[512,128]{1,0:T(8,128)(2,1)S(1)}, bf16[512,128]{1,0:T(8,128)(2,1)S(1)}, u32[]{:S(2)}, u32[]{:S(2)}) collective-permute-start(bf16[512,128]{1,0:T(8,128)(2,1)S(1)} %add_convert_fusion.1.refs_0_), channel_id=1, source_target_pairs={{0,4},{1,5},{2,6},{3,7},{4,8},{5,9},{6,10},{7,11},{8,12},{9,13},{1... | collective-permute-start | bytes 393224 | tf_op jit(solution)/shard_map/ppermute | solution.py:271
  56.9 10.2 %collective-permute-start.16 = (bf16[512,128]{1,0:T(8,128)(2,1)S(1)}, bf16[512,128]{1,0:T(8,128)(2,1)S(1)}, u32[]{:S(2)}, u32[]{:S(2)}) collective-permute-start(bf16[512,128]{1,0:T(8,128)(2,1)S(1)} %add_convert_fusion.1.refs_0_), channel_id=1, source_target_pairs={{0,12},{1,13},{2,14},{3,15},{4,0},{5,1},{6,2},{7,3},{8,4},{9,5},{1... | collective-permute-start | bytes 393224 | tf_op jit(solution)/shard_map/ppermute | solution.py:271
  59.7 35.2 %copy-start = (bf16[2048,1024]{1,0:T(8,128)(2,1)S(1)}, bf16[2048,1024]{1,0:T(8,128)(2,1)}, u32[]{:S(2)}) copy-start(bf16[2048,1024]{1,0:T(8,128)(2,1)} %refs_4_.1) | copy-start | bytes 12582916
  63.3 19.8 %collective-permute-start.22 = (bf16[512,128]{1,0:T(8,128)(2,1)S(1)}, bf16[512,128]{1,0:T(8,128)(2,1)S(1)}, u32[]{:S(2)}, u32[]{:S(2)}) collective-permute-start(bf16[512,128]{1,0:T(8,128)(2,1)S(1)} %add_convert_fusion.1.refs_0_), channel_id=1, source_target_pairs={{0,8},{1,9},{2,10},{3,11},{4,12},{5,13},{6,14},{7,15},{8,0},{9,1},... | collective-permute-start | bytes 393224 | tf_op jit(solution)/shard_map/ppermute | solution.py:271
  67.1 6.1 %collective-permute-start.14 = (bf16[32,1024]{1,0:T(8,128)(2,1)S(1)}, bf16[32,1024]{1,0:T(8,128)(2,1)S(1)}, u32[]{:S(2)}, u32[]{:S(2)}) collective-permute-start(bf16[32,1024]{1,0:T(8,128)(2,1)S(1)} %get-tuple-element.48), channel_id=1, source_target_pairs={{0,2},{1,3},{2,0},{3,1},{4,6},{5,7},{6,4},{7,5},{8,10},{9,11},{10,... | collective-permute-start | bytes 196616 | tf_op jit(solution)/shard_map/ppermute | solution.py:271
  69.3 7.1 %collective-permute-start.19 = (bf16[512,128]{1,0:T(8,128)(2,1)S(1)}, bf16[512,128]{1,0:T(8,128)(2,1)S(1)}, u32[]{:S(2)}, u32[]{:S(2)}) collective-permute-start(bf16[512,128]{1,0:T(8,128)(2,1)S(1)} %multiply_convert_fusion.refs_0_), channel_id=1, source_target_pairs={{0,4},{1,5},{2,6},{3,7},{4,8},{5,9},{6,10},{7,11},{8,12},{9,13},{1... | collective-permute-start | bytes 393224 | tf_op jit(solution)/shard_map/ppermute | solution.py:271
  69.4 11.6 %collective-permute-start.20 = (bf16[512,128]{1,0:T(8,128)(2,1)S(1)}, bf16[512,128]{1,0:T(8,128)(2,1)S(1)}, u32[]{:S(2)}, u32[]{:S(2)}) collective-permute-start(bf16[512,128]{1,0:T(8,128)(2,1)S(1)} %multiply_convert_fusion.refs_0_), channel_id=1, source_target_pairs={{0,8},{1,9},{2,10},{3,11},{4,12},{5,13},{6,14},{7,15},{8,0},{9,1},... | collective-permute-start | bytes 393224 | tf_op jit(solution)/shard_map/ppermute | solution.py:271
  70.4 10.6 %collective-permute-start.21 = (bf16[512,128]{1,0:T(8,128)(2,1)S(1)}, bf16[512,128]{1,0:T(8,128)(2,1)S(1)}, u32[]{:S(2)}, u32[]{:S(2)}) collective-permute-start(bf16[512,128]{1,0:T(8,128)(2,1)S(1)} %multiply_convert_fusion.refs_0_), channel_id=1, source_target_pairs={{0,12},{1,13},{2,14},{3,15},{4,0},{5,1},{6,2},{7,3},{8,4},{9,5},{1... | collective-permute-start | bytes 393224 | tf_op jit(solution)/shard_map/ppermute | solution.py:271
  83.8 5.0 %collective-permute-start.23 = (bf16[64,1024]{1,0:T(8,128)(2,1)S(1)}, bf16[64,1024]{1,0:T(8,128)(2,1)S(1)}, u32[]{:S(2)}, u32[]{:S(2)}) collective-permute-start(bf16[64,1024]{1,0:T(8,128)(2,1)S(1)} %mix.1.refs_0_), channel_id=1, source_target_pairs={{0,2},{1,3},{2,0},{3,1},{4,6},{5,7},{6,4},{7,5},{8,10},{9,11},{10,... | collective-permute-start | bytes 393224 | tf_op jit(solution)/shard_map/ppermute | solution.py:271
  84.8 8.2 %collective-permute-start.24 = (bf16[64,1024]{1,0:T(8,128)(2,1)S(1)}, bf16[64,1024]{1,0:T(8,128)(2,1)S(1)}, u32[]{:S(2)}, u32[]{:S(2)}) collective-permute-start(bf16[64,1024]{1,0:T(8,128)(2,1)S(1)} %mix.1.refs_0_), channel_id=1, source_target_pairs={{0,4},{1,5},{2,6},{3,7},{4,8},{5,9},{6,10},{7,11},{8,12},{9,13},{1... | collective-permute-start | bytes 393224 | tf_op jit(solution)/shard_map/ppermute | solution.py:271
  87.1 7.0 %collective-permute-start.27 = (bf16[64,1024]{1,0:T(8,128)(2,1)S(1)}, bf16[64,1024]{1,0:T(8,128)(2,1)S(1)}, u32[]{:S(2)}, u32[]{:S(2)}) collective-permute-start(bf16[64,1024]{1,0:T(8,128)(2,1)S(1)} %mix.1.refs_0_), channel_id=1, source_target_pairs={{0,12},{1,13},{2,14},{3,15},{4,0},{5,1},{6,2},{7,3},{8,4},{9,5},{1... | collective-permute-start | bytes 393224 | tf_op jit(solution)/shard_map/ppermute | solution.py:271
  88.6 9.5 %collective-permute-start.26 = (bf16[64,1024]{1,0:T(8,128)(2,1)S(1)}, bf16[64,1024]{1,0:T(8,128)(2,1)S(1)}, u32[]{:S(2)}, u32[]{:S(2)}) collective-permute-start(bf16[64,1024]{1,0:T(8,128)(2,1)S(1)} %mix.1.refs_0_), channel_id=1, source_target_pairs={{0,8},{1,9},{2,10},{3,11},{4,12},{5,13},{6,14},{7,15},{8,0},{9,1},... | collective-permute-start | bytes 393224 | tf_op jit(solution)/shard_map/ppermute | solution.py:271
  93.0 5.1 %collective-permute-start.25 = (bf16[64,1024]{1,0:T(8,128)(2,1)S(1)}, bf16[64,1024]{1,0:T(8,128)(2,1)S(1)}, u32[]{:S(2)}, u32[]{:S(2)}) collective-permute-start(bf16[64,1024]{1,0:T(8,128)(2,1)S(1)} %collective-permute-done.24.refs_1_), channel_id=1, source_target_pairs={{0,2},{1,3},{2,0},{3,1},{4,6},{5,7},{6,4},{7,5},{8,10},{9,11},{10,... | collective-permute-start | bytes 393224 | tf_op jit(solution)/shard_map/ppermute | solution.py:271
  94.1 6.0 %collective-permute-start.29 = (bf16[64,1024]{1,0:T(8,128)(2,1)S(1)}, bf16[64,1024]{1,0:T(8,128)(2,1)S(1)}, u32[]{:S(2)}, u32[]{:S(2)}) collective-permute-start(bf16[64,1024]{1,0:T(8,128)(2,1)S(1)} %collective-permute-done.27.refs_2_), channel_id=1, source_target_pairs={{0,2},{1,3},{2,0},{3,1},{4,6},{5,7},{6,4},{7,5},{8,10},{9,11},{10,... | collective-permute-start | bytes 393224 | tf_op jit(solution)/shard_map/ppermute | solution.py:271
  98.1 5.0 %collective-permute-start.28 = (bf16[64,1024]{1,0:T(8,128)(2,1)S(1)}, bf16[64,1024]{1,0:T(8,128)(2,1)S(1)}, u32[]{:S(2)}, u32[]{:S(2)}) collective-permute-start(bf16[64,1024]{1,0:T(8,128)(2,1)S(1)} %collective-permute-done.26.refs_0_), channel_id=1, source_target_pairs={{0,2},{1,3},{2,0},{3,1},{4,6},{5,7},{6,4},{7,5},{8,10},{9,11},{10,... | collective-permute-start | bytes 393224 | tf_op jit(solution)/shard_map/ppermute | solution.py:271
  99.7 6.2 %copy-start.5 = (bf16[128,1024]{1,0:T(8,128)(2,1)S(1)}, bf16[128,1024]{1,0:T(8,128)(2,1)}, u32[]{:S(2)}) copy-start(bf16[128,1024]{1,0:T(8,128)(2,1)} %param.14) | copy-start | bytes 786436
  104.4 1.6 %collective-permute-start.30 = (bf16[128,1024]{1,0:T(8,128)(2,1)S(1)}, bf16[128,1024]{1,0:T(8,128)(2,1)S(1)}, u32[]{:S(2)}, u32[]{:S(2)}) collective-permute-start(bf16[128,1024]{1,0:T(8,128)(2,1)S(1)} %get-tuple-element.62), channel_id=1, source_target_pairs={{0,1},{1,0},{2,3},{3,2},{4,5},{5,4},{6,7},{7,6},{8,9},{9,8},{10,11... | collective-permute-start | bytes 786440 | tf_op jit(solution)/shard_map/ppermute | solution.py:271

commit v12 on v8

--- a/solution.py
+++ b/solution.py
@@ -51,7 +51,7 @@
 
 def project_kernel(groups, pairs, shifts, scalars, *refs):
     count = groups * 2
-    near, far, slabs = refs[:count], refs[count : 2 * count], refs[2 * count : -2 * count - 1]
+    slabs, near, far = refs[: -4 * count - 1], refs[-4 * count - 1 : -3 * count - 1], refs[-3 * count - 1 : -2 * count - 1]
     outs, placed = refs[-2 * count - 1 : -1], refs[-1]
     half = near[0].shape[0]
     side, place = scalars[0], scalars[1]
@@ -99,7 +99,7 @@
         scratch_shapes=[pltpu.VMEM((pairs,) + slabs[0].shape, bf16)],
         compiler_params=pltpu.CompilerParams(vmem_limit_bytes=VMEM_BYTES),
         name="project",
-    )(jnp.stack([side, place]).astype(jnp.int32), *near, *far, *slabs)
+    )(jnp.stack([side, place]).astype(jnp.int32), *slabs, *near, *far)
 
 
 def score_kernel(heads, q_ref, *refs):
@@ -298,10 +298,10 @@
         return [up, down]
 
     near_shifts = [k for k in range(1, pairs) if k != middle]
-    shifts = [0] + near_shifts + ([middle, (middle,)] if middle else [])
+    shifts = [0] + near_shifts + ([(middle,), middle] if middle else [])
 
     def line_slabs(own, pieces, far):
-        return [own] + [pieces[k] for k in near_shifts] + far[::-1]
+        return [own] + [pieces[k] for k in near_shifts] + far
 
     def all_pairs(array):
         return [array] + [line_shift(array, k) for k in range(1, pairs)]
@@ -332,7 +332,7 @@
 
     received = [after(piece, near[0], far[0]) for piece in received]
     near = [*near, *received]
-    slab_far = line_far({k: after(s, near[0], far[0]) for k, s in slab_near.items()})
+    slab_far = line_far({k: after(s, near[0], far[0], q_own, q_send) for k, s in slab_near.items()})
     far = [*far] + [core_swap(piece) for piece in received]
 
     def scatter(pieces):

time: 107 us -> 109 us (1.019)
  waiting for transfers between devices: 36 us -> 44.4 us
  starting transfers between devices: 43 us -> 35.2 us
    ppermute x31, waiting for transfers between devices: 36 us -> 44.4 us  [permute(): return lax.ppermute(array, AXES, perm)]
    ppermute x31, starting transfers between devices: 43 us -> 35.2 us  [permute(): return lax.ppermute(array, AXES, perm)]
  transfers between devices with their start and end apart: 31 -> 31, of which waited for: 12 -> 14; matrix products, arithmetic and copies ran while one was open for 3% -> 3% of each run, Pallas kernels for 8% -> 8%
where the time goes in v12:
time: 109 us; the launch traced here: 108 us
  waiting for transfers between devices  44.4 us (41%)
  starting transfers between devices  35.2 us (32%)
  Pallas kernels  15.5 us (14%)
  local copies, waits for them, and re-layouts  8.69 us (8%)
  other arithmetic  2.76 us (3%)
    ppermute x31, waiting for transfers between devices, permute(): return lax.ppermute(array, AXES, perm)  44.4 us
    ppermute x31, starting transfers between devices, permute(): return lax.ppermute(array, AXES, perm)  35.2 us
    unnamed x23, local copies, waits for them, and re-layouts  6.08 us
    pallas_call x3, Pallas kernels, pack(): pl.pallas_call(functools.partial(pack_kernel, groups, pairs, part, count)...  5.32 us
    pallas_call x1, Pallas kernels, project(): pl.pallas_call(functools.partial(project_kernel, count // 2, pairs, shift...  5.08 us
  transfers between devices with their start and end apart: 31, of which 14 were waited for; matrix products, arithmetic and copies ran while one was open for 3% of the time, Pallas kernels for 8%

profile of v12, /device:TPU:0, one launch (start us, length us, event | category | flops | bytes accessed | tf_op | source)
XLA Modules:
  0.0 107.6 jit_solution(14658601947627502648)
XLA Ops:
  0.0 1.1 %constant_dynamic-slice_fusion = (bf16[480,256]{1,0:T(8,128)(2,1)S(1)}, bf16[480,256]{1,0:T(8,128)(2,1)S(1)}) fusion(bf16[960,256]{1,0:T(8,128)(2,1)} %param.12, s32[]{:T(128)S(6)} %select_n.62, bf16[960,256]{1,0:T(8,128)(2,1)} %param.11), kind=kLoop, calls=%fused_computation.22 | loop fusion | bytes 983044 | tf_op jit(solution)/shard_map/dynamic_slice | solution.py:314
  1.1 3.1 %collective-permute-start = (bf16[480,512]{1,0:T(8,128)(2,1)S(1)}, bf16[480,512]{1,0:T(8,128)(2,1)S(1)}, u32[]{:S(2)}, u32[]{:S(2)}) collective-permute-start(bf16[480,512]{1,0:T(8,128)(2,1)S(1)} %pad_maximum_fusion.refs_0_), channel_id=1, source_target_pairs={{0,4},{1,5},{2,6},{3,7},{4,8},{5,9},{6,10},{7,11},{8,12},{9,13},{1... | collective-permute-start | bytes 1474568 | tf_op jit(solution)/shard_map/ppermute | solution.py:271
  4.2 2.1 %collective-permute-start.1 = (bf16[480,512]{1,0:T(8,128)(2,1)S(1)}, bf16[480,512]{1,0:T(8,128)(2,1)S(1)}, u32[]{:S(2)}, u32[]{:S(2)}) collective-permute-start(bf16[480,512]{1,0:T(8,128)(2,1)S(1)} %pad_maximum_fusion.refs_0_), channel_id=1, source_target_pairs={{0,12},{1,13},{2,14},{3,15},{4,0},{5,1},{6,2},{7,3},{8,4},{9,5},{1... | collective-permute-start | bytes 1474568 | tf_op jit(solution)/shard_map/ppermute | solution.py:271
  6.3 0.1 pad_add_fusion.2.index_ref
  6.4 2.1 %copy-done.1 = bf16[256,7680]{1,0:T(8,128)(2,1)S(1)} copy-done((bf16[256,7680]{1,0:T(8,128)(2,1)S(1)}, bf16[256,7680]{1,0:T(8,128)(2,1)}, u32[]{:S(2)}) %copy-start.1) | copy-done | bytes 3932184
  8.5 3.2 %pack_sends.1 = (bf16[128,1920]{1,0:T(8,128)(2,1)}, bf16[128,1920]{1,0:T(8,128)(2,1)}, bf16[128,1920]{1,0:T(8,128)(2,1)}) custom-call(s32[4]{0:T(128)S(1)} %pad_add_fusion.2.index_ref, bf16[256,7680]{1,0:T(8,128)(2,1)S(1)} %copy-done.1), custom_call_target="tpu_custom_call" | custom-call | tf_op jit(solution)/shard_map/pack_sends/pallas_call | solution.py:38
  11.7 1.7 %collective-permute-start.4 = (bf16[128,1920]{1,0:T(8,128)(2,1)}, bf16[128,1920]{1,0:T(8,128)(2,1)S(1)}, u32[]{:S(2)}, u32[]{:S(2)}) collective-permute-start(bf16[128,1920]{1,0:T(8,128)(2,1)} %get-tuple-element.34), channel_id=1, source_target_pairs={{0,2},{1,3},{2,0},{3,1},{4,6},{5,7},{6,4},{7,5},{8,10},{9,11},{10,... | collective-permute-start | bytes 1474568 | tf_op jit(solution)/shard_map/ppermute | solution.py:271
  13.4 1.5 %collective-permute-start.5 = (bf16[128,1920]{1,0:T(8,128)(2,1)}, bf16[128,1920]{1,0:T(8,128)(2,1)S(1)}, u32[]{:S(2)}, u32[]{:S(2)}) collective-permute-start(bf16[128,1920]{1,0:T(8,128)(2,1)} %get-tuple-element.35), channel_id=1, source_target_pairs={{0,16},{1,17},{2,18},{3,19},{4,20},{5,21},{6,22},{7,23},{8,24},{9,... | collective-permute-start | bytes 1474568 | tf_op jit(solution)/shard_map/ppermute | solution.py:271
  14.8 0.3 collective-permute-start.6
  15.2 0.1 pad_add_fusion.1
  15.2 2.1 %copy-done.2 = bf16[256,7680]{1,0:T(8,128)(2,1)S(1)} copy-done((bf16[256,7680]{1,0:T(8,128)(2,1)S(1)}, bf16[256,7680]{1,0:T(8,128)(2,1)}, u32[]{:S(2)}) %copy-start.2) | copy-done | bytes 3932184
  17.4 1.1 pack_far.1.refs_9_
  18.4 1.0 copy-done.3
  19.5 1.1 pack_near.1.refs_5_
  20.6 1.5 %constant_dynamic-slice_fusion.3 = (bf16[32,1024]{1,0:T(8,128)(2,1)S(1)}, bf16[32,1024]{1,0:T(8,128)(2,1)}) fusion(bf16[32,2048]{1,0:T(8,128)(2,1)} %param.9, s32[]{:T(128)S(6)} %select_n.60, s32[]{:T(128)S(6)} %select_n.61), kind=kLoop, calls=%fused_computation.25 | loop fusion | bytes 262152 | tf_op jit(solution)/shard_map/dynamic_slice | solution.py:330
  22.1 1.5 %collective-permute-start.2 = (bf16[480,512]{1,0:T(8,128)(2,1)S(1)}, bf16[480,512]{1,0:T(8,128)(2,1)}, u32[]{:S(2)}, u32[]{:S(2)}) collective-permute-start(bf16[480,512]{1,0:T(8,128)(2,1)S(1)} %collective-permute-done.refs_1_), channel_id=1, source_target_pairs={{4,8},{5,9},{6,10},{7,11},{8,12},{9,13},{10,14},{11,15},{20,24},{2... | collective-permute-start | bytes 1474568 | tf_op jit(solution)/shard_map/ppermute | solution.py:271
  23.5 3.9 %collective-permute-done.1.refs_2_ = bf16[480,512]{1,0:T(8,128)(2,1)S(1)} collective-permute-done((bf16[480,512]{1,0:T(8,128)(2,1)S(1)}, bf16[480,512]{1,0:T(8,128)(2,1)S(1)}, u32[]{:S(2)}, u32[]{:S(2)}) %collective-permute-start.1) | collective-permute-done | bytes 491552 | tf_op jit(solution)/shard_map/ppermute | solution.py:271
  27.4 1.3 %collective-permute-start.3 = (bf16[480,512]{1,0:T(8,128)(2,1)S(1)}, bf16[480,512]{1,0:T(8,128)(2,1)}, u32[]{:S(2)}, u32[]{:S(2)}) collective-permute-start(bf16[480,512]{1,0:T(8,128)(2,1)S(1)} %collective-permute-done.1.refs_2_), channel_id=1, source_target_pairs={{4,0},{5,1},{6,2},{7,3},{8,4},{9,5},{10,6},{11,7},{20,16},{21,17},... | collective-permute-start | bytes 1474568 | tf_op jit(solution)/shard_map/ppermute | solution.py:271
  28.7 7.7 %collective-permute-done.6.refs_8_ = bf16[128,1920]{1,0:T(8,128)(2,1)} collective-permute-done((bf16[128,1920]{1,0:T(8,128)(2,1)}, bf16[128,1920]{1,0:T(8,128)(2,1)}, u32[]{:S(2)}, u32[]{:S(2)}) %collective-permute-start.6) | collective-permute-done | bytes 491552 | tf_op jit(solution)/shard_map/ppermute | solution.py:271
  36.4 0.5 collective-permute-start.8
  36.9 0.1 pad_add_fusion.3.scalars
  37.0 5.1 %collective-permute-done.3.refs_4_ = bf16[480,512]{1,0:T(8,128)(2,1)} collective-permute-done((bf16[480,512]{1,0:T(8,128)(2,1)S(1)}, bf16[480,512]{1,0:T(8,128)(2,1)}, u32[]{:S(2)}, u32[]{:S(2)}) %collective-permute-start.3) | collective-permute-done | bytes 491552 | tf_op jit(solution)/shard_map/ppermute | solution.py:271
  42.1 5.1 %project.1 = (f32[512,128]{1,0:T(8,128)S(1)}, f32[512,128]{1,0:T(8,128)}, f32[512,128]{1,0:T(8,128)}, f32[512,128]{1,0:T(8,128)}, f32[512,128]{1,0:T(8,128)S(1)}...) custom-call(s32[2]{0:T(128)S(1)} %pad_add_fusion.3.scalars, ...), custom_call_target="tpu_custom_call" | custom-call | tf_op jit(solution)/shard_map/project/pallas_call | solution.py:91
  47.2 0.7 copy-done.4
  47.9 2.4 %collective-permute-start.12 = (bf16[512,128]{1,0:T(8,128)(2,1)S(1)}, bf16[512,128]{1,0:T(8,128)(2,1)S(1)}, u32[]{:S(2)}, u32[]{:S(2)}) collective-permute-start(bf16[512,128]{1,0:T(8,128)(2,1)S(1)} %get-tuple-element.47), channel_id=1, source_target_pairs={{0,18},{1,19},{2,16},{3,17},{4,22},{5,23},{6,20},{7,21},{8,26},{9,... | collective-permute-start | bytes 393224 | tf_op jit(solution)/shard_map/ppermute | solution.py:271
  50.3 0.5 collective-permute-start.11
  50.8 0.5 collective-permute-start.10
  51.4 2.4 %collective-permute-start.17 = (f32[512,128]{1,0:T(8,128)}, f32[512,128]{1,0:T(8,128)S(1)}, u32[]{:S(2)}, u32[]{:S(2)}) collective-permute-start(f32[512,128]{1,0:T(8,128)} %get-tuple-element.54), channel_id=1, source_target_pairs={{0,18},{1,19},{2,16},{3,17},{4,22},{5,23},{6,20},{7,21},{8,26},{9,... | collective-permute-start | bytes 786440 | tf_op jit(solution)/shard_map/ppermute | solution.py:271
  53.8 0.5 collective-permute-start.16
  54.3 0.9 collective-permute-done.12
  55.2 1.5 %collective-permute-start.15 = (f32[512,128]{1,0:T(8,128)}, f32[512,128]{1,0:T(8,128)S(1)}, u32[]{:S(2)}, u32[]{:S(2)}) collective-permute-start(f32[512,128]{1,0:T(8,128)} %get-tuple-element.50), channel_id=1, source_target_pairs={{0,2},{1,3},{2,0},{3,1},{4,6},{5,7},{6,4},{7,5},{8,10},{9,11},{10,... | collective-permute-start | bytes 786440 | tf_op jit(solution)/shard_map/ppermute | solution.py:271
  56.8 1.3 %collective-permute-done.11 = bf16[512,128]{1,0:T(8,128)(2,1)S(1)} collective-permute-done((bf16[512,128]{1,0:T(8,128)(2,1)S(1)}, bf16[512,128]{1,0:T(8,128)(2,1)S(1)}, u32[]{:S(2)}, u32[]{:S(2)}) %collective-permute-start.11) | collective-permute-done | bytes 131104 | tf_op jit(solution)/shard_map/ppermute | solution.py:271
  58.0 2.7 %collective-permute-done.10 = bf16[512,128]{1,0:T(8,128)(2,1)S(1)} collective-permute-done((bf16[512,128]{1,0:T(8,128)(2,1)S(1)}, bf16[512,128]{1,0:T(8,128)(2,1)S(1)}, u32[]{:S(2)}, u32[]{:S(2)}) %collective-permute-start.10) | collective-permute-done | bytes 131104 | tf_op jit(solution)/shard_map/ppermute | solution.py:271
  60.9 2.3 %collective-permute-start.21 = (bf16[512,128]{1,0:T(8,128)(2,1)S(1)}, bf16[512,128]{1,0:T(8,128)(2,1)S(1)}, u32[]{:S(2)}, u32[]{:S(2)}) collective-permute-start(bf16[512,128]{1,0:T(8,128)(2,1)S(1)} %add_convert_fusion.1.refs_0_), channel_id=1, source_target_pairs={{0,8},{1,9},{2,10},{3,11},{4,12},{5,13},{6,14},{7,15},{8,0},{9,1},... | collective-permute-start | bytes 393224 | tf_op jit(solution)/shard_map/ppermute | solution.py:271
  63.2 4.6 %collective-permute-done.13.refs_1_ = bf16[512,128]{1,0:T(8,128)(2,1)S(1)} collective-permute-done((bf16[512,128]{1,0:T(8,128)(2,1)S(1)}, bf16[512,128]{1,0:T(8,128)(2,1)S(1)}, u32[]{:S(2)}, u32[]{:S(2)}) %collective-permute-start.13) | collective-permute-done | bytes 131104 | tf_op jit(solution)/shard_map/ppermute | solution.py:271
  67.8 1.0 collective-permute-start.22
  68.7 0.4 collective-permute-start.14
  69.1 1.1 %multiply_reduce_fusion = (f32[512]{0:T(512)S(1)}, f32[512,128]{1,0:T(8,128)S(1)}) fusion(f32[512,128]{1,0:T(8,128)S(1)} %collective-permute-done.17, f32[512,128]{1,0:T(8,128)S(1)} %collective-permute-done.16, f32[512,128]{1,0:T(8,128)} %copy-done.4, f32[512,128]{1,0:T(8,128)S(1)} %collective-permute-done.15), kind=kLoop, calls=%fused_computation.8 | loop fusion | flops 327168 | bytes 1312768 | tf_op jit(solution)/shard_map/reduce_sum | solution.py:232
  70.2 0.1 multiply_convert_fusion.refs_0_
  70.4 2.1 %collective-permute-start.18 = (bf16[512,128]{1,0:T(8,128)(2,1)S(1)}, bf16[512,128]{1,0:T(8,128)(2,1)S(1)}, u32[]{:S(2)}, u32[]{:S(2)}) collective-permute-start(bf16[512,128]{1,0:T(8,128)(2,1)S(1)} %multiply_convert_fusion.refs_0_), channel_id=1, source_target_pairs={{0,4},{1,5},{2,6},{3,7},{4,8},{5,9},{6,10},{7,11},{8,12},{9,13},{1... | collective-permute-start | bytes 393224 | tf_op jit(solution)/shard_map/ppermute | solution.py:271
  72.4 0.8 collective-permute-done.14
  73.2 1.7 %collective-permute-start.20 = (bf16[512,128]{1,0:T(8,128)(2,1)S(1)}, bf16[512,128]{1,0:T(8,128)(2,1)S(1)}, u32[]{:S(2)}, u32[]{:S(2)}) collective-permute-start(bf16[512,128]{1,0:T(8,128)(2,1)S(1)} %multiply_convert_fusion.refs_0_), channel_id=1, source_target_pairs={{0,12},{1,13},{2,14},{3,15},{4,0},{5,1},{6,2},{7,3},{8,4},{9,5},{1... | collective-permute-start | bytes 393224 | tf_op jit(solution)/shard_map/ppermute | solution.py:271
  75.1 0.1 fusion
  75.2 0.1 fusion.2.q_ref
  75.4 2.6 %collective-permute-done.18.refs_1_ = bf16[512,128]{1,0:T(8,128)(2,1)S(1)} collective-permute-done((bf16[512,128]{1,0:T(8,128)(2,1)S(1)}, bf16[512,128]{1,0:T(8,128)(2,1)S(1)}, u32[]{:S(2)}, u32[]{:S(2)}) %collective-permute-start.18) | collective-permute-done | bytes 131104 | tf_op jit(solution)/shard_map/ppermute | solution.py:271
  78.0 3.3 %collective-permute-done.19.refs_2_ = bf16[512,128]{1,0:T(8,128)(2,1)S(1)} collective-permute-done((bf16[512,128]{1,0:T(8,128)(2,1)S(1)}, bf16[512,128]{1,0:T(8,128)(2,1)S(1)}, u32[]{:S(2)}, u32[]{:S(2)}) %collective-permute-start.19) | collective-permute-done | bytes 131104 | tf_op jit(solution)/shard_map/ppermute | solution.py:271
  81.3 2.0 %score.1 = (bf16[512,2048]{1,0:T(8,128)(2,1)S(1)}, f32[512,128]{1,0:T(8,128)S(1)}) custom-call(bf16[512,128]{1,0:T(8,128)(2,1)S(1)} %fusion.2.q_ref, bf16[512,128]{1,0:T(8,128)(2,1)S(1)} %multiply_convert_fusion.refs_0_, bf16[512,128]{1,0:T(8,128)(2,1)S(1)} %collective-permute-done.18.refs_1_, bf16[512,128]{1,0:T(8,128)(2,1)S(1)} %collective-permute-done.19.refs_2_, ...), custom_call_target="tpu_custom_call" | custom-call | tf_op jit(solution)/shard_map/score/pallas_call | solution.py:131
  83.3 0.7 mix.1.refs_0_
  84.0 1.0 collective-permute-start.23
  85.1 2.0 %collective-permute-start.24 = (bf16[64,1024]{1,0:T(8,128)(2,1)S(1)}, bf16[64,1024]{1,0:T(8,128)(2,1)S(1)}, u32[]{:S(2)}, u32[]{:S(2)}) collective-permute-start(bf16[64,1024]{1,0:T(8,128)(2,1)S(1)} %mix.1.refs_0_), channel_id=1, source_target_pairs={{0,4},{1,5},{2,6},{3,7},{4,8},{5,9},{6,10},{7,11},{8,12},{9,13},{1... | collective-permute-start | bytes 393224 | tf_op jit(solution)/shard_map/ppermute | solution.py:271
  87.0 1.9 %collective-permute-start.27 = (bf16[64,1024]{1,0:T(8,128)(2,1)S(1)}, bf16[64,1024]{1,0:T(8,128)(2,1)S(1)}, u32[]{:S(2)}, u32[]{:S(2)}) collective-permute-start(bf16[64,1024]{1,0:T(8,128)(2,1)S(1)} %mix.1.refs_0_), channel_id=1, source_target_pairs={{0,12},{1,13},{2,14},{3,15},{4,0},{5,1},{6,2},{7,3},{8,4},{9,5},{1... | collective-permute-start | bytes 393224 | tf_op jit(solution)/shard_map/ppermute | solution.py:271
  88.9 0.4 collective-permute-start.26
  89.3 4.1 %collective-permute-done.24.refs_1_ = bf16[64,1024]{1,0:T(8,128)(2,1)S(1)} collective-permute-done((bf16[64,1024]{1,0:T(8,128)(2,1)S(1)}, bf16[64,1024]{1,0:T(8,128)(2,1)S(1)}, u32[]{:S(2)}, u32[]{:S(2)}) %collective-permute-start.24) | collective-permute-done | bytes 131104 | tf_op jit(solution)/shard_map/ppermute | solution.py:271
  93.4 0.8 collective-permute-start.25
  94.2 1.2 %collective-permute-start.29 = (bf16[64,1024]{1,0:T(8,128)(2,1)S(1)}, bf16[64,1024]{1,0:T(8,128)(2,1)S(1)}, u32[]{:S(2)}, u32[]{:S(2)}) collective-permute-start(bf16[64,1024]{1,0:T(8,128)(2,1)S(1)} %collective-permute-done.27.refs_2_), channel_id=1, source_target_pairs={{0,2},{1,3},{2,0},{3,1},{4,6},{5,7},{6,4},{7,5},{8,10},{9,11},{10,... | collective-permute-start | bytes 393224 | tf_op jit(solution)/shard_map/ppermute | solution.py:271
  95.4 0.6 output_near.1.refs_5_
  96.0 2.9 %collective-permute-done.26.refs_0_ = bf16[64,1024]{1,0:T(8,128)(2,1)S(1)} collective-permute-done((bf16[64,1024]{1,0:T(8,128)(2,1)S(1)}, bf16[64,1024]{1,0:T(8,128)(2,1)S(1)}, u32[]{:S(2)}, u32[]{:S(2)}) %collective-permute-start.26) | collective-permute-done | bytes 131104 | tf_op jit(solution)/shard_map/ppermute | solution.py:271
  98.9 0.6 collective-permute-start.28
  99.5 0.1 pad_add_fusion.scalars
  99.6 0.5 output_far.1.refs_6_
  100.1 3.8 %collective-permute-done.28.refs_2_ = bf16[64,1024]{1,0:T(8,128)(2,1)S(1)} collective-permute-done((bf16[64,1024]{1,0:T(8,128)(2,1)S(1)}, bf16[64,1024]{1,0:T(8,128)(2,1)S(1)}, u32[]{:S(2)}, u32[]{:S(2)}) %collective-permute-start.28) | collective-permute-done | bytes 131104 | tf_op jit(solution)/shard_map/ppermute | solution.py:271
  103.9 1.3 %output_other.1 = (f32[128,1024]{1,0:T(8,128)S(1)}, bf16[128,1024]{1,0:T(8,128)(2,1)S(1)}) custom-call(s32[3]{0:T(128)S(1)} %pad_add_fusion.scalars, bf16[64,1024]{1,0:T(8,128)(2,1)S(1)} %collective-permute-done.23.refs_0_, bf16[64,1024]{1,0:T(8,128)(2,1)S(1)} %collective-permute-done.25.refs_1_, bf16[64,1024]{1,0:T(8,128)(2,1)S(1)} %collective-permute-done.28.refs_2_, ...), custom_call_target="tpu_custom_call" | custom-call | tf_op jit(solution)/shard_map/output_other/pallas_call | solution.py:210
  106.0 0.8 collective-permute-done.30
  106.8 0.8 add_convert_fusion
  (47 shorter events, 0.4 us)
Async XLA Ops:
  1.1 20.9 %collective-permute-start = (bf16[480,512]{1,0:T(8,128)(2,1)S(1)}, bf16[480,512]{1,0:T(8,128)(2,1)S(1)}, u32[]{:S(2)}, u32[]{:S(2)}) collective-permute-start(bf16[480,512]{1,0:T(8,128)(2,1)S(1)} %pad_maximum_fusion.refs_0_), channel_id=1, source_target_pairs={{0,4},{1,5},{2,6},{3,7},{4,8},{5,9},{6,10},{7,11},{8,12},{9,13},{1... | collective-permute-start | bytes 1474568 | tf_op jit(solution)/shard_map/ppermute | solution.py:271
  4.2 23.2 %collective-permute-start.1 = (bf16[480,512]{1,0:T(8,128)(2,1)S(1)}, bf16[480,512]{1,0:T(8,128)(2,1)S(1)}, u32[]{:S(2)}, u32[]{:S(2)}) collective-permute-start(bf16[480,512]{1,0:T(8,128)(2,1)S(1)} %pad_maximum_fusion.refs_0_), channel_id=1, source_target_pairs={{0,12},{1,13},{2,14},{3,15},{4,0},{5,1},{6,2},{7,3},{8,4},{9,5},{1... | collective-permute-start | bytes 1474568 | tf_op jit(solution)/shard_map/ppermute | solution.py:271
  6.4 2.1 %copy-start.1 = (bf16[256,7680]{1,0:T(8,128)(2,1)S(1)}, bf16[256,7680]{1,0:T(8,128)(2,1)}, u32[]{:S(2)}) copy-start(bf16[256,7680]{1,0:T(8,128)(2,1)} %rows_ref.3) | copy-start | bytes 11796484
  11.7 17.0 %collective-permute-start.4 = (bf16[128,1920]{1,0:T(8,128)(2,1)}, bf16[128,1920]{1,0:T(8,128)(2,1)S(1)}, u32[]{:S(2)}, u32[]{:S(2)}) collective-permute-start(bf16[128,1920]{1,0:T(8,128)(2,1)} %get-tuple-element.34), channel_id=1, source_target_pairs={{0,2},{1,3},{2,0},{3,1},{4,6},{5,7},{6,4},{7,5},{8,10},{9,11},{10,... | collective-permute-start | bytes 1474568 | tf_op jit(solution)/shard_map/ppermute | solution.py:271
  13.4 15.4 %collective-permute-start.5 = (bf16[128,1920]{1,0:T(8,128)(2,1)}, bf16[128,1920]{1,0:T(8,128)(2,1)S(1)}, u32[]{:S(2)}, u32[]{:S(2)}) collective-permute-start(bf16[128,1920]{1,0:T(8,128)(2,1)} %get-tuple-element.35), channel_id=1, source_target_pairs={{0,16},{1,17},{2,18},{3,19},{4,20},{5,21},{6,22},{7,23},{8,24},{9,... | collective-permute-start | bytes 1474568 | tf_op jit(solution)/shard_map/ppermute | solution.py:271
  14.8 21.5 %collective-permute-start.6 = (bf16[128,1920]{1,0:T(8,128)(2,1)}, bf16[128,1920]{1,0:T(8,128)(2,1)}, u32[]{:S(2)}, u32[]{:S(2)}) collective-permute-start(bf16[128,1920]{1,0:T(8,128)(2,1)} %get-tuple-element.36), channel_id=1, source_target_pairs={{0,18},{1,19},{2,16},{3,17},{4,22},{5,23},{6,20},{7,21},{8,26},{9,... | collective-permute-start | bytes 1474568 | tf_op jit(solution)/shard_map/ppermute | solution.py:271
  15.2 2.1 %copy-start.2 = (bf16[256,7680]{1,0:T(8,128)(2,1)S(1)}, bf16[256,7680]{1,0:T(8,128)(2,1)}, u32[]{:S(2)}) copy-start(bf16[256,7680]{1,0:T(8,128)(2,1)} %rows_ref.3) | copy-start | bytes 11796484
  17.4 2.1 %copy-start.3 = (bf16[256,7680]{1,0:T(8,128)(2,1)S(1)}, bf16[256,7680]{1,0:T(8,128)(2,1)}, u32[]{:S(2)}) copy-start(bf16[256,7680]{1,0:T(8,128)(2,1)} %rows_ref.3) | copy-start | bytes 11796484
  22.1 14.9 %collective-permute-start.2 = (bf16[480,512]{1,0:T(8,128)(2,1)S(1)}, bf16[480,512]{1,0:T(8,128)(2,1)}, u32[]{:S(2)}, u32[]{:S(2)}) collective-permute-start(bf16[480,512]{1,0:T(8,128)(2,1)S(1)} %collective-permute-done.refs_1_), channel_id=1, source_target_pairs={{4,8},{5,9},{6,10},{7,11},{8,12},{9,13},{10,14},{11,15},{20,24},{2... | collective-permute-start | bytes 1474568 | tf_op jit(solution)/shard_map/ppermute | solution.py:271
  27.4 14.6 %collective-permute-start.3 = (bf16[480,512]{1,0:T(8,128)(2,1)S(1)}, bf16[480,512]{1,0:T(8,128)(2,1)}, u32[]{:S(2)}, u32[]{:S(2)}) collective-permute-start(bf16[480,512]{1,0:T(8,128)(2,1)S(1)} %collective-permute-done.1.refs_2_), channel_id=1, source_target_pairs={{4,0},{5,1},{6,2},{7,3},{8,4},{9,5},{10,6},{11,7},{20,16},{21,17},... | collective-permute-start | bytes 1474568 | tf_op jit(solution)/shard_map/ppermute | solution.py:271
  36.4 5.7 %collective-permute-start.7 = (bf16[128,1920]{1,0:T(8,128)(2,1)S(1)}, bf16[128,1920]{1,0:T(8,128)(2,1)}, u32[]{:S(2)}, u32[]{:S(2)}) collective-permute-start(bf16[128,1920]{1,0:T(8,128)(2,1)S(1)} %collective-permute-done.4.refs_6_), channel_id=1, source_target_pairs={{0,1},{1,0},{2,3},{3,2},{4,5},{5,4},{6,7},{7,6},{8,9},{9,8},{10,11... | collective-permute-start | bytes 1474568 | tf_op jit(solution)/shard_map/ppermute | solution.py:271
  36.4 5.7 %collective-permute-start.8 = (bf16[128,1920]{1,0:T(8,128)(2,1)S(1)}, bf16[128,1920]{1,0:T(8,128)(2,1)}, u32[]{:S(2)}, u32[]{:S(2)}) collective-permute-start(bf16[128,1920]{1,0:T(8,128)(2,1)S(1)} %collective-permute-done.5.refs_7_), channel_id=1, source_target_pairs={{0,1},{1,0},{2,3},{3,2},{4,5},{5,4},{6,7},{7,6},{8,9},{9,8},{10,11... | collective-permute-start | bytes 1474568 | tf_op jit(solution)/shard_map/ppermute | solution.py:271
  36.9 5.2 %collective-permute-start.9 = (bf16[128,1920]{1,0:T(8,128)(2,1)}, bf16[128,1920]{1,0:T(8,128)(2,1)}, u32[]{:S(2)}, u32[]{:S(2)}) collective-permute-start(bf16[128,1920]{1,0:T(8,128)(2,1)} %collective-permute-done.6.refs_8_), channel_id=1, source_target_pairs={{0,1},{1,0},{2,3},{3,2},{4,5},{5,4},{6,7},{7,6},{8,9},{9,8},{10,11... | collective-permute-start | bytes 1474568 | tf_op jit(solution)/shard_map/ppermute | solution.py:271
  37.0 33.2 %copy-start.6 = (f32[128]{0:T(128)S(1)}, f32[128]{0:T(128)}, u32[]{:S(2)}) copy-start(f32[128]{0:T(128)} %param.16) | copy-start | bytes 1540
  37.0 38.2 %copy-start.7 = (f32[128]{0:T(128)S(1)}, f32[128]{0:T(128)}, u32[]{:S(2)}) copy-start(f32[128]{0:T(128)} %param.15) | copy-start | bytes 1540
  47.2 0.7 copy-start.4
  47.9 7.4 %collective-permute-start.12 = (bf16[512,128]{1,0:T(8,128)(2,1)S(1)}, bf16[512,128]{1,0:T(8,128)(2,1)S(1)}, u32[]{:S(2)}, u32[]{:S(2)}) collective-permute-start(bf16[512,128]{1,0:T(8,128)(2,1)S(1)} %get-tuple-element.47), channel_id=1, source_target_pairs={{0,18},{1,19},{2,16},{3,17},{4,22},{5,23},{6,20},{7,21},{8,26},{9,... | collective-permute-start | bytes 393224 | tf_op jit(solution)/shard_map/ppermute | solution.py:271
  50.3 7.7 %collective-permute-start.11 = (bf16[512,128]{1,0:T(8,128)(2,1)S(1)}, bf16[512,128]{1,0:T(8,128)(2,1)S(1)}, u32[]{:S(2)}, u32[]{:S(2)}) collective-permute-start(bf16[512,128]{1,0:T(8,128)(2,1)S(1)} %get-tuple-element.46), channel_id=1, source_target_pairs={{0,16},{1,17},{2,18},{3,19},{4,20},{5,21},{6,22},{7,23},{8,24},{9,... | collective-permute-start | bytes 393224 | tf_op jit(solution)/shard_map/ppermute | solution.py:271
  50.8 9.9 %collective-permute-start.10 = (bf16[512,128]{1,0:T(8,128)(2,1)S(1)}, bf16[512,128]{1,0:T(8,128)(2,1)S(1)}, u32[]{:S(2)}, u32[]{:S(2)}) collective-permute-start(bf16[512,128]{1,0:T(8,128)(2,1)S(1)} %get-tuple-element.45), channel_id=1, source_target_pairs={{0,2},{1,3},{2,0},{3,1},{4,6},{5,7},{6,4},{7,5},{8,10},{9,11},{10,... | collective-permute-start | bytes 393224 | tf_op jit(solution)/shard_map/ppermute | solution.py:271
  51.4 17.4 %collective-permute-start.17 = (f32[512,128]{1,0:T(8,128)}, f32[512,128]{1,0:T(8,128)S(1)}, u32[]{:S(2)}, u32[]{:S(2)}) collective-permute-start(f32[512,128]{1,0:T(8,128)} %get-tuple-element.54), channel_id=1, source_target_pairs={{0,18},{1,19},{2,16},{3,17},{4,22},{5,23},{6,20},{7,21},{8,26},{9,... | collective-permute-start | bytes 786440 | tf_op jit(solution)/shard_map/ppermute | solution.py:271
  53.8 15.3 %collective-permute-start.16 = (f32[512,128]{1,0:T(8,128)}, f32[512,128]{1,0:T(8,128)S(1)}, u32[]{:S(2)}, u32[]{:S(2)}) collective-permute-start(f32[512,128]{1,0:T(8,128)} %get-tuple-element.52), channel_id=1, source_target_pairs={{0,16},{1,17},{2,18},{3,19},{4,20},{5,21},{6,22},{7,23},{8,24},{9,... | collective-permute-start | bytes 786440 | tf_op jit(solution)/shard_map/ppermute | solution.py:271
  55.2 13.9 %collective-permute-start.15 = (f32[512,128]{1,0:T(8,128)}, f32[512,128]{1,0:T(8,128)S(1)}, u32[]{:S(2)}, u32[]{:S(2)}) collective-permute-start(f32[512,128]{1,0:T(8,128)} %get-tuple-element.50), channel_id=1, source_target_pairs={{0,2},{1,3},{2,0},{3,1},{4,6},{5,7},{6,4},{7,5},{8,10},{9,11},{10,... | collective-permute-start | bytes 786440 | tf_op jit(solution)/shard_map/ppermute | solution.py:271
  60.8 6.9 %collective-permute-start.13 = (bf16[512,128]{1,0:T(8,128)(2,1)S(1)}, bf16[512,128]{1,0:T(8,128)(2,1)S(1)}, u32[]{:S(2)}, u32[]{:S(2)}) collective-permute-start(bf16[512,128]{1,0:T(8,128)(2,1)S(1)} %add_convert_fusion.1.refs_0_), channel_id=1, source_target_pairs={{0,4},{1,5},{2,6},{3,7},{4,8},{5,9},{6,10},{7,11},{8,12},{9,13},{1... | collective-permute-start | bytes 393224 | tf_op jit(solution)/shard_map/ppermute | solution.py:271
  60.9 34.5 %copy-start = (bf16[2048,1024]{1,0:T(8,128)(2,1)S(1)}, bf16[2048,1024]{1,0:T(8,128)(2,1)}, u32[]{:S(2)}) copy-start(bf16[2048,1024]{1,0:T(8,128)(2,1)} %refs_4_.1) | copy-start | bytes 12582916
  60.9 22.4 %collective-permute-start.21 = (bf16[512,128]{1,0:T(8,128)(2,1)S(1)}, bf16[512,128]{1,0:T(8,128)(2,1)S(1)}, u32[]{:S(2)}, u32[]{:S(2)}) collective-permute-start(bf16[512,128]{1,0:T(8,128)(2,1)S(1)} %add_convert_fusion.1.refs_0_), channel_id=1, source_target_pairs={{0,8},{1,9},{2,10},{3,11},{4,12},{5,13},{6,14},{7,15},{8,0},{9,1},... | collective-permute-start | bytes 393224 | tf_op jit(solution)/shard_map/ppermute | solution.py:271
  67.8 15.6 %collective-permute-start.22 = (bf16[512,128]{1,0:T(8,128)(2,1)S(1)}, bf16[512,128]{1,0:T(8,128)(2,1)S(1)}, u32[]{:S(2)}, u32[]{:S(2)}) collective-permute-start(bf16[512,128]{1,0:T(8,128)(2,1)S(1)} %add_convert_fusion.1.refs_0_), channel_id=1, source_target_pairs={{0,12},{1,13},{2,14},{3,15},{4,0},{5,1},{6,2},{7,3},{8,4},{9,5},{1... | collective-permute-start | bytes 393224 | tf_op jit(solution)/shard_map/ppermute | solution.py:271
  68.7 4.5 %collective-permute-start.14 = (bf16[32,1024]{1,0:T(8,128)(2,1)}, bf16[32,1024]{1,0:T(8,128)(2,1)S(1)}, u32[]{:S(2)}, u32[]{:S(2)}) collective-permute-start(bf16[32,1024]{1,0:T(8,128)(2,1)} %get-tuple-element.48), channel_id=1, source_target_pairs={{0,2},{1,3},{2,0},{3,1},{4,6},{5,7},{6,4},{7,5},{8,10},{9,11},{10,... | collective-permute-start | bytes 196616 | tf_op jit(solution)/shard_map/ppermute | solution.py:271
  70.4 7.6 %collective-permute-start.18 = (bf16[512,128]{1,0:T(8,128)(2,1)S(1)}, bf16[512,128]{1,0:T(8,128)(2,1)S(1)}, u32[]{:S(2)}, u32[]{:S(2)}) collective-permute-start(bf16[512,128]{1,0:T(8,128)(2,1)S(1)} %multiply_convert_fusion.refs_0_), channel_id=1, source_target_pairs={{0,4},{1,5},{2,6},{3,7},{4,8},{5,9},{6,10},{7,11},{8,12},{9,13},{1... | collective-permute-start | bytes 393224 | tf_op jit(solution)/shard_map/ppermute | solution.py:271
  72.4 8.8 %collective-permute-start.19 = (bf16[512,128]{1,0:T(8,128)(2,1)S(1)}, bf16[512,128]{1,0:T(8,128)(2,1)S(1)}, u32[]{:S(2)}, u32[]{:S(2)}) collective-permute-start(bf16[512,128]{1,0:T(8,128)(2,1)S(1)} %multiply_convert_fusion.refs_0_), channel_id=1, source_target_pairs={{0,8},{1,9},{2,10},{3,11},{4,12},{5,13},{6,14},{7,15},{8,0},{9,1},... | collective-permute-start | bytes 393224 | tf_op jit(solution)/shard_map/ppermute | solution.py:271
  73.2 8.0 %collective-permute-start.20 = (bf16[512,128]{1,0:T(8,128)(2,1)S(1)}, bf16[512,128]{1,0:T(8,128)(2,1)S(1)}, u32[]{:S(2)}, u32[]{:S(2)}) collective-permute-start(bf16[512,128]{1,0:T(8,128)(2,1)S(1)} %multiply_convert_fusion.refs_0_), channel_id=1, source_target_pairs={{0,12},{1,13},{2,14},{3,15},{4,0},{5,1},{6,2},{7,3},{8,4},{9,5},{1... | collective-permute-start | bytes 393224 | tf_op jit(solution)/shard_map/ppermute | solution.py:271
  84.0 5.2 %collective-permute-start.23 = (bf16[64,1024]{1,0:T(8,128)(2,1)S(1)}, bf16[64,1024]{1,0:T(8,128)(2,1)S(1)}, u32[]{:S(2)}, u32[]{:S(2)}) collective-permute-start(bf16[64,1024]{1,0:T(8,128)(2,1)S(1)} %mix.1.refs_0_), channel_id=1, source_target_pairs={{0,2},{1,3},{2,0},{3,1},{4,6},{5,7},{6,4},{7,5},{8,10},{9,11},{10,... | collective-permute-start | bytes 393224 | tf_op jit(solution)/shard_map/ppermute | solution.py:271
  85.1 8.3 %collective-permute-start.24 = (bf16[64,1024]{1,0:T(8,128)(2,1)S(1)}, bf16[64,1024]{1,0:T(8,128)(2,1)S(1)}, u32[]{:S(2)}, u32[]{:S(2)}) collective-permute-start(bf16[64,1024]{1,0:T(8,128)(2,1)S(1)} %mix.1.refs_0_), channel_id=1, source_target_pairs={{0,4},{1,5},{2,6},{3,7},{4,8},{5,9},{6,10},{7,11},{8,12},{9,13},{1... | collective-permute-start | bytes 393224 | tf_op jit(solution)/shard_map/ppermute | solution.py:271
  87.0 7.1 %collective-permute-start.27 = (bf16[64,1024]{1,0:T(8,128)(2,1)S(1)}, bf16[64,1024]{1,0:T(8,128)(2,1)S(1)}, u32[]{:S(2)}, u32[]{:S(2)}) collective-permute-start(bf16[64,1024]{1,0:T(8,128)(2,1)S(1)} %mix.1.refs_0_), channel_id=1, source_target_pairs={{0,12},{1,13},{2,14},{3,15},{4,0},{5,1},{6,2},{7,3},{8,4},{9,5},{1... | collective-permute-start | bytes 393224 | tf_op jit(solution)/shard_map/ppermute | solution.py:271
  88.9 10.0 %collective-permute-start.26 = (bf16[64,1024]{1,0:T(8,128)(2,1)S(1)}, bf16[64,1024]{1,0:T(8,128)(2,1)S(1)}, u32[]{:S(2)}, u32[]{:S(2)}) collective-permute-start(bf16[64,1024]{1,0:T(8,128)(2,1)S(1)} %mix.1.refs_0_), channel_id=1, source_target_pairs={{0,8},{1,9},{2,10},{3,11},{4,12},{5,13},{6,14},{7,15},{8,0},{9,1},... | collective-permute-start | bytes 393224 | tf_op jit(solution)/shard_map/ppermute | solution.py:271
  93.4 5.5 %collective-permute-start.25 = (bf16[64,1024]{1,0:T(8,128)(2,1)S(1)}, bf16[64,1024]{1,0:T(8,128)(2,1)S(1)}, u32[]{:S(2)}, u32[]{:S(2)}) collective-permute-start(bf16[64,1024]{1,0:T(8,128)(2,1)S(1)} %collective-permute-done.24.refs_1_), channel_id=1, source_target_pairs={{0,2},{1,3},{2,0},{3,1},{4,6},{5,7},{6,4},{7,5},{8,10},{9,11},{10,... | collective-permute-start | bytes 393224 | tf_op jit(solution)/shard_map/ppermute | solution.py:271
  94.2 5.9 %collective-permute-start.29 = (bf16[64,1024]{1,0:T(8,128)(2,1)S(1)}, bf16[64,1024]{1,0:T(8,128)(2,1)S(1)}, u32[]{:S(2)}, u32[]{:S(2)}) collective-permute-start(bf16[64,1024]{1,0:T(8,128)(2,1)S(1)} %collective-permute-done.27.refs_2_), channel_id=1, source_target_pairs={{0,2},{1,3},{2,0},{3,1},{4,6},{5,7},{6,4},{7,5},{8,10},{9,11},{10,... | collective-permute-start | bytes 393224 | tf_op jit(solution)/shard_map/ppermute | solution.py:271
  98.9 5.0 %collective-permute-start.28 = (bf16[64,1024]{1,0:T(8,128)(2,1)S(1)}, bf16[64,1024]{1,0:T(8,128)(2,1)S(1)}, u32[]{:S(2)}, u32[]{:S(2)}) collective-permute-start(bf16[64,1024]{1,0:T(8,128)(2,1)S(1)} %collective-permute-done.26.refs_0_), channel_id=1, source_target_pairs={{0,2},{1,3},{2,0},{3,1},{4,6},{5,7},{6,4},{7,5},{8,10},{9,11},{10,... | collective-permute-start | bytes 393224 | tf_op jit(solution)/shard_map/ppermute | solution.py:271
  100.1 6.7 %copy-start.5 = (bf16[128,1024]{1,0:T(8,128)(2,1)S(1)}, bf16[128,1024]{1,0:T(8,128)(2,1)}, u32[]{:S(2)}) copy-start(bf16[128,1024]{1,0:T(8,128)(2,1)} %param.14) | copy-start | bytes 786436
  105.2 1.6 %collective-permute-start.30 = (bf16[128,1024]{1,0:T(8,128)(2,1)S(1)}, bf16[128,1024]{1,0:T(8,128)(2,1)S(1)}, u32[]{:S(2)}, u32[]{:S(2)}) collective-permute-start(bf16[128,1024]{1,0:T(8,128)(2,1)S(1)} %get-tuple-element.62), channel_id=1, source_target_pairs={{0,1},{1,0},{2,3},{3,2},{4,5},{5,4},{6,7},{7,6},{8,9},{9,8},{10,11... | collective-permute-start | bytes 786440 | tf_op jit(solution)/shard_map/ppermute | solution.py:271

commit v13 on v8

--- a/solution.py
+++ b/solution.py
@@ -30,7 +30,7 @@
 def pack(vision, index, core, groups, pairs, part, name):
     rows, width = vision.shape
     half = rows // 2
-    block = 32
+    block = min(64, half)
     steps = half // block
     count = len(index)
     depth = pairs * part

time: 107 us -> 107 us (level)
  waiting for transfers between devices: 36 us -> 37.1 us
  Pallas kernels: 15.5 us -> 14.4 us
    pallas_call x3, Pallas kernels: 5.32 us -> 4.14 us  [pack(): pl.pallas_call(functools.partial(pack_kernel, groups, pairs, part, count)...]
    ppermute x31, waiting for transfers between devices: 36 us -> 37.1 us  [permute(): return lax.ppermute(array, AXES, perm)]
  transfers between devices with their start and end apart: 31 -> 31, of which waited for: 12 -> 12; matrix products, arithmetic and copies ran while one was open for 3% -> 3% of each run, Pallas kernels for 8% -> 7%
where the time goes in v13:
time: 107 us
  starting transfers between devices  43 us (40%)
  waiting for transfers between devices  37.1 us (35%)
  Pallas kernels  14.4 us (13%)
  local copies, waits for them, and re-layouts  8.42 us (8%)
  other arithmetic  2.76 us (3%)
    ppermute x31, starting transfers between devices, permute(): return lax.ppermute(array, AXES, perm)  43 us
    ppermute x31, waiting for transfers between devices, permute(): return lax.ppermute(array, AXES, perm)  37.1 us
    unnamed x23, local copies, waits for them, and re-layouts  6.28 us
    pallas_call x1, Pallas kernels, project(): pl.pallas_call(functools.partial(project_kernel, count // 2, pairs, shift...  5.08 us
    pallas_call x3, Pallas kernels, pack(): pl.pallas_call(functools.partial(pack_kernel, groups, pairs, part, count)...  4.14 us
  transfers between devices with their start and end apart: 31, of which 12 were waited for; matrix products, arithmetic and copies ran while one was open for 3% of the time, Pallas kernels for 7%

profile of v13, /device:TPU:0, one launch (start us, length us, event | category | flops | bytes accessed | tf_op | source)
XLA Modules:
  0.0 106.7 jit_solution(9417686602669933457)
XLA Ops:
  0.0 1.1 %constant_dynamic-slice_fusion = (bf16[480,256]{1,0:T(8,128)(2,1)S(1)}, bf16[480,256]{1,0:T(8,128)(2,1)S(1)}) fusion(bf16[960,256]{1,0:T(8,128)(2,1)} %param.12, s32[]{:T(128)S(6)} %select_n.62, bf16[960,256]{1,0:T(8,128)(2,1)} %param.11), kind=kLoop, calls=%fused_computation.22 | loop fusion | bytes 983044 | tf_op jit(solution)/shard_map/dynamic_slice | solution.py:314
  1.1 5.1 %collective-permute-start.7 = (bf16[480,512]{1,0:T(8,128)(2,1)S(1)}, bf16[480,512]{1,0:T(8,128)(2,1)S(1)}, u32[]{:S(2)}, u32[]{:S(2)}) collective-permute-start(bf16[480,512]{1,0:T(8,128)(2,1)S(1)} %pad_maximum_fusion.refs_8_), channel_id=1, source_target_pairs={{0,12},{1,13},{2,14},{3,15},{4,0},{5,1},{6,2},{7,3},{8,4},{9,5},{1... | collective-permute-start | bytes 1474568 | tf_op jit(solution)/shard_map/ppermute | solution.py:271
  6.2 0.1 pad_add_fusion.2.index_ref
  6.3 2.1 %copy-done.1 = bf16[256,7680]{1,0:T(8,128)(2,1)S(1)} copy-done((bf16[256,7680]{1,0:T(8,128)(2,1)S(1)}, bf16[256,7680]{1,0:T(8,128)(2,1)}, u32[]{:S(2)}) %copy-start.1) | copy-done | bytes 3932184
  8.4 2.4 %pack_sends.1 = (bf16[128,1920]{1,0:T(8,128)(2,1)}, bf16[128,1920]{1,0:T(8,128)(2,1)}, bf16[128,1920]{1,0:T(8,128)(2,1)}) custom-call(s32[4]{0:T(128)S(1)} %pad_add_fusion.2.index_ref, bf16[256,7680]{1,0:T(8,128)(2,1)S(1)} %copy-done.1), custom_call_target="tpu_custom_call" | custom-call | tf_op jit(solution)/shard_map/pack_sends/pallas_call | solution.py:38
  10.8 2.4 %collective-permute-start.2 = (bf16[128,1920]{1,0:T(8,128)(2,1)}, bf16[128,1920]{1,0:T(8,128)(2,1)S(1)}, u32[]{:S(2)}, u32[]{:S(2)}) collective-permute-start(bf16[128,1920]{1,0:T(8,128)(2,1)} %get-tuple-element.36), channel_id=1, source_target_pairs={{0,18},{1,19},{2,16},{3,17},{4,22},{5,23},{6,20},{7,21},{8,26},{9,... | collective-permute-start | bytes 1474568 | tf_op jit(solution)/shard_map/ppermute | solution.py:271
  13.3 0.5 collective-permute-start.1
  13.8 0.5 collective-permute-start
  14.3 0.1 pad_add_fusion.1
  14.4 2.1 %copy-done.2 = bf16[256,7680]{1,0:T(8,128)(2,1)S(1)} copy-done((bf16[256,7680]{1,0:T(8,128)(2,1)S(1)}, bf16[256,7680]{1,0:T(8,128)(2,1)}, u32[]{:S(2)}) %copy-start.2) | copy-done | bytes 3932184
  16.5 0.9 pack_near.1.refs_0_
  17.4 1.2 %copy-done.3 = bf16[256,7680]{1,0:T(8,128)(2,1)S(1)} copy-done((bf16[256,7680]{1,0:T(8,128)(2,1)S(1)}, bf16[256,7680]{1,0:T(8,128)(2,1)}, u32[]{:S(2)}) %copy-start.3) | copy-done | bytes 3932184
  18.6 0.9 pack_far.1.refs_4_
  19.5 1.3 %collective-permute-start.8 = (bf16[480,512]{1,0:T(8,128)(2,1)S(1)}, bf16[480,512]{1,0:T(8,128)(2,1)}, u32[]{:S(2)}, u32[]{:S(2)}) collective-permute-start(bf16[480,512]{1,0:T(8,128)(2,1)S(1)} %collective-permute-done.7.refs_10_), channel_id=1, source_target_pairs={{4,0},{5,1},{6,2},{7,3},{8,4},{9,5},{10,6},{11,7},{20,16},{21,17},... | collective-permute-start | bytes 1474568 | tf_op jit(solution)/shard_map/ppermute | solution.py:271
  20.8 7.5 %collective-permute-done.6.refs_9_ = bf16[480,512]{1,0:T(8,128)(2,1)S(1)} collective-permute-done((bf16[480,512]{1,0:T(8,128)(2,1)S(1)}, bf16[480,512]{1,0:T(8,128)(2,1)S(1)}, u32[]{:S(2)}, u32[]{:S(2)}) %collective-permute-start.6) | collective-permute-done | bytes 491552 | tf_op jit(solution)/shard_map/ppermute | solution.py:271
  28.3 1.4 %collective-permute-start.9 = (bf16[480,512]{1,0:T(8,128)(2,1)S(1)}, bf16[480,512]{1,0:T(8,128)(2,1)}, u32[]{:S(2)}, u32[]{:S(2)}) collective-permute-start(bf16[480,512]{1,0:T(8,128)(2,1)S(1)} %collective-permute-done.6.refs_9_), channel_id=1, source_target_pairs={{4,8},{5,9},{6,10},{7,11},{8,12},{9,13},{10,14},{11,15},{20,24},{2... | collective-permute-start | bytes 1474568 | tf_op jit(solution)/shard_map/ppermute | solution.py:271
  29.8 5.5 %collective-permute-done.1.refs_2_ = bf16[128,1920]{1,0:T(8,128)(2,1)S(1)} collective-permute-done((bf16[128,1920]{1,0:T(8,128)(2,1)}, bf16[128,1920]{1,0:T(8,128)(2,1)S(1)}, u32[]{:S(2)}, u32[]{:S(2)}) %collective-permute-start.1) | collective-permute-done | bytes 491552 | tf_op jit(solution)/shard_map/ppermute | solution.py:271
  35.3 0.5 collective-permute-start.3
  35.8 0.1 pad_add_fusion.3.scalars
  35.8 3.0 %collective-permute-done.8.refs_11_ = bf16[480,512]{1,0:T(8,128)(2,1)} collective-permute-done((bf16[480,512]{1,0:T(8,128)(2,1)S(1)}, bf16[480,512]{1,0:T(8,128)(2,1)}, u32[]{:S(2)}, u32[]{:S(2)}) %collective-permute-start.8) | collective-permute-done | bytes 491552 | tf_op jit(solution)/shard_map/ppermute | solution.py:271
  38.9 5.1 %project.1 = (f32[512,128]{1,0:T(8,128)S(1)}, f32[512,128]{1,0:T(8,128)}, f32[512,128]{1,0:T(8,128)}, f32[512,128]{1,0:T(8,128)}, f32[512,128]{1,0:T(8,128)S(1)}...) custom-call(s32[2]{0:T(128)S(1)} %pad_add_fusion.3.scalars, ...), custom_call_target="tpu_custom_call" | custom-call | tf_op jit(solution)/shard_map/project/pallas_call | solution.py:91
  44.0 0.7 copy-done.4
  44.7 1.5 %collective-permute-start.10 = (bf16[512,128]{1,0:T(8,128)(2,1)S(1)}, bf16[512,128]{1,0:T(8,128)(2,1)S(1)}, u32[]{:S(2)}, u32[]{:S(2)}) collective-permute-start(bf16[512,128]{1,0:T(8,128)(2,1)S(1)} %get-tuple-element.45), channel_id=1, source_target_pairs={{0,2},{1,3},{2,0},{3,1},{4,6},{5,7},{6,4},{7,5},{8,10},{9,11},{10,... | collective-permute-start | bytes 393224 | tf_op jit(solution)/shard_map/ppermute | solution.py:271
  46.2 1.5 %collective-permute-start.11 = (bf16[512,128]{1,0:T(8,128)(2,1)S(1)}, bf16[512,128]{1,0:T(8,128)(2,1)S(1)}, u32[]{:S(2)}, u32[]{:S(2)}) collective-permute-start(bf16[512,128]{1,0:T(8,128)(2,1)S(1)} %get-tuple-element.46), channel_id=1, source_target_pairs={{0,16},{1,17},{2,18},{3,19},{4,20},{5,21},{6,22},{7,23},{8,24},{9,... | collective-permute-start | bytes 393224 | tf_op jit(solution)/shard_map/ppermute | solution.py:271
  47.7 0.5 collective-permute-start.12
  48.2 1.5 %collective-permute-start.15 = (f32[512,128]{1,0:T(8,128)}, f32[512,128]{1,0:T(8,128)S(1)}, u32[]{:S(2)}, u32[]{:S(2)}) collective-permute-start(f32[512,128]{1,0:T(8,128)} %get-tuple-element.50), channel_id=1, source_target_pairs={{0,2},{1,3},{2,0},{3,1},{4,6},{5,7},{6,4},{7,5},{8,10},{9,11},{10,... | collective-permute-start | bytes 786440 | tf_op jit(solution)/shard_map/ppermute | solution.py:271
  49.7 1.5 %collective-permute-start.16 = (f32[512,128]{1,0:T(8,128)}, f32[512,128]{1,0:T(8,128)S(1)}, u32[]{:S(2)}, u32[]{:S(2)}) collective-permute-start(f32[512,128]{1,0:T(8,128)} %get-tuple-element.52), channel_id=1, source_target_pairs={{0,16},{1,17},{2,18},{3,19},{4,20},{5,21},{6,22},{7,23},{8,24},{9,... | collective-permute-start | bytes 786440 | tf_op jit(solution)/shard_map/ppermute | solution.py:271
  51.2 1.4 %collective-permute-start.17 = (f32[512,128]{1,0:T(8,128)}, f32[512,128]{1,0:T(8,128)S(1)}, u32[]{:S(2)}, u32[]{:S(2)}) collective-permute-start(f32[512,128]{1,0:T(8,128)} %get-tuple-element.54), channel_id=1, source_target_pairs={{0,18},{1,19},{2,16},{3,17},{4,22},{5,23},{6,20},{7,21},{8,26},{9,... | collective-permute-start | bytes 786440 | tf_op jit(solution)/shard_map/ppermute | solution.py:271
  52.6 2.4 %collective-permute-done.12 = bf16[512,128]{1,0:T(8,128)(2,1)S(1)} collective-permute-done((bf16[512,128]{1,0:T(8,128)(2,1)S(1)}, bf16[512,128]{1,0:T(8,128)(2,1)S(1)}, u32[]{:S(2)}, u32[]{:S(2)}) %collective-permute-start.12) | collective-permute-done | bytes 131104 | tf_op jit(solution)/shard_map/ppermute | solution.py:271
  55.0 0.1 add_convert_fusion.1.refs_0_
  55.1 2.5 %collective-permute-start.13 = (bf16[512,128]{1,0:T(8,128)(2,1)S(1)}, bf16[512,128]{1,0:T(8,128)(2,1)S(1)}, u32[]{:S(2)}, u32[]{:S(2)}) collective-permute-start(bf16[512,128]{1,0:T(8,128)(2,1)S(1)} %add_convert_fusion.1.refs_0_), channel_id=1, source_target_pairs={{0,4},{1,5},{2,6},{3,7},{4,8},{5,9},{6,10},{7,11},{8,12},{9,13},{1... | collective-permute-start | bytes 393224 | tf_op jit(solution)/shard_map/ppermute | solution.py:271
  57.6 1.0 constant_dynamic-slice_fusion.3
  58.7 3.4 %collective-permute-start.21 = (bf16[512,128]{1,0:T(8,128)(2,1)S(1)}, bf16[512,128]{1,0:T(8,128)(2,1)S(1)}, u32[]{:S(2)}, u32[]{:S(2)}) collective-permute-start(bf16[512,128]{1,0:T(8,128)(2,1)S(1)} %add_convert_fusion.1.refs_0_), channel_id=1, source_target_pairs={{0,8},{1,9},{2,10},{3,11},{4,12},{5,13},{6,14},{7,15},{8,0},{9,1},... | collective-permute-start | bytes 393224 | tf_op jit(solution)/shard_map/ppermute | solution.py:271
  62.1 1.9 %collective-permute-done.13.refs_1_ = bf16[512,128]{1,0:T(8,128)(2,1)S(1)} collective-permute-done((bf16[512,128]{1,0:T(8,128)(2,1)S(1)}, bf16[512,128]{1,0:T(8,128)(2,1)S(1)}, u32[]{:S(2)}, u32[]{:S(2)}) %collective-permute-start.13) | collective-permute-done | bytes 131104 | tf_op jit(solution)/shard_map/ppermute | solution.py:271
  64.0 2.7 %collective-permute-start.22 = (bf16[512,128]{1,0:T(8,128)(2,1)S(1)}, bf16[512,128]{1,0:T(8,128)(2,1)S(1)}, u32[]{:S(2)}, u32[]{:S(2)}) collective-permute-start(bf16[512,128]{1,0:T(8,128)(2,1)S(1)} %add_convert_fusion.1.refs_0_), channel_id=1, source_target_pairs={{0,12},{1,13},{2,14},{3,15},{4,0},{5,1},{6,2},{7,3},{8,4},{9,5},{1... | collective-permute-start | bytes 393224 | tf_op jit(solution)/shard_map/ppermute | solution.py:271
  66.7 1.4 %collective-permute-start.14 = (bf16[32,1024]{1,0:T(8,128)(2,1)S(1)}, bf16[32,1024]{1,0:T(8,128)(2,1)S(1)}, u32[]{:S(2)}, u32[]{:S(2)}) collective-permute-start(bf16[32,1024]{1,0:T(8,128)(2,1)S(1)} %get-tuple-element.48), channel_id=1, source_target_pairs={{0,2},{1,3},{2,0},{3,1},{4,6},{5,7},{6,4},{7,5},{8,10},{9,11},{10,... | collective-permute-start | bytes 196616 | tf_op jit(solution)/shard_map/ppermute | solution.py:271
  68.1 1.1 %multiply_reduce_fusion = (f32[512]{0:T(512)S(1)}, f32[512,128]{1,0:T(8,128)S(1)}) fusion(f32[512,128]{1,0:T(8,128)S(1)} %collective-permute-done.17, f32[512,128]{1,0:T(8,128)S(1)} %collective-permute-done.16, f32[512,128]{1,0:T(8,128)} %copy-done.4, f32[512,128]{1,0:T(8,128)S(1)} %collective-permute-done.15), kind=kLoop, calls=%fused_computation.8 | loop fusion | flops 327168 | bytes 1312768 | tf_op jit(solution)/shard_map/reduce_sum | solution.py:232
  69.2 0.1 multiply_convert_fusion.refs_0_
  69.4 1.5 %collective-permute-start.19 = (bf16[512,128]{1,0:T(8,128)(2,1)S(1)}, bf16[512,128]{1,0:T(8,128)(2,1)S(1)}, u32[]{:S(2)}, u32[]{:S(2)}) collective-permute-start(bf16[512,128]{1,0:T(8,128)(2,1)S(1)} %multiply_convert_fusion.refs_0_), channel_id=1, source_target_pairs={{0,8},{1,9},{2,10},{3,11},{4,12},{5,13},{6,14},{7,15},{8,0},{9,1},... | collective-permute-start | bytes 393224 | tf_op jit(solution)/shard_map/ppermute | solution.py:271
  70.9 0.1 collective-permute-done.14
  70.9 2.3 %collective-permute-start.20 = (bf16[512,128]{1,0:T(8,128)(2,1)S(1)}, bf16[512,128]{1,0:T(8,128)(2,1)S(1)}, u32[]{:S(2)}, u32[]{:S(2)}) collective-permute-start(bf16[512,128]{1,0:T(8,128)(2,1)S(1)} %multiply_convert_fusion.refs_0_), channel_id=1, source_target_pairs={{0,12},{1,13},{2,14},{3,15},{4,0},{5,1},{6,2},{7,3},{8,4},{9,5},{1... | collective-permute-start | bytes 393224 | tf_op jit(solution)/shard_map/ppermute | solution.py:271
  73.4 0.1 fusion
  73.6 0.1 fusion.2.q_ref
  73.7 2.6 %collective-permute-done.18.refs_1_ = bf16[512,128]{1,0:T(8,128)(2,1)S(1)} collective-permute-done((bf16[512,128]{1,0:T(8,128)(2,1)S(1)}, bf16[512,128]{1,0:T(8,128)(2,1)S(1)}, u32[]{:S(2)}, u32[]{:S(2)}) %collective-permute-start.18) | collective-permute-done | bytes 131104 | tf_op jit(solution)/shard_map/ppermute | solution.py:271
  76.3 2.9 %collective-permute-done.19.refs_2_ = bf16[512,128]{1,0:T(8,128)(2,1)S(1)} collective-permute-done((bf16[512,128]{1,0:T(8,128)(2,1)S(1)}, bf16[512,128]{1,0:T(8,128)(2,1)S(1)}, u32[]{:S(2)}, u32[]{:S(2)}) %collective-permute-start.19) | collective-permute-done | bytes 131104 | tf_op jit(solution)/shard_map/ppermute | solution.py:271
  79.3 2.0 %score.1 = (bf16[512,2048]{1,0:T(8,128)(2,1)S(1)}, f32[512,128]{1,0:T(8,128)S(1)}) custom-call(bf16[512,128]{1,0:T(8,128)(2,1)S(1)} %fusion.2.q_ref, bf16[512,128]{1,0:T(8,128)(2,1)S(1)} %multiply_convert_fusion.refs_0_, bf16[512,128]{1,0:T(8,128)(2,1)S(1)} %collective-permute-done.18.refs_1_, bf16[512,128]{1,0:T(8,128)(2,1)S(1)} %collective-permute-done.19.refs_2_, ...), custom_call_target="tpu_custom_call" | custom-call | tf_op jit(solution)/shard_map/score/pallas_call | solution.py:131
  81.3 0.7 mix.1.refs_0_
  82.0 1.1 %collective-permute-start.23 = (bf16[64,1024]{1,0:T(8,128)(2,1)S(1)}, bf16[64,1024]{1,0:T(8,128)(2,1)S(1)}, u32[]{:S(2)}, u32[]{:S(2)}) collective-permute-start(bf16[64,1024]{1,0:T(8,128)(2,1)S(1)} %mix.1.refs_0_), channel_id=1, source_target_pairs={{0,2},{1,3},{2,0},{3,1},{4,6},{5,7},{6,4},{7,5},{8,10},{9,11},{10,... | collective-permute-start | bytes 393224 | tf_op jit(solution)/shard_map/ppermute | solution.py:271
  83.1 2.1 %collective-permute-start.24 = (bf16[64,1024]{1,0:T(8,128)(2,1)S(1)}, bf16[64,1024]{1,0:T(8,128)(2,1)S(1)}, u32[]{:S(2)}, u32[]{:S(2)}) collective-permute-start(bf16[64,1024]{1,0:T(8,128)(2,1)S(1)} %mix.1.refs_0_), channel_id=1, source_target_pairs={{0,4},{1,5},{2,6},{3,7},{4,8},{5,9},{6,10},{7,11},{8,12},{9,13},{1... | collective-permute-start | bytes 393224 | tf_op jit(solution)/shard_map/ppermute | solution.py:271
  85.3 1.9 %collective-permute-start.27 = (bf16[64,1024]{1,0:T(8,128)(2,1)S(1)}, bf16[64,1024]{1,0:T(8,128)(2,1)S(1)}, u32[]{:S(2)}, u32[]{:S(2)}) collective-permute-start(bf16[64,1024]{1,0:T(8,128)(2,1)S(1)} %mix.1.refs_0_), channel_id=1, source_target_pairs={{0,12},{1,13},{2,14},{3,15},{4,0},{5,1},{6,2},{7,3},{8,4},{9,5},{1... | collective-permute-start | bytes 393224 | tf_op jit(solution)/shard_map/ppermute | solution.py:271
  87.2 0.6 collective-permute-start.26
  87.8 3.8 %collective-permute-done.24.refs_1_ = bf16[64,1024]{1,0:T(8,128)(2,1)S(1)} collective-permute-done((bf16[64,1024]{1,0:T(8,128)(2,1)S(1)}, bf16[64,1024]{1,0:T(8,128)(2,1)S(1)}, u32[]{:S(2)}, u32[]{:S(2)}) %collective-permute-start.24) | collective-permute-done | bytes 131104 | tf_op jit(solution)/shard_map/ppermute | solution.py:271
  91.6 1.4 %collective-permute-start.25 = (bf16[64,1024]{1,0:T(8,128)(2,1)S(1)}, bf16[64,1024]{1,0:T(8,128)(2,1)S(1)}, u32[]{:S(2)}, u32[]{:S(2)}) collective-permute-start(bf16[64,1024]{1,0:T(8,128)(2,1)S(1)} %collective-permute-done.24.refs_1_), channel_id=1, source_target_pairs={{0,2},{1,3},{2,0},{3,1},{4,6},{5,7},{6,4},{7,5},{8,10},{9,11},{10,... | collective-permute-start | bytes 393224 | tf_op jit(solution)/shard_map/ppermute | solution.py:271
  93.0 0.6 collective-permute-start.29
  93.6 0.6 output_near.1.refs_5_
  94.2 3.7 %collective-permute-done.26.refs_0_ = bf16[64,1024]{1,0:T(8,128)(2,1)S(1)} collective-permute-done((bf16[64,1024]{1,0:T(8,128)(2,1)S(1)}, bf16[64,1024]{1,0:T(8,128)(2,1)S(1)}, u32[]{:S(2)}, u32[]{:S(2)}) %collective-permute-start.26) | collective-permute-done | bytes 131104 | tf_op jit(solution)/shard_map/ppermute | solution.py:271
  97.9 1.7 %collective-permute-start.28 = (bf16[64,1024]{1,0:T(8,128)(2,1)S(1)}, bf16[64,1024]{1,0:T(8,128)(2,1)S(1)}, u32[]{:S(2)}, u32[]{:S(2)}) collective-permute-start(bf16[64,1024]{1,0:T(8,128)(2,1)S(1)} %collective-permute-done.26.refs_0_), channel_id=1, source_target_pairs={{0,2},{1,3},{2,0},{3,1},{4,6},{5,7},{6,4},{7,5},{8,10},{9,11},{10,... | collective-permute-start | bytes 393224 | tf_op jit(solution)/shard_map/ppermute | solution.py:271
  99.6 0.1 pad_add_fusion.scalars
  99.7 0.5 output_far.1.refs_6_
  100.2 2.7 %collective-permute-done.28.refs_2_ = bf16[64,1024]{1,0:T(8,128)(2,1)S(1)} collective-permute-done((bf16[64,1024]{1,0:T(8,128)(2,1)S(1)}, bf16[64,1024]{1,0:T(8,128)(2,1)S(1)}, u32[]{:S(2)}, u32[]{:S(2)}) %collective-permute-start.28) | collective-permute-done | bytes 131104 | tf_op jit(solution)/shard_map/ppermute | solution.py:271
  102.9 1.3 %output_other.1 = (f32[128,1024]{1,0:T(8,128)S(1)}, bf16[128,1024]{1,0:T(8,128)(2,1)S(1)}) custom-call(s32[3]{0:T(128)S(1)} %pad_add_fusion.scalars, bf16[64,1024]{1,0:T(8,128)(2,1)S(1)} %collective-permute-done.23.refs_0_, bf16[64,1024]{1,0:T(8,128)(2,1)S(1)} %collective-permute-done.25.refs_1_, bf16[64,1024]{1,0:T(8,128)(2,1)S(1)} %collective-permute-done.28.refs_2_, ...), custom_call_target="tpu_custom_call" | custom-call | tf_op jit(solution)/shard_map/output_other/pallas_call | solution.py:210
  104.2 0.1 collective-permute-start.30
  105.0 0.8 collective-permute-done.30
  105.8 0.8 add_convert_fusion
  (47 shorter events, 0.3 us)
Async XLA Ops:
  1.1 18.4 %collective-permute-start.7 = (bf16[480,512]{1,0:T(8,128)(2,1)S(1)}, bf16[480,512]{1,0:T(8,128)(2,1)S(1)}, u32[]{:S(2)}, u32[]{:S(2)}) collective-permute-start(bf16[480,512]{1,0:T(8,128)(2,1)S(1)} %pad_maximum_fusion.refs_8_), channel_id=1, source_target_pairs={{0,12},{1,13},{2,14},{3,15},{4,0},{5,1},{6,2},{7,3},{8,4},{9,5},{1... | collective-permute-start | bytes 1474568 | tf_op jit(solution)/shard_map/ppermute | solution.py:271
  6.2 22.1 %collective-permute-start.6 = (bf16[480,512]{1,0:T(8,128)(2,1)S(1)}, bf16[480,512]{1,0:T(8,128)(2,1)S(1)}, u32[]{:S(2)}, u32[]{:S(2)}) collective-permute-start(bf16[480,512]{1,0:T(8,128)(2,1)S(1)} %pad_maximum_fusion.refs_8_), channel_id=1, source_target_pairs={{0,4},{1,5},{2,6},{3,7},{4,8},{5,9},{6,10},{7,11},{8,12},{9,13},{1... | collective-permute-start | bytes 1474568 | tf_op jit(solution)/shard_map/ppermute | solution.py:271
  6.3 2.1 %copy-start.1 = (bf16[256,7680]{1,0:T(8,128)(2,1)S(1)}, bf16[256,7680]{1,0:T(8,128)(2,1)}, u32[]{:S(2)}) copy-start(bf16[256,7680]{1,0:T(8,128)(2,1)} %rows_ref.3) | copy-start | bytes 11796484
  10.8 18.9 %collective-permute-start.2 = (bf16[128,1920]{1,0:T(8,128)(2,1)}, bf16[128,1920]{1,0:T(8,128)(2,1)S(1)}, u32[]{:S(2)}, u32[]{:S(2)}) collective-permute-start(bf16[128,1920]{1,0:T(8,128)(2,1)} %get-tuple-element.36), channel_id=1, source_target_pairs={{0,18},{1,19},{2,16},{3,17},{4,22},{5,23},{6,20},{7,21},{8,26},{9,... | collective-permute-start | bytes 1474568 | tf_op jit(solution)/shard_map/ppermute | solution.py:271
  13.3 22.0 %collective-permute-start.1 = (bf16[128,1920]{1,0:T(8,128)(2,1)}, bf16[128,1920]{1,0:T(8,128)(2,1)S(1)}, u32[]{:S(2)}, u32[]{:S(2)}) collective-permute-start(bf16[128,1920]{1,0:T(8,128)(2,1)} %get-tuple-element.35), channel_id=1, source_target_pairs={{0,16},{1,17},{2,18},{3,19},{4,20},{5,21},{6,22},{7,23},{8,24},{9,... | collective-permute-start | bytes 1474568 | tf_op jit(solution)/shard_map/ppermute | solution.py:271
  13.8 21.5 %collective-permute-start = (bf16[128,1920]{1,0:T(8,128)(2,1)}, bf16[128,1920]{1,0:T(8,128)(2,1)}, u32[]{:S(2)}, u32[]{:S(2)}) collective-permute-start(bf16[128,1920]{1,0:T(8,128)(2,1)} %get-tuple-element.34), channel_id=1, source_target_pairs={{0,2},{1,3},{2,0},{3,1},{4,6},{5,7},{6,4},{7,5},{8,10},{9,11},{10,... | collective-permute-start | bytes 1474568 | tf_op jit(solution)/shard_map/ppermute | solution.py:271
  14.4 2.1 %copy-start.2 = (bf16[256,7680]{1,0:T(8,128)(2,1)S(1)}, bf16[256,7680]{1,0:T(8,128)(2,1)}, u32[]{:S(2)}) copy-start(bf16[256,7680]{1,0:T(8,128)(2,1)} %rows_ref.3) | copy-start | bytes 11796484
  16.5 2.1 %copy-start.3 = (bf16[256,7680]{1,0:T(8,128)(2,1)S(1)}, bf16[256,7680]{1,0:T(8,128)(2,1)}, u32[]{:S(2)}) copy-start(bf16[256,7680]{1,0:T(8,128)(2,1)} %rows_ref.3) | copy-start | bytes 11796484
  19.5 19.4 %collective-permute-start.8 = (bf16[480,512]{1,0:T(8,128)(2,1)S(1)}, bf16[480,512]{1,0:T(8,128)(2,1)}, u32[]{:S(2)}, u32[]{:S(2)}) collective-permute-start(bf16[480,512]{1,0:T(8,128)(2,1)S(1)} %collective-permute-done.7.refs_10_), channel_id=1, source_target_pairs={{4,0},{5,1},{6,2},{7,3},{8,4},{9,5},{10,6},{11,7},{20,16},{21,17},... | collective-permute-start | bytes 1474568 | tf_op jit(solution)/shard_map/ppermute | solution.py:271
  28.3 10.5 %collective-permute-start.9 = (bf16[480,512]{1,0:T(8,128)(2,1)S(1)}, bf16[480,512]{1,0:T(8,128)(2,1)}, u32[]{:S(2)}, u32[]{:S(2)}) collective-permute-start(bf16[480,512]{1,0:T(8,128)(2,1)S(1)} %collective-permute-done.6.refs_9_), channel_id=1, source_target_pairs={{4,8},{5,9},{6,10},{7,11},{8,12},{9,13},{10,14},{11,15},{20,24},{2... | collective-permute-start | bytes 1474568 | tf_op jit(solution)/shard_map/ppermute | solution.py:271
  29.8 9.1 %collective-permute-start.5 = (bf16[128,1920]{1,0:T(8,128)(2,1)S(1)}, bf16[128,1920]{1,0:T(8,128)(2,1)}, u32[]{:S(2)}, u32[]{:S(2)}) collective-permute-start(bf16[128,1920]{1,0:T(8,128)(2,1)S(1)} %collective-permute-done.2.refs_3_), channel_id=1, source_target_pairs={{0,1},{1,0},{2,3},{3,2},{4,5},{5,4},{6,7},{7,6},{8,9},{9,8},{10,11... | collective-permute-start | bytes 1474568 | tf_op jit(solution)/shard_map/ppermute | solution.py:271
  35.2 3.7 %collective-permute-start.4 = (bf16[128,1920]{1,0:T(8,128)(2,1)S(1)}, bf16[128,1920]{1,0:T(8,128)(2,1)}, u32[]{:S(2)}, u32[]{:S(2)}) collective-permute-start(bf16[128,1920]{1,0:T(8,128)(2,1)S(1)} %collective-permute-done.1.refs_2_), channel_id=1, source_target_pairs={{0,1},{1,0},{2,3},{3,2},{4,5},{5,4},{6,7},{7,6},{8,9},{9,8},{10,11... | collective-permute-start | bytes 1474568 | tf_op jit(solution)/shard_map/ppermute | solution.py:271
  35.3 3.6 %collective-permute-start.3 = (bf16[128,1920]{1,0:T(8,128)(2,1)}, bf16[128,1920]{1,0:T(8,128)(2,1)}, u32[]{:S(2)}, u32[]{:S(2)}) collective-permute-start(bf16[128,1920]{1,0:T(8,128)(2,1)} %collective-permute-done.refs_1_), channel_id=1, source_target_pairs={{0,1},{1,0},{2,3},{3,2},{4,5},{5,4},{6,7},{7,6},{8,9},{9,8},{10,11... | collective-permute-start | bytes 1474568 | tf_op jit(solution)/shard_map/ppermute | solution.py:271
  35.8 33.3 %copy-start.6 = (f32[128]{0:T(128)S(1)}, f32[128]{0:T(128)}, u32[]{:S(2)}) copy-start(f32[128]{0:T(128)} %param.16) | copy-start | bytes 1540
  35.8 37.7 %copy-start.7 = (f32[128]{0:T(128)S(1)}, f32[128]{0:T(128)}, u32[]{:S(2)}) copy-start(f32[128]{0:T(128)} %param.15) | copy-start | bytes 1540
  44.0 0.7 copy-start.4
  44.7 6.5 %collective-permute-start.10 = (bf16[512,128]{1,0:T(8,128)(2,1)S(1)}, bf16[512,128]{1,0:T(8,128)(2,1)S(1)}, u32[]{:S(2)}, u32[]{:S(2)}) collective-permute-start(bf16[512,128]{1,0:T(8,128)(2,1)S(1)} %get-tuple-element.45), channel_id=1, source_target_pairs={{0,2},{1,3},{2,0},{3,1},{4,6},{5,7},{6,4},{7,5},{8,10},{9,11},{10,... | collective-permute-start | bytes 393224 | tf_op jit(solution)/shard_map/ppermute | solution.py:271
  46.2 6.4 %collective-permute-start.11 = (bf16[512,128]{1,0:T(8,128)(2,1)S(1)}, bf16[512,128]{1,0:T(8,128)(2,1)S(1)}, u32[]{:S(2)}, u32[]{:S(2)}) collective-permute-start(bf16[512,128]{1,0:T(8,128)(2,1)S(1)} %get-tuple-element.46), channel_id=1, source_target_pairs={{0,16},{1,17},{2,18},{3,19},{4,20},{5,21},{6,22},{7,23},{8,24},{9,... | collective-permute-start | bytes 393224 | tf_op jit(solution)/shard_map/ppermute | solution.py:271
  47.7 7.3 %collective-permute-start.12 = (bf16[512,128]{1,0:T(8,128)(2,1)S(1)}, bf16[512,128]{1,0:T(8,128)(2,1)S(1)}, u32[]{:S(2)}, u32[]{:S(2)}) collective-permute-start(bf16[512,128]{1,0:T(8,128)(2,1)S(1)} %get-tuple-element.47), channel_id=1, source_target_pairs={{0,18},{1,19},{2,16},{3,17},{4,22},{5,23},{6,20},{7,21},{8,26},{9,... | collective-permute-start | bytes 393224 | tf_op jit(solution)/shard_map/ppermute | solution.py:271
  48.2 18.5 %collective-permute-start.15 = (f32[512,128]{1,0:T(8,128)}, f32[512,128]{1,0:T(8,128)S(1)}, u32[]{:S(2)}, u32[]{:S(2)}) collective-permute-start(f32[512,128]{1,0:T(8,128)} %get-tuple-element.50), channel_id=1, source_target_pairs={{0,2},{1,3},{2,0},{3,1},{4,6},{5,7},{6,4},{7,5},{8,10},{9,11},{10,... | collective-permute-start | bytes 786440 | tf_op jit(solution)/shard_map/ppermute | solution.py:271
  49.7 18.4 %collective-permute-start.16 = (f32[512,128]{1,0:T(8,128)}, f32[512,128]{1,0:T(8,128)S(1)}, u32[]{:S(2)}, u32[]{:S(2)}) collective-permute-start(f32[512,128]{1,0:T(8,128)} %get-tuple-element.52), channel_id=1, source_target_pairs={{0,16},{1,17},{2,18},{3,19},{4,20},{5,21},{6,22},{7,23},{8,24},{9,... | collective-permute-start | bytes 786440 | tf_op jit(solution)/shard_map/ppermute | solution.py:271
  51.2 16.9 %collective-permute-start.17 = (f32[512,128]{1,0:T(8,128)}, f32[512,128]{1,0:T(8,128)S(1)}, u32[]{:S(2)}, u32[]{:S(2)}) collective-permute-start(f32[512,128]{1,0:T(8,128)} %get-tuple-element.54), channel_id=1, source_target_pairs={{0,18},{1,19},{2,16},{3,17},{4,22},{5,23},{6,20},{7,21},{8,26},{9,... | collective-permute-start | bytes 786440 | tf_op jit(solution)/shard_map/ppermute | solution.py:271
  55.1 8.9 %collective-permute-start.13 = (bf16[512,128]{1,0:T(8,128)(2,1)S(1)}, bf16[512,128]{1,0:T(8,128)(2,1)S(1)}, u32[]{:S(2)}, u32[]{:S(2)}) collective-permute-start(bf16[512,128]{1,0:T(8,128)(2,1)S(1)} %add_convert_fusion.1.refs_0_), channel_id=1, source_target_pairs={{0,4},{1,5},{2,6},{3,7},{4,8},{5,9},{6,10},{7,11},{8,12},{9,13},{1... | collective-permute-start | bytes 393224 | tf_op jit(solution)/shard_map/ppermute | solution.py:271
  57.6 36.0 %copy-start = (bf16[2048,1024]{1,0:T(8,128)(2,1)S(1)}, bf16[2048,1024]{1,0:T(8,128)(2,1)}, u32[]{:S(2)}) copy-start(bf16[2048,1024]{1,0:T(8,128)(2,1)} %refs_4_.1) | copy-start | bytes 12582916
  58.7 22.7 %collective-permute-start.21 = (bf16[512,128]{1,0:T(8,128)(2,1)S(1)}, bf16[512,128]{1,0:T(8,128)(2,1)S(1)}, u32[]{:S(2)}, u32[]{:S(2)}) collective-permute-start(bf16[512,128]{1,0:T(8,128)(2,1)S(1)} %add_convert_fusion.1.refs_0_), channel_id=1, source_target_pairs={{0,8},{1,9},{2,10},{3,11},{4,12},{5,13},{6,14},{7,15},{8,0},{9,1},... | collective-permute-start | bytes 393224 | tf_op jit(solution)/shard_map/ppermute | solution.py:271
  64.0 17.3 %collective-permute-start.22 = (bf16[512,128]{1,0:T(8,128)(2,1)S(1)}, bf16[512,128]{1,0:T(8,128)(2,1)S(1)}, u32[]{:S(2)}, u32[]{:S(2)}) collective-permute-start(bf16[512,128]{1,0:T(8,128)(2,1)S(1)} %add_convert_fusion.1.refs_0_), channel_id=1, source_target_pairs={{0,12},{1,13},{2,14},{3,15},{4,0},{5,1},{6,2},{7,3},{8,4},{9,5},{1... | collective-permute-start | bytes 393224 | tf_op jit(solution)/shard_map/ppermute | solution.py:271
  66.7 4.3 %collective-permute-start.14 = (bf16[32,1024]{1,0:T(8,128)(2,1)S(1)}, bf16[32,1024]{1,0:T(8,128)(2,1)S(1)}, u32[]{:S(2)}, u32[]{:S(2)}) collective-permute-start(bf16[32,1024]{1,0:T(8,128)(2,1)S(1)} %get-tuple-element.48), channel_id=1, source_target_pairs={{0,2},{1,3},{2,0},{3,1},{4,6},{5,7},{6,4},{7,5},{8,10},{9,11},{10,... | collective-permute-start | bytes 196616 | tf_op jit(solution)/shard_map/ppermute | solution.py:271
  69.3 7.0 %collective-permute-start.18 = (bf16[512,128]{1,0:T(8,128)(2,1)S(1)}, bf16[512,128]{1,0:T(8,128)(2,1)S(1)}, u32[]{:S(2)}, u32[]{:S(2)}) collective-permute-start(bf16[512,128]{1,0:T(8,128)(2,1)S(1)} %multiply_convert_fusion.refs_0_), channel_id=1, source_target_pairs={{0,4},{1,5},{2,6},{3,7},{4,8},{5,9},{6,10},{7,11},{8,12},{9,13},{1... | collective-permute-start | bytes 393224 | tf_op jit(solution)/shard_map/ppermute | solution.py:271
  69.4 9.9 %collective-permute-start.19 = (bf16[512,128]{1,0:T(8,128)(2,1)S(1)}, bf16[512,128]{1,0:T(8,128)(2,1)S(1)}, u32[]{:S(2)}, u32[]{:S(2)}) collective-permute-start(bf16[512,128]{1,0:T(8,128)(2,1)S(1)} %multiply_convert_fusion.refs_0_), channel_id=1, source_target_pairs={{0,8},{1,9},{2,10},{3,11},{4,12},{5,13},{6,14},{7,15},{8,0},{9,1},... | collective-permute-start | bytes 393224 | tf_op jit(solution)/shard_map/ppermute | solution.py:271
  70.9 8.3 %collective-permute-start.20 = (bf16[512,128]{1,0:T(8,128)(2,1)S(1)}, bf16[512,128]{1,0:T(8,128)(2,1)S(1)}, u32[]{:S(2)}, u32[]{:S(2)}) collective-permute-start(bf16[512,128]{1,0:T(8,128)(2,1)S(1)} %multiply_convert_fusion.refs_0_), channel_id=1, source_target_pairs={{0,12},{1,13},{2,14},{3,15},{4,0},{5,1},{6,2},{7,3},{8,4},{9,5},{1... | collective-permute-start | bytes 393224 | tf_op jit(solution)/shard_map/ppermute | solution.py:271
  82.0 5.7 %collective-permute-start.23 = (bf16[64,1024]{1,0:T(8,128)(2,1)S(1)}, bf16[64,1024]{1,0:T(8,128)(2,1)S(1)}, u32[]{:S(2)}, u32[]{:S(2)}) collective-permute-start(bf16[64,1024]{1,0:T(8,128)(2,1)S(1)} %mix.1.refs_0_), channel_id=1, source_target_pairs={{0,2},{1,3},{2,0},{3,1},{4,6},{5,7},{6,4},{7,5},{8,10},{9,11},{10,... | collective-permute-start | bytes 393224 | tf_op jit(solution)/shard_map/ppermute | solution.py:271
  83.1 8.4 %collective-permute-start.24 = (bf16[64,1024]{1,0:T(8,128)(2,1)S(1)}, bf16[64,1024]{1,0:T(8,128)(2,1)S(1)}, u32[]{:S(2)}, u32[]{:S(2)}) collective-permute-start(bf16[64,1024]{1,0:T(8,128)(2,1)S(1)} %mix.1.refs_0_), channel_id=1, source_target_pairs={{0,4},{1,5},{2,6},{3,7},{4,8},{5,9},{6,10},{7,11},{8,12},{9,13},{1... | collective-permute-start | bytes 393224 | tf_op jit(solution)/shard_map/ppermute | solution.py:271
  85.3 7.7 %collective-permute-start.27 = (bf16[64,1024]{1,0:T(8,128)(2,1)S(1)}, bf16[64,1024]{1,0:T(8,128)(2,1)S(1)}, u32[]{:S(2)}, u32[]{:S(2)}) collective-permute-start(bf16[64,1024]{1,0:T(8,128)(2,1)S(1)} %mix.1.refs_0_), channel_id=1, source_target_pairs={{0,12},{1,13},{2,14},{3,15},{4,0},{5,1},{6,2},{7,3},{8,4},{9,5},{1... | collective-permute-start | bytes 393224 | tf_op jit(solution)/shard_map/ppermute | solution.py:271
  87.2 10.7 %collective-permute-start.26 = (bf16[64,1024]{1,0:T(8,128)(2,1)S(1)}, bf16[64,1024]{1,0:T(8,128)(2,1)S(1)}, u32[]{:S(2)}, u32[]{:S(2)}) collective-permute-start(bf16[64,1024]{1,0:T(8,128)(2,1)S(1)} %mix.1.refs_0_), channel_id=1, source_target_pairs={{0,8},{1,9},{2,10},{3,11},{4,12},{5,13},{6,14},{7,15},{8,0},{9,1},... | collective-permute-start | bytes 393224 | tf_op jit(solution)/shard_map/ppermute | solution.py:271
  91.6 6.4 %collective-permute-start.25 = (bf16[64,1024]{1,0:T(8,128)(2,1)S(1)}, bf16[64,1024]{1,0:T(8,128)(2,1)S(1)}, u32[]{:S(2)}, u32[]{:S(2)}) collective-permute-start(bf16[64,1024]{1,0:T(8,128)(2,1)S(1)} %collective-permute-done.24.refs_1_), channel_id=1, source_target_pairs={{0,2},{1,3},{2,0},{3,1},{4,6},{5,7},{6,4},{7,5},{8,10},{9,11},{10,... | collective-permute-start | bytes 393224 | tf_op jit(solution)/shard_map/ppermute | solution.py:271
  93.0 7.2 %collective-permute-start.29 = (bf16[64,1024]{1,0:T(8,128)(2,1)S(1)}, bf16[64,1024]{1,0:T(8,128)(2,1)S(1)}, u32[]{:S(2)}, u32[]{:S(2)}) collective-permute-start(bf16[64,1024]{1,0:T(8,128)(2,1)S(1)} %collective-permute-done.27.refs_2_), channel_id=1, source_target_pairs={{0,2},{1,3},{2,0},{3,1},{4,6},{5,7},{6,4},{7,5},{8,10},{9,11},{10,... | collective-permute-start | bytes 393224 | tf_op jit(solution)/shard_map/ppermute | solution.py:271
  97.9 5.0 %collective-permute-start.28 = (bf16[64,1024]{1,0:T(8,128)(2,1)S(1)}, bf16[64,1024]{1,0:T(8,128)(2,1)S(1)}, u32[]{:S(2)}, u32[]{:S(2)}) collective-permute-start(bf16[64,1024]{1,0:T(8,128)(2,1)S(1)} %collective-permute-done.26.refs_0_), channel_id=1, source_target_pairs={{0,2},{1,3},{2,0},{3,1},{4,6},{5,7},{6,4},{7,5},{8,10},{9,11},{10,... | collective-permute-start | bytes 393224 | tf_op jit(solution)/shard_map/ppermute | solution.py:271
  100.2 5.7 %copy-start.5 = (bf16[128,1024]{1,0:T(8,128)(2,1)S(1)}, bf16[128,1024]{1,0:T(8,128)(2,1)}, u32[]{:S(2)}) copy-start(bf16[128,1024]{1,0:T(8,128)(2,1)} %param.14) | copy-start | bytes 786436
  104.2 1.6 %collective-permute-start.30 = (bf16[128,1024]{1,0:T(8,128)(2,1)S(1)}, bf16[128,1024]{1,0:T(8,128)(2,1)S(1)}, u32[]{:S(2)}, u32[]{:S(2)}) collective-permute-start(bf16[128,1024]{1,0:T(8,128)(2,1)S(1)} %get-tuple-element.62), channel_id=1, source_target_pairs={{0,1},{1,0},{2,3},{3,2},{4,5},{5,4},{6,7},{7,6},{8,9},{9,8},{10,11... | collective-permute-start | bytes 786440 | tf_op jit(solution)/shard_map/ppermute | solution.py:271
